TPU v7x, 128 devices: a whole 4x4x4 slice. The times are simulated.
128 devices in a mesh: row: 8 (over y, x_hi), col: 16 (over x_lo, z, core).
Axes of the slice: x: 4 (x_hi: 2, x_lo: 2; x = x_hi * 2 + x_lo), y: 4, z: 4, core: 2. Of those that a mesh axis runs over, the one named last changes fastest.
Arguments:
- weight: bfloat16 [4096, 8192], P('row', 'col'), may hold values from -0.4375 to 0.4375
- anchor: bfloat16 [4096, 8192], P('row', 'col'), may hold values from -0.4375 to 0.4375
- input_factor: bfloat16 [8192, 8192], P('row', 'col'), may hold values from -2 to 50
- output_factor: bfloat16 [4096, 4096], P('row', 'col'), may hold values from -8 to 200
- task_grad: bfloat16 [4096, 8192], P(('row', 'col')), may hold values from -6 to 6
Outputs:
- updated_grad: bfloat16 [4096, 8192], P(('row', 'col'))
All inputs are finite; a program needn't handle non-finite values.
Results may differ from a plain program's by a relative error of at most 0.0059.
Values may be sent and summed in bfloat16 or wider, within the bound.
No kernel may reach another device: no remote copies, remote signals or barrier semaphores. Data moves between devices by JAX's collectives and lax.ppermute only.
A program may use at most 64 MiB of HBM per device.

v0:
```python
import jax
import jax.numpy as jnp
from jax import lax
from jax.sharding import PartitionSpec as P


def body(weight, anchor, input_factor, output_factor, task_grad):
    change = (weight.astype(jnp.float32) - anchor.astype(jnp.float32)).astype(jnp.bfloat16)
    factor_cols = lax.all_gather(input_factor, "row", axis=0, tiled=True)
    factor_piece = factor_cols
    projected = jnp.dot(
        lax.all_gather(change, "col", axis=1, tiled=True),
        factor_piece,
        preferred_element_type=jnp.float32,
    )
    projected = projected.astype(jnp.bfloat16)
    output_full = lax.all_gather(output_factor, "col", axis=1, tiled=True)
    factor_piece = output_full
    penalty = jnp.dot(
        factor_piece,
        lax.all_gather(projected, "row", axis=0, tiled=True),
        preferred_element_type=jnp.float32,
    )
    owned_rows = lax.all_to_all(penalty, "col", split_axis=0, concat_axis=1, tiled=True)
    return (task_grad.astype(jnp.float32) + owned_rows).astype(jnp.bfloat16)


def solution(mesh):
    placed = (
        P("row", "col"),
        P("row", "col"),
        P("row", "col"),
        P("row", "col"),
        P(("row", "col"), None),
    )
    return jax.shard_map(
        body, mesh=mesh, in_specs=placed, out_specs=P(("row", "col"), None), check_vma=False
    )
```

profile of v0, /device:TPU:1, one launch (start us, length us, event | category | flops | bytes accessed | tf_op | source)
XLA Modules:
  0.0 326.9 jit_solution(4316638524077676610)
XLA Ops:
  6.5 0.0 all-gather.7.cloned.1.call-start
  6.5 0.7 all-gather.7.cloned.1.call-update
  7.3 0.0 all-gather.5.cloned.1.call-start
  7.3 2.1 subtract_convert_fusion
  9.4 0.0 all-gather.5.cloned.1.call-update
  9.5 0.0 all-gather.11.cloned.1.call-start
  9.5 0.7 all-gather.11.cloned.1.call-update
  10.2 0.0 all-gather.9.cloned.1.call-start
  10.2 109.3 %all-gather.7.cloned.1.call-done = bf16[8192,512]{1,0:T(8,128)(2,1)} async-done(((bf16[1024,512]{1,0:T(8,128)(2,1)}), bf16[8192,512]{1,0:T(8,128)(2,1)}) %all-gather.7.cloned.1.call-update) | async-done | bytes 8388624 | tf_op jit(solution)/shard_map/all_gather | solution.py:9
  119.5 52.6 %all-gather.5.cloned.1.call-done = bf16[512,8192]{1,0:T(8,128)(2,1)} async-done(((bf16[512,512]{1,0:T(8,128)(2,1)}), bf16[512,8192]{1,0:T(8,128)(2,1)}) %all-gather.5.cloned.1.call-update) | async-done | bytes 8388624 | tf_op jit(solution)/shard_map/all_gather | solution.py:12
  172.1 11.0 %convolution_convert_fusion = bf16[512,512]{1,0:T(8,128)(2,1)} fusion(bf16[512,8192]{1,0:T(8,128)(2,1)} %all-gather.5.cloned.1.call-done, bf16[8192,512]{1,0:T(8,128)(2,1)} %all-gather.7.cloned.1.call-done), kind=kOutput, calls=%fused_computation | convolution fusion | flops 4295229440 | bytes 17301504 | tf_op jit(solution)/shard_map/dot_general | solution.py:11
  183.1 0.0 all-gather.9.cloned.1.call-update
  183.2 0.0 copy-start
  183.2 37.0 %all-gather.11.cloned.1.call-done = bf16[512,4096]{1,0:T(8,128)(2,1)} async-done(((bf16[512,256]{1,0:T(8,128)(2,1)}), bf16[512,4096]{1,0:T(8,128)(2,1)}) %all-gather.11.cloned.1.call-update) | async-done | bytes 4194320 | tf_op jit(solution)/shard_map/all_gather | solution.py:17
  220.2 72.6 %all-gather.9.cloned.1.call-done = bf16[4096,512]{1,0:T(8,128)(2,1)} async-done(((bf16[512,512]{1,0:T(8,128)(2,1)}), bf16[4096,512]{1,0:T(8,128)(2,1)}) %all-gather.9.cloned.1.call-update) | async-done | bytes 4194320 | tf_op jit(solution)/shard_map/all_gather | solution.py:21
  292.9 5.8 %fusion = f32[512,512]{0,1:T(8,128)S(1)} fusion(bf16[512,4096]{1,0:T(8,128)(2,1)} %all-gather.11.cloned.1.call-done, bf16[4096,512]{1,0:T(8,128)(2,1)} %all-gather.9.cloned.1.call-done), kind=kOutput, calls=%fused_computation.3 | convolution fusion | flops 2147483648 | bytes 9437184 | tf_op jit(solution)/shard_map/dot_general | solution.py:19
  298.6 20.7 %all_to_all.19 = f32[16,32,512]{2,1,0:T(8,128)S(1)} all-to-all(f32[16,32,512]{2,1,0:T(8,128)S(1)} %bitcast.12), channel_id=1, replica_groups=mesh['row'=8,'col'=16] {'col'}, dimensions={0} | all-to-all | bytes 2097152 | tf_op jit(solution)/shard_map/all_to_all | solution.py:24
  319.4 0.1 copy.7
  319.5 0.0 copy-done
  319.5 0.9 add_convert_fusion
Async XLA Ops:
  6.5 113.0 %all-gather.7.cloned.1.call-start = ((), (), s32[]{:S(2)}) async-start(), calls=%async_computation.2 | async-start | bytes 9437184 | tf_op jit(solution)/shard_map/all_gather | solution.py:9
  7.3 164.8 %all-gather.5.cloned.1.call-start = ((), (), s32[]{:S(2)}) async-start(), calls=%async_computation.1 | async-start | bytes 8912896 | tf_op jit(solution)/shard_map/all_gather | solution.py:12
  9.5 210.8 %all-gather.11.cloned.1.call-start = ((), (), s32[]{:S(2)}) async-start(), calls=%async_computation.4 | async-start | bytes 4456448 | tf_op jit(solution)/shard_map/all_gather | solution.py:17
  10.2 282.7 %all-gather.9.cloned.1.call-start = ((), (), s32[]{:S(2)}) async-start(), calls=%async_computation.3 | async-start | bytes 4718592 | tf_op jit(solution)/shard_map/all_gather | solution.py:21
  183.2 136.3 %copy-start = (bf16[32,8192]{1,0:T(8,128)(2,1)S(1)}, bf16[32,8192]{1,0:T(8,128)(2,1)}, u32[]{:S(2)}) copy-start(bf16[32,8192]{1,0:T(8,128)(2,1)} %param.9) | copy-start | bytes 1572868
Sparse Core Ops, SparseCore 0:
  9.7 109.7 all-gather.6
  121.2 50.8 all-gather.4
  173.7 46.4 all-gather.10
  222.4 70.3 all-gather.8
where the time goes:
time: 327 us
  waiting for transfers between devices  273 us (83%)
  blocking collectives  20.7 us (6%)
  matrix products  16.8 us (5%)
  between operations  13.2 us (4%)
    all_gather x1, waiting for transfers between devices, body(): factor_cols = lax.all_gather(input_factor, 'row', axis=0, tiled=True)  109 us
    all_gather x1, waiting for transfers between devices, body(): lax.all_gather(projected, 'row', axis=0, tiled=True)  72.6 us
    all_gather x1, waiting for transfers between devices, body(): lax.all_gather(change, 'col', axis=1, tiled=True)  52.6 us
    all_gather x1, waiting for transfers between devices, body(): output_full = lax.all_gather(output_factor, 'col', axis=1, tiled=True)  37 us
    all_to_all x1, blocking collectives, body(): lax.all_to_all(penalty, 'col', split_axis=0, concat_axis=1, tiled=True)  20.7 us
    dot_general x1, matrix products, body(): jnp.dot(lax.all_gather(change, 'col', axis=1, tiled=True), factor_piece,...  11 us
  transfers between devices with their start and end apart: 4, of which 4 were waited for; matrix products, arithmetic and copies ran while one was open for 4% of the time, Pallas kernels for 0%

commit v1 on v0

v1 whole, which is shorter than its diff:
```python
import jax
import jax.numpy as jnp
from jax import lax
from jax.sharding import Mesh, PartitionSpec as P

ROW = ("y", "xh")
COL = ("xl", "z", "core")
F32, BF16 = jnp.float32, jnp.bfloat16


def shift(v, axis, by):
    n = lax.axis_size(axis)
    return lax.ppermute(v, axis, [(i, (i + by) % n) for i in range(n)])


def turn(v):
    pairs = [(xh * 4 + z, (z & 1) * 4 + (z & ~1) + xh) for xh in range(2) for z in range(4)]
    return lax.ppermute(v, ("xh", "z"), pairs)


def ring(v, axis):
    half = v.shape[0] // 2
    below, above = shift(v, axis, 1), shift(v, axis, -1)
    far = [shift(below[:half], axis, 1), shift(above[half:], axis, -1)]
    return below, above, jnp.concatenate(far, axis=0)


def across(v):
    half = v.shape[0] // 2
    up, down = v[:half], v[half:]
    for _ in range(2):
        up, down = shift(up, ("xh", "xl"), 1), shift(down, ("xh", "xl"), -1)
    return jnp.concatenate([up, down], axis=0)


def dot(a, b):
    return jnp.dot(a, b, preferred_element_type=F32)


def body(weight, anchor, input_factor, output_factor, task_grad):
    y, xh, xl, z, core = (lax.axis_index(a) for a in ROW + COL)
    change = (weight.astype(F32) - anchor.astype(F32)).astype(BF16)

    depth = input_factor.shape[0] // 2
    mine = lax.dynamic_slice_in_dim(input_factor, core * depth, depth, 0)
    other = lax.dynamic_slice_in_dim(input_factor, (1 - core) * depth, depth, 0)
    pair = jnp.concatenate([mine, shift(other, "core", 1)], axis=1)
    factor = lax.all_gather(pair, "y", axis=0, tiled=True)

    a = turn(change)
    am, ap, a2 = ring(a, "z")
    b = shift(a, "xl", 1)
    bm, bp = shift(b, "z", 1), shift(b, "z", -1)
    b2 = shift(a2, "xl", 1)

    out_turned = turn(output_factor)
    out_cols = lax.all_gather(out_turned, COL, axis=0)

    def term(block, dxl, dz):
        at = ((xl + dxl) % 2) * 2 + ((z + dz) % 4) // 2
        return dot(block, lax.dynamic_slice_in_dim(factor, at * depth, depth, 0))

    even = term(a, 0, 0) + term(a2, 0, 2) + term(b, 1, 0) + term(b2, 1, 2)
    odd = term(am, 0, -1) + term(ap, 0, 1) + term(bm, 1, -1) + term(bp, 1, 1)
    same = (z % 2) == xh
    keep = jnp.where(same, even, odd)
    send = jnp.where(same, odd, even)
    cols = weight.shape[1]
    theirs = jnp.concatenate([send[:, cols:], keep[:, cols:]], axis=0).astype(BF16)
    got = shift(theirs, "core", 1).astype(F32)
    rows = weight.shape[0]
    send = (send[:, :cols] + got[:rows]).astype(BF16)
    keep = keep[:, :cols] + got[rows:]
    projected = (keep + across(send).astype(F32)).astype(BF16)

    pm, pp, p2 = ring(projected, "y")
    n = output_factor.shape[1]
    left = out_cols.reshape(4, 2, 2, rows, n).transpose(0, 1, 3, 2, 4).reshape(4, 2 * rows, 2 * n)

    def share(block, dy):
        return dot(lax.dynamic_index_in_dim(left, (y + dy) % 4, 0, keepdims=False), block)

    penalty = share(projected, 0) + share(pm, -1) + share(pp, 1) + share(p2, 2)
    owned = lax.all_to_all(penalty.astype(BF16), ("xh",) + COL, split_axis=0, concat_axis=0, tiled=True)
    owned = owned.reshape(2, 16, task_grad.shape[0], cols).astype(F32).sum(axis=0)
    owned = owned.transpose(1, 0, 2).reshape(task_grad.shape)
    return (task_grad.astype(F32) + owned).astype(BF16)


def solution(mesh):
    fine = Mesh(mesh.devices.reshape(4, 2, 2, 4, 2), ROW + COL)
    block = P(ROW, COL)
    placed = (block, block, block, block, P(ROW + COL, None))
    return jax.shard_map(
        body, mesh=fine, in_specs=placed, out_specs=P(ROW + COL, None), check_vma=False
    )
```

time: 327 us -> 178 us (0.54)
  waiting for transfers between devices: 273 us -> 43.3 us
  starting transfers between devices: 0.12 us -> 60 us
  local copies, waits for them, and re-layouts: 0.09 us -> 19.6 us
  blocking collectives: 20.7 us -> 24 us
    all_gather x4 -> x2, waiting for transfers between devices: 272 us -> 0.01 us  [the longest x1 0.01 us: body(): out_cols = lax.all_gather(out_turned, COL, axis=0)]
    ppermute x0 -> x20, starting transfers between devices: none -> 59.9 us  [the longest x18 58.5 us: shift(): return lax.ppermute(v, axis, [(i, (i + by) % n) for i in range(n)])]
    ppermute x0 -> x20, waiting for transfers between devices: none -> 43.3 us  [the longest x18 43.3 us: shift(): return lax.ppermute(v, axis, [(i, (i + by) % n) for i in range(n)])]
    reshape x0 -> x3, local copies, waits for them, and re-layouts: none -> 16.2 us  [the longest x2 16.1 us: body(): out_cols.reshape(4, 2, 2, rows, n).transpose(0, 1, 3, 2, 4)]
    dot_general x2 -> x12, matrix products: 16.8 us -> 13.9 us  [dot(): return jnp.dot(a, b, preferred_element_type=F32)]
  transfers between devices with their start and end apart: 4 -> 22, of which waited for: 4 -> 11; matrix products, arithmetic and copies ran while one was open for 4% -> 17% of each run, Pallas kernels for 0% -> 0%
where the time goes in v1:
time: 178 us
  starting transfers between devices  60 us (34%)
  waiting for transfers between devices  43.3 us (24%)
  blocking collectives  24 us (13%)
  local copies, waits for them, and re-layouts  19.6 us (11%)
  matrix products  13.9 us (8%)
  between operations  13.7 us (8%)
  other arithmetic  3.26 us (2%)
    ppermute x18, starting transfers between devices, shift(): return lax.ppermute(v, axis, [(i, (i + by) % n) for i in range(n)])  58.5 us
    ppermute x18, waiting for transfers between devices, shift(): return lax.ppermute(v, axis, [(i, (i + by) % n) for i in range(n)])  43.3 us
    all_to_all x1, blocking collectives, body(): lax.all_to_all(penalty.astype(BF16), ('xh',) + COL, split_axis=0, concat_...  24 us
    reshape x2, local copies, waits for them, and re-layouts, body(): out_cols.reshape(4, 2, 2, rows, n).transpose(0, 1, 3, 2, 4)  16.1 us
    dot_general x12, matrix products, dot(): return jnp.dot(a, b, preferred_element_type=F32)  13.9 us
  transfers between devices with their start and end apart: 22, of which 11 were waited for; matrix products, arithmetic and copies ran while one was open for 17% of the time, Pallas kernels for 0%

profile of v1, /device:TPU:1, one launch (start us, length us, event | category | flops | bytes accessed | tf_op | source)
XLA Modules:
  0.0 177.8 jit_solution(13331786760981274830)
XLA Ops:
  6.5 1.3 constant_dynamic-slice_fusion.1
  7.8 0.0 copy-start.6
  7.8 1.5 collective-permute-start.2
  9.3 1.5 collective-permute-done.2
  10.9 1.2 pad_maximum_fusion
  12.0 0.0 all-gather.4.cloned.1.call-update
  12.1 0.0 all-gather.6.cloned.1.call-start
  12.1 0.7 collective-permute-start
  12.8 0.0 copy-start.5
  12.8 0.7 copy-done.5
  13.5 0.0 all-gather.6.cloned.1.call-update
  13.6 0.1 subtract_convert_fusion
  13.7 0.7 collective-permute-start.1
  14.4 28.6 %collective-permute-start.3 = (bf16[512,512]{1,0:T(8,128)(2,1)S(1)}, bf16[512,512]{1,0:T(8,128)(2,1)S(1)}, u32[]{:S(2)}, u32[]{:S(2)}) collective-permute-start(bf16[512,512]{1,0:T(8,128)(2,1)S(1)} %collective-permute-done.1), channel_id=1, source_target_pairs={{0,2},{2,4},{4,6},{6,0},{1,3},{3,5},{5,7},{7,1},{8,10},{10,12},{12... | collective-permute-start | bytes 1572872 | tf_op jit(solution)/shard_map/ppermute | solution.py:13
  43.1 2.1 %collective-permute-start.5 = (bf16[512,512]{1,0:T(8,128)(2,1)S(1)}, bf16[512,512]{1,0:T(8,128)(2,1)S(1)}, u32[]{:S(2)}, u32[]{:S(2)}) collective-permute-start(bf16[512,512]{1,0:T(8,128)(2,1)S(1)} %collective-permute-done.1), channel_id=1, source_target_pairs={{0,6},{2,0},{4,2},{6,4},{1,7},{3,1},{5,3},{7,5},{8,14},{10,8},{12,... | collective-permute-start | bytes 1572872 | tf_op jit(solution)/shard_map/ppermute | solution.py:13
  45.2 1.2 collective-permute-start.7
  46.4 9.0 %collective-permute-done.3 = bf16[512,512]{1,0:T(8,128)(2,1)S(1)} collective-permute-done((bf16[512,512]{1,0:T(8,128)(2,1)S(1)}, bf16[512,512]{1,0:T(8,128)(2,1)S(1)}, u32[]{:S(2)}, u32[]{:S(2)}) %collective-permute-start.3) | collective-permute-done | bytes 524320 | tf_op jit(solution)/shard_map/ppermute | solution.py:13
  55.4 0.1 collective-permute-start.4
  55.5 2.7 %collective-permute-start.6 = (bf16[256,512]{1,0:T(8,128)(2,1)S(1)}, bf16[256,512]{1,0:T(8,128)(2,1)S(1)}, u32[]{:S(2)}, u32[]{:S(2)}) collective-permute-start(bf16[256,512]{1,0:T(8,128)(2,1)S(1)} %slice.51), channel_id=1, source_target_pairs={{0,6},{2,0},{4,2},{6,4},{1,7},{3,1},{5,3},{7,5},{8,14},{10,8},{12,... | collective-permute-start | bytes 786440 | tf_op jit(solution)/shard_map/ppermute | solution.py:13
  58.3 0.3 collective-permute-start.10
  58.5 1.2 collective-permute-start.9
  59.7 2.6 %collective-permute-done.4 = bf16[256,512]{1,0:T(8,128)(2,1)S(1)} collective-permute-done((bf16[256,512]{1,0:T(8,128)(2,1)S(1)}, bf16[256,512]{1,0:T(8,128)(2,1)S(1)}, u32[]{:S(2)}, u32[]{:S(2)}) %collective-permute-start.4) | collective-permute-done | bytes 262176 | tf_op jit(solution)/shard_map/ppermute | solution.py:13
  62.4 1.3 collective-permute-start.8
  63.7 2.1 %fusion.31 = f32[512,1024]{1,0:T(8,128)S(1)} fusion(bf16[512,512]{1,0:T(8,128)(2,1)S(1)} %collective-permute-done.1, bf16[2048,1024]{1,0:T(8,128)(2,1)} %all-gather.4.cloned.1.call-done, s32[]{:T(128)S(6)} %select_n.148), kind=kOutput, calls=%fused_computation.39 | convolution fusion | flops 536870912 | bytes 3670020 | tf_op jit(solution)/shard_map/dot_general | solution.py:37
  65.8 0.4 copy-done
  66.2 0.7 fusion.29
  66.9 0.7 fusion.24
  67.7 0.7 fusion.22
  68.4 2.5 %collective-permute-done.8 = bf16[512,512]{1,0:T(8,128)(2,1)S(1)} collective-permute-done((bf16[512,512]{1,0:T(8,128)(2,1)S(1)}, bf16[512,512]{1,0:T(8,128)(2,1)S(1)}, u32[]{:S(2)}, u32[]{:S(2)}) %collective-permute-start.8) | collective-permute-done | bytes 524320 | tf_op jit(solution)/shard_map/ppermute | solution.py:13
  70.9 0.7 fusion.26
  71.6 2.3 %collective-permute-done.9 = bf16[512,512]{1,0:T(8,128)(2,1)S(1)} collective-permute-done((bf16[512,512]{1,0:T(8,128)(2,1)}, bf16[512,512]{1,0:T(8,128)(2,1)S(1)}, u32[]{:S(2)}, u32[]{:S(2)}) %collective-permute-start.9) | collective-permute-done | bytes 524320 | tf_op jit(solution)/shard_map/ppermute | solution.py:13
  73.9 0.7 fusion.20
  74.6 2.0 %add_add_fusion.1 = f32[512,1024]{1,0:T(8,128)S(1)} fusion(f32[512,1024]{1,0:T(8,128)S(1)} %fusion.26, f32[512,1024]{1,0:T(8,128)S(1)} %fusion.31, f32[512,1024]{1,0:T(8,128)S(1)} %fusion.29, bf16[512,512]{1,0:T(8,128)(2,1)} %collective-permute-done.7, bf16[2048,1024]{1,0:T(8,128)(2,1)S(1)} %copy-done, s32[]{:T(128)S(6)} %select_n.153), kind=kOutput, calls=%fused_computation.4 | convolution fusion | flops 538443776 | bytes 9961476 | tf_op jit(solution)/shard_map/dot_general | solution.py:37
  76.6 2.0 %broadcast_select_fusion = (f32[512,1024]{1,0:T(8,128)S(1)}, f32[512,1024]{1,0:T(8,128)S(1)}) fusion(f32[512,1024]{1,0:T(8,128)S(1)} %add_add_fusion.1, pred[]{:T(512)S(6)} %eq.25, bf16[512,512]{1,0:T(8,128)(2,1)} %collective-permute-done.10, bf16[2048,1024]{1,0:T(8,128)(2,1)S(1)} %copy-done, s32[]{:T(128)S(6)} %select_n.162, f32[512,1024]{1,0:T(8,128)S(1)} %fusion.20, ...), kind=kOutput, calls=%fused_computation.43 | convolution fusion | flops 539492352 | bytes 14155781 | tf_op jit(solution)/shard_map/dot_general | solution.py:37
  78.6 0.1 slice.74
  78.7 0.1 slice.75
  78.8 0.1 pad_maximum_fusion.1
  78.9 8.3 %collective-permute-start.11 = (bf16[1024,512]{1,0:T(8,128)(2,1)S(1)}, bf16[1024,512]{1,0:T(8,128)(2,1)S(1)}, u32[]{:S(2)}, u32[]{:S(2)}) collective-permute-start(bf16[1024,512]{1,0:T(8,128)(2,1)S(1)} %pad_maximum_fusion.1), channel_id=1, source_target_pairs={{0,1},{1,0},{2,3},{3,2},{4,5},{5,4},{6,7},{7,6},{8,9},{9,8},{10,11... | collective-permute-start | bytes 3145736 | tf_op jit(solution)/shard_map/ppermute | solution.py:13
  87.1 2.3 %collective-permute-done.11 = bf16[1024,512]{1,0:T(8,128)(2,1)S(1)} collective-permute-done((bf16[1024,512]{1,0:T(8,128)(2,1)S(1)}, bf16[1024,512]{1,0:T(8,128)(2,1)S(1)}, u32[]{:S(2)}, u32[]{:S(2)}) %collective-permute-start.11) | collective-permute-done | bytes 1048608 | tf_op jit(solution)/shard_map/ppermute | solution.py:13
  89.4 0.3 convert_element_type.41
  89.7 0.3 fusion
  90.0 0.1 collective-permute-start.14
  90.1 2.3 %collective-permute-start.12 = (bf16[256,512]{1,0:T(8,128)(2,1)S(1)}, bf16[256,512]{1,0:T(8,128)(2,1)S(1)}, u32[]{:S(2)}, u32[]{:S(2)}) collective-permute-start(bf16[256,512]{1,0:T(8,128)(2,1)S(1)} %get-tuple-element.9), channel_id=1, source_target_pairs={{0,8},{8,16},{16,24},{24,0},{1,9},{9,17},{17,25},{25,1},{2,10},{10... | collective-permute-start | bytes 786440 | tf_op jit(solution)/shard_map/ppermute | solution.py:13
  92.4 11.3 %collective-permute-done.14 = bf16[256,512]{1,0:T(8,128)(2,1)S(1)} collective-permute-done((bf16[256,512]{1,0:T(8,128)(2,1)S(1)}, bf16[256,512]{1,0:T(8,128)(2,1)S(1)}, u32[]{:S(2)}, u32[]{:S(2)}) %collective-permute-start.14) | collective-permute-done | bytes 262176 | tf_op jit(solution)/shard_map/ppermute | solution.py:13
  103.7 1.8 collective-permute-start.13
  105.5 5.1 %collective-permute-done.15 = bf16[256,512]{1,0:T(8,128)(2,1)S(1)} collective-permute-done((bf16[256,512]{1,0:T(8,128)(2,1)S(1)}, bf16[256,512]{1,0:T(8,128)(2,1)S(1)}, u32[]{:S(2)}, u32[]{:S(2)}) %collective-permute-start.15) | collective-permute-done | bytes 262176 | tf_op jit(solution)/shard_map/ppermute | solution.py:13
  110.6 1.2 collective-permute-done.13
  111.8 0.3 fusion.2
  112.1 4.3 %collective-permute-start.17 = (bf16[512,512]{1,0:T(8,128)(2,1)S(1)}, bf16[512,512]{1,0:T(8,128)(2,1)S(1)}, u32[]{:S(2)}, u32[]{:S(2)}) collective-permute-start(bf16[512,512]{1,0:T(8,128)(2,1)S(1)} %fusion.2), channel_id=1, source_target_pairs={{0,96},{32,0},{64,32},{96,64},{1,97},{33,1},{65,33},{97,65},{2,98}... | collective-permute-start | bytes 1572872 | tf_op jit(solution)/shard_map/ppermute | solution.py:13
  116.4 8.5 %copy.12 = bf16[4,2,2,512,256]{4,2,3,1,0:T(2,128)(2,1)} copy(bf16[4,2,2,512,256]{4,3,2,1,0:T(8,128)(2,1)} %bitcast.37) | data formatting | bytes 8388608 | tf_op jit(solution)/shard_map/reshape | solution.py:78
  124.9 7.6 %reshape.16 = bf16[4,1024,512]{2,1,0:T(8,128)(2,1)} reshape(bf16[4,2,512,2,256]{4,3,2,1,0:T(2,128)(2,1)} %bitcast.35) | data formatting | bytes 8388608 | tf_op jit(solution)/shard_map/reshape | solution.py:78
  132.5 2.1 %fusion.11 = f32[1024,512]{1,0:T(8,128)S(1)} fusion(bf16[512,512]{1,0:T(8,128)(2,1)S(1)} %fusion.2, bf16[4,1024,512]{2,1,0:T(8,128)(2,1)} %reshape.16, s32[]{:T(128)S(6)} %select_n.140), kind=kOutput, calls=%fused_computation.20 | convolution fusion | flops 536870912 | bytes 3670020 | tf_op jit(solution)/shard_map/dot_general | solution.py:37
  134.6 2.7 %collective-permute-start.19 = (bf16[256,512]{1,0:T(8,128)(2,1)S(1)}, bf16[256,512]{1,0:T(8,128)(2,1)S(1)}, u32[]{:S(2)}, u32[]{:S(2)}) collective-permute-start(bf16[256,512]{1,0:T(8,128)(2,1)S(1)} %slice.61), channel_id=1, source_target_pairs={{0,96},{32,0},{64,32},{96,64},{1,97},{33,1},{65,33},{97,65},{2,98}... | collective-permute-start | bytes 786440 | tf_op jit(solution)/shard_map/ppermute | solution.py:13
  137.4 0.1 collective-permute-start.18
  137.4 0.7 fusion.7
  138.2 0.7 fusion.9
  138.9 2.2 %collective-permute-done.19 = bf16[256,512]{1,0:T(8,128)(2,1)S(1)} collective-permute-done((bf16[256,512]{1,0:T(8,128)(2,1)S(1)}, bf16[256,512]{1,0:T(8,128)(2,1)S(1)}, u32[]{:S(2)}, u32[]{:S(2)}) %collective-permute-start.19) | collective-permute-done | bytes 262176 | tf_op jit(solution)/shard_map/ppermute | solution.py:13
  141.1 3.2 %collective-permute-done.18 = bf16[256,512]{1,0:T(8,128)(2,1)S(1)} collective-permute-done((bf16[256,512]{1,0:T(8,128)(2,1)S(1)}, bf16[256,512]{1,0:T(8,128)(2,1)S(1)}, u32[]{:S(2)}, u32[]{:S(2)}) %collective-permute-start.18) | collective-permute-done | bytes 262176 | tf_op jit(solution)/shard_map/ppermute | solution.py:13
  144.3 0.7 add_convert_fusion
  145.0 24.0 %all_to_all.9 = bf16[32,32,512]{2,1,0:T(8,128)(2,1)S(1)} all-to-all(bf16[32,32,512]{2,1,0:T(8,128)(2,1)S(1)} %bitcast.36), channel_id=1, replica_groups=mesh['y'=4,'xh'=2,'xl'=2,'z'=4,'core'=2] {'xh','xl','z','core'}, dimensions={0} | all-to-all | bytes 2097152 | tf_op jit(solution)/shard_map/all_to_all | solution.py:84
  169.0 0.2 convert_reduce_fusion
  169.2 0.1 copy.10
  169.3 0.7 copy-done.4
  170.1 0.9 add_convert_fusion.1
  (30 shorter events, 0.2 us)
Async XLA Ops:
  6.5 57.1 %all-gather.4.cloned.1.call-start = ((), (), s32[]{:S(2)}) async-start(), calls=%async_computation.1 | async-start | bytes 5242880 | tf_op jit(solution)/shard_map/all_gather | solution.py:48
  7.8 4.3 %copy-start.6 = (bf16[512,256]{1,0:T(8,128)(2,1)S(1)}, bf16[512,256]{1,0:T(8,128)(2,1)}, u32[]{:S(2)}) copy-start(bf16[512,256]{1,0:T(8,128)(2,1)} %param.8) | copy-start | bytes 786436
  7.8 5.7 %copy-start.2 = (bf16[512,512]{1,0:T(8,128)(2,1)S(1)}, bf16[512,512]{1,0:T(8,128)(2,1)}, u32[]{:S(2)}) copy-start(bf16[512,512]{1,0:T(8,128)(2,1)} %param.6) | copy-start | bytes 1572868
  7.8 5.7 %copy-start.3 = (bf16[512,512]{1,0:T(8,128)(2,1)S(1)}, bf16[512,512]{1,0:T(8,128)(2,1)}, u32[]{:S(2)}) copy-start(bf16[512,512]{1,0:T(8,128)(2,1)} %param.5) | copy-start | bytes 1572868
  7.8 3.0 %collective-permute-start.2 = (bf16[512,512]{1,0:T(8,128)(2,1)S(1)}, bf16[512,512]{1,0:T(8,128)(2,1)S(1)}, u32[]{:S(2)}, u32[]{:S(2)}) collective-permute-start(bf16[512,512]{1,0:T(8,128)(2,1)S(1)} %get-tuple-element.8), channel_id=1, source_target_pairs={{0,1},{1,0},{2,3},{3,2},{4,5},{5,4},{6,7},{7,6},{8,9},{9,8},{10,11... | collective-permute-start | bytes 1572872 | tf_op jit(solution)/shard_map/ppermute | solution.py:13
  12.1 104.3 %all-gather.6.cloned.1.call-start = ((), (), s32[]{:S(2)}) async-start(), calls=%async_computation.2 | async-start | bytes 4456448 | tf_op jit(solution)/shard_map/all_gather | solution.py:57
  12.1 0.7 collective-permute-start
  12.8 0.7 copy-start.5
  13.7 0.7 collective-permute-start.1
  14.4 41.0 %collective-permute-start.3 = (bf16[512,512]{1,0:T(8,128)(2,1)S(1)}, bf16[512,512]{1,0:T(8,128)(2,1)S(1)}, u32[]{:S(2)}, u32[]{:S(2)}) collective-permute-start(bf16[512,512]{1,0:T(8,128)(2,1)S(1)} %collective-permute-done.1), channel_id=1, source_target_pairs={{0,2},{2,4},{4,6},{6,0},{1,3},{3,5},{5,7},{7,1},{8,10},{10,12},{12... | collective-permute-start | bytes 1572872 | tf_op jit(solution)/shard_map/ppermute | solution.py:13
  43.1 12.4 %collective-permute-start.5 = (bf16[512,512]{1,0:T(8,128)(2,1)S(1)}, bf16[512,512]{1,0:T(8,128)(2,1)S(1)}, u32[]{:S(2)}, u32[]{:S(2)}) collective-permute-start(bf16[512,512]{1,0:T(8,128)(2,1)S(1)} %collective-permute-done.1), channel_id=1, source_target_pairs={{0,6},{2,0},{4,2},{6,4},{1,7},{3,1},{5,3},{7,5},{8,14},{10,8},{12,... | collective-permute-start | bytes 1572872 | tf_op jit(solution)/shard_map/ppermute | solution.py:13
  45.2 13.1 %collective-permute-start.7 = (bf16[512,512]{1,0:T(8,128)(2,1)S(1)}, bf16[512,512]{1,0:T(8,128)(2,1)}, u32[]{:S(2)}, u32[]{:S(2)}) collective-permute-start(bf16[512,512]{1,0:T(8,128)(2,1)S(1)} %collective-permute-done.1), channel_id=1, source_target_pairs={{0,8},{8,0},{1,9},{9,1},{2,10},{10,2},{3,11},{11,3},{4,12},{12,4},... | collective-permute-start | bytes 1572872 | tf_op jit(solution)/shard_map/ppermute | solution.py:13
  55.4 6.9 %collective-permute-start.4 = (bf16[256,512]{1,0:T(8,128)(2,1)S(1)}, bf16[256,512]{1,0:T(8,128)(2,1)S(1)}, u32[]{:S(2)}, u32[]{:S(2)}) collective-permute-start(bf16[256,512]{1,0:T(8,128)(2,1)S(1)} %slice.50), channel_id=1, source_target_pairs={{0,2},{2,4},{4,6},{6,0},{1,3},{3,5},{5,7},{7,1},{8,10},{10,12},{12... | collective-permute-start | bytes 786440 | tf_op jit(solution)/shard_map/ppermute | solution.py:13
  55.5 6.8 %collective-permute-start.6 = (bf16[256,512]{1,0:T(8,128)(2,1)S(1)}, bf16[256,512]{1,0:T(8,128)(2,1)S(1)}, u32[]{:S(2)}, u32[]{:S(2)}) collective-permute-start(bf16[256,512]{1,0:T(8,128)(2,1)S(1)} %slice.51), channel_id=1, source_target_pairs={{0,6},{2,0},{4,2},{6,4},{1,7},{3,1},{5,3},{7,5},{8,14},{10,8},{12,... | collective-permute-start | bytes 786440 | tf_op jit(solution)/shard_map/ppermute | solution.py:13
  58.3 18.3 %collective-permute-start.10 = (bf16[512,512]{1,0:T(8,128)(2,1)}, bf16[512,512]{1,0:T(8,128)(2,1)}, u32[]{:S(2)}, u32[]{:S(2)}) collective-permute-start(bf16[512,512]{1,0:T(8,128)(2,1)} %collective-permute-done.7), channel_id=1, source_target_pairs={{0,6},{2,0},{4,2},{6,4},{1,7},{3,1},{5,3},{7,5},{8,14},{10,8},{12,... | collective-permute-start | bytes 1572872 | tf_op jit(solution)/shard_map/ppermute | solution.py:13
  58.5 15.4 %collective-permute-start.9 = (bf16[512,512]{1,0:T(8,128)(2,1)}, bf16[512,512]{1,0:T(8,128)(2,1)S(1)}, u32[]{:S(2)}, u32[]{:S(2)}) collective-permute-start(bf16[512,512]{1,0:T(8,128)(2,1)} %collective-permute-done.7), channel_id=1, source_target_pairs={{0,2},{2,4},{4,6},{6,0},{1,3},{3,5},{5,7},{7,1},{8,10},{10,12},{12... | collective-permute-start | bytes 1572872 | tf_op jit(solution)/shard_map/ppermute | solution.py:13
  62.4 8.5 %collective-permute-start.8 = (bf16[512,512]{1,0:T(8,128)(2,1)S(1)}, bf16[512,512]{1,0:T(8,128)(2,1)S(1)}, u32[]{:S(2)}, u32[]{:S(2)}) collective-permute-start(bf16[512,512]{1,0:T(8,128)(2,1)S(1)} %constant_dynamic-update-slice_fusion), channel_id=1, source_target_pairs={{0,8},{8,0},{1,9},{9,1},{2,10},{10,2},{3,11},{11,3},{4,12},{12,4},... | collective-permute-start | bytes 1572872 | tf_op jit(solution)/shard_map/ppermute | solution.py:13
  63.7 2.5 %copy-start = (bf16[2048,1024]{1,0:T(8,128)(2,1)S(1)}, bf16[2048,1024]{1,0:T(8,128)(2,1)}, u32[]{:S(2)}) copy-start(bf16[2048,1024]{1,0:T(8,128)(2,1)} %all-gather.4.cloned.1.call-done) | copy-start | bytes 12582916
  78.9 10.6 %collective-permute-start.11 = (bf16[1024,512]{1,0:T(8,128)(2,1)S(1)}, bf16[1024,512]{1,0:T(8,128)(2,1)S(1)}, u32[]{:S(2)}, u32[]{:S(2)}) collective-permute-start(bf16[1024,512]{1,0:T(8,128)(2,1)S(1)} %pad_maximum_fusion.1), channel_id=1, source_target_pairs={{0,1},{1,0},{2,3},{3,2},{4,5},{5,4},{6,7},{7,6},{8,9},{9,8},{10,11... | collective-permute-start | bytes 3145736 | tf_op jit(solution)/shard_map/ppermute | solution.py:13
  90.0 13.7 %collective-permute-start.14 = (bf16[256,512]{1,0:T(8,128)(2,1)S(1)}, bf16[256,512]{1,0:T(8,128)(2,1)S(1)}, u32[]{:S(2)}, u32[]{:S(2)}) collective-permute-start(bf16[256,512]{1,0:T(8,128)(2,1)S(1)} %get-tuple-element.10), channel_id=1, source_target_pairs={{0,24},{8,0},{16,8},{24,16},{1,25},{9,1},{17,9},{25,17},{2,26},{10... | collective-permute-start | bytes 786440 | tf_op jit(solution)/shard_map/ppermute | solution.py:13
  90.1 13.6 %collective-permute-start.12 = (bf16[256,512]{1,0:T(8,128)(2,1)S(1)}, bf16[256,512]{1,0:T(8,128)(2,1)S(1)}, u32[]{:S(2)}, u32[]{:S(2)}) collective-permute-start(bf16[256,512]{1,0:T(8,128)(2,1)S(1)} %get-tuple-element.9), channel_id=1, source_target_pairs={{0,8},{8,16},{16,24},{24,0},{1,9},{9,17},{17,25},{25,1},{2,10},{10... | collective-permute-start | bytes 786440 | tf_op jit(solution)/shard_map/ppermute | solution.py:13
  103.7 6.8 %collective-permute-start.15 = (bf16[256,512]{1,0:T(8,128)(2,1)S(1)}, bf16[256,512]{1,0:T(8,128)(2,1)S(1)}, u32[]{:S(2)}, u32[]{:S(2)}) collective-permute-start(bf16[256,512]{1,0:T(8,128)(2,1)S(1)} %collective-permute-done.14), channel_id=1, source_target_pairs={{0,24},{8,0},{16,8},{24,16},{1,25},{9,1},{17,9},{25,17},{2,26},{10... | collective-permute-start | bytes 786440 | tf_op jit(solution)/shard_map/ppermute | solution.py:13
  103.7 8.0 %collective-permute-start.13 = (bf16[256,512]{1,0:T(8,128)(2,1)S(1)}, bf16[256,512]{1,0:T(8,128)(2,1)S(1)}, u32[]{:S(2)}, u32[]{:S(2)}) collective-permute-start(bf16[256,512]{1,0:T(8,128)(2,1)S(1)} %collective-permute-done.12), channel_id=1, source_target_pairs={{0,8},{8,16},{16,24},{24,0},{1,9},{9,17},{17,25},{25,1},{2,10},{10... | collective-permute-start | bytes 786440 | tf_op jit(solution)/shard_map/ppermute | solution.py:13
  112.1 22.5 %collective-permute-start.17 = (bf16[512,512]{1,0:T(8,128)(2,1)S(1)}, bf16[512,512]{1,0:T(8,128)(2,1)S(1)}, u32[]{:S(2)}, u32[]{:S(2)}) collective-permute-start(bf16[512,512]{1,0:T(8,128)(2,1)S(1)} %fusion.2), channel_id=1, source_target_pairs={{0,96},{32,0},{64,32},{96,64},{1,97},{33,1},{65,33},{97,65},{2,98}... | collective-permute-start | bytes 1572872 | tf_op jit(solution)/shard_map/ppermute | solution.py:13
  116.4 21.0 %collective-permute-start.16 = (bf16[512,512]{1,0:T(8,128)(2,1)S(1)}, bf16[512,512]{1,0:T(8,128)(2,1)S(1)}, u32[]{:S(2)}, u32[]{:S(2)}) collective-permute-start(bf16[512,512]{1,0:T(8,128)(2,1)S(1)} %fusion.2), channel_id=1, source_target_pairs={{0,32},{32,64},{64,96},{96,0},{1,33},{33,65},{65,97},{97,1},{2,34}... | collective-permute-start | bytes 1572872 | tf_op jit(solution)/shard_map/ppermute | solution.py:13
  132.5 5.0 %copy-start.1 = (bf16[4,1024,512]{2,1,0:T(8,128)(2,1)S(1)}, bf16[4,1024,512]{2,1,0:T(8,128)(2,1)}, u32[]{:S(2)}) copy-start(bf16[4,1024,512]{2,1,0:T(8,128)(2,1)} %reshape.16) | copy-start | bytes 12582916
  134.6 6.5 %collective-permute-start.19 = (bf16[256,512]{1,0:T(8,128)(2,1)S(1)}, bf16[256,512]{1,0:T(8,128)(2,1)S(1)}, u32[]{:S(2)}, u32[]{:S(2)}) collective-permute-start(bf16[256,512]{1,0:T(8,128)(2,1)S(1)} %slice.61), channel_id=1, source_target_pairs={{0,96},{32,0},{64,32},{96,64},{1,97},{33,1},{65,33},{97,65},{2,98}... | collective-permute-start | bytes 786440 | tf_op jit(solution)/shard_map/ppermute | solution.py:13
  137.4 7.0 %collective-permute-start.18 = (bf16[256,512]{1,0:T(8,128)(2,1)S(1)}, bf16[256,512]{1,0:T(8,128)(2,1)S(1)}, u32[]{:S(2)}, u32[]{:S(2)}) collective-permute-start(bf16[256,512]{1,0:T(8,128)(2,1)S(1)} %slice.60), channel_id=1, source_target_pairs={{0,32},{32,64},{64,96},{96,0},{1,33},{33,65},{65,97},{97,1},{2,34}... | collective-permute-start | bytes 786440 | tf_op jit(solution)/shard_map/ppermute | solution.py:13
  169.0 1.0 copy-start.4
Sparse Core Ops, SparseCore 0:
  12.2 50.4 all-gather.3
  64.4 42.3 all-gather.5

commit v2 on v1

v2 whole, which is shorter than its diff:
```python
import jax
import jax.numpy as jnp
from jax import lax
from jax.sharding import Mesh, PartitionSpec as P

ROW = ("y", "xh")
COL = ("xl", "z", "core")
F32, BF16 = jnp.float32, jnp.bfloat16


def shift(v, axis, by):
    n = lax.axis_size(axis)
    return lax.ppermute(v, axis, [(i, (i + by) % n) for i in range(n)])


def turn(v, flip):
    pairs = []
    for xh in range(2):
        for xl in range(2):
            for z in range(4):
                to = ((z & 1) * 2 + (xl ^ flip)) * 4 + (z & ~1) + xh
                pairs.append(((xh * 2 + xl) * 4 + z, to))
    return lax.ppermute(v, ("xh", "xl", "z"), pairs)


def after(v, *done):
    return lax.optimization_barrier((v, *done))[0]


def dot(a, b):
    return jnp.dot(a, b, preferred_element_type=F32)


def body(weight, anchor, input_factor, output_factor, task_grad):
    y, xh, xl, z, core = (lax.axis_index(a) for a in ROW + COL)
    change = (weight.astype(F32) - anchor.astype(F32)).astype(BF16)
    rows, cols = weight.shape

    a, b = turn(change, 0), turn(change, 1)

    depth = input_factor.shape[0] // 2
    mine = lax.dynamic_slice_in_dim(input_factor, core * depth, depth, 0)
    other = lax.dynamic_slice_in_dim(input_factor, (1 - core) * depth, depth, 0)
    pair = jnp.concatenate([mine, shift(other, "core", 1)], axis=1)
    below, above = shift(pair, "y", 1), shift(pair, "y", -1)
    far = [shift(below[: depth // 2], "y", 1), shift(above[depth // 2 :], "y", -1)]
    factor = jnp.concatenate([pair, above, *far, below], axis=0)

    am, bp = shift(a, "z", 1), shift(b, "z", -1)
    bm, ap = shift(b, "z", 1), shift(a, "z", -1)
    a2, b2 = shift(am, "z", 1), shift(bp, "z", -1)

    part = after(output_factor, am, bp)
    part = jnp.concatenate([turn(part, 0), turn(part, 1)], axis=0)
    left = lax.all_gather(part, ("z", "core"), axis=1, tiled=True)

    def term(block, dxl, dz):
        at = (xl ^ dxl) * 2 + (((z + dz) & 3) >> 1)
        return dot(block, lax.dynamic_slice_in_dim(factor, ((at - y) & 3) * depth, depth, 0))

    odd = term(am, 0, -1) + term(ap, 0, 1) + term(bm, 1, -1) + term(bp, 1, 1)
    even = term(a, 0, 0) + term(b, 1, 0) + term(a2, 0, 2) + term(b2, 1, 2)
    same = (z & 1) == xh
    keep = jnp.where(same, even, odd)
    send = jnp.where(same, odd, even)
    theirs = jnp.concatenate([send[:, cols:], keep[:, cols:]], axis=0).astype(BF16)
    got = shift(theirs, "core", 1).astype(F32)
    send = (send[:, :cols] + got[:rows]).astype(BF16)
    keep = keep[:, :cols] + got[rows:]
    projected = (keep + shift(send, "xh", 1).astype(F32)).astype(BF16)

    half = rows // 2
    pm, pp = shift(projected, "y", 1), shift(projected, "y", -1)
    p2 = jnp.concatenate([shift(pm[:half], "y", 1), shift(pp[half:], "y", -1)], axis=0)

    def share(block, dy, to):
        at = (y + dy) & 3
        corner = (((at >> 1) ^ xl) * rows, ((at & 1) * 2 + to) * rows)
        return dot(lax.dynamic_slice(left, corner, (rows, rows)), block)

    penalty = [
        share(projected, 0, to) + share(pm, -1, to) + share(pp, 1, to) + share(p2, 2, to)
        for to in range(2)
    ]
    penalty = jnp.concatenate(penalty, axis=0).astype(BF16)
    owned = lax.all_to_all(penalty, ("xh",) + COL, split_axis=0, concat_axis=0, tiled=True)
    owned = owned.reshape(2, 16, task_grad.shape[0], cols).astype(F32).sum(axis=0)
    owned = owned.transpose(1, 0, 2).reshape(task_grad.shape)
    return (task_grad.astype(F32) + owned).astype(BF16)


def solution(mesh):
    fine = Mesh(mesh.devices.reshape(4, 2, 2, 4, 2), ROW + COL)
    block = P(ROW, COL)
    placed = (block, block, block, block, P(ROW + COL, None))
    return jax.shard_map(
        body, mesh=fine, in_specs=placed, out_specs=P(ROW + COL, None), check_vma=False
    )
```

time: 178 us -> 202 us (1.13)
  waiting for transfers between devices: 43.3 us -> 71.1 us
  local copies, waits for them, and re-layouts: 19.6 us -> 9.74 us
  starting transfers between devices: 60 us -> 64.7 us
  other arithmetic: 3.26 us -> 6.04 us
    ppermute x18 -> x17, waiting for transfers between devices: 43.3 us -> 65.9 us  [shift(): return lax.ppermute(v, axis, [(i, (i + by) % n) for i in range(n)])]
    reshape x2 -> x0, local copies, waits for them, and re-layouts: 16.1 us -> none  [body(): out_cols.reshape(4, 2, 2, rows, n).transpose(0, 1, 3, 2, 4)]
    ppermute x2 -> x4, waiting for transfers between devices: 0.01 us -> 5.17 us  [turn(): return lax.ppermute(v, ('xh', 'xl', 'z'), pairs)]
    unnamed x15 -> x20, local copies, waits for them, and re-layouts: 1.9 us -> 5.39 us
    ppermute x2 -> x4, starting transfers between devices: 1.37 us -> 4.7 us  [turn(): return lax.ppermute(v, ('xh', 'xl', 'z'), pairs)]
    ppermute x18 -> x17, starting transfers between devices: 58.5 us -> 60 us  [shift(): return lax.ppermute(v, axis, [(i, (i + by) % n) for i in range(n)])]
    dot_general x12 -> x16, matrix products: 13.9 us -> 13.4 us  [dot(): return jnp.dot(a, b, preferred_element_type=F32)]
  transfers between devices with their start and end apart: 22 -> 22, of which waited for: 11 -> 10; matrix products, arithmetic and copies ran while one was open for 17% -> 10% of each run, Pallas kernels for 0% -> 0%
where the time goes in v2:
time: 202 us; the launch traced here: 201 us
  waiting for transfers between devices  71.1 us (35%)
  starting transfers between devices  64.7 us (32%)
  blocking collectives  22.8 us (11%)
  between operations  13.7 us (7%)
  matrix products  13.4 us (7%)
  local copies, waits for them, and re-layouts  9.74 us (5%)
  other arithmetic  6.04 us (3%)
    ppermute x17, waiting for transfers between devices, shift(): return lax.ppermute(v, axis, [(i, (i + by) % n) for i in range(n)])  65.9 us
    ppermute x17, starting transfers between devices, shift(): return lax.ppermute(v, axis, [(i, (i + by) % n) for i in range(n)])  60 us
    all_to_all x1, blocking collectives, body(): lax.all_to_all(penalty, ('xh',) + COL, split_axis=0, concat_axis=0, tiled...  22.8 us
    dot_general x16, matrix products, dot(): return jnp.dot(a, b, preferred_element_type=F32)  13.4 us
    unnamed x20, local copies, waits for them, and re-layouts  5.39 us
    ppermute x4, waiting for transfers between devices, turn(): return lax.ppermute(v, ('xh', 'xl', 'z'), pairs)  5.17 us
    ppermute x4, starting transfers between devices, turn(): return lax.ppermute(v, ('xh', 'xl', 'z'), pairs)  4.7 us
  transfers between devices with their start and end apart: 22, of which 10 were waited for; matrix products, arithmetic and copies ran while one was open for 10% of the time, Pallas kernels for 0%

profile of v2, /device:TPU:1, one launch (start us, length us, event | category | flops | bytes accessed | tf_op | source)
XLA Modules:
  0.0 201.5 jit_solution(14350748355884358160)
XLA Ops:
  6.5 1.4 subtract_convert_fusion
  7.9 0.7 collective-permute-start
  8.6 2.1 %collective-permute-start.2 = (bf16[512,512]{1,0:T(8,128)(2,1)S(1)}, bf16[512,512]{1,0:T(8,128)(2,1)S(1)}, u32[]{:S(2)}, u32[]{:S(2)}) collective-permute-start(bf16[512,512]{1,0:T(8,128)(2,1)S(1)} %subtract_convert_fusion), channel_id=1, source_target_pairs={{0,8},{2,24},{4,12},{6,28},{8,0},{10,16},{12,4},{14,20},{16,10},{1... | collective-permute-start | bytes 1572872 | tf_op jit(solution)/shard_map/ppermute | solution.py:23
  10.7 1.3 constant_dynamic-slice_fusion.1
  12.0 1.0 collective-permute-start.6
  13.0 14.5 %collective-permute-start.1 = (bf16[512,512]{1,0:T(8,128)(2,1)S(1)}, bf16[512,512]{1,0:T(8,128)(2,1)S(1)}, u32[]{:S(2)}, u32[]{:S(2)}) collective-permute-start(bf16[512,512]{1,0:T(8,128)(2,1)S(1)} %collective-permute-done), channel_id=1, source_target_pairs={{0,2},{2,4},{4,6},{6,0},{1,3},{3,5},{5,7},{7,1},{8,10},{10,12},{12... | collective-permute-start | bytes 1572872 | tf_op jit(solution)/shard_map/ppermute | solution.py:13
  27.5 14.4 %collective-permute-start.3 = (bf16[512,512]{1,0:T(8,128)(2,1)S(1)}, bf16[512,512]{1,0:T(8,128)(2,1)S(1)}, u32[]{:S(2)}, u32[]{:S(2)}) collective-permute-start(bf16[512,512]{1,0:T(8,128)(2,1)S(1)} %collective-permute-done.2), channel_id=1, source_target_pairs={{0,6},{2,0},{4,2},{6,4},{1,7},{3,1},{5,3},{7,5},{8,14},{10,8},{12,... | collective-permute-start | bytes 1572872 | tf_op jit(solution)/shard_map/ppermute | solution.py:13
  41.9 1.7 pad_maximum_fusion
  43.6 1.3 collective-permute-start.8
  44.9 1.4 collective-permute-start.7
  46.4 2.4 %collective-permute-done.1 = bf16[512,512]{1,0:T(8,128)(2,1)S(1)} collective-permute-done((bf16[512,512]{1,0:T(8,128)(2,1)S(1)}, bf16[512,512]{1,0:T(8,128)(2,1)S(1)}, u32[]{:S(2)}, u32[]{:S(2)}) %collective-permute-start.1) | collective-permute-done | bytes 524320 | tf_op jit(solution)/shard_map/ppermute | solution.py:13
  48.8 3.8 %collective-permute-done.3 = bf16[512,512]{1,0:T(8,128)(2,1)S(1)} collective-permute-done((bf16[512,512]{1,0:T(8,128)(2,1)S(1)}, bf16[512,512]{1,0:T(8,128)(2,1)S(1)}, u32[]{:S(2)}, u32[]{:S(2)}) %collective-permute-start.3) | collective-permute-done | bytes 524320 | tf_op jit(solution)/shard_map/ppermute | solution.py:13
  52.7 0.7 collective-permute-start.4
  53.3 0.2 copy-done.4
  53.5 1.2 collective-permute-start.5
  54.7 5.2 %collective-permute-done.5 = bf16[512,256]{1,0:T(8,128)(2,1)S(1)} collective-permute-done((bf16[512,256]{1,0:T(8,128)(2,1)S(1)}, bf16[512,256]{1,0:T(8,128)(2,1)S(1)}, u32[]{:S(2)}, u32[]{:S(2)}) %collective-permute-start.5) | collective-permute-done | bytes 262176 | tf_op jit(solution)/shard_map/ppermute | solution.py:23
  59.9 0.8 pad_maximum_fusion.3
  60.7 8.3 %collective-permute-done.8 = bf16[512,1024]{1,0:T(8,128)(2,1)S(1)} collective-permute-done((bf16[512,1024]{1,0:T(8,128)(2,1)}, bf16[512,1024]{1,0:T(8,128)(2,1)S(1)}, u32[]{:S(2)}, u32[]{:S(2)}) %collective-permute-start.8) | collective-permute-done | bytes 1048608 | tf_op jit(solution)/shard_map/ppermute | solution.py:13
  69.0 0.8 slice.42
  69.9 0.8 slice.43
  70.7 2.7 %collective-permute-start.10 = (bf16[256,1024]{1,0:T(8,128)(2,1)}, bf16[256,1024]{1,0:T(8,128)(2,1)}, u32[]{:S(2)}, u32[]{:S(2)}) collective-permute-start(bf16[256,1024]{1,0:T(8,128)(2,1)} %slice.43), channel_id=1, source_target_pairs={{0,96},{32,0},{64,32},{96,64},{1,97},{33,1},{65,33},{97,65},{2,98}... | collective-permute-start | bytes 1572872 | tf_op jit(solution)/shard_map/ppermute | solution.py:13
  73.4 6.1 %collective-permute-start.13 = (bf16[512,512]{1,0:T(8,128)(2,1)S(1)}, bf16[512,512]{1,0:T(8,128)(2,1)S(1)}, u32[]{:S(2)}, u32[]{:S(2)}) collective-permute-start(bf16[512,512]{1,0:T(8,128)(2,1)S(1)} %collective-permute-done), channel_id=1, source_target_pairs={{0,6},{2,0},{4,2},{6,4},{1,7},{3,1},{5,3},{7,5},{8,14},{10,8},{12,... | collective-permute-start | bytes 1572872 | tf_op jit(solution)/shard_map/ppermute | solution.py:13
  79.5 1.1 constant_dynamic-update-slice_fusion.3
  80.6 2.6 %collective-permute-done.9 = bf16[256,1024]{1,0:T(8,128)(2,1)} collective-permute-done((bf16[256,1024]{1,0:T(8,128)(2,1)}, bf16[256,1024]{1,0:T(8,128)(2,1)}, u32[]{:S(2)}, u32[]{:S(2)}) %collective-permute-start.9) | collective-permute-done | bytes 524320 | tf_op jit(solution)/shard_map/ppermute | solution.py:13
  83.1 7.4 %collective-permute-start.12 = (bf16[512,512]{1,0:T(8,128)(2,1)}, bf16[512,512]{1,0:T(8,128)(2,1)S(1)}, u32[]{:S(2)}, u32[]{:S(2)}) collective-permute-start(bf16[512,512]{1,0:T(8,128)(2,1)} %copy-done.4), channel_id=1, source_target_pairs={{0,6},{2,0},{4,2},{6,4},{1,7},{3,1},{5,3},{7,5},{8,14},{10,8},{12,... | collective-permute-start | bytes 1572872 | tf_op jit(solution)/shard_map/ppermute | solution.py:13
  90.6 1.9 constant_dynamic-update-slice_fusion.2
  92.5 1.9 constant_dynamic-update-slice_fusion.1
  94.3 1.1 constant_dynamic-update-slice_fusion
  95.5 2.1 %fusion.17 = f32[512,1024]{1,0:T(8,128)S(1)} fusion(bf16[512,512]{1,0:T(8,128)(2,1)S(1)} %copy-done.3, bf16[2048,1024]{1,0:T(8,128)(2,1)} %constant_dynamic-update-slice_fusion, s32[]{:T(128)S(6)} %select_n.91), kind=kOutput, calls=%fused_computation.28 | convolution fusion | flops 536870912 | bytes 3670020 | tf_op jit(solution)/shard_map/dot_general | solution.py:31
  97.6 0.4 copy-done
  98.0 0.7 fusion.25
  98.7 0.7 fusion.27
  99.5 0.7 fusion.15
  100.2 0.7 fusion.13
  101.0 16.9 %collective-permute-done.11 = bf16[512,512]{1,0:T(8,128)(2,1)S(1)} collective-permute-done((bf16[512,512]{1,0:T(8,128)(2,1)}, bf16[512,512]{1,0:T(8,128)(2,1)S(1)}, u32[]{:S(2)}, u32[]{:S(2)}) %collective-permute-start.11) | collective-permute-done | bytes 524320 | tf_op jit(solution)/shard_map/ppermute | solution.py:13
  117.9 0.7 fusion.23
  118.7 0.9 add_add_fusion
  119.6 0.9 broadcast_select_fusion
  120.5 0.1 slice.64
  120.7 5.3 %collective-permute-start.15 = (bf16[1024,512]{1,0:T(8,128)(2,1)S(1)}, bf16[1024,512]{1,0:T(8,128)(2,1)S(1)}, u32[]{:S(2)}, u32[]{:S(2)}) collective-permute-start(bf16[1024,512]{1,0:T(8,128)(2,1)S(1)} %pad_maximum_fusion.1), channel_id=1, source_target_pairs={{0,1},{1,0},{2,3},{3,2},{4,5},{5,4},{6,7},{7,6},{8,9},{9,8},{10,11... | collective-permute-start | bytes 3145736 | tf_op jit(solution)/shard_map/ppermute | solution.py:13
  126.0 2.3 %collective-permute-done.15 = bf16[1024,512]{1,0:T(8,128)(2,1)S(1)} collective-permute-done((bf16[1024,512]{1,0:T(8,128)(2,1)S(1)}, bf16[1024,512]{1,0:T(8,128)(2,1)S(1)}, u32[]{:S(2)}, u32[]{:S(2)}) %collective-permute-start.15) | collective-permute-done | bytes 1048608 | tf_op jit(solution)/shard_map/ppermute | solution.py:13
  128.3 0.3 convert_element_type.43
  128.6 0.3 fusion.6
  128.8 0.1 collective-permute-start.16
  128.9 14.6 %collective-permute-done.16 = bf16[512,512]{1,0:T(8,128)(2,1)S(1)} collective-permute-done((bf16[512,512]{1,0:T(8,128)(2,1)S(1)}, bf16[512,512]{1,0:T(8,128)(2,1)S(1)}, u32[]{:S(2)}, u32[]{:S(2)}) %collective-permute-start.16) | collective-permute-done | bytes 524320 | tf_op jit(solution)/shard_map/ppermute | solution.py:13
  143.6 0.3 fusion.8
  143.9 0.3 collective-permute-start.17
  144.1 2.7 %collective-permute-start.18 = (bf16[512,512]{1,0:T(8,128)(2,1)S(1)}, bf16[512,512]{1,0:T(8,128)(2,1)S(1)}, u32[]{:S(2)}, u32[]{:S(2)}) collective-permute-start(bf16[512,512]{1,0:T(8,128)(2,1)S(1)} %fusion.8), channel_id=1, source_target_pairs={{0,96},{32,0},{64,32},{96,64},{1,97},{33,1},{65,33},{97,65},{2,98}... | collective-permute-start | bytes 1572872 | tf_op jit(solution)/shard_map/ppermute | solution.py:13
  146.8 10.7 %collective-permute-done.17 = bf16[512,512]{1,0:T(8,128)(2,1)S(1)} collective-permute-done((bf16[512,512]{1,0:T(8,128)(2,1)S(1)}, bf16[512,512]{1,0:T(8,128)(2,1)S(1)}, u32[]{:S(2)}, u32[]{:S(2)}) %collective-permute-start.17) | collective-permute-done | bytes 524320 | tf_op jit(solution)/shard_map/ppermute | solution.py:13
  157.6 0.1 collective-permute-start.19
  157.7 2.7 %collective-permute-start.20 = (bf16[256,512]{1,0:T(8,128)(2,1)S(1)}, bf16[256,512]{1,0:T(8,128)(2,1)S(1)}, u32[]{:S(2)}, u32[]{:S(2)}) collective-permute-start(bf16[256,512]{1,0:T(8,128)(2,1)S(1)} %slice.51), channel_id=1, source_target_pairs={{0,96},{32,0},{64,32},{96,64},{1,97},{33,1},{65,33},{97,65},{2,98}... | collective-permute-start | bytes 786440 | tf_op jit(solution)/shard_map/ppermute | solution.py:13
  160.4 4.1 %collective-permute-done.19 = bf16[256,512]{1,0:T(8,128)(2,1)S(1)} collective-permute-done((bf16[256,512]{1,0:T(8,128)(2,1)S(1)}, bf16[256,512]{1,0:T(8,128)(2,1)S(1)}, u32[]{:S(2)}, u32[]{:S(2)}) %collective-permute-start.19) | collective-permute-done | bytes 262176 | tf_op jit(solution)/shard_map/ppermute | solution.py:13
  164.6 1.6 fusion.40
  166.3 1.5 fusion.33
  167.8 0.4 fusion.38
  168.2 0.4 fusion.31
  168.7 0.4 fusion.36
  169.1 0.4 fusion.29
  169.6 0.4 fusion.4
  170.0 0.5 fusion.5
  170.6 22.8 %all_to_all.6 = bf16[32,32,512]{2,1,0:T(8,128)(2,1)S(1)} all-to-all(bf16[32,32,512]{2,1,0:T(8,128)(2,1)S(1)} %bitcast.22), channel_id=1, replica_groups=mesh['y'=4,'xh'=2,'xl'=2,'z'=4,'core'=2] {'xh','xl','z','core'}, dimensions={0} | all-to-all | bytes 2097152 | tf_op jit(solution)/shard_map/all_to_all | solution.py:86
  193.4 0.2 convert_reduce_fusion
  193.6 0.1 copy.7
  193.7 0.9 add_convert_fusion
  (38 shorter events, 0.4 us)
Async XLA Ops:
  6.5 46.1 %copy-start.7 = (bf16[512,256]{1,0:T(8,128)(2,1)S(1)}, bf16[512,256]{1,0:T(8,128)(2,1)}, u32[]{:S(2)}) copy-start(bf16[512,256]{1,0:T(8,128)(2,1)} %param.8) | copy-start | bytes 786436
  6.5 158.1 %all-gather.2.cloned.1.call-start = ((), (), s32[]{:S(2)}) async-start(), calls=%async_computation.1 | async-start | bytes 4718592 | tf_op jit(solution)/shard_map/all_gather | solution.py:55
  7.9 5.1 %collective-permute-start = (bf16[512,512]{1,0:T(8,128)(2,1)S(1)}, bf16[512,512]{1,0:T(8,128)(2,1)S(1)}, u32[]{:S(2)}, u32[]{:S(2)}) collective-permute-start(bf16[512,512]{1,0:T(8,128)(2,1)S(1)} %subtract_convert_fusion), channel_id=1, source_target_pairs={{0,0},{2,16},{4,4},{6,20},{8,8},{10,24},{12,12},{14,28},{16,2},{18... | collective-permute-start | bytes 1572872 | tf_op jit(solution)/shard_map/ppermute | solution.py:23
  8.6 18.9 %collective-permute-start.2 = (bf16[512,512]{1,0:T(8,128)(2,1)S(1)}, bf16[512,512]{1,0:T(8,128)(2,1)S(1)}, u32[]{:S(2)}, u32[]{:S(2)}) collective-permute-start(bf16[512,512]{1,0:T(8,128)(2,1)S(1)} %subtract_convert_fusion), channel_id=1, source_target_pairs={{0,8},{2,24},{4,12},{6,28},{8,0},{10,16},{12,4},{14,20},{16,10},{1... | collective-permute-start | bytes 1572872 | tf_op jit(solution)/shard_map/ppermute | solution.py:23
  12.0 29.9 %collective-permute-start.6 = (bf16[512,512]{1,0:T(8,128)(2,1)S(1)}, bf16[512,512]{1,0:T(8,128)(2,1)S(1)}, u32[]{:S(2)}, u32[]{:S(2)}) collective-permute-start(bf16[512,512]{1,0:T(8,128)(2,1)S(1)} %get-tuple-element.12), channel_id=1, source_target_pairs={{0,1},{1,0},{2,3},{3,2},{4,5},{5,4},{6,7},{7,6},{8,9},{9,8},{10,11... | collective-permute-start | bytes 1572872 | tf_op jit(solution)/shard_map/ppermute | solution.py:13
  13.0 35.7 %collective-permute-start.1 = (bf16[512,512]{1,0:T(8,128)(2,1)S(1)}, bf16[512,512]{1,0:T(8,128)(2,1)S(1)}, u32[]{:S(2)}, u32[]{:S(2)}) collective-permute-start(bf16[512,512]{1,0:T(8,128)(2,1)S(1)} %collective-permute-done), channel_id=1, source_target_pairs={{0,2},{2,4},{4,6},{6,0},{1,3},{3,5},{5,7},{7,1},{8,10},{10,12},{12... | collective-permute-start | bytes 1572872 | tf_op jit(solution)/shard_map/ppermute | solution.py:13
  27.5 25.1 %collective-permute-start.3 = (bf16[512,512]{1,0:T(8,128)(2,1)S(1)}, bf16[512,512]{1,0:T(8,128)(2,1)S(1)}, u32[]{:S(2)}, u32[]{:S(2)}) collective-permute-start(bf16[512,512]{1,0:T(8,128)(2,1)S(1)} %collective-permute-done.2), channel_id=1, source_target_pairs={{0,6},{2,0},{4,2},{6,4},{1,7},{3,1},{5,3},{7,5},{8,14},{10,8},{12,... | collective-permute-start | bytes 1572872 | tf_op jit(solution)/shard_map/ppermute | solution.py:13
  43.6 25.4 %collective-permute-start.8 = (bf16[512,1024]{1,0:T(8,128)(2,1)}, bf16[512,1024]{1,0:T(8,128)(2,1)S(1)}, u32[]{:S(2)}, u32[]{:S(2)}) collective-permute-start(bf16[512,1024]{1,0:T(8,128)(2,1)} %get-tuple-element.9), channel_id=1, source_target_pairs={{0,32},{32,64},{64,96},{96,0},{1,33},{33,65},{65,97},{97,1},{2,34}... | collective-permute-start | bytes 3145736 | tf_op jit(solution)/shard_map/ppermute | solution.py:13
  44.9 24.9 %collective-permute-start.7 = (bf16[512,1024]{1,0:T(8,128)(2,1)}, bf16[512,1024]{1,0:T(8,128)(2,1)S(1)}, u32[]{:S(2)}, u32[]{:S(2)}) collective-permute-start(bf16[512,1024]{1,0:T(8,128)(2,1)} %get-tuple-element.9), channel_id=1, source_target_pairs={{0,96},{32,0},{64,32},{96,64},{1,97},{33,1},{65,33},{97,65},{2,98}... | collective-permute-start | bytes 3145736 | tf_op jit(solution)/shard_map/ppermute | solution.py:13
  48.8 3.9 %copy-start.2 = (bf16[512,512]{1,0:T(8,128)(2,1)}, bf16[512,512]{1,0:T(8,128)(2,1)S(1)}, u32[]{:S(2)}) copy-start(bf16[512,512]{1,0:T(8,128)(2,1)S(1)} %collective-permute-done.1) | copy-start | bytes 1572868
  52.7 0.8 copy-start.4
  52.7 2.0 %collective-permute-start.4 = (bf16[512,256]{1,0:T(8,128)(2,1)S(1)}, bf16[512,256]{1,0:T(8,128)(2,1)S(1)}, u32[]{:S(2)}, u32[]{:S(2)}) collective-permute-start(bf16[512,256]{1,0:T(8,128)(2,1)S(1)} %copy-done.7), channel_id=1, source_target_pairs={{0,0},{2,16},{4,4},{6,20},{8,8},{10,24},{12,12},{14,28},{16,2},{18... | collective-permute-start | bytes 786440 | tf_op jit(solution)/shard_map/ppermute | solution.py:23
  53.5 6.4 %collective-permute-start.5 = (bf16[512,256]{1,0:T(8,128)(2,1)S(1)}, bf16[512,256]{1,0:T(8,128)(2,1)S(1)}, u32[]{:S(2)}, u32[]{:S(2)}) collective-permute-start(bf16[512,256]{1,0:T(8,128)(2,1)S(1)} %copy-done.7), channel_id=1, source_target_pairs={{0,8},{2,24},{4,12},{6,28},{8,0},{10,16},{12,4},{14,20},{16,10},{1... | collective-permute-start | bytes 786440 | tf_op jit(solution)/shard_map/ppermute | solution.py:23
  69.9 13.3 %collective-permute-start.9 = (bf16[256,1024]{1,0:T(8,128)(2,1)}, bf16[256,1024]{1,0:T(8,128)(2,1)}, u32[]{:S(2)}, u32[]{:S(2)}) collective-permute-start(bf16[256,1024]{1,0:T(8,128)(2,1)} %slice.42), channel_id=1, source_target_pairs={{0,32},{32,64},{64,96},{96,0},{1,33},{33,65},{65,97},{97,1},{2,34}... | collective-permute-start | bytes 1572872 | tf_op jit(solution)/shard_map/ppermute | solution.py:13
  70.7 21.8 %collective-permute-start.10 = (bf16[256,1024]{1,0:T(8,128)(2,1)}, bf16[256,1024]{1,0:T(8,128)(2,1)}, u32[]{:S(2)}, u32[]{:S(2)}) collective-permute-start(bf16[256,1024]{1,0:T(8,128)(2,1)} %slice.43), channel_id=1, source_target_pairs={{0,96},{32,0},{64,32},{96,64},{1,97},{33,1},{65,33},{97,65},{2,98}... | collective-permute-start | bytes 1572872 | tf_op jit(solution)/shard_map/ppermute | solution.py:13
  73.4 22.1 %copy-start.3 = (bf16[512,512]{1,0:T(8,128)(2,1)S(1)}, bf16[512,512]{1,0:T(8,128)(2,1)}, u32[]{:S(2)}) copy-start(bf16[512,512]{1,0:T(8,128)(2,1)} %copy-done.2) | copy-start | bytes 1572868
  73.4 26.1 %collective-permute-start.13 = (bf16[512,512]{1,0:T(8,128)(2,1)S(1)}, bf16[512,512]{1,0:T(8,128)(2,1)S(1)}, u32[]{:S(2)}, u32[]{:S(2)}) collective-permute-start(bf16[512,512]{1,0:T(8,128)(2,1)S(1)} %collective-permute-done), channel_id=1, source_target_pairs={{0,6},{2,0},{4,2},{6,4},{1,7},{3,1},{5,3},{7,5},{8,14},{10,8},{12,... | collective-permute-start | bytes 1572872 | tf_op jit(solution)/shard_map/ppermute | solution.py:13
  79.5 20.7 %collective-permute-start.14 = (bf16[512,512]{1,0:T(8,128)(2,1)S(1)}, bf16[512,512]{1,0:T(8,128)(2,1)S(1)}, u32[]{:S(2)}, u32[]{:S(2)}) collective-permute-start(bf16[512,512]{1,0:T(8,128)(2,1)S(1)} %collective-permute-done.2), channel_id=1, source_target_pairs={{0,2},{2,4},{4,6},{6,0},{1,3},{3,5},{5,7},{7,1},{8,10},{10,12},{12... | collective-permute-start | bytes 1572872 | tf_op jit(solution)/shard_map/ppermute | solution.py:13
  79.5 38.4 %collective-permute-start.11 = (bf16[512,512]{1,0:T(8,128)(2,1)}, bf16[512,512]{1,0:T(8,128)(2,1)S(1)}, u32[]{:S(2)}, u32[]{:S(2)}) collective-permute-start(bf16[512,512]{1,0:T(8,128)(2,1)} %copy-done.2), channel_id=1, source_target_pairs={{0,2},{2,4},{4,6},{6,0},{1,3},{3,5},{5,7},{7,1},{8,10},{10,12},{12... | collective-permute-start | bytes 1572872 | tf_op jit(solution)/shard_map/ppermute | solution.py:13
  83.1 36.4 %collective-permute-start.12 = (bf16[512,512]{1,0:T(8,128)(2,1)}, bf16[512,512]{1,0:T(8,128)(2,1)S(1)}, u32[]{:S(2)}, u32[]{:S(2)}) collective-permute-start(bf16[512,512]{1,0:T(8,128)(2,1)} %copy-done.4), channel_id=1, source_target_pairs={{0,6},{2,0},{4,2},{6,4},{1,7},{3,1},{5,3},{7,5},{8,14},{10,8},{12,... | collective-permute-start | bytes 1572872 | tf_op jit(solution)/shard_map/ppermute | solution.py:13
  95.5 2.5 %copy-start = (bf16[2048,1024]{1,0:T(8,128)(2,1)S(1)}, bf16[2048,1024]{1,0:T(8,128)(2,1)}, u32[]{:S(2)}) copy-start(bf16[2048,1024]{1,0:T(8,128)(2,1)} %constant_dynamic-update-slice_fusion) | copy-start | bytes 12582916
  100.2 18.5 %copy-start.5 = (bf16[512,512]{1,0:T(8,128)(2,1)S(1)}, bf16[512,512]{1,0:T(8,128)(2,1)}, u32[]{:S(2)}) copy-start(bf16[512,512]{1,0:T(8,128)(2,1)} %copy-done.4) | copy-start | bytes 1572868
  120.7 7.6 %collective-permute-start.15 = (bf16[1024,512]{1,0:T(8,128)(2,1)S(1)}, bf16[1024,512]{1,0:T(8,128)(2,1)S(1)}, u32[]{:S(2)}, u32[]{:S(2)}) collective-permute-start(bf16[1024,512]{1,0:T(8,128)(2,1)S(1)} %pad_maximum_fusion.1), channel_id=1, source_target_pairs={{0,1},{1,0},{2,3},{3,2},{4,5},{5,4},{6,7},{7,6},{8,9},{9,8},{10,11... | collective-permute-start | bytes 3145736 | tf_op jit(solution)/shard_map/ppermute | solution.py:13
  128.8 14.7 %collective-permute-start.16 = (bf16[512,512]{1,0:T(8,128)(2,1)S(1)}, bf16[512,512]{1,0:T(8,128)(2,1)S(1)}, u32[]{:S(2)}, u32[]{:S(2)}) collective-permute-start(bf16[512,512]{1,0:T(8,128)(2,1)S(1)} %fusion.6), channel_id=1, source_target_pairs={{0,16},{16,0},{1,17},{17,1},{2,18},{18,2},{3,19},{19,3},{4,20},{20... | collective-permute-start | bytes 1572872 | tf_op jit(solution)/shard_map/ppermute | solution.py:13
  143.9 13.7 %collective-permute-start.17 = (bf16[512,512]{1,0:T(8,128)(2,1)S(1)}, bf16[512,512]{1,0:T(8,128)(2,1)S(1)}, u32[]{:S(2)}, u32[]{:S(2)}) collective-permute-start(bf16[512,512]{1,0:T(8,128)(2,1)S(1)} %fusion.8), channel_id=1, source_target_pairs={{0,32},{32,64},{64,96},{96,0},{1,33},{33,65},{65,97},{97,1},{2,34}... | collective-permute-start | bytes 1572872 | tf_op jit(solution)/shard_map/ppermute | solution.py:13
  144.1 13.5 %collective-permute-start.18 = (bf16[512,512]{1,0:T(8,128)(2,1)S(1)}, bf16[512,512]{1,0:T(8,128)(2,1)S(1)}, u32[]{:S(2)}, u32[]{:S(2)}) collective-permute-start(bf16[512,512]{1,0:T(8,128)(2,1)S(1)} %fusion.8), channel_id=1, source_target_pairs={{0,96},{32,0},{64,32},{96,64},{1,97},{33,1},{65,33},{97,65},{2,98}... | collective-permute-start | bytes 1572872 | tf_op jit(solution)/shard_map/ppermute | solution.py:13
  157.6 7.0 %collective-permute-start.19 = (bf16[256,512]{1,0:T(8,128)(2,1)S(1)}, bf16[256,512]{1,0:T(8,128)(2,1)S(1)}, u32[]{:S(2)}, u32[]{:S(2)}) collective-permute-start(bf16[256,512]{1,0:T(8,128)(2,1)S(1)} %slice.50), channel_id=1, source_target_pairs={{0,32},{32,64},{64,96},{96,0},{1,33},{33,65},{65,97},{97,1},{2,34}... | collective-permute-start | bytes 786440 | tf_op jit(solution)/shard_map/ppermute | solution.py:13
  157.7 6.9 %collective-permute-start.20 = (bf16[256,512]{1,0:T(8,128)(2,1)S(1)}, bf16[256,512]{1,0:T(8,128)(2,1)S(1)}, u32[]{:S(2)}, u32[]{:S(2)}) collective-permute-start(bf16[256,512]{1,0:T(8,128)(2,1)S(1)} %slice.51), channel_id=1, source_target_pairs={{0,96},{32,0},{64,32},{96,64},{1,97},{33,1},{65,33},{97,65},{2,98}... | collective-permute-start | bytes 786440 | tf_op jit(solution)/shard_map/ppermute | solution.py:13
  164.6 3.1 %copy-start.1 = (bf16[1024,2048]{1,0:T(8,128)(2,1)S(1)}, bf16[1024,2048]{1,0:T(8,128)(2,1)}, u32[]{:S(2)}) copy-start(bf16[1024,2048]{1,0:T(8,128)(2,1)} %all-gather.2.cloned.1.call-done) | copy-start | bytes 12582916
  170.5 23.2 %copy-start.6 = (bf16[32,8192]{1,0:T(8,128)(2,1)S(1)}, bf16[32,8192]{1,0:T(8,128)(2,1)}, u32[]{:S(2)}) copy-start(bf16[32,8192]{1,0:T(8,128)(2,1)} %param.9) | copy-start | bytes 1572868
Sparse Core Ops, SparseCore 0:
  60.9 63.9 all-gather.1

commit v3 on v2

--- a/solution.py
+++ b/solution.py
@@ -42,21 +42,19 @@
     mine = lax.dynamic_slice_in_dim(input_factor, core * depth, depth, 0)
     other = lax.dynamic_slice_in_dim(input_factor, (1 - core) * depth, depth, 0)
     pair = jnp.concatenate([mine, shift(other, "core", 1)], axis=1)
-    below, above = shift(pair, "y", 1), shift(pair, "y", -1)
-    far = [shift(below[: depth // 2], "y", 1), shift(above[depth // 2 :], "y", -1)]
-    factor = jnp.concatenate([pair, above, *far, below], axis=0)
+    factor = lax.all_gather(pair, "y", axis=0, tiled=True)
 
     am, bp = shift(a, "z", 1), shift(b, "z", -1)
     bm, ap = shift(b, "z", 1), shift(a, "z", -1)
     a2, b2 = shift(am, "z", 1), shift(bp, "z", -1)
 
-    part = after(output_factor, am, bp)
+    part = after(output_factor, am, ap, bm, bp)
     part = jnp.concatenate([turn(part, 0), turn(part, 1)], axis=0)
     left = lax.all_gather(part, ("z", "core"), axis=1, tiled=True)
 
     def term(block, dxl, dz):
         at = (xl ^ dxl) * 2 + (((z + dz) & 3) >> 1)
-        return dot(block, lax.dynamic_slice_in_dim(factor, ((at - y) & 3) * depth, depth, 0))
+        return dot(block, lax.dynamic_slice_in_dim(factor, at * depth, depth, 0))
 
     odd = term(am, 0, -1) + term(ap, 0, 1) + term(bm, 1, -1) + term(bp, 1, 1)
     even = term(a, 0, 0) + term(b, 1, 0) + term(a2, 0, 2) + term(b2, 1, 2)

time: 202 us -> 183 us (0.906)
  waiting for transfers between devices: 71.1 us -> 60.1 us
  local copies, waits for them, and re-layouts: 9.74 us -> 3.55 us
  starting transfers between devices: 64.7 us -> 60.3 us
  blocking collectives: 22.8 us -> 26.1 us
    ppermute x17 -> x13, waiting for transfers between devices: 65.9 us -> 53.9 us  [shift(): return lax.ppermute(v, axis, [(i, (i + by) % n) for i in range(n)])]
    ppermute x17 -> x13, starting transfers between devices: 60 us -> 56.3 us  [shift(): return lax.ppermute(v, axis, [(i, (i + by) % n) for i in range(n)])]
    unnamed x20 -> x17, local copies, waits for them, and re-layouts: 5.39 us -> 2 us
    all_to_all x1, blocking collectives: 22.8 us -> 26.1 us  [body(): lax.all_to_all(penalty, ('xh',) + COL, split_axis=0, concat_axis=0, tiled...]
  transfers between devices with their start and end apart: 22 -> 19, of which waited for: 10 -> 8; matrix products, arithmetic and copies ran while one was open for 10% -> 8% of each run, Pallas kernels for 0% -> 0%
where the time goes in v3:
time: 183 us; the launch traced here: 182 us
  starting transfers between devices  60.3 us (33%)
  waiting for transfers between devices  60.1 us (33%)
  blocking collectives  26.1 us (14%)
  matrix products  14.4 us (8%)
  between operations  13.8 us (8%)
  other arithmetic  4.19 us (2%)
  local copies, waits for them, and re-layouts  3.55 us (2%)
    ppermute x13, starting transfers between devices, shift(): return lax.ppermute(v, axis, [(i, (i + by) % n) for i in range(n)])  56.3 us
    ppermute x13, waiting for transfers between devices, shift(): return lax.ppermute(v, axis, [(i, (i + by) % n) for i in range(n)])  53.9 us
    all_to_all x1, blocking collectives, body(): lax.all_to_all(penalty, ('xh',) + COL, split_axis=0, concat_axis=0, tiled...  26.1 us
    dot_general x16, matrix products, dot(): return jnp.dot(a, b, preferred_element_type=F32)  14.4 us
    ppermute x4, waiting for transfers between devices, turn(): return lax.ppermute(v, ('xh', 'xl', 'z'), pairs)  6.19 us
    ppermute x4, starting transfers between devices, turn(): return lax.ppermute(v, ('xh', 'xl', 'z'), pairs)  4.03 us
  transfers between devices with their start and end apart: 19, of which 8 were waited for; matrix products, arithmetic and copies ran while one was open for 8% of the time, Pallas kernels for 0%

profile of v3, /device:TPU:1, one launch (start us, length us, event | category | flops | bytes accessed | tf_op | source)
XLA Modules:
  0.0 182.4 jit_solution(7652979134354303704)
XLA Ops:
  6.5 1.3 constant_dynamic-slice_fusion.1
  7.8 0.0 copy-start.2
  7.8 0.0 copy-start.3
  7.8 1.5 collective-permute-start.8
  9.3 1.5 collective-permute-done.8
  10.9 1.2 pad_maximum_fusion
  12.0 0.0 all-gather.5.cloned.1.call-update
  12.1 0.0 all-gather.3.cloned.1.call-start
  12.1 0.1 subtract_convert_fusion
  12.3 0.7 collective-permute-start
  13.0 1.4 collective-permute-start.3
  14.4 17.1 %collective-permute-start.1 = (bf16[512,512]{1,0:T(8,128)(2,1)S(1)}, bf16[512,512]{1,0:T(8,128)(2,1)S(1)}, u32[]{:S(2)}, u32[]{:S(2)}) collective-permute-start(bf16[512,512]{1,0:T(8,128)(2,1)S(1)} %collective-permute-done), channel_id=1, source_target_pairs={{0,2},{2,4},{4,6},{6,0},{1,3},{3,5},{5,7},{7,1},{8,10},{10,12},{12... | collective-permute-start | bytes 1572872 | tf_op jit(solution)/shard_map/ppermute | solution.py:13
  31.5 2.1 %collective-permute-start.2 = (bf16[512,512]{1,0:T(8,128)(2,1)S(1)}, bf16[512,512]{1,0:T(8,128)(2,1)S(1)}, u32[]{:S(2)}, u32[]{:S(2)}) collective-permute-start(bf16[512,512]{1,0:T(8,128)(2,1)S(1)} %collective-permute-done), channel_id=1, source_target_pairs={{0,6},{2,0},{4,2},{6,4},{1,7},{3,1},{5,3},{7,5},{8,14},{10,8},{12,... | collective-permute-start | bytes 1572872 | tf_op jit(solution)/shard_map/ppermute | solution.py:13
  33.6 9.8 %collective-permute-start.4 = (bf16[512,512]{1,0:T(8,128)(2,1)S(1)}, bf16[512,512]{1,0:T(8,128)(2,1)S(1)}, u32[]{:S(2)}, u32[]{:S(2)}) collective-permute-start(bf16[512,512]{1,0:T(8,128)(2,1)S(1)} %collective-permute-done.3), channel_id=1, source_target_pairs={{0,2},{2,4},{4,6},{6,0},{1,3},{3,5},{5,7},{7,1},{8,10},{10,12},{12... | collective-permute-start | bytes 1572872 | tf_op jit(solution)/shard_map/ppermute | solution.py:13
  43.4 2.1 %collective-permute-start.5 = (bf16[512,512]{1,0:T(8,128)(2,1)S(1)}, bf16[512,512]{1,0:T(8,128)(2,1)S(1)}, u32[]{:S(2)}, u32[]{:S(2)}) collective-permute-start(bf16[512,512]{1,0:T(8,128)(2,1)S(1)} %collective-permute-done.3), channel_id=1, source_target_pairs={{0,6},{2,0},{4,2},{6,4},{1,7},{3,1},{5,3},{7,5},{8,14},{10,8},{12,... | collective-permute-start | bytes 1572872 | tf_op jit(solution)/shard_map/ppermute | solution.py:13
  45.5 6.9 %collective-permute-done.1 = bf16[512,512]{1,0:T(8,128)(2,1)S(1)} collective-permute-done((bf16[512,512]{1,0:T(8,128)(2,1)S(1)}, bf16[512,512]{1,0:T(8,128)(2,1)S(1)}, u32[]{:S(2)}, u32[]{:S(2)}) %collective-permute-start.1) | collective-permute-done | bytes 524320 | tf_op jit(solution)/shard_map/ppermute | solution.py:13
  52.4 11.2 %collective-permute-done.4 = bf16[512,512]{1,0:T(8,128)(2,1)S(1)} collective-permute-done((bf16[512,512]{1,0:T(8,128)(2,1)S(1)}, bf16[512,512]{1,0:T(8,128)(2,1)S(1)}, u32[]{:S(2)}, u32[]{:S(2)}) %collective-permute-start.4) | collective-permute-done | bytes 524320 | tf_op jit(solution)/shard_map/ppermute | solution.py:13
  63.7 0.8 copy-done.4
  64.5 0.7 collective-permute-start.6
  65.1 1.3 collective-permute-start.7
  66.4 6.2 %collective-permute-done.7 = bf16[512,256]{1,0:T(8,128)(2,1)S(1)} collective-permute-done((bf16[512,256]{1,0:T(8,128)(2,1)S(1)}, bf16[512,256]{1,0:T(8,128)(2,1)S(1)}, u32[]{:S(2)}, u32[]{:S(2)}) %collective-permute-start.7) | collective-permute-done | bytes 262176 | tf_op jit(solution)/shard_map/ppermute | solution.py:23
  72.6 0.8 pad_maximum_fusion.3
  73.4 0.0 all-gather.3.cloned.1.call-update
  73.5 12.3 %collective-permute-start.9 = (bf16[512,512]{1,0:T(8,128)(2,1)S(1)}, bf16[512,512]{1,0:T(8,128)(2,1)S(1)}, u32[]{:S(2)}, u32[]{:S(2)}) collective-permute-start(bf16[512,512]{1,0:T(8,128)(2,1)S(1)} %collective-permute-done.1), channel_id=1, source_target_pairs={{0,2},{2,4},{4,6},{6,0},{1,3},{3,5},{5,7},{7,1},{8,10},{10,12},{12... | collective-permute-start | bytes 1572872 | tf_op jit(solution)/shard_map/ppermute | solution.py:13
  85.8 2.2 %collective-permute-start.10 = (bf16[512,512]{1,0:T(8,128)(2,1)}, bf16[512,512]{1,0:T(8,128)(2,1)}, u32[]{:S(2)}, u32[]{:S(2)}) collective-permute-start(bf16[512,512]{1,0:T(8,128)(2,1)} %copy-done.4), channel_id=1, source_target_pairs={{0,6},{2,0},{4,2},{6,4},{1,7},{3,1},{5,3},{7,5},{8,14},{10,8},{12,... | collective-permute-start | bytes 1572872 | tf_op jit(solution)/shard_map/ppermute | solution.py:13
  88.0 2.1 %fusion.17 = f32[512,1024]{1,0:T(8,128)S(1)} fusion(bf16[512,512]{1,0:T(8,128)(2,1)S(1)} %collective-permute-done.1, bf16[2048,1024]{1,0:T(8,128)(2,1)} %all-gather.5.cloned.1.call-done, s32[]{:T(128)S(6)} %select_n.91), kind=kOutput, calls=%fused_computation.28 | convolution fusion | flops 536870912 | bytes 3670020 | tf_op jit(solution)/shard_map/dot_general | solution.py:31
  90.0 0.4 copy-done
  90.5 0.7 fusion.15
  91.2 0.7 fusion.13
  91.9 0.7 fusion.25
  92.7 0.7 fusion.27
  93.4 6.3 %collective-permute-done.9 = bf16[512,512]{1,0:T(8,128)(2,1)S(1)} collective-permute-done((bf16[512,512]{1,0:T(8,128)(2,1)S(1)}, bf16[512,512]{1,0:T(8,128)(2,1)S(1)}, u32[]{:S(2)}, u32[]{:S(2)}) %collective-permute-start.9) | collective-permute-done | bytes 524320 | tf_op jit(solution)/shard_map/ppermute | solution.py:13
  99.7 0.7 fusion.23
  100.5 0.9 add_add_fusion
  101.4 2.0 %broadcast_select_fusion = (f32[512,1024]{1,0:T(8,128)S(1)}, f32[512,1024]{1,0:T(8,128)S(1)}) fusion(f32[512,1024]{1,0:T(8,128)S(1)} %add_add_fusion, pred[]{:T(512)S(6)} %eq.3, bf16[512,512]{1,0:T(8,128)(2,1)} %collective-permute-done.10, bf16[2048,1024]{1,0:T(8,128)(2,1)S(1)} %copy-done, s32[]{:T(128)S(6)} %select_n.90, f32[512,1024]{1,0:T(8,128)S(1)} %fusion.23, ...), kind=kOutput, calls=%fused_computation.39 | convolution fusion | flops 539492352 | bytes 14155781 | tf_op jit(solution)/shard_map/dot_general | solution.py:31
  103.4 0.1 slice.54
  103.5 0.1 slice.55
  103.5 0.1 pad_maximum_fusion.1
  103.6 3.0 %collective-permute-start.11 = (bf16[1024,512]{1,0:T(8,128)(2,1)S(1)}, bf16[1024,512]{1,0:T(8,128)(2,1)S(1)}, u32[]{:S(2)}, u32[]{:S(2)}) collective-permute-start(bf16[1024,512]{1,0:T(8,128)(2,1)S(1)} %pad_maximum_fusion.1), channel_id=1, source_target_pairs={{0,1},{1,0},{2,3},{3,2},{4,5},{5,4},{6,7},{7,6},{8,9},{9,8},{10,11... | collective-permute-start | bytes 3145736 | tf_op jit(solution)/shard_map/ppermute | solution.py:13
  106.6 2.7 %collective-permute-done.11 = bf16[1024,512]{1,0:T(8,128)(2,1)S(1)} collective-permute-done((bf16[1024,512]{1,0:T(8,128)(2,1)S(1)}, bf16[1024,512]{1,0:T(8,128)(2,1)S(1)}, u32[]{:S(2)}, u32[]{:S(2)}) %collective-permute-start.11) | collective-permute-done | bytes 1048608 | tf_op jit(solution)/shard_map/ppermute | solution.py:13
  109.3 0.3 convert_element_type.43
  109.6 0.3 fusion.6
  109.9 0.3 collective-permute-start.12
  110.1 14.4 %collective-permute-done.12 = bf16[512,512]{1,0:T(8,128)(2,1)S(1)} collective-permute-done((bf16[512,512]{1,0:T(8,128)(2,1)S(1)}, bf16[512,512]{1,0:T(8,128)(2,1)S(1)}, u32[]{:S(2)}, u32[]{:S(2)}) %collective-permute-start.12) | collective-permute-done | bytes 524320 | tf_op jit(solution)/shard_map/ppermute | solution.py:13
  124.6 0.3 fusion.8
  124.9 1.4 collective-permute-start.13
  126.3 1.5 collective-permute-start.14
  127.8 10.8 %collective-permute-done.13 = bf16[512,512]{1,0:T(8,128)(2,1)S(1)} collective-permute-done((bf16[512,512]{1,0:T(8,128)(2,1)S(1)}, bf16[512,512]{1,0:T(8,128)(2,1)S(1)}, u32[]{:S(2)}, u32[]{:S(2)}) %collective-permute-start.13) | collective-permute-done | bytes 524320 | tf_op jit(solution)/shard_map/ppermute | solution.py:13
  138.6 0.1 collective-permute-start.15
  138.7 2.9 %collective-permute-start.16 = (bf16[256,512]{1,0:T(8,128)(2,1)S(1)}, bf16[256,512]{1,0:T(8,128)(2,1)S(1)}, u32[]{:S(2)}, u32[]{:S(2)}) collective-permute-start(bf16[256,512]{1,0:T(8,128)(2,1)S(1)} %slice.41), channel_id=1, source_target_pairs={{0,96},{32,0},{64,32},{96,64},{1,97},{33,1},{65,33},{97,65},{2,98}... | collective-permute-start | bytes 786440 | tf_op jit(solution)/shard_map/ppermute | solution.py:13
  141.6 1.6 fusion.40
  143.2 1.5 fusion.33
  144.7 0.4 fusion.38
  145.2 0.4 fusion.31
  145.7 0.4 fusion.36
  146.1 0.4 fusion.29
  146.6 0.4 fusion.4
  147.0 0.5 fusion.5
  147.5 0.1 pad_maximum_fusion.2
  147.6 26.1 %all_to_all.6 = bf16[32,32,512]{2,1,0:T(8,128)(2,1)S(1)} all-to-all(bf16[32,32,512]{2,1,0:T(8,128)(2,1)S(1)} %bitcast.22), channel_id=1, replica_groups=mesh['y'=4,'xh'=2,'xl'=2,'z'=4,'core'=2] {'xh','xl','z','core'}, dimensions={0} | all-to-all | bytes 2097152 | tf_op jit(solution)/shard_map/all_to_all | solution.py:84
  173.6 0.2 convert_reduce_fusion
  173.8 0.1 copy.7
  173.9 0.7 copy-done.6
  174.7 0.9 add_convert_fusion
  (27 shorter events, 0.1 us)
Async XLA Ops:
  6.5 81.4 %all-gather.5.cloned.1.call-start = ((), (), s32[]{:S(2)}) async-start(), calls=%async_computation.2 | async-start | bytes 5242880 | tf_op jit(solution)/shard_map/all_gather | solution.py:45
  7.8 4.3 %copy-start.2 = (bf16[512,512]{1,0:T(8,128)(2,1)S(1)}, bf16[512,512]{1,0:T(8,128)(2,1)}, u32[]{:S(2)}) copy-start(bf16[512,512]{1,0:T(8,128)(2,1)} %param.6) | copy-start | bytes 1572868
  7.8 4.3 %copy-start.3 = (bf16[512,512]{1,0:T(8,128)(2,1)S(1)}, bf16[512,512]{1,0:T(8,128)(2,1)}, u32[]{:S(2)}) copy-start(bf16[512,512]{1,0:T(8,128)(2,1)} %param.5) | copy-start | bytes 1572868
  7.8 3.0 %collective-permute-start.8 = (bf16[512,512]{1,0:T(8,128)(2,1)S(1)}, bf16[512,512]{1,0:T(8,128)(2,1)S(1)}, u32[]{:S(2)}, u32[]{:S(2)}) collective-permute-start(bf16[512,512]{1,0:T(8,128)(2,1)S(1)} %get-tuple-element.10), channel_id=1, source_target_pairs={{0,1},{1,0},{2,3},{3,2},{4,5},{5,4},{6,7},{7,6},{8,9},{9,8},{10,11... | collective-permute-start | bytes 1572872 | tf_op jit(solution)/shard_map/ppermute | solution.py:13
  10.9 53.6 %copy-start.7 = (bf16[512,256]{1,0:T(8,128)(2,1)S(1)}, bf16[512,256]{1,0:T(8,128)(2,1)}, u32[]{:S(2)}) copy-start(bf16[512,256]{1,0:T(8,128)(2,1)} %param.8) | copy-start | bytes 786436
  12.1 129.5 %all-gather.3.cloned.1.call-start = ((), (), s32[]{:S(2)}) async-start(), calls=%async_computation.1 | async-start | bytes 4718592 | tf_op jit(solution)/shard_map/all_gather | solution.py:53
  12.3 2.1 %collective-permute-start = (bf16[512,512]{1,0:T(8,128)(2,1)S(1)}, bf16[512,512]{1,0:T(8,128)(2,1)S(1)}, u32[]{:S(2)}, u32[]{:S(2)}) collective-permute-start(bf16[512,512]{1,0:T(8,128)(2,1)S(1)} %subtract_convert_fusion), channel_id=1, source_target_pairs={{0,0},{2,16},{4,4},{6,20},{8,8},{10,24},{12,12},{14,28},{16,2},{18... | collective-permute-start | bytes 1572872 | tf_op jit(solution)/shard_map/ppermute | solution.py:23
  13.0 20.6 %collective-permute-start.3 = (bf16[512,512]{1,0:T(8,128)(2,1)S(1)}, bf16[512,512]{1,0:T(8,128)(2,1)S(1)}, u32[]{:S(2)}, u32[]{:S(2)}) collective-permute-start(bf16[512,512]{1,0:T(8,128)(2,1)S(1)} %subtract_convert_fusion), channel_id=1, source_target_pairs={{0,8},{2,24},{4,12},{6,28},{8,0},{10,16},{12,4},{14,20},{16,10},{1... | collective-permute-start | bytes 1572872 | tf_op jit(solution)/shard_map/ppermute | solution.py:23
  14.4 38.0 %collective-permute-start.1 = (bf16[512,512]{1,0:T(8,128)(2,1)S(1)}, bf16[512,512]{1,0:T(8,128)(2,1)S(1)}, u32[]{:S(2)}, u32[]{:S(2)}) collective-permute-start(bf16[512,512]{1,0:T(8,128)(2,1)S(1)} %collective-permute-done), channel_id=1, source_target_pairs={{0,2},{2,4},{4,6},{6,0},{1,3},{3,5},{5,7},{7,1},{8,10},{10,12},{12... | collective-permute-start | bytes 1572872 | tf_op jit(solution)/shard_map/ppermute | solution.py:13
  31.5 20.9 %collective-permute-start.2 = (bf16[512,512]{1,0:T(8,128)(2,1)S(1)}, bf16[512,512]{1,0:T(8,128)(2,1)S(1)}, u32[]{:S(2)}, u32[]{:S(2)}) collective-permute-start(bf16[512,512]{1,0:T(8,128)(2,1)S(1)} %collective-permute-done), channel_id=1, source_target_pairs={{0,6},{2,0},{4,2},{6,4},{1,7},{3,1},{5,3},{7,5},{8,14},{10,8},{12,... | collective-permute-start | bytes 1572872 | tf_op jit(solution)/shard_map/ppermute | solution.py:13
  33.6 30.0 %collective-permute-start.4 = (bf16[512,512]{1,0:T(8,128)(2,1)S(1)}, bf16[512,512]{1,0:T(8,128)(2,1)S(1)}, u32[]{:S(2)}, u32[]{:S(2)}) collective-permute-start(bf16[512,512]{1,0:T(8,128)(2,1)S(1)} %collective-permute-done.3), channel_id=1, source_target_pairs={{0,2},{2,4},{4,6},{6,0},{1,3},{3,5},{5,7},{7,1},{8,10},{10,12},{12... | collective-permute-start | bytes 1572872 | tf_op jit(solution)/shard_map/ppermute | solution.py:13
  43.4 20.2 %collective-permute-start.5 = (bf16[512,512]{1,0:T(8,128)(2,1)S(1)}, bf16[512,512]{1,0:T(8,128)(2,1)S(1)}, u32[]{:S(2)}, u32[]{:S(2)}) collective-permute-start(bf16[512,512]{1,0:T(8,128)(2,1)S(1)} %collective-permute-done.3), channel_id=1, source_target_pairs={{0,6},{2,0},{4,2},{6,4},{1,7},{3,1},{5,3},{7,5},{8,14},{10,8},{12,... | collective-permute-start | bytes 1572872 | tf_op jit(solution)/shard_map/ppermute | solution.py:13
  63.7 0.8 copy-start.4
  64.5 2.0 %collective-permute-start.6 = (bf16[512,256]{1,0:T(8,128)(2,1)S(1)}, bf16[512,256]{1,0:T(8,128)(2,1)S(1)}, u32[]{:S(2)}, u32[]{:S(2)}) collective-permute-start(bf16[512,256]{1,0:T(8,128)(2,1)S(1)} %copy-done.7), channel_id=1, source_target_pairs={{0,0},{2,16},{4,4},{6,20},{8,8},{10,24},{12,12},{14,28},{16,2},{18... | collective-permute-start | bytes 786440 | tf_op jit(solution)/shard_map/ppermute | solution.py:23
  65.1 7.5 %collective-permute-start.7 = (bf16[512,256]{1,0:T(8,128)(2,1)S(1)}, bf16[512,256]{1,0:T(8,128)(2,1)S(1)}, u32[]{:S(2)}, u32[]{:S(2)}) collective-permute-start(bf16[512,256]{1,0:T(8,128)(2,1)S(1)} %copy-done.7), channel_id=1, source_target_pairs={{0,8},{2,24},{4,12},{6,28},{8,0},{10,16},{12,4},{14,20},{16,10},{1... | collective-permute-start | bytes 786440 | tf_op jit(solution)/shard_map/ppermute | solution.py:23
  73.5 26.2 %collective-permute-start.9 = (bf16[512,512]{1,0:T(8,128)(2,1)S(1)}, bf16[512,512]{1,0:T(8,128)(2,1)S(1)}, u32[]{:S(2)}, u32[]{:S(2)}) collective-permute-start(bf16[512,512]{1,0:T(8,128)(2,1)S(1)} %collective-permute-done.1), channel_id=1, source_target_pairs={{0,2},{2,4},{4,6},{6,0},{1,3},{3,5},{5,7},{7,1},{8,10},{10,12},{12... | collective-permute-start | bytes 1572872 | tf_op jit(solution)/shard_map/ppermute | solution.py:13
  85.8 15.6 %collective-permute-start.10 = (bf16[512,512]{1,0:T(8,128)(2,1)}, bf16[512,512]{1,0:T(8,128)(2,1)}, u32[]{:S(2)}, u32[]{:S(2)}) collective-permute-start(bf16[512,512]{1,0:T(8,128)(2,1)} %copy-done.4), channel_id=1, source_target_pairs={{0,6},{2,0},{4,2},{6,4},{1,7},{3,1},{5,3},{7,5},{8,14},{10,8},{12,... | collective-permute-start | bytes 1572872 | tf_op jit(solution)/shard_map/ppermute | solution.py:13
  88.0 2.5 %copy-start = (bf16[2048,1024]{1,0:T(8,128)(2,1)S(1)}, bf16[2048,1024]{1,0:T(8,128)(2,1)}, u32[]{:S(2)}) copy-start(bf16[2048,1024]{1,0:T(8,128)(2,1)} %all-gather.5.cloned.1.call-done) | copy-start | bytes 12582916
  93.4 7.0 %copy-start.5 = (bf16[512,512]{1,0:T(8,128)(2,1)S(1)}, bf16[512,512]{1,0:T(8,128)(2,1)}, u32[]{:S(2)}) copy-start(bf16[512,512]{1,0:T(8,128)(2,1)} %copy-done.4) | copy-start | bytes 1572868
  103.6 5.7 %collective-permute-start.11 = (bf16[1024,512]{1,0:T(8,128)(2,1)S(1)}, bf16[1024,512]{1,0:T(8,128)(2,1)S(1)}, u32[]{:S(2)}, u32[]{:S(2)}) collective-permute-start(bf16[1024,512]{1,0:T(8,128)(2,1)S(1)} %pad_maximum_fusion.1), channel_id=1, source_target_pairs={{0,1},{1,0},{2,3},{3,2},{4,5},{5,4},{6,7},{7,6},{8,9},{9,8},{10,11... | collective-permute-start | bytes 3145736 | tf_op jit(solution)/shard_map/ppermute | solution.py:13
  109.9 14.7 %collective-permute-start.12 = (bf16[512,512]{1,0:T(8,128)(2,1)S(1)}, bf16[512,512]{1,0:T(8,128)(2,1)S(1)}, u32[]{:S(2)}, u32[]{:S(2)}) collective-permute-start(bf16[512,512]{1,0:T(8,128)(2,1)S(1)} %fusion.6), channel_id=1, source_target_pairs={{0,16},{16,0},{1,17},{17,1},{2,18},{18,2},{3,19},{19,3},{4,20},{20... | collective-permute-start | bytes 1572872 | tf_op jit(solution)/shard_map/ppermute | solution.py:13
  124.9 13.7 %collective-permute-start.13 = (bf16[512,512]{1,0:T(8,128)(2,1)S(1)}, bf16[512,512]{1,0:T(8,128)(2,1)S(1)}, u32[]{:S(2)}, u32[]{:S(2)}) collective-permute-start(bf16[512,512]{1,0:T(8,128)(2,1)S(1)} %fusion.8), channel_id=1, source_target_pairs={{0,32},{32,64},{64,96},{96,0},{1,33},{33,65},{65,97},{97,1},{2,34}... | collective-permute-start | bytes 1572872 | tf_op jit(solution)/shard_map/ppermute | solution.py:13
  126.3 12.4 %collective-permute-start.14 = (bf16[512,512]{1,0:T(8,128)(2,1)S(1)}, bf16[512,512]{1,0:T(8,128)(2,1)S(1)}, u32[]{:S(2)}, u32[]{:S(2)}) collective-permute-start(bf16[512,512]{1,0:T(8,128)(2,1)S(1)} %fusion.8), channel_id=1, source_target_pairs={{0,96},{32,0},{64,32},{96,64},{1,97},{33,1},{65,33},{97,65},{2,98}... | collective-permute-start | bytes 1572872 | tf_op jit(solution)/shard_map/ppermute | solution.py:13
  138.6 7.0 %collective-permute-start.15 = (bf16[256,512]{1,0:T(8,128)(2,1)S(1)}, bf16[256,512]{1,0:T(8,128)(2,1)S(1)}, u32[]{:S(2)}, u32[]{:S(2)}) collective-permute-start(bf16[256,512]{1,0:T(8,128)(2,1)S(1)} %slice.40), channel_id=1, source_target_pairs={{0,32},{32,64},{64,96},{96,0},{1,33},{33,65},{65,97},{97,1},{2,34}... | collective-permute-start | bytes 786440 | tf_op jit(solution)/shard_map/ppermute | solution.py:13
  138.7 7.0 %collective-permute-start.16 = (bf16[256,512]{1,0:T(8,128)(2,1)S(1)}, bf16[256,512]{1,0:T(8,128)(2,1)S(1)}, u32[]{:S(2)}, u32[]{:S(2)}) collective-permute-start(bf16[256,512]{1,0:T(8,128)(2,1)S(1)} %slice.41), channel_id=1, source_target_pairs={{0,96},{32,0},{64,32},{96,64},{1,97},{33,1},{65,33},{97,65},{2,98}... | collective-permute-start | bytes 786440 | tf_op jit(solution)/shard_map/ppermute | solution.py:13
  141.6 3.1 %copy-start.1 = (bf16[1024,2048]{1,0:T(8,128)(2,1)S(1)}, bf16[1024,2048]{1,0:T(8,128)(2,1)}, u32[]{:S(2)}) copy-start(bf16[1024,2048]{1,0:T(8,128)(2,1)} %all-gather.3.cloned.1.call-done) | copy-start | bytes 12582916
  173.6 1.0 copy-start.6
Sparse Core Ops, SparseCore 0:
  12.2 50.4 all-gather.4
  73.6 50.9 all-gather.2

commit v4 on v3

v4 whole, which is shorter than its diff:
```python
import jax
import jax.numpy as jnp
from jax import lax
from jax.experimental import pallas as pl
from jax.experimental.pallas import tpu as pltpu
from jax.sharding import Mesh, PartitionSpec as P

ROW = ("y", "xh")
COL = ("xl", "z", "core")
F32, BF16 = jnp.float32, jnp.bfloat16


def shift(v, axis, by):
    n = lax.axis_size(axis)
    return lax.ppermute(v, axis, [(i, (i + by) % n) for i in range(n)])


def turn(v):
    pairs = []
    for xh in range(2):
        for xl in range(2):
            for z in range(4):
                to = ((z & 1) * 2 + 1 - xl) * 4 + (z & ~1) + xh
                pairs.append(((xh * 2 + xl) * 4 + z, to))
    return lax.ppermute(v, ("xh", "xl", "z"), pairs)


def after(v, *done):
    return lax.optimization_barrier((v, *done))[0]


def together(*arrays):
    return lax.optimization_barrier(arrays)


def dot(a, b):
    return lax.dot_general(a, b, (((a.ndim - 1,), (0,)), ((), ())), preferred_element_type=F32)


def early_kernel(n, m, at, *refs):
    blocks, factor = refs[: n + m], refs[n + m]
    theirs, own, part, held, right, total, came = refs[n + m + 1 :]
    size, depth = blocks[0].shape
    cols = own.shape[1]
    rows = [pl.ds(pl.multiple_of(at[i] * depth, depth), depth) for i in range(n + m)]
    copies = []
    for i in range(n + m):
        copies.append([pltpu.make_async_copy(blocks[i], held.at[i], came.at[2 * i])])
        if i < n:
            copies[i].append(pltpu.make_async_copy(factor.at[rows[i]], right.at[rows[i]], came.at[2 * i + 1]))
    for copy in sum(copies, []):
        copy.start()
    step = min(256, cols)
    for lo, hi in ((0, n // 2), (n // 2, n), (n, n + m)):
        for copy in sum(copies[lo:hi], []):
            copy.wait()
        for c in range(0, 2 * cols, step):
            here = slice(c, c + step)
            value = None
            for i in range(lo, hi):
                more = dot(held[i], right[rows[i], here])
                value = more if value is None else value + more
            if lo == 0:
                total[:, here] = value
            elif hi > n:
                part[:, here] = value
            elif c < cols:
                own[:, here] = total[:, here] + value
            else:
                theirs[:, c - cols : c - cols + step] = (total[:, here] + value).astype(BF16)


def early(odd, even, factor, at):
    n, m = len(odd), len(even)
    size, depth = odd[0].shape
    wide = factor.shape[1]
    return pl.pallas_call(
        lambda *refs: early_kernel(n, m, *refs),
        out_shape=(
            jax.ShapeDtypeStruct((size, wide // 2), BF16),
            jax.ShapeDtypeStruct((size, wide // 2), F32),
            jax.ShapeDtypeStruct((size, wide), F32),
        ),
        in_specs=[pl.BlockSpec(memory_space=pltpu.SMEM)] + [pl.BlockSpec(memory_space=pl.ANY)] * (n + m + 1),
        out_specs=(pl.BlockSpec(memory_space=pltpu.VMEM),) * 3,
        scratch_shapes=[
            pltpu.VMEM((n + m, size, depth), BF16),
            pltpu.VMEM(factor.shape, BF16),
            pltpu.VMEM((size, wide), F32),
            pltpu.SemaphoreType.DMA((2 * (n + m),)),
        ],
        compiler_params=pltpu.CompilerParams(vmem_limit_bytes=56 * 2**20),
        cost_estimate=pl.CostEstimate(
            flops=2 * (n + m) * size * depth * wide, bytes_accessed=12 * 2**20, transcendentals=0
        ),
    )(jnp.stack(at).astype(jnp.int32), *odd, *even, factor)


def body(weight, anchor, input_factor, output_factor, task_grad):
    y, xh, xl, z, core = (lax.axis_index(a) for a in ROW + COL)
    change = (weight.astype(F32) - anchor.astype(F32)).astype(BF16)
    rows, cols = weight.shape
    half = rows // 2

    depth = input_factor.shape[0] // 2
    mine = lax.dynamic_slice_in_dim(input_factor, core * depth, depth, 0)
    other = lax.dynamic_slice_in_dim(input_factor, (1 - core) * depth, depth, 0)
    pair = jnp.concatenate([mine, shift(other, "core", 1)], axis=1)
    factor = lax.all_gather(pair, "y", axis=0, tiled=True)

    b = turn(change)
    bm, bp, a = together(shift(b, "z", 1), shift(b, "z", -1), shift(b, "xl", 1))
    am, ap, b2 = together(shift(bm, "xl", 1), shift(a, "z", -1), shift(bm, "z", 1))
    far = [shift(am[:half], "z", 1), shift(ap[half:], "z", -1)]
    *far, part = together(*far, turn(after(output_factor, am, ap, b2, factor)))

    def place(dxl, dz):
        return (xl ^ dxl) * 2 + (((z + dz) & 3) >> 1)

    at = [place(0, -1), place(0, 1), place(1, -1), place(1, 1), place(0, 0), place(1, 0), place(1, 2)]
    theirs, own, even = early([am, ap, bm, bp], [a, b, b2], factor, at)
    far_off = shift(after(part, own), "xl", 1)
    odd = own + shift(theirs, "core", 1).astype(F32)

    def more(side):
        right = lax.dynamic_slice(factor, (place(0, 2) * depth, side * cols), (depth, cols))
        last = jnp.concatenate([dot(v, right) for v in far], axis=0)
        return even[:, side * cols : (side + 1) * cols] + last

    theirs, own = more(1).astype(BF16), more(0)
    got = shift(theirs, "core", 1)
    part = jnp.concatenate([after(far_off, got), part], axis=0)
    part = lax.all_gather(part, "z", axis=0)
    even = got.astype(F32) + own
    same = (z & 1) == xh
    send = shift(jnp.where(same, odd, even).astype(BF16), "xh", 1)
    keep = jnp.where(same, even, odd)

    p = [(keep[r] + send[r].astype(F32)).astype(BF16) for r in (slice(half), slice(half, rows))]
    below = [shift(p[0], "y", 1), shift(p[1], "y", 1)]
    above = [shift(p[0], "y", -1), shift(p[1], "y", -1)]
    beyond = [shift(below[0], "y", 1), shift(above[1], "y", -1)]
    swapped = shift(after(part, *below, *above), "core", 1)
    first = core == 0
    left = [jnp.where(first, part, swapped), jnp.where(first, swapped, part)]

    def share(blocks, dy):
        at = (y + dy) & 3
        corner, size = ((at & 1) * 2, ((at >> 1) ^ xl) * rows, 0), (2, rows, half)
        terms = [dot(lax.dynamic_slice(v, corner, size), w) for v, w in zip(left, blocks)]
        return terms[0] + terms[1]

    penalty = ((share(p, 0) + share(below, -1)) + share(above, 1)) + share(beyond, 2)
    penalty = penalty.astype(BF16).reshape(2 * rows, cols)
    owned = lax.all_to_all(penalty, ("xh",) + COL, split_axis=0, concat_axis=0, tiled=True)
    owned = owned.reshape(2, 16, task_grad.shape[0], cols).astype(F32).sum(axis=0)
    owned = owned.transpose(1, 0, 2).reshape(task_grad.shape)
    return (task_grad.astype(F32) + owned).astype(BF16)


def solution(mesh):
    fine = Mesh(mesh.devices.reshape(4, 2, 2, 4, 2), ROW + COL)
    cut = P(ROW, COL)
    placed = (cut, cut, cut, cut, P(ROW + COL, None))
    return jax.shard_map(
        body, mesh=fine, in_specs=placed, out_specs=P(ROW + COL, None), check_vma=False
    )
```

time: 183 us -> 167 us (0.913)
  starting transfers between devices: 60.3 us -> 29.2 us
  waiting for transfers between devices: 60.1 us -> 70.8 us
  Pallas kernels: 0 us -> 8.22 us
  matrix products: 14.4 us -> 9.47 us
  other arithmetic: 4.19 us -> 6.97 us
  blocking collectives: 26.1 us -> 23.9 us
    ppermute x13 -> x20, starting transfers between devices: 56.3 us -> 26.6 us  [shift(): return lax.ppermute(v, axis, [(i, (i + by) % n) for i in range(n)])]
    pallas_call x0 -> x1, Pallas kernels: none -> 8.22 us  [early(): pl.pallas_call(lambda *refs: early_kernel(n, m, *refs), out_shape=(jax.Sh...]
    ppermute x4 -> x2, waiting for transfers between devices: 6.19 us -> 11.8 us  [turn(): return lax.ppermute(v, ('xh', 'xl', 'z'), pairs)]
    dot_general x16 -> x12, matrix products: 14.4 us -> 9.47 us  [dot(): lax.dot_general(a, b, (((a.ndim - 1,), (0,)), ((), ())), preferred_elemen...]
    all_gather x1, waiting for transfers between devices: 0.01 us -> 3.35 us  [body(): factor = lax.all_gather(pair, 'y', axis=0, tiled=True)]
    all_to_all x1, blocking collectives: 26.1 us -> 23.9 us  [body(): lax.all_to_all(penalty, ('xh',) + COL, split_axis=0, concat_axis=0, tiled...]
    select_n x0 -> x1, other arithmetic: none -> 1.86 us  [body(): left = [jnp.where(first, part, swapped), jnp.where(first, swapped, part)]]
    ppermute x13 -> x20, waiting for transfers between devices: 53.9 us -> 55.6 us  [shift(): return lax.ppermute(v, axis, [(i, (i + by) % n) for i in range(n)])]
  transfers between devices with their start and end apart: 19 -> 24, of which waited for: 8 -> 15; matrix products, arithmetic and copies ran while one was open for 8% -> 6% of each run, Pallas kernels for 0% -> 5%
where the time goes in v4:
time: 167 us
  waiting for transfers between devices  70.8 us (42%)
  starting transfers between devices  29.2 us (17%)
  blocking collectives  23.9 us (14%)
  between operations  13.7 us (8%)
  matrix products  9.47 us (6%)
  Pallas kernels  8.22 us (5%)
  other arithmetic  6.97 us (4%)
  local copies, waits for them, and re-layouts  4.83 us (3%)
    ppermute x20, waiting for transfers between devices, shift(): return lax.ppermute(v, axis, [(i, (i + by) % n) for i in range(n)])  55.6 us
    ppermute x20, starting transfers between devices, shift(): return lax.ppermute(v, axis, [(i, (i + by) % n) for i in range(n)])  26.6 us
    all_to_all x1, blocking collectives, body(): lax.all_to_all(penalty, ('xh',) + COL, split_axis=0, concat_axis=0, tiled...  23.9 us
    ppermute x2, waiting for transfers between devices, turn(): return lax.ppermute(v, ('xh', 'xl', 'z'), pairs)  11.8 us
    dot_general x12, matrix products, dot(): lax.dot_general(a, b, (((a.ndim - 1,), (0,)), ((), ())), preferred_elemen...  9.47 us
    pallas_call x1, Pallas kernels, early(): pl.pallas_call(lambda *refs: early_kernel(n, m, *refs), out_shape=(jax.Sh...  8.22 us
    all_gather x1, waiting for transfers between devices, body(): factor = lax.all_gather(pair, 'y', axis=0, tiled=True)  3.35 us
  transfers between devices with their start and end apart: 24, of which 15 were waited for; matrix products, arithmetic and copies ran while one was open for 6% of the time, Pallas kernels for 5%

profile of v4, /device:TPU:1, one launch (start us, length us, event | category | flops | bytes accessed | tf_op | source)
XLA Modules:
  0.0 167.0 jit_solution(2217940996043891208)
XLA Ops:
  6.5 1.3 constant_dynamic-slice_fusion.1
  7.8 1.5 collective-permute-start.9
  9.3 1.5 collective-permute-done.9
  10.9 1.1 pad_maximum_fusion
  12.1 0.1 subtract_convert_fusion
  12.2 1.4 collective-permute-start
  13.6 11.8 %collective-permute-done.refs_6_ = bf16[512,512]{1,0:T(8,128)(2,1)S(1)} collective-permute-done((bf16[512,512]{1,0:T(8,128)(2,1)S(1)}, bf16[512,512]{1,0:T(8,128)(2,1)S(1)}, u32[]{:S(2)}, u32[]{:S(2)}) %collective-permute-start) | collective-permute-done | bytes 524320 | tf_op jit(solution)/shard_map/ppermute | solution.py:25
  25.5 1.3 collective-permute-start.3
  26.7 4.7 %collective-permute-start.2 = (bf16[512,512]{1,0:T(8,128)(2,1)S(1)}, bf16[512,512]{1,0:T(8,128)(2,1)S(1)}, u32[]{:S(2)}, u32[]{:S(2)}) collective-permute-start(bf16[512,512]{1,0:T(8,128)(2,1)S(1)} %collective-permute-done.refs_6_), channel_id=1, source_target_pairs={{0,6},{2,0},{4,2},{6,4},{1,7},{3,1},{5,3},{7,5},{8,14},{10,8},{12,... | collective-permute-start | bytes 1572872 | tf_op jit(solution)/shard_map/ppermute | solution.py:15
  31.4 6.4 %collective-permute-done.3.refs_5_ = bf16[512,512]{1,0:T(8,128)(2,1)S(1)} collective-permute-done((bf16[512,512]{1,0:T(8,128)(2,1)S(1)}, bf16[512,512]{1,0:T(8,128)(2,1)S(1)}, u32[]{:S(2)}, u32[]{:S(2)}) %collective-permute-start.3) | collective-permute-done | bytes 524320 | tf_op jit(solution)/shard_map/ppermute | solution.py:15
  37.8 3.4 %collective-permute-done.2.refs_4_ = bf16[512,512]{1,0:T(8,128)(2,1)S(1)} collective-permute-done((bf16[512,512]{1,0:T(8,128)(2,1)S(1)}, bf16[512,512]{1,0:T(8,128)(2,1)S(1)}, u32[]{:S(2)}, u32[]{:S(2)}) %collective-permute-start.2) | collective-permute-done | bytes 524320 | tf_op jit(solution)/shard_map/ppermute | solution.py:15
  41.1 3.2 %collective-permute-done.1.refs_3_ = bf16[512,512]{1,0:T(8,128)(2,1)S(1)} collective-permute-done((bf16[512,512]{1,0:T(8,128)(2,1)S(1)}, bf16[512,512]{1,0:T(8,128)(2,1)S(1)}, u32[]{:S(2)}, u32[]{:S(2)}) %collective-permute-start.1) | collective-permute-done | bytes 524320 | tf_op jit(solution)/shard_map/ppermute | solution.py:15
  44.4 0.3 collective-permute-start.5
  44.7 1.1 collective-permute-start.6
  45.9 1.5 collective-permute-start.4
  47.3 0.7 stack.31.refs_0_
  48.0 7.4 %collective-permute-done.5.refs_2_ = bf16[512,512]{1,0:T(8,128)(2,1)S(1)} collective-permute-done((bf16[512,512]{1,0:T(8,128)(2,1)S(1)}, bf16[512,512]{1,0:T(8,128)(2,1)S(1)}, u32[]{:S(2)}, u32[]{:S(2)}) %collective-permute-start.5) | collective-permute-done | bytes 524320 | tf_op jit(solution)/shard_map/ppermute | solution.py:15
  55.3 1.6 collective-permute-done.6.refs_7_
  56.9 0.8 copy-done.13
  57.7 0.5 collective-permute-start.8
  58.2 1.1 collective-permute-start.7
  59.3 3.3 %all-gather.4.cloned.1.call-done.refs_8_ = bf16[2048,1024]{1,0:T(8,128)(2,1)} async-done(((bf16[512,1024]{1,0:T(8,128)(2,1)}), bf16[2048,1024]{1,0:T(8,128)(2,1)}) %all-gather.4.cloned.1.call-update) | async-done | bytes 4194320 | tf_op jit(solution)/shard_map/all_gather | solution.py:109
  62.6 1.2 collective-permute-start.10
  63.8 8.2 %shard_map.55 = (bf16[512,512]{1,0:T(8,128)(2,1)}, f32[512,512]{1,0:T(8,128)}, f32[512,1024]{1,0:T(8,128)}) custom-call(s32[7]{0:T(128)} %stack.31.refs_0_, bf16[512,512]{1,0:T(8,128)(2,1)} %copy-done.8, bf16[512,512]{1,0:T(8,128)(2,1)} %copy-done.7, bf16[512,512]{1,0:T(8,128)(2,1)} %copy-done.12, bf16[512,512]{1,0:T(8,128)(2,1)} %copy-done.11, ...), custom_call_target="tpu_custom_call" | custom-call | flops 3758096384 | bytes 12582912 | tf_op jit(solution)/shard_map/pallas_call | solution.py:77
  72.1 1.5 fusion.26
  73.6 1.3 fusion.24
  74.9 0.3 fusion
  75.2 1.2 collective-permute-start.12
  76.5 0.8 collective-permute-start.11
  77.3 7.1 %collective-permute-done.11 = bf16[512,256]{1,0:T(8,128)(2,1)S(1)} collective-permute-done((bf16[512,256]{1,0:T(8,128)(2,1)S(1)}, bf16[512,256]{1,0:T(8,128)(2,1)S(1)}, u32[]{:S(2)}, u32[]{:S(2)}) %collective-permute-start.11) | collective-permute-done | bytes 262176 | tf_op jit(solution)/shard_map/ppermute | solution.py:15
  84.3 0.8 pad_maximum_fusion.1
  85.2 1.0 collective-permute-start.13
  86.1 1.4 fusion.22
  87.6 1.3 fusion.20
  88.9 1.5 select_convert_fusion
  90.4 2.7 %collective-permute-start.14 = (bf16[512,512]{1,0:T(8,128)(2,1)S(1)}, bf16[512,512]{1,0:T(8,128)(2,1)S(1)}, u32[]{:S(2)}, u32[]{:S(2)}) collective-permute-start(bf16[512,512]{1,0:T(8,128)(2,1)S(1)} %get-tuple-element.37), channel_id=1, source_target_pairs={{0,16},{16,0},{1,17},{17,1},{2,18},{18,2},{3,19},{19,3},{4,20},{20... | collective-permute-start | bytes 1572872 | tf_op jit(solution)/shard_map/ppermute | solution.py:15
  93.1 12.4 %collective-permute-done.14 = bf16[512,512]{1,0:T(8,128)(2,1)S(1)} collective-permute-done((bf16[512,512]{1,0:T(8,128)(2,1)S(1)}, bf16[512,512]{1,0:T(8,128)(2,1)S(1)}, u32[]{:S(2)}, u32[]{:S(2)}) %collective-permute-start.14) | collective-permute-done | bytes 524320 | tf_op jit(solution)/shard_map/ppermute | solution.py:15
  105.5 0.2 fusion.3
  105.7 2.8 %collective-permute-start.18 = (bf16[256,512]{1,0:T(8,128)(2,1)S(1)}, bf16[256,512]{1,0:T(8,128)(2,1)S(1)}, u32[]{:S(2)}, u32[]{:S(2)}) collective-permute-start(bf16[256,512]{1,0:T(8,128)(2,1)S(1)} %get-tuple-element.41), channel_id=1, source_target_pairs={{0,96},{32,0},{64,32},{96,64},{1,97},{33,1},{65,33},{97,65},{2,98}... | collective-permute-start | bytes 786440 | tf_op jit(solution)/shard_map/ppermute | solution.py:15
  108.5 2.7 %collective-permute-start.17 = (bf16[256,512]{1,0:T(8,128)(2,1)S(1)}, bf16[256,512]{1,0:T(8,128)(2,1)S(1)}, u32[]{:S(2)}, u32[]{:S(2)}) collective-permute-start(bf16[256,512]{1,0:T(8,128)(2,1)S(1)} %get-tuple-element.42), channel_id=1, source_target_pairs={{0,96},{32,0},{64,32},{96,64},{1,97},{33,1},{65,33},{97,65},{2,98}... | collective-permute-start | bytes 786440 | tf_op jit(solution)/shard_map/ppermute | solution.py:15
  111.2 2.1 %collective-permute-done.18 = bf16[256,512]{1,0:T(8,128)(2,1)S(1)} collective-permute-done((bf16[256,512]{1,0:T(8,128)(2,1)S(1)}, bf16[256,512]{1,0:T(8,128)(2,1)S(1)}, u32[]{:S(2)}, u32[]{:S(2)}) %collective-permute-start.18) | collective-permute-done | bytes 262176 | tf_op jit(solution)/shard_map/ppermute | solution.py:15
  113.3 3.2 %collective-permute-done.16 = bf16[256,512]{1,0:T(8,128)(2,1)S(1)} collective-permute-done((bf16[256,512]{1,0:T(8,128)(2,1)S(1)}, bf16[256,512]{1,0:T(8,128)(2,1)S(1)}, u32[]{:S(2)}, u32[]{:S(2)}) %collective-permute-start.16) | collective-permute-done | bytes 262176 | tf_op jit(solution)/shard_map/ppermute | solution.py:15
  116.5 2.4 %collective-permute-done.17 = bf16[256,512]{1,0:T(8,128)(2,1)S(1)} collective-permute-done((bf16[256,512]{1,0:T(8,128)(2,1)S(1)}, bf16[256,512]{1,0:T(8,128)(2,1)S(1)}, u32[]{:S(2)}, u32[]{:S(2)}) %collective-permute-start.17) | collective-permute-done | bytes 262176 | tf_op jit(solution)/shard_map/ppermute | solution.py:15
  118.9 0.7 copy-done.5
  119.6 2.4 %collective-permute-done.15 = bf16[256,512]{1,0:T(8,128)(2,1)S(1)} collective-permute-done((bf16[256,512]{1,0:T(8,128)(2,1)S(1)}, bf16[256,512]{1,0:T(8,128)(2,1)S(1)}, u32[]{:S(2)}, u32[]{:S(2)}) %collective-permute-start.15) | collective-permute-done | bytes 262176 | tf_op jit(solution)/shard_map/ppermute | solution.py:15
  122.0 2.0 %collective-permute-start.19 = (bf16[4,1024,256]{2,1,0:T(8,128)(2,1)}, bf16[4,1024,256]{2,1,0:T(8,128)(2,1)S(1)}, u32[]{:S(2)}, u32[]{:S(2)}) collective-permute-start(bf16[4,1024,256]{2,1,0:T(8,128)(2,1)} %bitcast.46), channel_id=1, source_target_pairs={{0,1},{1,0},{2,3},{3,2},{4,5},{5,4},{6,7},{7,6},{8,9},{9,8},{10,11... | collective-permute-start | bytes 6291464 | tf_op jit(solution)/shard_map/ppermute | solution.py:15
  124.1 0.7 collective-permute-start.21
  124.8 0.8 collective-permute-start.20
  125.5 2.5 %collective-permute-done.19 = bf16[4,1024,256]{2,1,0:T(8,128)(2,1)S(1)} collective-permute-done((bf16[4,1024,256]{2,1,0:T(8,128)(2,1)}, bf16[4,1024,256]{2,1,0:T(8,128)(2,1)S(1)}, u32[]{:S(2)}, u32[]{:S(2)}) %collective-permute-start.19) | collective-permute-done | bytes 2097184 | tf_op jit(solution)/shard_map/ppermute | solution.py:15
  128.1 1.9 %broadcast_select_fusion.1 = (bf16[4,1024,256]{2,1,0:T(8,128)(2,1)S(1)}, bf16[4,1024,256]{2,1,0:T(8,128)(2,1)S(1)}) fusion(bf16[4,1024,256]{2,1,0:T(8,128)(2,1)} %bitcast.47, bf16[4,1024,256]{2,1,0:T(8,128)(2,1)S(1)} %collective-permute-done.19, pred[]{:T(512)S(6)} %eq.6), kind=kLoop, calls=%fused_computation.3 | loop fusion | flops 2097152 | bytes 8388609 | tf_op jit(solution)/shard_map/jit(_where)/select_n | solution.py:145
  129.9 0.4 fusion.18
  130.4 0.4 fusion.16
  130.8 0.5 copy-done.6
  131.3 0.4 fusion.10
  131.8 0.4 fusion.8
  132.2 0.4 fusion.14
  132.6 0.4 fusion.12
  133.1 0.4 fusion.5
  133.5 0.9 add_convert_fusion
  134.4 23.9 %all_to_all.9 = bf16[32,32,512]{2,1,0:T(8,128)(2,1)S(1)} all-to-all(bf16[32,32,512]{2,1,0:T(8,128)(2,1)S(1)} %bitcast.42), channel_id=1, replica_groups=mesh['y'=4,'xh'=2,'xl'=2,'z'=4,'core'=2] {'xh','xl','z','core'}, dimensions={0} | all-to-all | bytes 2097152 | tf_op jit(solution)/shard_map/all_to_all | solution.py:155
  158.3 0.2 convert_reduce_fusion
  158.5 0.1 copy.7
  158.6 0.7 copy-done.4
  159.3 0.9 add_convert_fusion.1
  (44 shorter events, 0.2 us)
Async XLA Ops:
  6.5 56.1 %all-gather.4.cloned.1.call-start = ((), (), s32[]{:S(2)}) async-start(), calls=%async_computation.1 | async-start | bytes 5242880 | tf_op jit(solution)/shard_map/all_gather | solution.py:109
  7.8 4.3 %copy-start.2 = (bf16[512,512]{1,0:T(8,128)(2,1)S(1)}, bf16[512,512]{1,0:T(8,128)(2,1)}, u32[]{:S(2)}) copy-start(bf16[512,512]{1,0:T(8,128)(2,1)} %param.6) | copy-start | bytes 1572868
  7.8 4.3 %copy-start.3 = (bf16[512,512]{1,0:T(8,128)(2,1)S(1)}, bf16[512,512]{1,0:T(8,128)(2,1)}, u32[]{:S(2)}) copy-start(bf16[512,512]{1,0:T(8,128)(2,1)} %param.5) | copy-start | bytes 1572868
  7.8 3.0 %collective-permute-start.9 = (bf16[512,512]{1,0:T(8,128)(2,1)S(1)}, bf16[512,512]{1,0:T(8,128)(2,1)S(1)}, u32[]{:S(2)}, u32[]{:S(2)}) collective-permute-start(bf16[512,512]{1,0:T(8,128)(2,1)S(1)} %get-tuple-element.44), channel_id=1, source_target_pairs={{0,1},{1,0},{2,3},{3,2},{4,5},{5,4},{6,7},{7,6},{8,9},{9,8},{10,11... | collective-permute-start | bytes 1572872 | tf_op jit(solution)/shard_map/ppermute | solution.py:15
  12.0 50.6 %copy-start.14 = (bf16[512,256]{1,0:T(8,128)(2,1)S(1)}, bf16[512,256]{1,0:T(8,128)(2,1)}, u32[]{:S(2)}) copy-start(bf16[512,256]{1,0:T(8,128)(2,1)} %param.8) | copy-start | bytes 786436
  12.0 110.0 %all-gather.6.cloned.1.call-start = ((), (), s32[]{:S(2)}) async-start(), calls=%async_computation.2 | async-start | bytes 2621440 | tf_op jit(solution)/shard_map/all_gather | solution.py:133
  12.2 13.2 %collective-permute-start = (bf16[512,512]{1,0:T(8,128)(2,1)S(1)}, bf16[512,512]{1,0:T(8,128)(2,1)S(1)}, u32[]{:S(2)}, u32[]{:S(2)}) collective-permute-start(bf16[512,512]{1,0:T(8,128)(2,1)S(1)} %subtract_convert_fusion), channel_id=1, source_target_pairs={{0,8},{2,24},{4,12},{6,28},{8,0},{10,16},{12,4},{14,20},{16,10},{1... | collective-permute-start | bytes 1572872 | tf_op jit(solution)/shard_map/ppermute | solution.py:25
  25.4 38.4 %copy-start.9 = (bf16[512,512]{1,0:T(8,128)(2,1)}, bf16[512,512]{1,0:T(8,128)(2,1)S(1)}, u32[]{:S(2)}) copy-start(bf16[512,512]{1,0:T(8,128)(2,1)S(1)} %collective-permute-done.refs_6_) | copy-start | bytes 1572868
  25.5 12.3 %collective-permute-start.3 = (bf16[512,512]{1,0:T(8,128)(2,1)S(1)}, bf16[512,512]{1,0:T(8,128)(2,1)S(1)}, u32[]{:S(2)}, u32[]{:S(2)}) collective-permute-start(bf16[512,512]{1,0:T(8,128)(2,1)S(1)} %collective-permute-done.refs_6_), channel_id=1, source_target_pairs={{0,8},{8,0},{1,9},{9,1},{2,10},{10,2},{3,11},{11,3},{4,12},{12,4},... | collective-permute-start | bytes 1572872 | tf_op jit(solution)/shard_map/ppermute | solution.py:15
  26.7 14.4 %collective-permute-start.2 = (bf16[512,512]{1,0:T(8,128)(2,1)S(1)}, bf16[512,512]{1,0:T(8,128)(2,1)S(1)}, u32[]{:S(2)}, u32[]{:S(2)}) collective-permute-start(bf16[512,512]{1,0:T(8,128)(2,1)S(1)} %collective-permute-done.refs_6_), channel_id=1, source_target_pairs={{0,6},{2,0},{4,2},{6,4},{1,7},{3,1},{5,3},{7,5},{8,14},{10,8},{12,... | collective-permute-start | bytes 1572872 | tf_op jit(solution)/shard_map/ppermute | solution.py:15
  31.4 13.0 %collective-permute-start.1 = (bf16[512,512]{1,0:T(8,128)(2,1)S(1)}, bf16[512,512]{1,0:T(8,128)(2,1)S(1)}, u32[]{:S(2)}, u32[]{:S(2)}) collective-permute-start(bf16[512,512]{1,0:T(8,128)(2,1)S(1)} %collective-permute-done.refs_6_), channel_id=1, source_target_pairs={{0,2},{2,4},{4,6},{6,0},{1,3},{3,5},{5,7},{7,1},{8,10},{10,12},{12... | collective-permute-start | bytes 1572872 | tf_op jit(solution)/shard_map/ppermute | solution.py:15
  37.8 26.0 %copy-start.10 = (bf16[512,512]{1,0:T(8,128)(2,1)}, bf16[512,512]{1,0:T(8,128)(2,1)S(1)}, u32[]{:S(2)}) copy-start(bf16[512,512]{1,0:T(8,128)(2,1)S(1)} %collective-permute-done.3.refs_5_) | copy-start | bytes 1572868
  41.1 3.6 %copy-start.11 = (bf16[512,512]{1,0:T(8,128)(2,1)}, bf16[512,512]{1,0:T(8,128)(2,1)S(1)}, u32[]{:S(2)}) copy-start(bf16[512,512]{1,0:T(8,128)(2,1)S(1)} %collective-permute-done.2.refs_4_) | copy-start | bytes 1572868
  44.4 13.3 %copy-start.12 = (bf16[512,512]{1,0:T(8,128)(2,1)}, bf16[512,512]{1,0:T(8,128)(2,1)S(1)}, u32[]{:S(2)}) copy-start(bf16[512,512]{1,0:T(8,128)(2,1)S(1)} %collective-permute-done.1.refs_3_) | copy-start | bytes 1572868
  44.4 10.9 %collective-permute-start.5 = (bf16[512,512]{1,0:T(8,128)(2,1)S(1)}, bf16[512,512]{1,0:T(8,128)(2,1)S(1)}, u32[]{:S(2)}, u32[]{:S(2)}) collective-permute-start(bf16[512,512]{1,0:T(8,128)(2,1)S(1)} %collective-permute-done.3.refs_5_), channel_id=1, source_target_pairs={{0,6},{2,0},{4,2},{6,4},{1,7},{3,1},{5,3},{7,5},{8,14},{10,8},{12,... | collective-permute-start | bytes 1572872 | tf_op jit(solution)/shard_map/ppermute | solution.py:15
  44.7 12.2 %collective-permute-start.6 = (bf16[512,512]{1,0:T(8,128)(2,1)S(1)}, bf16[512,512]{1,0:T(8,128)(2,1)S(1)}, u32[]{:S(2)}, u32[]{:S(2)}) collective-permute-start(bf16[512,512]{1,0:T(8,128)(2,1)S(1)} %collective-permute-done.1.refs_3_), channel_id=1, source_target_pairs={{0,2},{2,4},{4,6},{6,0},{1,3},{3,5},{5,7},{7,1},{8,10},{10,12},{12... | collective-permute-start | bytes 1572872 | tf_op jit(solution)/shard_map/ppermute | solution.py:15
  45.9 11.8 %collective-permute-start.4 = (bf16[512,512]{1,0:T(8,128)(2,1)S(1)}, bf16[512,512]{1,0:T(8,128)(2,1)S(1)}, u32[]{:S(2)}, u32[]{:S(2)}) collective-permute-start(bf16[512,512]{1,0:T(8,128)(2,1)S(1)} %collective-permute-done.1.refs_3_), channel_id=1, source_target_pairs={{0,8},{8,0},{1,9},{9,1},{2,10},{10,2},{3,11},{11,3},{4,12},{12,4},... | collective-permute-start | bytes 1572872 | tf_op jit(solution)/shard_map/ppermute | solution.py:15
  55.3 8.5 %copy-start.7 = (bf16[512,512]{1,0:T(8,128)(2,1)}, bf16[512,512]{1,0:T(8,128)(2,1)S(1)}, u32[]{:S(2)}) copy-start(bf16[512,512]{1,0:T(8,128)(2,1)S(1)} %collective-permute-done.5.refs_2_) | copy-start | bytes 1572868
  56.9 0.8 copy-start.13
  57.7 6.1 %copy-start.8 = (bf16[512,512]{1,0:T(8,128)(2,1)}, bf16[512,512]{1,0:T(8,128)(2,1)S(1)}, u32[]{:S(2)}) copy-start(bf16[512,512]{1,0:T(8,128)(2,1)S(1)} %collective-permute-done.4.refs_1_) | copy-start | bytes 1572868
  57.7 14.3 %collective-permute-start.8 = (bf16[256,512]{1,0:T(8,128)(2,1)S(1)}, bf16[256,512]{1,0:T(8,128)(2,1)S(1)}, u32[]{:S(2)}, u32[]{:S(2)}) collective-permute-start(bf16[256,512]{1,0:T(8,128)(2,1)S(1)} %slice.25), channel_id=1, source_target_pairs={{0,6},{2,0},{4,2},{6,4},{1,7},{3,1},{5,3},{7,5},{8,14},{10,8},{12,... | collective-permute-start | bytes 786440 | tf_op jit(solution)/shard_map/ppermute | solution.py:15
  58.2 13.9 %collective-permute-start.7 = (bf16[256,512]{1,0:T(8,128)(2,1)S(1)}, bf16[256,512]{1,0:T(8,128)(2,1)S(1)}, u32[]{:S(2)}, u32[]{:S(2)}) collective-permute-start(bf16[256,512]{1,0:T(8,128)(2,1)S(1)} %slice.24), channel_id=1, source_target_pairs={{0,2},{2,4},{4,6},{6,0},{1,3},{3,5},{5,7},{7,1},{8,10},{10,12},{12... | collective-permute-start | bytes 786440 | tf_op jit(solution)/shard_map/ppermute | solution.py:15
  62.6 9.5 %collective-permute-start.10 = (bf16[512,256]{1,0:T(8,128)(2,1)S(1)}, bf16[512,256]{1,0:T(8,128)(2,1)S(1)}, u32[]{:S(2)}, u32[]{:S(2)}) collective-permute-start(bf16[512,256]{1,0:T(8,128)(2,1)S(1)} %copy-done.14), channel_id=1, source_target_pairs={{0,8},{2,24},{4,12},{6,28},{8,0},{10,16},{12,4},{14,20},{16,10},{1... | collective-permute-start | bytes 786440 | tf_op jit(solution)/shard_map/ppermute | solution.py:25
  72.1 2.9 %copy-start = (f32[512,1024]{1,0:T(8,128)S(1)}, f32[512,1024]{1,0:T(8,128)}, u32[]{:S(2)}) copy-start(f32[512,1024]{1,0:T(8,128)} %get-tuple-element.31) | copy-start | bytes 6291460
  75.2 9.1 %collective-permute-start.12 = (bf16[512,512]{1,0:T(8,128)(2,1)S(1)}, bf16[512,512]{1,0:T(8,128)(2,1)S(1)}, u32[]{:S(2)}, u32[]{:S(2)}) collective-permute-start(bf16[512,512]{1,0:T(8,128)(2,1)S(1)} %fusion), channel_id=1, source_target_pairs={{0,1},{1,0},{2,3},{3,2},{4,5},{5,4},{6,7},{7,6},{8,9},{9,8},{10,11... | collective-permute-start | bytes 1572872 | tf_op jit(solution)/shard_map/ppermute | solution.py:15
  76.5 7.9 %collective-permute-start.11 = (bf16[512,256]{1,0:T(8,128)(2,1)S(1)}, bf16[512,256]{1,0:T(8,128)(2,1)S(1)}, u32[]{:S(2)}, u32[]{:S(2)}) collective-permute-start(bf16[512,256]{1,0:T(8,128)(2,1)S(1)} %collective-permute-done.10), channel_id=1, source_target_pairs={{0,8},{8,0},{1,9},{9,1},{2,10},{10,2},{3,11},{11,3},{4,12},{12,4},... | collective-permute-start | bytes 786440 | tf_op jit(solution)/shard_map/ppermute | solution.py:15
  85.2 3.7 %collective-permute-start.13 = (bf16[512,512]{1,0:T(8,128)(2,1)}, bf16[512,512]{1,0:T(8,128)(2,1)}, u32[]{:S(2)}, u32[]{:S(2)}) collective-permute-start(bf16[512,512]{1,0:T(8,128)(2,1)} %get-tuple-element.35), channel_id=1, source_target_pairs={{0,1},{1,0},{2,3},{3,2},{4,5},{5,4},{6,7},{7,6},{8,9},{9,8},{10,11... | collective-permute-start | bytes 1572872 | tf_op jit(solution)/shard_map/ppermute | solution.py:15
  86.1 2.8 %copy-start.1 = (f32[512,512]{1,0:T(8,128)S(1)}, f32[512,512]{1,0:T(8,128)}, u32[]{:S(2)}) copy-start(f32[512,512]{1,0:T(8,128)} %get-tuple-element.29) | copy-start | bytes 3145732
  90.4 15.1 %collective-permute-start.14 = (bf16[512,512]{1,0:T(8,128)(2,1)S(1)}, bf16[512,512]{1,0:T(8,128)(2,1)S(1)}, u32[]{:S(2)}, u32[]{:S(2)}) collective-permute-start(bf16[512,512]{1,0:T(8,128)(2,1)S(1)} %get-tuple-element.37), channel_id=1, source_target_pairs={{0,16},{16,0},{1,17},{17,1},{2,18},{18,2},{3,19},{19,3},{4,20},{20... | collective-permute-start | bytes 1572872 | tf_op jit(solution)/shard_map/ppermute | solution.py:15
  105.7 7.6 %collective-permute-start.18 = (bf16[256,512]{1,0:T(8,128)(2,1)S(1)}, bf16[256,512]{1,0:T(8,128)(2,1)S(1)}, u32[]{:S(2)}, u32[]{:S(2)}) collective-permute-start(bf16[256,512]{1,0:T(8,128)(2,1)S(1)} %get-tuple-element.41), channel_id=1, source_target_pairs={{0,96},{32,0},{64,32},{96,64},{1,97},{33,1},{65,33},{97,65},{2,98}... | collective-permute-start | bytes 786440 | tf_op jit(solution)/shard_map/ppermute | solution.py:15
  108.5 8.0 %collective-permute-start.16 = (bf16[256,512]{1,0:T(8,128)(2,1)S(1)}, bf16[256,512]{1,0:T(8,128)(2,1)S(1)}, u32[]{:S(2)}, u32[]{:S(2)}) collective-permute-start(bf16[256,512]{1,0:T(8,128)(2,1)S(1)} %get-tuple-element.41), channel_id=1, source_target_pairs={{0,32},{32,64},{64,96},{96,0},{1,33},{33,65},{65,97},{97,1},{2,34}... | collective-permute-start | bytes 786440 | tf_op jit(solution)/shard_map/ppermute | solution.py:15
  108.5 10.4 %collective-permute-start.17 = (bf16[256,512]{1,0:T(8,128)(2,1)S(1)}, bf16[256,512]{1,0:T(8,128)(2,1)S(1)}, u32[]{:S(2)}, u32[]{:S(2)}) collective-permute-start(bf16[256,512]{1,0:T(8,128)(2,1)S(1)} %get-tuple-element.42), channel_id=1, source_target_pairs={{0,96},{32,0},{64,32},{96,64},{1,97},{33,1},{65,33},{97,65},{2,98}... | collective-permute-start | bytes 786440 | tf_op jit(solution)/shard_map/ppermute | solution.py:15
  111.2 10.8 %collective-permute-start.15 = (bf16[256,512]{1,0:T(8,128)(2,1)S(1)}, bf16[256,512]{1,0:T(8,128)(2,1)S(1)}, u32[]{:S(2)}, u32[]{:S(2)}) collective-permute-start(bf16[256,512]{1,0:T(8,128)(2,1)S(1)} %get-tuple-element.42), channel_id=1, source_target_pairs={{0,32},{32,64},{64,96},{96,0},{1,33},{33,65},{65,97},{97,1},{2,34}... | collective-permute-start | bytes 786440 | tf_op jit(solution)/shard_map/ppermute | solution.py:15
  118.9 0.7 copy-start.5
  122.0 6.0 %collective-permute-start.19 = (bf16[4,1024,256]{2,1,0:T(8,128)(2,1)}, bf16[4,1024,256]{2,1,0:T(8,128)(2,1)S(1)}, u32[]{:S(2)}, u32[]{:S(2)}) collective-permute-start(bf16[4,1024,256]{2,1,0:T(8,128)(2,1)} %bitcast.46), channel_id=1, source_target_pairs={{0,1},{1,0},{2,3},{3,2},{4,5},{5,4},{6,7},{7,6},{8,9},{9,8},{10,11... | collective-permute-start | bytes 6291464 | tf_op jit(solution)/shard_map/ppermute | solution.py:15
  124.1 9.0 %collective-permute-start.21 = (bf16[256,512]{1,0:T(8,128)(2,1)S(1)}, bf16[256,512]{1,0:T(8,128)(2,1)S(1)}, u32[]{:S(2)}, u32[]{:S(2)}) collective-permute-start(bf16[256,512]{1,0:T(8,128)(2,1)S(1)} %collective-permute-done.18), channel_id=1, source_target_pairs={{0,96},{32,0},{64,32},{96,64},{1,97},{33,1},{65,33},{97,65},{2,98}... | collective-permute-start | bytes 786440 | tf_op jit(solution)/shard_map/ppermute | solution.py:15
  124.8 8.7 %collective-permute-start.20 = (bf16[256,512]{1,0:T(8,128)(2,1)S(1)}, bf16[256,512]{1,0:T(8,128)(2,1)S(1)}, u32[]{:S(2)}, u32[]{:S(2)}) collective-permute-start(bf16[256,512]{1,0:T(8,128)(2,1)S(1)} %collective-permute-done.15), channel_id=1, source_target_pairs={{0,32},{32,64},{64,96},{96,0},{1,33},{33,65},{65,97},{97,1},{2,34}... | collective-permute-start | bytes 786440 | tf_op jit(solution)/shard_map/ppermute | solution.py:15
  130.4 1.0 copy-start.6
  158.3 1.0 copy-start.4
Sparse Core Ops, SparseCore 0:
  12.1 50.4 all-gather.3
  85.3 31.5 all-gather.5

commit v5 on v4

--- a/solution.py
+++ b/solution.py
@@ -111,43 +111,39 @@
     b = turn(change)
     bm, bp, a = together(shift(b, "z", 1), shift(b, "z", -1), shift(b, "xl", 1))
     am, ap, b2 = together(shift(bm, "xl", 1), shift(a, "z", -1), shift(bm, "z", 1))
+    turned = turn(after(output_factor, bm, bp, a))
     far = [shift(am[:half], "z", 1), shift(ap[half:], "z", -1)]
-    *far, part = together(*far, turn(after(output_factor, am, ap, b2, factor)))
+    *far, part = together(*far, shift(after(turned, factor), "xl", 1))
 
     def place(dxl, dz):
         return (xl ^ dxl) * 2 + (((z + dz) & 3) >> 1)
 
     at = [place(0, -1), place(0, 1), place(1, -1), place(1, 1), place(0, 0), place(1, 0), place(1, 2)]
     theirs, own, even = early([am, ap, bm, bp], [a, b, b2], factor, at)
-    far_off = shift(after(part, own), "xl", 1)
-    odd = own + shift(theirs, "core", 1).astype(F32)
+    part = jnp.concatenate([after(part, own), turned], axis=0)
+    left = lax.all_gather(part, ("core", "z"), axis=0)
 
     def more(side):
         right = lax.dynamic_slice(factor, (place(0, 2) * depth, side * cols), (depth, cols))
         last = jnp.concatenate([dot(v, right) for v in far], axis=0)
         return even[:, side * cols : (side + 1) * cols] + last
 
-    theirs, own = more(1).astype(BF16), more(0)
-    got = shift(theirs, "core", 1)
-    part = jnp.concatenate([after(far_off, got), part], axis=0)
-    part = lax.all_gather(part, "z", axis=0)
-    even = got.astype(F32) + own
+    theirs = [after(theirs, more(1)), more(1).astype(BF16)]
+    odd, even = [v + shift(w, "core", 1).astype(F32) for v, w in zip((own, more(0)), theirs)]
     same = (z & 1) == xh
-    send = shift(jnp.where(same, odd, even).astype(BF16), "xh", 1)
-    keep = jnp.where(same, even, odd)
+    send, keep = jnp.where(same, odd, even).astype(BF16), jnp.where(same, even, odd)
+    send = shift(send, "xh", 1)
 
     p = [(keep[r] + send[r].astype(F32)).astype(BF16) for r in (slice(half), slice(half, rows))]
     below = [shift(p[0], "y", 1), shift(p[1], "y", 1)]
     above = [shift(p[0], "y", -1), shift(p[1], "y", -1)]
     beyond = [shift(below[0], "y", 1), shift(above[1], "y", -1)]
-    swapped = shift(after(part, *below, *above), "core", 1)
-    first = core == 0
-    left = [jnp.where(first, part, swapped), jnp.where(first, swapped, part)]
 
     def share(blocks, dy):
         at = (y + dy) & 3
-        corner, size = ((at & 1) * 2, ((at >> 1) ^ xl) * rows, 0), (2, rows, half)
-        terms = [dot(lax.dynamic_slice(v, corner, size), w) for v, w in zip(left, blocks)]
+        size = (2, rows, half)
+        corners = [(4 * h + (at & 1) * 2, ((at >> 1) ^ xl) * rows, 0) for h in range(2)]
+        terms = [dot(lax.dynamic_slice(left, c, size), v) for c, v in zip(corners, blocks)]
         return terms[0] + terms[1]
 
     penalty = ((share(p, 0) + share(below, -1)) + share(above, 1)) + share(beyond, 2)

time: 167 us -> 153 us (0.916)
  waiting for transfers between devices: 70.8 us -> 59.4 us
  local copies, waits for them, and re-layouts: 4.83 us -> 2.75 us
  matrix products: 9.47 us -> 11.5 us
    ppermute x20 -> x19, waiting for transfers between devices: 55.6 us -> 47.3 us  [shift(): return lax.ppermute(v, axis, [(i, (i + by) % n) for i in range(n)])]
    all_gather x1, waiting for transfers between devices: 3.35 us -> 0.27 us  [body(): factor = lax.all_gather(pair, 'y', axis=0, tiled=True)]
    dot_general x12, matrix products: 9.47 us -> 11.5 us  [dot(): lax.dot_general(a, b, (((a.ndim - 1,), (0,)), ((), ())), preferred_elemen...]
    unnamed x30 -> x24, local copies, waits for them, and re-layouts: 2.79 us -> 0.79 us
    select_n x1 -> x0, other arithmetic: 1.86 us -> none  [body(): left = [jnp.where(first, part, swapped), jnp.where(first, swapped, part)]]
    ppermute x20 -> x19, starting transfers between devices: 26.6 us -> 26.3 us  [shift(): return lax.ppermute(v, axis, [(i, (i + by) % n) for i in range(n)])]
  transfers between devices with their start and end apart: 24 -> 23, of which waited for: 15 -> 12; matrix products, arithmetic and copies ran while one was open for 6% -> 9% of each run, Pallas kernels for 5% -> 5%
where the time goes in v5:
time: 153 us; the launch traced here: 152 us
  waiting for transfers between devices  59.4 us (39%)
  starting transfers between devices  27.7 us (18%)
  blocking collectives  23.1 us (15%)
  between operations  13.7 us (9%)
  matrix products  11.5 us (8%)
  Pallas kernels  8.21 us (5%)
  other arithmetic  5.86 us (4%)
  local copies, waits for them, and re-layouts  2.75 us (2%)
    ppermute x19, waiting for transfers between devices, shift(): return lax.ppermute(v, axis, [(i, (i + by) % n) for i in range(n)])  47.3 us
    ppermute x19, starting transfers between devices, shift(): return lax.ppermute(v, axis, [(i, (i + by) % n) for i in range(n)])  26.3 us
    all_to_all x1, blocking collectives, body(): lax.all_to_all(penalty, ('xh',) + COL, split_axis=0, concat_axis=0, tiled...  23.1 us
    ppermute x2, waiting for transfers between devices, turn(): return lax.ppermute(v, ('xh', 'xl', 'z'), pairs)  11.8 us
    dot_general x12, matrix products, dot(): lax.dot_general(a, b, (((a.ndim - 1,), (0,)), ((), ())), preferred_elemen...  11.5 us
    pallas_call x1, Pallas kernels, early(): pl.pallas_call(lambda *refs: early_kernel(n, m, *refs), out_shape=(jax.Sh...  8.21 us
  transfers between devices with their start and end apart: 23, of which 12 were waited for; matrix products, arithmetic and copies ran while one was open for 9% of the time, Pallas kernels for 5%

profile of v5, /device:TPU:1, one launch (start us, length us, event | category | flops | bytes accessed | tf_op | source)
XLA Modules:
  0.0 152.2 jit_solution(8855379649122851898)
XLA Ops:
  6.5 1.3 constant_dynamic-slice_fusion.1
  7.8 0.0 copy-start.3
  7.8 0.0 copy-start.4
  7.8 1.5 collective-permute-start.10
  9.3 1.5 %collective-permute-done.10 = bf16[512,512]{1,0:T(8,128)(2,1)S(1)} collective-permute-done((bf16[512,512]{1,0:T(8,128)(2,1)S(1)}, bf16[512,512]{1,0:T(8,128)(2,1)S(1)}, u32[]{:S(2)}, u32[]{:S(2)}) %collective-permute-start.10) | collective-permute-done | bytes 524320 | tf_op jit(solution)/shard_map/ppermute | solution.py:15
  10.9 1.1 pad_maximum_fusion
  12.0 0.0 all-gather.4.cloned.1.call-update
  12.0 0.0 all-gather.6.cloned.1.call-start
  12.1 0.1 subtract_convert_fusion
  12.2 1.4 collective-permute-start
  13.6 11.8 %collective-permute-done.refs_6_ = bf16[512,512]{1,0:T(8,128)(2,1)S(1)} collective-permute-done((bf16[512,512]{1,0:T(8,128)(2,1)S(1)}, bf16[512,512]{1,0:T(8,128)(2,1)S(1)}, u32[]{:S(2)}, u32[]{:S(2)}) %collective-permute-start) | collective-permute-done | bytes 524320 | tf_op jit(solution)/shard_map/ppermute | solution.py:25
  25.5 1.3 collective-permute-start.3
  26.8 4.7 %collective-permute-start.2 = (bf16[512,512]{1,0:T(8,128)(2,1)S(1)}, bf16[512,512]{1,0:T(8,128)(2,1)S(1)}, u32[]{:S(2)}, u32[]{:S(2)}) collective-permute-start(bf16[512,512]{1,0:T(8,128)(2,1)S(1)} %collective-permute-done.refs_6_), channel_id=1, source_target_pairs={{0,6},{2,0},{4,2},{6,4},{1,7},{3,1},{5,3},{7,5},{8,14},{10,8},{12,... | collective-permute-start | bytes 1572872 | tf_op jit(solution)/shard_map/ppermute | solution.py:15
  31.4 6.4 %collective-permute-done.3.refs_5_ = bf16[512,512]{1,0:T(8,128)(2,1)S(1)} collective-permute-done((bf16[512,512]{1,0:T(8,128)(2,1)S(1)}, bf16[512,512]{1,0:T(8,128)(2,1)S(1)}, u32[]{:S(2)}, u32[]{:S(2)}) %collective-permute-start.3) | collective-permute-done | bytes 524320 | tf_op jit(solution)/shard_map/ppermute | solution.py:15
  37.8 3.4 %collective-permute-done.2.refs_4_ = bf16[512,512]{1,0:T(8,128)(2,1)S(1)} collective-permute-done((bf16[512,512]{1,0:T(8,128)(2,1)S(1)}, bf16[512,512]{1,0:T(8,128)(2,1)S(1)}, u32[]{:S(2)}, u32[]{:S(2)}) %collective-permute-start.2) | collective-permute-done | bytes 524320 | tf_op jit(solution)/shard_map/ppermute | solution.py:15
  41.2 3.2 %collective-permute-done.1.refs_3_ = bf16[512,512]{1,0:T(8,128)(2,1)S(1)} collective-permute-done((bf16[512,512]{1,0:T(8,128)(2,1)S(1)}, bf16[512,512]{1,0:T(8,128)(2,1)S(1)}, u32[]{:S(2)}, u32[]{:S(2)}) %collective-permute-start.1) | collective-permute-done | bytes 524320 | tf_op jit(solution)/shard_map/ppermute | solution.py:15
  44.4 0.3 collective-permute-start.5
  44.7 1.1 collective-permute-start.6
  45.9 1.5 collective-permute-start.4
  47.3 0.0 collective-permute-start.9
  47.4 0.6 stack.31.refs_0_
  47.9 7.4 %collective-permute-done.5.refs_2_ = bf16[512,512]{1,0:T(8,128)(2,1)S(1)} collective-permute-done((bf16[512,512]{1,0:T(8,128)(2,1)S(1)}, bf16[512,512]{1,0:T(8,128)(2,1)S(1)}, u32[]{:S(2)}, u32[]{:S(2)}) %collective-permute-start.5) | collective-permute-done | bytes 524320 | tf_op jit(solution)/shard_map/ppermute | solution.py:15
  55.3 4.5 %collective-permute-done.6.refs_7_ = bf16[512,512]{1,0:T(8,128)(2,1)} collective-permute-done((bf16[512,512]{1,0:T(8,128)(2,1)S(1)}, bf16[512,512]{1,0:T(8,128)(2,1)}, u32[]{:S(2)}, u32[]{:S(2)}) %collective-permute-start.6) | collective-permute-done | bytes 524320 | tf_op jit(solution)/shard_map/ppermute | solution.py:15
  59.8 0.0 collective-permute-done.4.refs_1_
  59.9 1.9 %collective-permute-start.8 = (bf16[256,512]{1,0:T(8,128)(2,1)S(1)}, bf16[256,512]{1,0:T(8,128)(2,1)S(1)}, u32[]{:S(2)}, u32[]{:S(2)}) collective-permute-start(bf16[256,512]{1,0:T(8,128)(2,1)S(1)} %slice.26), channel_id=1, source_target_pairs={{0,6},{2,0},{4,2},{6,4},{1,7},{3,1},{5,3},{7,5},{8,14},{10,8},{12,... | collective-permute-start | bytes 786440 | tf_op jit(solution)/shard_map/ppermute | solution.py:15
  61.8 0.6 collective-permute-start.7
  62.4 0.3 all-gather.4.cloned.1.call-done.refs_8_
  62.6 3.3 %collective-permute-start.11 = (bf16[512,256]{1,0:T(8,128)(2,1)S(1)}, bf16[512,256]{1,0:T(8,128)(2,1)S(1)}, u32[]{:S(2)}, u32[]{:S(2)}) collective-permute-start(bf16[512,256]{1,0:T(8,128)(2,1)S(1)} %collective-permute-done.9), channel_id=1, source_target_pairs={{0,8},{8,0},{1,9},{9,1},{2,10},{10,2},{3,11},{11,3},{4,12},{12,4},... | collective-permute-start | bytes 786440 | tf_op jit(solution)/shard_map/ppermute | solution.py:15
  66.0 8.2 %shard_map.55 = (bf16[512,512]{1,0:T(8,128)(2,1)}, f32[512,512]{1,0:T(8,128)}, f32[512,1024]{1,0:T(8,128)}) custom-call(s32[7]{0:T(128)} %stack.31.refs_0_, bf16[512,512]{1,0:T(8,128)(2,1)} %copy-done.7, bf16[512,512]{1,0:T(8,128)(2,1)} %copy-done.6, bf16[512,512]{1,0:T(8,128)(2,1)} %copy-done.11, bf16[512,512]{1,0:T(8,128)(2,1)} %copy-done.10, ...), custom_call_target="tpu_custom_call" | custom-call | flops 3758096384 | bytes 12582912 | tf_op jit(solution)/shard_map/pallas_call | solution.py:77
  74.2 0.0 collective-permute-done.8
  74.2 0.0 collective-permute-done.11
  74.2 0.8 pad_maximum_fusion.1
  75.0 0.0 all-gather.6.cloned.1.call-update
  75.1 1.3 fusion.21
  76.4 1.3 fusion.19
  77.8 1.0 maximum_add_fusion.1
  78.8 2.2 %collective-permute-start.13 = (bf16[512,512]{1,0:T(8,128)(2,1)}, bf16[512,512]{1,0:T(8,128)(2,1)S(1)}, u32[]{:S(2)}, u32[]{:S(2)}) collective-permute-start(bf16[512,512]{1,0:T(8,128)(2,1)} %get-tuple-element.36), channel_id=1, source_target_pairs={{0,1},{1,0},{2,3},{3,2},{4,5},{5,4},{6,7},{7,6},{8,9},{9,8},{10,11... | collective-permute-start | bytes 1572872 | tf_op jit(solution)/shard_map/ppermute | solution.py:15
  81.0 1.4 fusion.25
  82.4 1.3 fusion.23
  83.8 1.5 %select_convert_fusion = (bf16[512,512]{1,0:T(8,128)(2,1)S(1)}, f32[512,512]{1,0:T(8,128)S(1)}) fusion(f32[512,512]{1,0:T(8,128)S(1)} %copy-done.2, bf16[512,512]{1,0:T(8,128)(2,1)S(1)} %collective-permute-done.13, pred[]{:T(512)S(6)} %eq.3, bf16[512,512]{1,0:T(8,128)(2,1)} %collective-permute-done.12, f32[256,512]{1,0:T(8,128)S(1)} %fusion.23, ...), kind=kLoop, calls=%fused_computation.7 | loop fusion | flops 2359296 | bytes 5767169 | tf_op jit(solution)/shard_map/convert_element_type | solution.py:134
  85.4 0.9 collective-permute-start.14
  86.2 13.7 %collective-permute-done.14 = bf16[512,512]{1,0:T(8,128)(2,1)S(1)} collective-permute-done((bf16[512,512]{1,0:T(8,128)(2,1)S(1)}, bf16[512,512]{1,0:T(8,128)(2,1)S(1)}, u32[]{:S(2)}, u32[]{:S(2)}) %collective-permute-start.14) | collective-permute-done | bytes 524320 | tf_op jit(solution)/shard_map/ppermute | solution.py:15
  99.9 0.2 fusion.3
  100.1 1.3 collective-permute-start.15
  101.3 1.6 %collective-permute-start.18 = (bf16[256,512]{1,0:T(8,128)(2,1)S(1)}, bf16[256,512]{1,0:T(8,128)(2,1)S(1)}, u32[]{:S(2)}, u32[]{:S(2)}) collective-permute-start(bf16[256,512]{1,0:T(8,128)(2,1)S(1)} %get-tuple-element.40), channel_id=1, source_target_pairs={{0,96},{32,0},{64,32},{96,64},{1,97},{33,1},{65,33},{97,65},{2,98}... | collective-permute-start | bytes 786440 | tf_op jit(solution)/shard_map/ppermute | solution.py:15
  103.0 1.4 collective-permute-start.17
  104.3 0.1 collective-permute-start.16
  104.4 3.5 %collective-permute-done.15 = bf16[256,512]{1,0:T(8,128)(2,1)S(1)} collective-permute-done((bf16[256,512]{1,0:T(8,128)(2,1)S(1)}, bf16[256,512]{1,0:T(8,128)(2,1)S(1)}, u32[]{:S(2)}, u32[]{:S(2)}) %collective-permute-start.15) | collective-permute-done | bytes 262176 | tf_op jit(solution)/shard_map/ppermute | solution.py:15
  107.9 2.7 %collective-permute-start.20 = (bf16[256,512]{1,0:T(8,128)(2,1)S(1)}, bf16[256,512]{1,0:T(8,128)(2,1)S(1)}, u32[]{:S(2)}, u32[]{:S(2)}) collective-permute-start(bf16[256,512]{1,0:T(8,128)(2,1)S(1)} %collective-permute-done.18), channel_id=1, source_target_pairs={{0,96},{32,0},{64,32},{96,64},{1,97},{33,1},{65,33},{97,65},{2,98}... | collective-permute-start | bytes 786440 | tf_op jit(solution)/shard_map/ppermute | solution.py:15
  110.6 1.6 %fusion.15 = f32[2,512,512]{2,1,0:T(8,128)S(1)} fusion(bf16[8,1024,256]{2,1,0:T(8,128)(2,1)} %bitcast.46, s32[]{:T(128)S(6)} %select_n.71, s32[]{:T(128)S(6)} %select_n.66, bf16[256,512]{1,0:T(8,128)(2,1)S(1)} %get-tuple-element.40), kind=kOutput, calls=%fused_computation.27 | convolution fusion | flops 268435456 | bytes 2883592 | tf_op jit(solution)/shard_map/dot_general | solution.py:37
  112.2 1.5 fusion.17
  113.7 0.4 fusion.13
  114.2 0.4 fusion.11
  114.6 0.4 fusion.7
  115.0 0.4 fusion.9
  115.5 3.3 %collective-permute-done.20 = bf16[256,512]{1,0:T(8,128)(2,1)S(1)} collective-permute-done((bf16[256,512]{1,0:T(8,128)(2,1)S(1)}, bf16[256,512]{1,0:T(8,128)(2,1)S(1)}, u32[]{:S(2)}, u32[]{:S(2)}) %collective-permute-start.20) | collective-permute-done | bytes 262176 | tf_op jit(solution)/shard_map/ppermute | solution.py:15
  118.7 0.4 fusion.4
  119.2 0.4 collective-permute-done.19
  119.6 0.8 add_convert_fusion
  120.4 23.1 %all_to_all.9 = bf16[32,32,512]{2,1,0:T(8,128)(2,1)S(1)} all-to-all(bf16[32,32,512]{2,1,0:T(8,128)(2,1)S(1)} %bitcast.42), channel_id=1, replica_groups=mesh['y'=4,'xh'=2,'xl'=2,'z'=4,'core'=2] {'xh','xl','z','core'}, dimensions={0} | all-to-all | bytes 2097152 | tf_op jit(solution)/shard_map/all_to_all | solution.py:151
  143.5 0.2 convert_reduce_fusion
  143.7 0.1 copy.7
  143.8 0.7 copy-done.5
  144.5 0.9 add_convert_fusion.1
  (35 shorter events, 0.1 us)
Async XLA Ops:
  6.5 56.1 %all-gather.4.cloned.1.call-start = ((), (), s32[]{:S(2)}) async-start(), calls=%async_computation.1 | async-start | bytes 5242880 | tf_op jit(solution)/shard_map/all_gather | solution.py:109
  7.8 4.3 %copy-start.3 = (bf16[512,512]{1,0:T(8,128)(2,1)S(1)}, bf16[512,512]{1,0:T(8,128)(2,1)}, u32[]{:S(2)}) copy-start(bf16[512,512]{1,0:T(8,128)(2,1)} %param.6) | copy-start | bytes 1572868
  7.8 4.3 %copy-start.4 = (bf16[512,512]{1,0:T(8,128)(2,1)S(1)}, bf16[512,512]{1,0:T(8,128)(2,1)}, u32[]{:S(2)}) copy-start(bf16[512,512]{1,0:T(8,128)(2,1)} %param.5) | copy-start | bytes 1572868
  7.8 3.0 %collective-permute-start.10 = (bf16[512,512]{1,0:T(8,128)(2,1)S(1)}, bf16[512,512]{1,0:T(8,128)(2,1)S(1)}, u32[]{:S(2)}, u32[]{:S(2)}) collective-permute-start(bf16[512,512]{1,0:T(8,128)(2,1)S(1)} %get-tuple-element.42), channel_id=1, source_target_pairs={{0,1},{1,0},{2,3},{3,2},{4,5},{5,4},{6,7},{7,6},{8,9},{9,8},{10,11... | collective-permute-start | bytes 1572872 | tf_op jit(solution)/shard_map/ppermute | solution.py:15
  12.0 98.6 %all-gather.6.cloned.1.call-start = ((), (), s32[]{:S(2)}) async-start(), calls=%async_computation.2 | async-start | bytes 4718592 | tf_op jit(solution)/shard_map/all_gather | solution.py:124
  12.2 13.2 %collective-permute-start = (bf16[512,512]{1,0:T(8,128)(2,1)S(1)}, bf16[512,512]{1,0:T(8,128)(2,1)S(1)}, u32[]{:S(2)}, u32[]{:S(2)}) collective-permute-start(bf16[512,512]{1,0:T(8,128)(2,1)S(1)} %subtract_convert_fusion), channel_id=1, source_target_pairs={{0,8},{2,24},{4,12},{6,28},{8,0},{10,16},{12,4},{14,20},{16,10},{1... | collective-permute-start | bytes 1572872 | tf_op jit(solution)/shard_map/ppermute | solution.py:25
  25.5 40.5 %copy-start.8 = (bf16[512,512]{1,0:T(8,128)(2,1)}, bf16[512,512]{1,0:T(8,128)(2,1)S(1)}, u32[]{:S(2)}) copy-start(bf16[512,512]{1,0:T(8,128)(2,1)S(1)} %collective-permute-done.refs_6_) | copy-start | bytes 1572868
  25.5 12.3 %collective-permute-start.3 = (bf16[512,512]{1,0:T(8,128)(2,1)S(1)}, bf16[512,512]{1,0:T(8,128)(2,1)S(1)}, u32[]{:S(2)}, u32[]{:S(2)}) collective-permute-start(bf16[512,512]{1,0:T(8,128)(2,1)S(1)} %collective-permute-done.refs_6_), channel_id=1, source_target_pairs={{0,8},{8,0},{1,9},{9,1},{2,10},{10,2},{3,11},{11,3},{4,12},{12,4},... | collective-permute-start | bytes 1572872 | tf_op jit(solution)/shard_map/ppermute | solution.py:15
  26.8 14.4 %collective-permute-start.2 = (bf16[512,512]{1,0:T(8,128)(2,1)S(1)}, bf16[512,512]{1,0:T(8,128)(2,1)S(1)}, u32[]{:S(2)}, u32[]{:S(2)}) collective-permute-start(bf16[512,512]{1,0:T(8,128)(2,1)S(1)} %collective-permute-done.refs_6_), channel_id=1, source_target_pairs={{0,6},{2,0},{4,2},{6,4},{1,7},{3,1},{5,3},{7,5},{8,14},{10,8},{12,... | collective-permute-start | bytes 1572872 | tf_op jit(solution)/shard_map/ppermute | solution.py:15
  31.4 13.0 %collective-permute-start.1 = (bf16[512,512]{1,0:T(8,128)(2,1)S(1)}, bf16[512,512]{1,0:T(8,128)(2,1)S(1)}, u32[]{:S(2)}, u32[]{:S(2)}) collective-permute-start(bf16[512,512]{1,0:T(8,128)(2,1)S(1)} %collective-permute-done.refs_6_), channel_id=1, source_target_pairs={{0,2},{2,4},{4,6},{6,0},{1,3},{3,5},{5,7},{7,1},{8,10},{10,12},{12... | collective-permute-start | bytes 1572872 | tf_op jit(solution)/shard_map/ppermute | solution.py:15
  37.8 28.2 %copy-start.9 = (bf16[512,512]{1,0:T(8,128)(2,1)}, bf16[512,512]{1,0:T(8,128)(2,1)S(1)}, u32[]{:S(2)}) copy-start(bf16[512,512]{1,0:T(8,128)(2,1)S(1)} %collective-permute-done.3.refs_5_) | copy-start | bytes 1572868
  41.2 18.7 %copy-start.10 = (bf16[512,512]{1,0:T(8,128)(2,1)}, bf16[512,512]{1,0:T(8,128)(2,1)S(1)}, u32[]{:S(2)}) copy-start(bf16[512,512]{1,0:T(8,128)(2,1)S(1)} %collective-permute-done.2.refs_4_) | copy-start | bytes 1572868
  44.4 15.4 %copy-start.11 = (bf16[512,512]{1,0:T(8,128)(2,1)}, bf16[512,512]{1,0:T(8,128)(2,1)S(1)}, u32[]{:S(2)}) copy-start(bf16[512,512]{1,0:T(8,128)(2,1)S(1)} %collective-permute-done.1.refs_3_) | copy-start | bytes 1572868
  44.4 10.9 %collective-permute-start.5 = (bf16[512,512]{1,0:T(8,128)(2,1)S(1)}, bf16[512,512]{1,0:T(8,128)(2,1)S(1)}, u32[]{:S(2)}, u32[]{:S(2)}) collective-permute-start(bf16[512,512]{1,0:T(8,128)(2,1)S(1)} %collective-permute-done.3.refs_5_), channel_id=1, source_target_pairs={{0,6},{2,0},{4,2},{6,4},{1,7},{3,1},{5,3},{7,5},{8,14},{10,8},{12,... | collective-permute-start | bytes 1572872 | tf_op jit(solution)/shard_map/ppermute | solution.py:15
  44.7 15.1 %collective-permute-start.6 = (bf16[512,512]{1,0:T(8,128)(2,1)S(1)}, bf16[512,512]{1,0:T(8,128)(2,1)}, u32[]{:S(2)}, u32[]{:S(2)}) collective-permute-start(bf16[512,512]{1,0:T(8,128)(2,1)S(1)} %collective-permute-done.1.refs_3_), channel_id=1, source_target_pairs={{0,2},{2,4},{4,6},{6,0},{1,3},{3,5},{5,7},{7,1},{8,10},{10,12},{12... | collective-permute-start | bytes 1572872 | tf_op jit(solution)/shard_map/ppermute | solution.py:15
  45.9 14.0 %collective-permute-start.4 = (bf16[512,512]{1,0:T(8,128)(2,1)S(1)}, bf16[512,512]{1,0:T(8,128)(2,1)S(1)}, u32[]{:S(2)}, u32[]{:S(2)}) collective-permute-start(bf16[512,512]{1,0:T(8,128)(2,1)S(1)} %collective-permute-done.1.refs_3_), channel_id=1, source_target_pairs={{0,8},{8,0},{1,9},{9,1},{2,10},{10,2},{3,11},{11,3},{4,12},{12,4},... | collective-permute-start | bytes 1572872 | tf_op jit(solution)/shard_map/ppermute | solution.py:15
  47.3 15.0 %collective-permute-start.9 = (bf16[512,256]{1,0:T(8,128)(2,1)}, bf16[512,256]{1,0:T(8,128)(2,1)S(1)}, u32[]{:S(2)}, u32[]{:S(2)}) collective-permute-start(bf16[512,256]{1,0:T(8,128)(2,1)} %param.8), channel_id=1, source_target_pairs={{0,8},{2,24},{4,12},{6,28},{8,0},{10,16},{12,4},{14,20},{16,10},{1... | collective-permute-start | bytes 786440 | tf_op jit(solution)/shard_map/ppermute | solution.py:25
  55.3 10.6 %copy-start.6 = (bf16[512,512]{1,0:T(8,128)(2,1)}, bf16[512,512]{1,0:T(8,128)(2,1)S(1)}, u32[]{:S(2)}) copy-start(bf16[512,512]{1,0:T(8,128)(2,1)S(1)} %collective-permute-done.5.refs_2_) | copy-start | bytes 1572868
  59.8 6.1 %copy-start.7 = (bf16[512,512]{1,0:T(8,128)(2,1)}, bf16[512,512]{1,0:T(8,128)(2,1)S(1)}, u32[]{:S(2)}) copy-start(bf16[512,512]{1,0:T(8,128)(2,1)S(1)} %collective-permute-done.4.refs_1_) | copy-start | bytes 1572868
  59.9 14.3 %collective-permute-start.8 = (bf16[256,512]{1,0:T(8,128)(2,1)S(1)}, bf16[256,512]{1,0:T(8,128)(2,1)S(1)}, u32[]{:S(2)}, u32[]{:S(2)}) collective-permute-start(bf16[256,512]{1,0:T(8,128)(2,1)S(1)} %slice.26), channel_id=1, source_target_pairs={{0,6},{2,0},{4,2},{6,4},{1,7},{3,1},{5,3},{7,5},{8,14},{10,8},{12,... | collective-permute-start | bytes 786440 | tf_op jit(solution)/shard_map/ppermute | solution.py:15
  61.8 12.4 %collective-permute-start.7 = (bf16[256,512]{1,0:T(8,128)(2,1)S(1)}, bf16[256,512]{1,0:T(8,128)(2,1)S(1)}, u32[]{:S(2)}, u32[]{:S(2)}) collective-permute-start(bf16[256,512]{1,0:T(8,128)(2,1)S(1)} %slice.25), channel_id=1, source_target_pairs={{0,2},{2,4},{4,6},{6,0},{1,3},{3,5},{5,7},{7,1},{8,10},{10,12},{12... | collective-permute-start | bytes 786440 | tf_op jit(solution)/shard_map/ppermute | solution.py:15
  62.6 11.6 %collective-permute-start.11 = (bf16[512,256]{1,0:T(8,128)(2,1)S(1)}, bf16[512,256]{1,0:T(8,128)(2,1)S(1)}, u32[]{:S(2)}, u32[]{:S(2)}) collective-permute-start(bf16[512,256]{1,0:T(8,128)(2,1)S(1)} %collective-permute-done.9), channel_id=1, source_target_pairs={{0,8},{8,0},{1,9},{9,1},{2,10},{10,2},{3,11},{11,3},{4,12},{12,4},... | collective-permute-start | bytes 786440 | tf_op jit(solution)/shard_map/ppermute | solution.py:15
  74.2 3.6 %copy-start.1 = (f32[512,1024]{1,0:T(8,128)S(1)}, f32[512,1024]{1,0:T(8,128)}, u32[]{:S(2)}) copy-start(f32[512,1024]{1,0:T(8,128)} %get-tuple-element.32) | copy-start | bytes 6291460
  78.8 5.0 %collective-permute-start.13 = (bf16[512,512]{1,0:T(8,128)(2,1)}, bf16[512,512]{1,0:T(8,128)(2,1)S(1)}, u32[]{:S(2)}, u32[]{:S(2)}) collective-permute-start(bf16[512,512]{1,0:T(8,128)(2,1)} %get-tuple-element.36), channel_id=1, source_target_pairs={{0,1},{1,0},{2,3},{3,2},{4,5},{5,4},{6,7},{7,6},{8,9},{9,8},{10,11... | collective-permute-start | bytes 1572872 | tf_op jit(solution)/shard_map/ppermute | solution.py:15
  81.0 2.8 %collective-permute-start.12 = (bf16[512,512]{1,0:T(8,128)(2,1)}, bf16[512,512]{1,0:T(8,128)(2,1)}, u32[]{:S(2)}, u32[]{:S(2)}) collective-permute-start(bf16[512,512]{1,0:T(8,128)(2,1)} %maximum_add_fusion.1), channel_id=1, source_target_pairs={{0,1},{1,0},{2,3},{3,2},{4,5},{5,4},{6,7},{7,6},{8,9},{9,8},{10,11... | collective-permute-start | bytes 1572872 | tf_op jit(solution)/shard_map/ppermute | solution.py:15
  81.0 2.8 %copy-start.2 = (f32[512,512]{1,0:T(8,128)S(1)}, f32[512,512]{1,0:T(8,128)}, u32[]{:S(2)}) copy-start(f32[512,512]{1,0:T(8,128)} %get-tuple-element.30) | copy-start | bytes 3145732
  85.4 14.6 %collective-permute-start.14 = (bf16[512,512]{1,0:T(8,128)(2,1)S(1)}, bf16[512,512]{1,0:T(8,128)(2,1)S(1)}, u32[]{:S(2)}, u32[]{:S(2)}) collective-permute-start(bf16[512,512]{1,0:T(8,128)(2,1)S(1)} %get-tuple-element.37), channel_id=1, source_target_pairs={{0,16},{16,0},{1,17},{17,1},{2,18},{18,2},{3,19},{19,3},{4,20},{20... | collective-permute-start | bytes 1572872 | tf_op jit(solution)/shard_map/ppermute | solution.py:15
  100.1 7.8 %collective-permute-start.15 = (bf16[256,512]{1,0:T(8,128)(2,1)S(1)}, bf16[256,512]{1,0:T(8,128)(2,1)S(1)}, u32[]{:S(2)}, u32[]{:S(2)}) collective-permute-start(bf16[256,512]{1,0:T(8,128)(2,1)S(1)} %get-tuple-element.39), channel_id=1, source_target_pairs={{0,32},{32,64},{64,96},{96,0},{1,33},{33,65},{65,97},{97,1},{2,34}... | collective-permute-start | bytes 786440 | tf_op jit(solution)/shard_map/ppermute | solution.py:15
  101.3 6.6 %collective-permute-start.18 = (bf16[256,512]{1,0:T(8,128)(2,1)S(1)}, bf16[256,512]{1,0:T(8,128)(2,1)S(1)}, u32[]{:S(2)}, u32[]{:S(2)}) collective-permute-start(bf16[256,512]{1,0:T(8,128)(2,1)S(1)} %get-tuple-element.40), channel_id=1, source_target_pairs={{0,96},{32,0},{64,32},{96,64},{1,97},{33,1},{65,33},{97,65},{2,98}... | collective-permute-start | bytes 786440 | tf_op jit(solution)/shard_map/ppermute | solution.py:15
  103.0 12.1 %collective-permute-start.17 = (bf16[256,512]{1,0:T(8,128)(2,1)S(1)}, bf16[256,512]{1,0:T(8,128)(2,1)S(1)}, u32[]{:S(2)}, u32[]{:S(2)}) collective-permute-start(bf16[256,512]{1,0:T(8,128)(2,1)S(1)} %get-tuple-element.39), channel_id=1, source_target_pairs={{0,96},{32,0},{64,32},{96,64},{1,97},{33,1},{65,33},{97,65},{2,98}... | collective-permute-start | bytes 786440 | tf_op jit(solution)/shard_map/ppermute | solution.py:15
  104.3 9.8 %collective-permute-start.16 = (bf16[256,512]{1,0:T(8,128)(2,1)S(1)}, bf16[256,512]{1,0:T(8,128)(2,1)S(1)}, u32[]{:S(2)}, u32[]{:S(2)}) collective-permute-start(bf16[256,512]{1,0:T(8,128)(2,1)S(1)} %get-tuple-element.40), channel_id=1, source_target_pairs={{0,32},{32,64},{64,96},{96,0},{1,33},{33,65},{65,97},{97,1},{2,34}... | collective-permute-start | bytes 786440 | tf_op jit(solution)/shard_map/ppermute | solution.py:15
  107.9 11.7 %collective-permute-start.19 = (bf16[256,512]{1,0:T(8,128)(2,1)S(1)}, bf16[256,512]{1,0:T(8,128)(2,1)S(1)}, u32[]{:S(2)}, u32[]{:S(2)}) collective-permute-start(bf16[256,512]{1,0:T(8,128)(2,1)S(1)} %collective-permute-done.15), channel_id=1, source_target_pairs={{0,32},{32,64},{64,96},{96,0},{1,33},{33,65},{65,97},{97,1},{2,34}... | collective-permute-start | bytes 786440 | tf_op jit(solution)/shard_map/ppermute | solution.py:15
  107.9 10.8 %collective-permute-start.20 = (bf16[256,512]{1,0:T(8,128)(2,1)S(1)}, bf16[256,512]{1,0:T(8,128)(2,1)S(1)}, u32[]{:S(2)}, u32[]{:S(2)}) collective-permute-start(bf16[256,512]{1,0:T(8,128)(2,1)S(1)} %collective-permute-done.18), channel_id=1, source_target_pairs={{0,96},{32,0},{64,32},{96,64},{1,97},{33,1},{65,33},{97,65},{2,98}... | collective-permute-start | bytes 786440 | tf_op jit(solution)/shard_map/ppermute | solution.py:15
  110.6 3.1 %copy-start = (bf16[8192,256]{1,0:T(8,128)(2,1)S(1)}, bf16[8192,256]{1,0:T(8,128)(2,1)}, u32[]{:S(2)}) copy-start(bf16[8192,256]{1,0:T(8,128)(2,1)} %all-gather.6.cloned.1.call-done) | copy-start | bytes 12582916
  143.5 1.0 copy-start.5
Sparse Core Ops, SparseCore 0:
  12.2 50.4 all-gather.3
  75.2 32.7 all-gather.5

commit v6 on v5

--- a/solution.py
+++ b/solution.py
@@ -15,12 +15,13 @@
     return lax.ppermute(v, axis, [(i, (i + by) % n) for i in range(n)])
 
 
-def turn(v):
+def turn(v, flip=True):
     pairs = []
     for xh in range(2):
         for xl in range(2):
             for z in range(4):
-                to = ((z & 1) * 2 + 1 - xl) * 4 + (z & ~1) + xh
+                new_xl = 1 - xl if flip or z & 1 != xh else xl
+                to = ((z & 1) * 2 + new_xl) * 4 + (z & ~1) + xh
                 pairs.append(((xh * 2 + xl) * 4 + z, to))
     return lax.ppermute(v, ("xh", "xl", "z"), pairs)
 
@@ -111,7 +112,7 @@
     b = turn(change)
     bm, bp, a = together(shift(b, "z", 1), shift(b, "z", -1), shift(b, "xl", 1))
     am, ap, b2 = together(shift(bm, "xl", 1), shift(a, "z", -1), shift(bm, "z", 1))
-    turned = turn(after(output_factor, bm, bp, a))
+    turned = turn(after(output_factor, bm, bp, a), flip=False)
     far = [shift(am[:half], "z", 1), shift(ap[half:], "z", -1)]
     *far, part = together(*far, shift(after(turned, factor), "xl", 1))
 
@@ -139,14 +140,18 @@
     above = [shift(p[0], "y", -1), shift(p[1], "y", -1)]
     beyond = [shift(below[0], "y", 1), shift(above[1], "y", -1)]
 
-    def share(blocks, dy):
+    def share(blocks, dy, to):
         at = (y + dy) & 3
-        size = (2, rows, half)
-        corners = [(4 * h + (at & 1) * 2, ((at >> 1) ^ xl) * rows, 0) for h in range(2)]
-        terms = [dot(lax.dynamic_slice(left, c, size), v) for c, v in zip(corners, blocks)]
-        return terms[0] + terms[1]
+        here = 1 - ((at >> 1) ^ xl ^ to ^ xh)
+        corners = [(4 * h + (at & 1) * 2 + to, here * rows, 0) for h in range(2)]
+        sides = [lax.dynamic_slice(left, c, (1, rows, half))[0] for c in corners]
+        return dot(sides[0], blocks[0]) + dot(sides[1], blocks[1])
 
-    penalty = ((share(p, 0) + share(below, -1)) + share(above, 1)) + share(beyond, 2)
+    penalty = [
+        ((share(p, 0, to) + share(below, -1, to)) + share(above, 1, to)) + share(beyond, 2, to)
+        for to in range(2)
+    ]
+    penalty = jnp.stack(penalty)
     penalty = penalty.astype(BF16).reshape(2 * rows, cols)
     owned = lax.all_to_all(penalty, ("xh",) + COL, split_axis=0, concat_axis=0, tiled=True)
     owned = owned.reshape(2, 16, task_grad.shape[0], cols).astype(F32).sum(axis=0)

time: 153 us -> 155 us (1.013)
  starting transfers between devices: 27.7 us -> 31.5 us
  waiting for transfers between devices: 59.4 us -> 56.5 us
    ppermute x19, waiting for transfers between devices: 47.3 us -> 44.6 us  [shift(): return lax.ppermute(v, axis, [(i, (i + by) % n) for i in range(n)])]
    ppermute x19, starting transfers between devices: 26.3 us -> 28.5 us  [shift(): return lax.ppermute(v, axis, [(i, (i + by) % n) for i in range(n)])]
    ppermute x2, starting transfers between devices: 1.41 us -> 2.98 us  [turn(): return lax.ppermute(v, ('xh', 'xl', 'z'), pairs)]
    dot_general x12 -> x20, matrix products: 11.5 us -> 12.1 us  [dot(): lax.dot_general(a, b, (((a.ndim - 1,), (0,)), ((), ())), preferred_elemen...]
  transfers between devices with their start and end apart: 23 -> 23, of which waited for: 12 -> 11; matrix products, arithmetic and copies ran while one was open for 9% -> 10% of each run, Pallas kernels for 5% -> 5%
where the time goes in v6:
time: 155 us; the launch traced here: 154 us
  waiting for transfers between devices  56.5 us (36%)
  starting transfers between devices  31.5 us (20%)
  blocking collectives  23.8 us (15%)
  between operations  13.7 us (9%)
  matrix products  12.1 us (8%)
  Pallas kernels  8.22 us (5%)
  other arithmetic  6.37 us (4%)
  local copies, waits for them, and re-layouts  2.15 us (1%)
    ppermute x19, waiting for transfers between devices, shift(): return lax.ppermute(v, axis, [(i, (i + by) % n) for i in range(n)])  44.6 us
    ppermute x19, starting transfers between devices, shift(): return lax.ppermute(v, axis, [(i, (i + by) % n) for i in range(n)])  28.5 us
    all_to_all x1, blocking collectives, body(): lax.all_to_all(penalty, ('xh',) + COL, split_axis=0, concat_axis=0, tiled...  23.8 us
    dot_general x20, matrix products, dot(): lax.dot_general(a, b, (((a.ndim - 1,), (0,)), ((), ())), preferred_elemen...  12.1 us
    ppermute x2, waiting for transfers between devices, turn(): return lax.ppermute(v, ('xh', 'xl', 'z'), pairs)  11.8 us
    pallas_call x1, Pallas kernels, early(): pl.pallas_call(lambda *refs: early_kernel(n, m, *refs), out_shape=(jax.Sh...  8.22 us
  transfers between devices with their start and end apart: 23, of which 11 were waited for; matrix products, arithmetic and copies ran while one was open for 10% of the time, Pallas kernels for 5%

profile of v6, /device:TPU:1, one launch (start us, length us, event | category | flops | bytes accessed | tf_op | source)
XLA Modules:
  0.0 154.4 jit_solution(17903029948365502132)
XLA Ops:
  6.5 1.4 constant_dynamic-slice_fusion.1
  7.9 1.5 collective-permute-start.10
  9.4 1.5 collective-permute-done.10
  10.9 1.1 pad_maximum_fusion
  12.1 0.0 all-gather.4.cloned.1.call-update
  12.1 0.0 all-gather.6.cloned.1.call-start
  12.2 0.1 subtract_convert_fusion
  12.3 1.4 collective-permute-start
  13.7 11.8 %collective-permute-done.refs_6_ = bf16[512,512]{1,0:T(8,128)(2,1)S(1)} collective-permute-done((bf16[512,512]{1,0:T(8,128)(2,1)S(1)}, bf16[512,512]{1,0:T(8,128)(2,1)S(1)}, u32[]{:S(2)}, u32[]{:S(2)}) %collective-permute-start) | collective-permute-done | bytes 524320 | tf_op jit(solution)/shard_map/ppermute | solution.py:26
  25.5 3.8 %collective-permute-start.1 = (bf16[512,512]{1,0:T(8,128)(2,1)S(1)}, bf16[512,512]{1,0:T(8,128)(2,1)S(1)}, u32[]{:S(2)}, u32[]{:S(2)}) collective-permute-start(bf16[512,512]{1,0:T(8,128)(2,1)S(1)} %collective-permute-done.refs_6_), channel_id=1, source_target_pairs={{0,2},{2,4},{4,6},{6,0},{1,3},{3,5},{5,7},{7,1},{8,10},{10,12},{12... | collective-permute-start | bytes 1572872 | tf_op jit(solution)/shard_map/ppermute | solution.py:15
  29.4 2.1 %collective-permute-start.2 = (bf16[512,512]{1,0:T(8,128)(2,1)S(1)}, bf16[512,512]{1,0:T(8,128)(2,1)S(1)}, u32[]{:S(2)}, u32[]{:S(2)}) collective-permute-start(bf16[512,512]{1,0:T(8,128)(2,1)S(1)} %collective-permute-done.refs_6_), channel_id=1, source_target_pairs={{0,6},{2,0},{4,2},{6,4},{1,7},{3,1},{5,3},{7,5},{8,14},{10,8},{12,... | collective-permute-start | bytes 1572872 | tf_op jit(solution)/shard_map/ppermute | solution.py:15
  31.5 11.1 %collective-permute-done.1.refs_3_ = bf16[512,512]{1,0:T(8,128)(2,1)S(1)} collective-permute-done((bf16[512,512]{1,0:T(8,128)(2,1)S(1)}, bf16[512,512]{1,0:T(8,128)(2,1)S(1)}, u32[]{:S(2)}, u32[]{:S(2)}) %collective-permute-start.1) | collective-permute-done | bytes 524320 | tf_op jit(solution)/shard_map/ppermute | solution.py:15
  42.6 0.9 collective-permute-done.3.refs_5_
  43.5 1.6 %collective-permute-start.5 = (bf16[512,512]{1,0:T(8,128)(2,1)S(1)}, bf16[512,512]{1,0:T(8,128)(2,1)S(1)}, u32[]{:S(2)}, u32[]{:S(2)}) collective-permute-start(bf16[512,512]{1,0:T(8,128)(2,1)S(1)} %collective-permute-done.3.refs_5_), channel_id=1, source_target_pairs={{0,6},{2,0},{4,2},{6,4},{1,7},{3,1},{5,3},{7,5},{8,14},{10,8},{12,... | collective-permute-start | bytes 1572872 | tf_op jit(solution)/shard_map/ppermute | solution.py:15
  45.2 1.6 %collective-permute-start.9 = (bf16[512,256]{1,0:T(8,128)(2,1)}, bf16[512,256]{1,0:T(8,128)(2,1)S(1)}, u32[]{:S(2)}, u32[]{:S(2)}) collective-permute-start(bf16[512,256]{1,0:T(8,128)(2,1)} %param.8), channel_id=1, source_target_pairs={{0,0},{2,24},{4,4},{6,28},{8,8},{10,16},{12,12},{14,20},{16,10},{1... | collective-permute-start | bytes 786440 | tf_op jit(solution)/shard_map/ppermute | solution.py:26
  46.8 0.6 stack.43.refs_0_
  47.4 7.3 %collective-permute-done.4.refs_1_ = bf16[512,512]{1,0:T(8,128)(2,1)S(1)} collective-permute-done((bf16[512,512]{1,0:T(8,128)(2,1)S(1)}, bf16[512,512]{1,0:T(8,128)(2,1)S(1)}, u32[]{:S(2)}, u32[]{:S(2)}) %collective-permute-start.4) | collective-permute-done | bytes 524320 | tf_op jit(solution)/shard_map/ppermute | solution.py:15
  54.8 4.6 %collective-permute-done.6.refs_7_ = bf16[512,512]{1,0:T(8,128)(2,1)} collective-permute-done((bf16[512,512]{1,0:T(8,128)(2,1)S(1)}, bf16[512,512]{1,0:T(8,128)(2,1)}, u32[]{:S(2)}, u32[]{:S(2)}) %collective-permute-start.6) | collective-permute-done | bytes 524320 | tf_op jit(solution)/shard_map/ppermute | solution.py:15
  59.4 2.4 %collective-permute-start.7 = (bf16[256,512]{1,0:T(8,128)(2,1)S(1)}, bf16[256,512]{1,0:T(8,128)(2,1)S(1)}, u32[]{:S(2)}, u32[]{:S(2)}) collective-permute-start(bf16[256,512]{1,0:T(8,128)(2,1)S(1)} %slice.25), channel_id=1, source_target_pairs={{0,2},{2,4},{4,6},{6,0},{1,3},{3,5},{5,7},{7,1},{8,10},{10,12},{12... | collective-permute-start | bytes 786440 | tf_op jit(solution)/shard_map/ppermute | solution.py:15
  61.8 1.3 collective-permute-start.8
  63.1 0.8 collective-permute-start.11
  63.9 8.2 %shard_map.55 = (bf16[512,512]{1,0:T(8,128)(2,1)}, f32[512,512]{1,0:T(8,128)}, f32[512,1024]{1,0:T(8,128)}) custom-call(s32[7]{0:T(128)} %stack.43.refs_0_, bf16[512,512]{1,0:T(8,128)(2,1)} %copy-done.5, bf16[512,512]{1,0:T(8,128)(2,1)} %copy-done.6, bf16[512,512]{1,0:T(8,128)(2,1)} %copy-done.8, bf16[512,512]{1,0:T(8,128)(2,1)} %copy-done.9, ...), custom_call_target="tpu_custom_call" | custom-call | flops 3758096384 | bytes 12582912 | tf_op jit(solution)/shard_map/pallas_call | solution.py:78
  72.2 0.9 pad_maximum_fusion.2
  73.0 0.0 all-gather.6.cloned.1.call-update
  73.1 1.3 fusion.14
  74.4 1.3 fusion.16
  75.8 1.0 maximum_add_fusion.1
  76.7 4.2 %collective-permute-start.13 = (bf16[512,512]{1,0:T(8,128)(2,1)}, bf16[512,512]{1,0:T(8,128)(2,1)S(1)}, u32[]{:S(2)}, u32[]{:S(2)}) collective-permute-start(bf16[512,512]{1,0:T(8,128)(2,1)} %get-tuple-element.36), channel_id=1, source_target_pairs={{0,1},{1,0},{2,3},{3,2},{4,5},{5,4},{6,7},{7,6},{8,9},{9,8},{10,11... | collective-permute-start | bytes 1572872 | tf_op jit(solution)/shard_map/ppermute | solution.py:15
  81.0 1.3 fusion.18
  82.3 1.3 fusion.20
  83.7 1.9 %select_convert_fusion = (bf16[512,512]{1,0:T(8,128)(2,1)S(1)}, f32[512,512]{1,0:T(8,128)S(1)}) fusion(f32[512,512]{1,0:T(8,128)} %get-tuple-element.30, bf16[512,512]{1,0:T(8,128)(2,1)S(1)} %collective-permute-done.13, pred[]{:T(512)S(6)} %eq.3, bf16[512,512]{1,0:T(8,128)(2,1)} %collective-permute-done.12, f32[256,512]{1,0:T(8,128)S(1)} %fusion.18, ...), kind=kLoop, calls=%fused_computation.25 | loop fusion | flops 2359296 | bytes 5767169 | tf_op jit(solution)/shard_map/convert_element_type | solution.py:135
  85.6 1.7 %collective-permute-start.14 = (bf16[512,512]{1,0:T(8,128)(2,1)S(1)}, bf16[512,512]{1,0:T(8,128)(2,1)S(1)}, u32[]{:S(2)}, u32[]{:S(2)}) collective-permute-start(bf16[512,512]{1,0:T(8,128)(2,1)S(1)} %get-tuple-element.37), channel_id=1, source_target_pairs={{0,16},{16,0},{1,17},{17,1},{2,18},{18,2},{3,19},{19,3},{4,20},{20... | collective-permute-start | bytes 1572872 | tf_op jit(solution)/shard_map/ppermute | solution.py:15
  87.3 12.9 %collective-permute-done.14 = bf16[512,512]{1,0:T(8,128)(2,1)S(1)} collective-permute-done((bf16[512,512]{1,0:T(8,128)(2,1)S(1)}, bf16[512,512]{1,0:T(8,128)(2,1)S(1)}, u32[]{:S(2)}, u32[]{:S(2)}) %collective-permute-start.14) | collective-permute-done | bytes 524320 | tf_op jit(solution)/shard_map/ppermute | solution.py:15
  100.2 0.2 fusion.13
  100.3 2.8 %collective-permute-start.18 = (bf16[256,512]{1,0:T(8,128)(2,1)S(1)}, bf16[256,512]{1,0:T(8,128)(2,1)S(1)}, u32[]{:S(2)}, u32[]{:S(2)}) collective-permute-start(bf16[256,512]{1,0:T(8,128)(2,1)S(1)} %get-tuple-element.40), channel_id=1, source_target_pairs={{0,96},{32,0},{64,32},{96,64},{1,97},{33,1},{65,33},{97,65},{2,98}... | collective-permute-start | bytes 786440 | tf_op jit(solution)/shard_map/ppermute | solution.py:15
  103.2 2.7 %collective-permute-start.17 = (bf16[256,512]{1,0:T(8,128)(2,1)S(1)}, bf16[256,512]{1,0:T(8,128)(2,1)S(1)}, u32[]{:S(2)}, u32[]{:S(2)}) collective-permute-start(bf16[256,512]{1,0:T(8,128)(2,1)S(1)} %get-tuple-element.39), channel_id=1, source_target_pairs={{0,96},{32,0},{64,32},{96,64},{1,97},{33,1},{65,33},{97,65},{2,98}... | collective-permute-start | bytes 786440 | tf_op jit(solution)/shard_map/ppermute | solution.py:15
  105.9 1.5 collective-permute-done.18
  107.4 3.4 %collective-permute-start.20 = (bf16[256,512]{1,0:T(8,128)(2,1)S(1)}, bf16[256,512]{1,0:T(8,128)(2,1)S(1)}, u32[]{:S(2)}, u32[]{:S(2)}) collective-permute-start(bf16[256,512]{1,0:T(8,128)(2,1)S(1)} %collective-permute-done.18), channel_id=1, source_target_pairs={{0,96},{32,0},{64,32},{96,64},{1,97},{33,1},{65,33},{97,65},{2,98}... | collective-permute-start | bytes 786440 | tf_op jit(solution)/shard_map/ppermute | solution.py:15
  110.8 0.0 all-gather.6.cloned.1.call-done
  110.9 1.4 fusion.31
  112.3 1.3 convolution_add_fusion.3
  113.5 0.3 fusion.43
  113.8 0.3 convolution_add_fusion.7
  114.1 2.0 %collective-permute-done.16 = bf16[256,512]{1,0:T(8,128)(2,1)S(1)} collective-permute-done((bf16[256,512]{1,0:T(8,128)(2,1)S(1)}, bf16[256,512]{1,0:T(8,128)(2,1)S(1)}, u32[]{:S(2)}, u32[]{:S(2)}) %collective-permute-start.16) | collective-permute-done | bytes 262176 | tf_op jit(solution)/shard_map/ppermute | solution.py:15
  116.2 0.3 fusion.28
  116.4 0.3 fusion.40
  116.7 0.3 fusion.2
  117.0 0.3 fusion.5
  117.3 0.3 fusion.25
  117.6 0.3 fusion.37
  118.0 0.3 fusion.1
  118.3 0.3 fusion.4
  118.6 0.1 collective-permute-done.20
  118.6 0.3 fusion.22
  118.9 0.3 fusion.34
  119.2 2.5 %collective-permute-done.19 = bf16[256,512]{1,0:T(8,128)(2,1)S(1)} collective-permute-done((bf16[256,512]{1,0:T(8,128)(2,1)S(1)}, bf16[256,512]{1,0:T(8,128)(2,1)S(1)}, u32[]{:S(2)}, u32[]{:S(2)}) %collective-permute-start.19) | collective-permute-done | bytes 262176 | tf_op jit(solution)/shard_map/ppermute | solution.py:15
  121.8 0.3 fusion.8
  122.1 0.3 fusion.9
  122.4 0.0 copy-start.4
  122.4 0.1 pad_maximum_fusion.1
  122.5 23.8 %all_to_all.6 = bf16[32,32,512]{2,1,0:T(8,128)(2,1)S(1)} all-to-all(bf16[32,32,512]{2,1,0:T(8,128)(2,1)S(1)} %bitcast.86), channel_id=1, replica_groups=mesh['y'=4,'xh'=2,'xl'=2,'z'=4,'core'=2] {'xh','xl','z','core'}, dimensions={0} | all-to-all | bytes 2097152 | tf_op jit(solution)/shard_map/all_to_all | solution.py:156
  146.3 0.2 convert_reduce_fusion
  146.5 0.1 copy.7
  146.6 0.9 add_convert_fusion
  (42 shorter events, 0.1 us)
Async XLA Ops:
  6.5 5.6 %copy-start.2 = (bf16[512,512]{1,0:T(8,128)(2,1)S(1)}, bf16[512,512]{1,0:T(8,128)(2,1)}, u32[]{:S(2)}) copy-start(bf16[512,512]{1,0:T(8,128)(2,1)} %param.6) | copy-start | bytes 1572868
  6.5 5.6 %copy-start.3 = (bf16[512,512]{1,0:T(8,128)(2,1)S(1)}, bf16[512,512]{1,0:T(8,128)(2,1)}, u32[]{:S(2)}) copy-start(bf16[512,512]{1,0:T(8,128)(2,1)} %param.5) | copy-start | bytes 1572868
  6.5 56.5 %all-gather.4.cloned.1.call-start = ((), (), s32[]{:S(2)}) async-start(), calls=%async_computation.1 | async-start | bytes 5242880 | tf_op jit(solution)/shard_map/all_gather | solution.py:110
  7.9 3.0 %collective-permute-start.10 = (bf16[512,512]{1,0:T(8,128)(2,1)S(1)}, bf16[512,512]{1,0:T(8,128)(2,1)S(1)}, u32[]{:S(2)}, u32[]{:S(2)}) collective-permute-start(bf16[512,512]{1,0:T(8,128)(2,1)S(1)} %get-tuple-element.42), channel_id=1, source_target_pairs={{0,1},{1,0},{2,3},{3,2},{4,5},{5,4},{6,7},{7,6},{8,9},{9,8},{10,11... | collective-permute-start | bytes 1572872 | tf_op jit(solution)/shard_map/ppermute | solution.py:15
  12.1 98.7 %all-gather.6.cloned.1.call-start = ((), (), s32[]{:S(2)}) async-start(), calls=%async_computation.2 | async-start | bytes 4718592 | tf_op jit(solution)/shard_map/all_gather | solution.py:125
  12.3 13.2 %collective-permute-start = (bf16[512,512]{1,0:T(8,128)(2,1)S(1)}, bf16[512,512]{1,0:T(8,128)(2,1)S(1)}, u32[]{:S(2)}, u32[]{:S(2)}) collective-permute-start(bf16[512,512]{1,0:T(8,128)(2,1)S(1)} %subtract_convert_fusion), channel_id=1, source_target_pairs={{0,8},{2,24},{4,12},{6,28},{8,0},{10,16},{12,4},{14,20},{16,10},{1... | collective-permute-start | bytes 1572872 | tf_op jit(solution)/shard_map/ppermute | solution.py:26
  25.5 38.4 %copy-start.7 = (bf16[512,512]{1,0:T(8,128)(2,1)}, bf16[512,512]{1,0:T(8,128)(2,1)S(1)}, u32[]{:S(2)}) copy-start(bf16[512,512]{1,0:T(8,128)(2,1)S(1)} %collective-permute-done.refs_6_) | copy-start | bytes 1572868
  25.5 17.1 %collective-permute-start.1 = (bf16[512,512]{1,0:T(8,128)(2,1)S(1)}, bf16[512,512]{1,0:T(8,128)(2,1)S(1)}, u32[]{:S(2)}, u32[]{:S(2)}) collective-permute-start(bf16[512,512]{1,0:T(8,128)(2,1)S(1)} %collective-permute-done.refs_6_), channel_id=1, source_target_pairs={{0,2},{2,4},{4,6},{6,0},{1,3},{3,5},{5,7},{7,1},{8,10},{10,12},{12... | collective-permute-start | bytes 1572872 | tf_op jit(solution)/shard_map/ppermute | solution.py:15
  29.4 13.3 %collective-permute-start.2 = (bf16[512,512]{1,0:T(8,128)(2,1)S(1)}, bf16[512,512]{1,0:T(8,128)(2,1)S(1)}, u32[]{:S(2)}, u32[]{:S(2)}) collective-permute-start(bf16[512,512]{1,0:T(8,128)(2,1)S(1)} %collective-permute-done.refs_6_), channel_id=1, source_target_pairs={{0,6},{2,0},{4,2},{6,4},{1,7},{3,1},{5,3},{7,5},{8,14},{10,8},{12,... | collective-permute-start | bytes 1572872 | tf_op jit(solution)/shard_map/ppermute | solution.py:15
  31.5 12.0 %collective-permute-start.3 = (bf16[512,512]{1,0:T(8,128)(2,1)S(1)}, bf16[512,512]{1,0:T(8,128)(2,1)S(1)}, u32[]{:S(2)}, u32[]{:S(2)}) collective-permute-start(bf16[512,512]{1,0:T(8,128)(2,1)S(1)} %collective-permute-done.refs_6_), channel_id=1, source_target_pairs={{0,8},{8,0},{1,9},{9,1},{2,10},{10,2},{3,11},{11,3},{4,12},{12,4},... | collective-permute-start | bytes 1572872 | tf_op jit(solution)/shard_map/ppermute | solution.py:15
  42.6 21.3 %copy-start.8 = (bf16[512,512]{1,0:T(8,128)(2,1)}, bf16[512,512]{1,0:T(8,128)(2,1)S(1)}, u32[]{:S(2)}) copy-start(bf16[512,512]{1,0:T(8,128)(2,1)S(1)} %collective-permute-done.1.refs_3_) | copy-start | bytes 1572868
  42.6 2.5 %copy-start.9 = (bf16[512,512]{1,0:T(8,128)(2,1)}, bf16[512,512]{1,0:T(8,128)(2,1)S(1)}, u32[]{:S(2)}) copy-start(bf16[512,512]{1,0:T(8,128)(2,1)S(1)} %collective-permute-done.2.refs_4_) | copy-start | bytes 1572868
  43.5 15.8 %copy-start.10 = (bf16[512,512]{1,0:T(8,128)(2,1)}, bf16[512,512]{1,0:T(8,128)(2,1)S(1)}, u32[]{:S(2)}) copy-start(bf16[512,512]{1,0:T(8,128)(2,1)S(1)} %collective-permute-done.3.refs_5_) | copy-start | bytes 1572868
  43.5 11.2 %collective-permute-start.4 = (bf16[512,512]{1,0:T(8,128)(2,1)S(1)}, bf16[512,512]{1,0:T(8,128)(2,1)S(1)}, u32[]{:S(2)}, u32[]{:S(2)}) collective-permute-start(bf16[512,512]{1,0:T(8,128)(2,1)S(1)} %collective-permute-done.1.refs_3_), channel_id=1, source_target_pairs={{0,8},{8,0},{1,9},{9,1},{2,10},{10,2},{3,11},{11,3},{4,12},{12,4},... | collective-permute-start | bytes 1572872 | tf_op jit(solution)/shard_map/ppermute | solution.py:15
  43.5 11.2 %collective-permute-start.5 = (bf16[512,512]{1,0:T(8,128)(2,1)S(1)}, bf16[512,512]{1,0:T(8,128)(2,1)S(1)}, u32[]{:S(2)}, u32[]{:S(2)}) collective-permute-start(bf16[512,512]{1,0:T(8,128)(2,1)S(1)} %collective-permute-done.3.refs_5_), channel_id=1, source_target_pairs={{0,6},{2,0},{4,2},{6,4},{1,7},{3,1},{5,3},{7,5},{8,14},{10,8},{12,... | collective-permute-start | bytes 1572872 | tf_op jit(solution)/shard_map/ppermute | solution.py:15
  45.2 14.2 %collective-permute-start.6 = (bf16[512,512]{1,0:T(8,128)(2,1)S(1)}, bf16[512,512]{1,0:T(8,128)(2,1)}, u32[]{:S(2)}, u32[]{:S(2)}) collective-permute-start(bf16[512,512]{1,0:T(8,128)(2,1)S(1)} %collective-permute-done.1.refs_3_), channel_id=1, source_target_pairs={{0,2},{2,4},{4,6},{6,0},{1,3},{3,5},{5,7},{7,1},{8,10},{10,12},{12... | collective-permute-start | bytes 1572872 | tf_op jit(solution)/shard_map/ppermute | solution.py:15
  45.2 17.9 %collective-permute-start.9 = (bf16[512,256]{1,0:T(8,128)(2,1)}, bf16[512,256]{1,0:T(8,128)(2,1)S(1)}, u32[]{:S(2)}, u32[]{:S(2)}) collective-permute-start(bf16[512,256]{1,0:T(8,128)(2,1)} %param.8), channel_id=1, source_target_pairs={{0,0},{2,24},{4,4},{6,28},{8,8},{10,16},{12,12},{14,20},{16,10},{1... | collective-permute-start | bytes 786440 | tf_op jit(solution)/shard_map/ppermute | solution.py:26
  54.8 9.1 %copy-start.5 = (bf16[512,512]{1,0:T(8,128)(2,1)}, bf16[512,512]{1,0:T(8,128)(2,1)S(1)}, u32[]{:S(2)}) copy-start(bf16[512,512]{1,0:T(8,128)(2,1)S(1)} %collective-permute-done.4.refs_1_) | copy-start | bytes 1572868
  54.8 9.1 %copy-start.6 = (bf16[512,512]{1,0:T(8,128)(2,1)}, bf16[512,512]{1,0:T(8,128)(2,1)S(1)}, u32[]{:S(2)}) copy-start(bf16[512,512]{1,0:T(8,128)(2,1)S(1)} %collective-permute-done.5.refs_2_) | copy-start | bytes 1572868
  59.4 12.8 %collective-permute-start.7 = (bf16[256,512]{1,0:T(8,128)(2,1)S(1)}, bf16[256,512]{1,0:T(8,128)(2,1)S(1)}, u32[]{:S(2)}, u32[]{:S(2)}) collective-permute-start(bf16[256,512]{1,0:T(8,128)(2,1)S(1)} %slice.25), channel_id=1, source_target_pairs={{0,2},{2,4},{4,6},{6,0},{1,3},{3,5},{5,7},{7,1},{8,10},{10,12},{12... | collective-permute-start | bytes 786440 | tf_op jit(solution)/shard_map/ppermute | solution.py:15
  61.8 10.4 %collective-permute-start.8 = (bf16[256,512]{1,0:T(8,128)(2,1)S(1)}, bf16[256,512]{1,0:T(8,128)(2,1)S(1)}, u32[]{:S(2)}, u32[]{:S(2)}) collective-permute-start(bf16[256,512]{1,0:T(8,128)(2,1)S(1)} %slice.26), channel_id=1, source_target_pairs={{0,6},{2,0},{4,2},{6,4},{1,7},{3,1},{5,3},{7,5},{8,14},{10,8},{12,... | collective-permute-start | bytes 786440 | tf_op jit(solution)/shard_map/ppermute | solution.py:15
  63.1 9.1 %collective-permute-start.11 = (bf16[512,256]{1,0:T(8,128)(2,1)S(1)}, bf16[512,256]{1,0:T(8,128)(2,1)S(1)}, u32[]{:S(2)}, u32[]{:S(2)}) collective-permute-start(bf16[512,256]{1,0:T(8,128)(2,1)S(1)} %collective-permute-done.9), channel_id=1, source_target_pairs={{0,8},{8,0},{1,9},{9,1},{2,10},{10,2},{3,11},{11,3},{4,12},{12,4},... | collective-permute-start | bytes 786440 | tf_op jit(solution)/shard_map/ppermute | solution.py:15
  72.1 3.6 %copy-start.1 = (f32[512,1024]{1,0:T(8,128)S(1)}, f32[512,1024]{1,0:T(8,128)}, u32[]{:S(2)}) copy-start(f32[512,1024]{1,0:T(8,128)} %get-tuple-element.32) | copy-start | bytes 6291460
  76.7 6.9 %collective-permute-start.13 = (bf16[512,512]{1,0:T(8,128)(2,1)}, bf16[512,512]{1,0:T(8,128)(2,1)S(1)}, u32[]{:S(2)}, u32[]{:S(2)}) collective-permute-start(bf16[512,512]{1,0:T(8,128)(2,1)} %get-tuple-element.36), channel_id=1, source_target_pairs={{0,1},{1,0},{2,3},{3,2},{4,5},{5,4},{6,7},{7,6},{8,9},{9,8},{10,11... | collective-permute-start | bytes 1572872 | tf_op jit(solution)/shard_map/ppermute | solution.py:15
  81.0 2.7 %collective-permute-start.12 = (bf16[512,512]{1,0:T(8,128)(2,1)}, bf16[512,512]{1,0:T(8,128)(2,1)}, u32[]{:S(2)}, u32[]{:S(2)}) collective-permute-start(bf16[512,512]{1,0:T(8,128)(2,1)} %maximum_add_fusion.1), channel_id=1, source_target_pairs={{0,1},{1,0},{2,3},{3,2},{4,5},{5,4},{6,7},{7,6},{8,9},{9,8},{10,11... | collective-permute-start | bytes 1572872 | tf_op jit(solution)/shard_map/ppermute | solution.py:15
  85.6 14.6 %collective-permute-start.14 = (bf16[512,512]{1,0:T(8,128)(2,1)S(1)}, bf16[512,512]{1,0:T(8,128)(2,1)S(1)}, u32[]{:S(2)}, u32[]{:S(2)}) collective-permute-start(bf16[512,512]{1,0:T(8,128)(2,1)S(1)} %get-tuple-element.37), channel_id=1, source_target_pairs={{0,16},{16,0},{1,17},{17,1},{2,18},{18,2},{3,19},{19,3},{4,20},{20... | collective-permute-start | bytes 1572872 | tf_op jit(solution)/shard_map/ppermute | solution.py:15
  100.3 7.1 %collective-permute-start.18 = (bf16[256,512]{1,0:T(8,128)(2,1)S(1)}, bf16[256,512]{1,0:T(8,128)(2,1)S(1)}, u32[]{:S(2)}, u32[]{:S(2)}) collective-permute-start(bf16[256,512]{1,0:T(8,128)(2,1)S(1)} %get-tuple-element.40), channel_id=1, source_target_pairs={{0,96},{32,0},{64,32},{96,64},{1,97},{33,1},{65,33},{97,65},{2,98}... | collective-permute-start | bytes 786440 | tf_op jit(solution)/shard_map/ppermute | solution.py:15
  103.2 7.7 %collective-permute-start.15 = (bf16[256,512]{1,0:T(8,128)(2,1)S(1)}, bf16[256,512]{1,0:T(8,128)(2,1)S(1)}, u32[]{:S(2)}, u32[]{:S(2)}) collective-permute-start(bf16[256,512]{1,0:T(8,128)(2,1)S(1)} %get-tuple-element.39), channel_id=1, source_target_pairs={{0,32},{32,64},{64,96},{96,0},{1,33},{33,65},{65,97},{97,1},{2,34}... | collective-permute-start | bytes 786440 | tf_op jit(solution)/shard_map/ppermute | solution.py:15
  103.2 13.0 %collective-permute-start.16 = (bf16[256,512]{1,0:T(8,128)(2,1)S(1)}, bf16[256,512]{1,0:T(8,128)(2,1)S(1)}, u32[]{:S(2)}, u32[]{:S(2)}) collective-permute-start(bf16[256,512]{1,0:T(8,128)(2,1)S(1)} %get-tuple-element.40), channel_id=1, source_target_pairs={{0,32},{32,64},{64,96},{96,0},{1,33},{33,65},{65,97},{97,1},{2,34}... | collective-permute-start | bytes 786440 | tf_op jit(solution)/shard_map/ppermute | solution.py:15
  103.2 14.8 %collective-permute-start.17 = (bf16[256,512]{1,0:T(8,128)(2,1)S(1)}, bf16[256,512]{1,0:T(8,128)(2,1)S(1)}, u32[]{:S(2)}, u32[]{:S(2)}) collective-permute-start(bf16[256,512]{1,0:T(8,128)(2,1)S(1)} %get-tuple-element.39), channel_id=1, source_target_pairs={{0,96},{32,0},{64,32},{96,64},{1,97},{33,1},{65,33},{97,65},{2,98}... | collective-permute-start | bytes 786440 | tf_op jit(solution)/shard_map/ppermute | solution.py:15
  107.4 11.2 %collective-permute-start.20 = (bf16[256,512]{1,0:T(8,128)(2,1)S(1)}, bf16[256,512]{1,0:T(8,128)(2,1)S(1)}, u32[]{:S(2)}, u32[]{:S(2)}) collective-permute-start(bf16[256,512]{1,0:T(8,128)(2,1)S(1)} %collective-permute-done.18), channel_id=1, source_target_pairs={{0,96},{32,0},{64,32},{96,64},{1,97},{33,1},{65,33},{97,65},{2,98}... | collective-permute-start | bytes 786440 | tf_op jit(solution)/shard_map/ppermute | solution.py:15
  110.8 11.0 %collective-permute-start.19 = (bf16[256,512]{1,0:T(8,128)(2,1)S(1)}, bf16[256,512]{1,0:T(8,128)(2,1)S(1)}, u32[]{:S(2)}, u32[]{:S(2)}) collective-permute-start(bf16[256,512]{1,0:T(8,128)(2,1)S(1)} %collective-permute-done.15), channel_id=1, source_target_pairs={{0,32},{32,64},{64,96},{96,0},{1,33},{33,65},{65,97},{97,1},{2,34}... | collective-permute-start | bytes 786440 | tf_op jit(solution)/shard_map/ppermute | solution.py:15
  110.8 2.7 %copy-start = (bf16[8192,256]{1,0:T(8,128)(2,1)S(1)}, bf16[8192,256]{1,0:T(8,128)(2,1)}, u32[]{:S(2)}) copy-start(bf16[8192,256]{1,0:T(8,128)(2,1)} %all-gather.6.cloned.1.call-done) | copy-start | bytes 12582916
  122.4 24.3 %copy-start.4 = (bf16[32,8192]{1,0:T(8,128)(2,1)S(1)}, bf16[32,8192]{1,0:T(8,128)(2,1)}, u32[]{:S(2)}) copy-start(bf16[32,8192]{1,0:T(8,128)(2,1)} %param.9) | copy-start | bytes 1572868
Sparse Core Ops, SparseCore 0:
  12.2 50.4 all-gather.3
  73.2 35.3 all-gather.5

commit v7 on v6

--- a/solution.py
+++ b/solution.py
@@ -15,15 +15,20 @@
     return lax.ppermute(v, axis, [(i, (i + by) % n) for i in range(n)])
 
 
-def turn(v, flip=True):
+def turn(v):
     pairs = []
     for xh in range(2):
         for xl in range(2):
             for z in range(4):
-                new_xl = 1 - xl if flip or z & 1 != xh else xl
-                to = ((z & 1) * 2 + new_xl) * 4 + (z & ~1) + xh
+                to = ((z & 1) * 2 + 1 - xl) * 4 + (z & ~1) + xh
                 pairs.append(((xh * 2 + xl) * 4 + z, to))
     return lax.ppermute(v, ("xh", "xl", "z"), pairs)
+
+
+def part_ways(v, where, to):
+    every = [(xh, xl, z) for xh in range(2) for xl in range(2) for z in range(4)]
+    pairs = [(p, to(*p)) for p in every if where(*p)]
+    return lax.ppermute(v, ("xh", "xl", "z"), [tuple((q[0] * 2 + q[1]) * 4 + q[2] for q in pair) for pair in pairs])
 
 
 def after(v, *done):
@@ -109,10 +114,13 @@
     pair = jnp.concatenate([mine, shift(other, "core", 1)], axis=1)
     factor = lax.all_gather(pair, "y", axis=0, tiled=True)
 
-    b = turn(change)
-    bm, bp, a = together(shift(b, "z", 1), shift(b, "z", -1), shift(b, "xl", 1))
+    moves = part_ways(output_factor, lambda xh, xl, z: z & 1 != xh, lambda xh, xl, z: (xh, xl, (z + 2 * (z & 1) - 1) & 3))
+    b, moves = together(turn(change), moves)
+    moves = part_ways(moves, lambda xh, xl, z: z & 1 == xh, lambda xh, xl, z: (1 - xh, 1 - xl, z))
+    bm, bp, a, moves = together(shift(b, "z", 1), shift(b, "z", -1), shift(b, "xl", 1), moves)
     am, ap, b2 = together(shift(bm, "xl", 1), shift(a, "z", -1), shift(bm, "z", 1))
-    turned = turn(after(output_factor, bm, bp, a), flip=False)
+    same = (z & 1) == xh
+    turned = jnp.where(same, output_factor, moves)
     far = [shift(am[:half], "z", 1), shift(ap[half:], "z", -1)]
     *far, part = together(*far, shift(after(turned, factor), "xl", 1))
 
@@ -131,7 +139,6 @@
 
     theirs = [after(theirs, more(1)), more(1).astype(BF16)]
     odd, even = [v + shift(w, "core", 1).astype(F32) for v, w in zip((own, more(0)), theirs)]
-    same = (z & 1) == xh
     send, keep = jnp.where(same, odd, even).astype(BF16), jnp.where(same, even, odd)
     send = shift(send, "xh", 1)
 
@@ -141,8 +148,8 @@
     beyond = [shift(below[0], "y", 1), shift(above[1], "y", -1)]
 
     def share(blocks, dy, to):
-        at = (y + dy) & 3
-        here = 1 - ((at >> 1) ^ xl ^ to ^ xh)
+        at = ((y + dy) & 3) ^ (3 * (to ^ xh))
+        here = 1 - ((at >> 1) ^ xl)
         corners = [(4 * h + (at & 1) * 2 + to, here * rows, 0) for h in range(2)]
         sides = [lax.dynamic_slice(left, c, (1, rows, half))[0] for c in corners]
         return dot(sides[0], blocks[0]) + dot(sides[1], blocks[1])

time: 155 us -> 150 us (0.968)
  waiting for transfers between devices: 56.5 us -> 53.6 us
  other arithmetic: 6.37 us -> 4.19 us
    ppermute x0 -> x2, waiting for transfers between devices: none -> 14.7 us  [part_ways(): lax.ppermute(v, ('xh', 'xl', 'z'), [tuple(((q[0] * 2 + q[1]) * 4 + q[2] f...]
    ppermute x2 -> x1, waiting for transfers between devices: 11.8 us -> 0.01 us  [turn(): return lax.ppermute(v, ('xh', 'xl', 'z'), pairs)]
    ppermute x19, waiting for transfers between devices: 44.6 us -> 37.1 us  [shift(): return lax.ppermute(v, axis, [(i, (i + by) % n) for i in range(n)])]
    ppermute x0 -> x2, starting transfers between devices: none -> 4.58 us  [part_ways(): lax.ppermute(v, ('xh', 'xl', 'z'), [tuple(((q[0] * 2 + q[1]) * 4 + q[2] f...]
    ppermute x19, starting transfers between devices: 28.5 us -> 26.3 us  [shift(): return lax.ppermute(v, axis, [(i, (i + by) % n) for i in range(n)])]
    all_gather x1, waiting for transfers between devices: 0.01 us -> 1.7 us  [body(): factor = lax.all_gather(pair, 'y', axis=0, tiled=True)]
    ppermute x2 -> x1, starting transfers between devices: 2.98 us -> 1.37 us  [turn(): return lax.ppermute(v, ('xh', 'xl', 'z'), pairs)]
    all_to_all x1, blocking collectives: 23.8 us -> 22.3 us  [body(): lax.all_to_all(penalty, ('xh',) + COL, split_axis=0, concat_axis=0, tiled...]
  transfers between devices with their start and end apart: 23 -> 24, of which waited for: 11 -> 12; matrix products, arithmetic and copies ran while one was open for 10% -> 9% of each run, Pallas kernels for 5% -> 5%
where the time goes in v7:
time: 150 us
  waiting for transfers between devices  53.6 us (36%)
  starting transfers between devices  32.3 us (22%)
  blocking collectives  22.3 us (15%)
  between operations  13.8 us (9%)
  matrix products  12.3 us (8%)
  Pallas kernels  8.19 us (5%)
  other arithmetic  4.19 us (3%)
  local copies, waits for them, and re-layouts  2.99 us (2%)
    ppermute x19, waiting for transfers between devices, shift(): return lax.ppermute(v, axis, [(i, (i + by) % n) for i in range(n)])  37.1 us
    ppermute x19, starting transfers between devices, shift(): return lax.ppermute(v, axis, [(i, (i + by) % n) for i in range(n)])  26.3 us
    all_to_all x1, blocking collectives, body(): lax.all_to_all(penalty, ('xh',) + COL, split_axis=0, concat_axis=0, tiled...  22.3 us
    ppermute x2, waiting for transfers between devices, part_ways(): lax.ppermute(v, ('xh', 'xl', 'z'), [tuple(((q[0] * 2 + q[1]) * 4 + q[2] f...  14.7 us
    dot_general x20, matrix products, dot(): lax.dot_general(a, b, (((a.ndim - 1,), (0,)), ((), ())), preferred_elemen...  12.3 us
    pallas_call x1, Pallas kernels, early(): pl.pallas_call(lambda *refs: early_kernel(n, m, *refs), out_shape=(jax.Sh...  8.19 us
    ppermute x2, starting transfers between devices, part_ways(): lax.ppermute(v, ('xh', 'xl', 'z'), [tuple(((q[0] * 2 + q[1]) * 4 + q[2] f...  4.58 us
  transfers between devices with their start and end apart: 24, of which 12 were waited for; matrix products, arithmetic and copies ran while one was open for 9% of the time, Pallas kernels for 5%

profile of v7, /device:TPU:1, one launch (start us, length us, event | category | flops | bytes accessed | tf_op | source)
XLA Modules:
  0.0 149.6 jit_solution(7039137483824733116)
XLA Ops:
  6.5 1.4 constant_dynamic-slice_fusion.1
  7.9 1.5 %collective-permute-start.11 = (bf16[512,512]{1,0:T(8,128)(2,1)S(1)}, bf16[512,512]{1,0:T(8,128)(2,1)S(1)}, u32[]{:S(2)}, u32[]{:S(2)}) collective-permute-start(bf16[512,512]{1,0:T(8,128)(2,1)S(1)} %get-tuple-element.46), channel_id=1, source_target_pairs={{0,1},{1,0},{2,3},{3,2},{4,5},{5,4},{6,7},{7,6},{8,9},{9,8},{10,11... | collective-permute-start | bytes 1572872 | tf_op jit(solution)/shard_map/ppermute | solution.py:15
  9.4 1.5 %collective-permute-done.11 = bf16[512,512]{1,0:T(8,128)(2,1)S(1)} collective-permute-done((bf16[512,512]{1,0:T(8,128)(2,1)S(1)}, bf16[512,512]{1,0:T(8,128)(2,1)S(1)}, u32[]{:S(2)}, u32[]{:S(2)}) %collective-permute-start.11) | collective-permute-done | bytes 524320 | tf_op jit(solution)/shard_map/ppermute | solution.py:15
  11.0 1.1 pad_maximum_fusion
  12.2 0.1 subtract_convert_fusion
  12.3 1.4 collective-permute-start
  13.7 1.3 collective-permute-start.1
  15.0 10.9 %collective-permute-done.1 = bf16[512,256]{1,0:T(8,128)(2,1)S(1)} collective-permute-done((bf16[512,256]{1,0:T(8,128)(2,1)S(1)}, bf16[512,256]{1,0:T(8,128)(2,1)S(1)}, u32[]{:S(2)}, u32[]{:S(2)}) %collective-permute-start.1) | collective-permute-done | bytes 262176 | tf_op jit(solution)/shard_map/ppermute | solution.py:31
  25.9 3.5 %collective-permute-start.2 = (bf16[512,512]{1,0:T(8,128)(2,1)S(1)}, bf16[512,512]{1,0:T(8,128)(2,1)S(1)}, u32[]{:S(2)}, u32[]{:S(2)}) collective-permute-start(bf16[512,512]{1,0:T(8,128)(2,1)S(1)} %collective-permute-done.refs_6_), channel_id=1, source_target_pairs={{0,2},{2,4},{4,6},{6,0},{1,3},{3,5},{5,7},{7,1},{8,10},{10,12},{12... | collective-permute-start | bytes 1572872 | tf_op jit(solution)/shard_map/ppermute | solution.py:15
  29.4 2.1 %collective-permute-start.3 = (bf16[512,512]{1,0:T(8,128)(2,1)S(1)}, bf16[512,512]{1,0:T(8,128)(2,1)S(1)}, u32[]{:S(2)}, u32[]{:S(2)}) collective-permute-start(bf16[512,512]{1,0:T(8,128)(2,1)S(1)} %collective-permute-done.refs_6_), channel_id=1, source_target_pairs={{0,6},{2,0},{4,2},{6,4},{1,7},{3,1},{5,3},{7,5},{8,14},{10,8},{12,... | collective-permute-start | bytes 1572872 | tf_op jit(solution)/shard_map/ppermute | solution.py:15
  31.5 3.3 %collective-permute-start.5 = (bf16[512,256]{1,0:T(8,128)(2,1)S(1)}, bf16[512,256]{1,0:T(8,128)(2,1)S(1)}, u32[]{:S(2)}, u32[]{:S(2)}) collective-permute-start(bf16[512,256]{1,0:T(8,128)(2,1)S(1)} %collective-permute-done.1), channel_id=1, source_target_pairs={{0,24},{4,28},{8,16},{12,20},{18,10},{22,14},{26,2},{30,6},{1,25},... | collective-permute-start | bytes 786440 | tf_op jit(solution)/shard_map/ppermute | solution.py:31
  34.8 3.8 %collective-permute-done.5 = bf16[512,256]{1,0:T(8,128)(2,1)S(1)} collective-permute-done((bf16[512,256]{1,0:T(8,128)(2,1)S(1)}, bf16[512,256]{1,0:T(8,128)(2,1)S(1)}, u32[]{:S(2)}, u32[]{:S(2)}) %collective-permute-start.5) | collective-permute-done | bytes 262176 | tf_op jit(solution)/shard_map/ppermute | solution.py:31
  38.6 4.0 %collective-permute-done.2.refs_3_ = bf16[512,512]{1,0:T(8,128)(2,1)S(1)} collective-permute-done((bf16[512,512]{1,0:T(8,128)(2,1)S(1)}, bf16[512,512]{1,0:T(8,128)(2,1)S(1)}, u32[]{:S(2)}, u32[]{:S(2)}) %collective-permute-start.2) | collective-permute-done | bytes 524320 | tf_op jit(solution)/shard_map/ppermute | solution.py:15
  42.6 0.8 copy-done.11
  43.5 2.4 %collective-permute-start.7 = (bf16[512,512]{1,0:T(8,128)(2,1)S(1)}, bf16[512,512]{1,0:T(8,128)(2,1)S(1)}, u32[]{:S(2)}, u32[]{:S(2)}) collective-permute-start(bf16[512,512]{1,0:T(8,128)(2,1)S(1)} %collective-permute-done.4.refs_5_), channel_id=1, source_target_pairs={{0,6},{2,0},{4,2},{6,4},{1,7},{3,1},{5,3},{7,5},{8,14},{10,8},{12,... | collective-permute-start | bytes 1572872 | tf_op jit(solution)/shard_map/ppermute | solution.py:15
  45.9 0.6 stack.43.refs_0_
  46.6 8.2 %collective-permute-done.6.refs_1_ = bf16[512,512]{1,0:T(8,128)(2,1)S(1)} collective-permute-done((bf16[512,512]{1,0:T(8,128)(2,1)S(1)}, bf16[512,512]{1,0:T(8,128)(2,1)S(1)}, u32[]{:S(2)}, u32[]{:S(2)}) %collective-permute-start.6) | collective-permute-done | bytes 524320 | tf_op jit(solution)/shard_map/ppermute | solution.py:15
  54.8 0.1 collective-permute-done.7.refs_2_
  54.9 3.2 %collective-permute-done.8.refs_7_ = bf16[512,512]{1,0:T(8,128)(2,1)} collective-permute-done((bf16[512,512]{1,0:T(8,128)(2,1)S(1)}, bf16[512,512]{1,0:T(8,128)(2,1)}, u32[]{:S(2)}, u32[]{:S(2)}) %collective-permute-start.8) | collective-permute-done | bytes 524320 | tf_op jit(solution)/shard_map/ppermute | solution.py:15
  58.2 0.1 collective-permute-start.9
  58.3 2.7 %collective-permute-start.10 = (bf16[256,512]{1,0:T(8,128)(2,1)S(1)}, bf16[256,512]{1,0:T(8,128)(2,1)S(1)}, u32[]{:S(2)}, u32[]{:S(2)}) collective-permute-start(bf16[256,512]{1,0:T(8,128)(2,1)S(1)} %slice.26), channel_id=1, source_target_pairs={{0,6},{2,0},{4,2},{6,4},{1,7},{3,1},{5,3},{7,5},{8,14},{10,8},{12,... | collective-permute-start | bytes 786440 | tf_op jit(solution)/shard_map/ppermute | solution.py:15
  61.0 1.7 %all-gather.4.cloned.1.call-done.refs_8_ = bf16[2048,1024]{1,0:T(8,128)(2,1)} async-done(((bf16[512,1024]{1,0:T(8,128)(2,1)}), bf16[2048,1024]{1,0:T(8,128)(2,1)}) %all-gather.4.cloned.1.call-update) | async-done | bytes 4194320 | tf_op jit(solution)/shard_map/all_gather | solution.py:115
  62.7 1.2 collective-permute-start.12
  63.9 8.2 %shard_map.55 = (bf16[512,512]{1,0:T(8,128)(2,1)}, f32[512,512]{1,0:T(8,128)}, f32[512,1024]{1,0:T(8,128)}) custom-call(s32[7]{0:T(128)} %stack.43.refs_0_, bf16[512,512]{1,0:T(8,128)(2,1)} %copy-done.7, bf16[512,512]{1,0:T(8,128)(2,1)} %copy-done.8, bf16[512,512]{1,0:T(8,128)(2,1)} %copy-done.10, bf16[512,512]{1,0:T(8,128)(2,1)} %copy-done.11, ...), custom_call_target="tpu_custom_call" | custom-call | flops 3758096384 | bytes 12582912 | tf_op jit(solution)/shard_map/pallas_call | solution.py:83
  72.2 0.8 pad_maximum_fusion.2
  73.0 1.4 fusion.14
  74.5 1.3 fusion.16
  75.8 0.3 maximum_add_fusion.1
  76.1 2.9 %collective-permute-start.14 = (bf16[512,512]{1,0:T(8,128)(2,1)S(1)}, bf16[512,512]{1,0:T(8,128)(2,1)S(1)}, u32[]{:S(2)}, u32[]{:S(2)}) collective-permute-start(bf16[512,512]{1,0:T(8,128)(2,1)S(1)} %copy-done.13), channel_id=1, source_target_pairs={{0,1},{1,0},{2,3},{3,2},{4,5},{5,4},{6,7},{7,6},{8,9},{9,8},{10,11... | collective-permute-start | bytes 1572872 | tf_op jit(solution)/shard_map/ppermute | solution.py:15
  79.0 0.1 collective-permute-start.13
  79.0 1.3 fusion.18
  80.4 1.3 fusion.20
  81.8 0.5 select_convert_fusion
  82.2 1.0 collective-permute-start.15
  83.2 13.7 %collective-permute-done.15 = bf16[512,512]{1,0:T(8,128)(2,1)S(1)} collective-permute-done((bf16[512,512]{1,0:T(8,128)(2,1)S(1)}, bf16[512,512]{1,0:T(8,128)(2,1)S(1)}, u32[]{:S(2)}, u32[]{:S(2)}) %collective-permute-start.15) | collective-permute-done | bytes 524320 | tf_op jit(solution)/shard_map/ppermute | solution.py:15
  96.9 0.2 fusion.13
  97.1 2.8 %collective-permute-start.19 = (bf16[256,512]{1,0:T(8,128)(2,1)S(1)}, bf16[256,512]{1,0:T(8,128)(2,1)S(1)}, u32[]{:S(2)}, u32[]{:S(2)}) collective-permute-start(bf16[256,512]{1,0:T(8,128)(2,1)S(1)} %get-tuple-element.44), channel_id=1, source_target_pairs={{0,96},{32,0},{64,32},{96,64},{1,97},{33,1},{65,33},{97,65},{2,98}... | collective-permute-start | bytes 786440 | tf_op jit(solution)/shard_map/ppermute | solution.py:15
  99.9 2.7 %collective-permute-start.18 = (bf16[256,512]{1,0:T(8,128)(2,1)S(1)}, bf16[256,512]{1,0:T(8,128)(2,1)S(1)}, u32[]{:S(2)}, u32[]{:S(2)}) collective-permute-start(bf16[256,512]{1,0:T(8,128)(2,1)S(1)} %get-tuple-element.43), channel_id=1, source_target_pairs={{0,96},{32,0},{64,32},{96,64},{1,97},{33,1},{65,33},{97,65},{2,98}... | collective-permute-start | bytes 786440 | tf_op jit(solution)/shard_map/ppermute | solution.py:15
  102.6 1.6 %collective-permute-done.19 = bf16[256,512]{1,0:T(8,128)(2,1)S(1)} collective-permute-done((bf16[256,512]{1,0:T(8,128)(2,1)S(1)}, bf16[256,512]{1,0:T(8,128)(2,1)S(1)}, u32[]{:S(2)}, u32[]{:S(2)}) %collective-permute-start.19) | collective-permute-done | bytes 262176 | tf_op jit(solution)/shard_map/ppermute | solution.py:15
  104.2 3.4 %collective-permute-start.21 = (bf16[256,512]{1,0:T(8,128)(2,1)S(1)}, bf16[256,512]{1,0:T(8,128)(2,1)S(1)}, u32[]{:S(2)}, u32[]{:S(2)}) collective-permute-start(bf16[256,512]{1,0:T(8,128)(2,1)S(1)} %collective-permute-done.19), channel_id=1, source_target_pairs={{0,96},{32,0},{64,32},{96,64},{1,97},{33,1},{65,33},{97,65},{2,98}... | collective-permute-start | bytes 786440 | tf_op jit(solution)/shard_map/ppermute | solution.py:15
  107.7 1.4 fusion.31
  109.1 1.2 convolution_add_fusion.3
  110.3 0.3 fusion.43
  110.6 0.3 convolution_add_fusion.7
  110.9 2.0 %collective-permute-done.17 = bf16[256,512]{1,0:T(8,128)(2,1)S(1)} collective-permute-done((bf16[256,512]{1,0:T(8,128)(2,1)S(1)}, bf16[256,512]{1,0:T(8,128)(2,1)S(1)}, u32[]{:S(2)}, u32[]{:S(2)}) %collective-permute-start.17) | collective-permute-done | bytes 262176 | tf_op jit(solution)/shard_map/ppermute | solution.py:15
  113.0 0.3 fusion.28
  113.3 0.3 fusion.40
  113.6 0.3 fusion.2
  113.9 0.3 fusion.5
  114.2 0.3 fusion.25
  114.5 0.3 fusion.37
  114.8 0.3 fusion.1
  115.1 0.3 fusion.4
  115.4 0.0 collective-permute-done.21
  115.5 0.3 fusion.22
  115.8 0.3 fusion.34
  116.1 2.5 %collective-permute-done.20 = bf16[256,512]{1,0:T(8,128)(2,1)S(1)} collective-permute-done((bf16[256,512]{1,0:T(8,128)(2,1)S(1)}, bf16[256,512]{1,0:T(8,128)(2,1)S(1)}, u32[]{:S(2)}, u32[]{:S(2)}) %collective-permute-start.20) | collective-permute-done | bytes 262176 | tf_op jit(solution)/shard_map/ppermute | solution.py:15
  118.6 0.3 fusion.8
  118.9 0.3 fusion.9
  119.2 0.1 pad_maximum_fusion.1
  119.3 22.3 %all_to_all.6 = bf16[32,32,512]{2,1,0:T(8,128)(2,1)S(1)} all-to-all(bf16[32,32,512]{2,1,0:T(8,128)(2,1)S(1)} %bitcast.86), channel_id=1, replica_groups=mesh['y'=4,'xh'=2,'xl'=2,'z'=4,'core'=2] {'xh','xl','z','core'}, dimensions={0} | all-to-all | bytes 2097152 | tf_op jit(solution)/shard_map/all_to_all | solution.py:163
  141.6 0.2 convert_reduce_fusion
  141.8 0.1 copy.7
  141.9 0.9 add_convert_fusion
  (51 shorter events, 0.3 us)
Async XLA Ops:
  6.5 5.6 %copy-start.3 = (bf16[512,512]{1,0:T(8,128)(2,1)S(1)}, bf16[512,512]{1,0:T(8,128)(2,1)}, u32[]{:S(2)}) copy-start(bf16[512,512]{1,0:T(8,128)(2,1)} %param.6) | copy-start | bytes 1572868
  6.5 5.6 %copy-start.4 = (bf16[512,512]{1,0:T(8,128)(2,1)S(1)}, bf16[512,512]{1,0:T(8,128)(2,1)}, u32[]{:S(2)}) copy-start(bf16[512,512]{1,0:T(8,128)(2,1)} %param.5) | copy-start | bytes 1572868
  6.5 7.2 %copy-start.6 = (bf16[512,256]{1,0:T(8,128)(2,1)S(1)}, bf16[512,256]{1,0:T(8,128)(2,1)}, u32[]{:S(2)}) copy-start(bf16[512,256]{1,0:T(8,128)(2,1)} %param.8) | copy-start | bytes 786436
  6.5 56.2 %all-gather.4.cloned.1.call-start = ((), (), s32[]{:S(2)}) async-start(), calls=%async_computation.1 | async-start | bytes 5242880 | tf_op jit(solution)/shard_map/all_gather | solution.py:115
  7.9 3.0 %collective-permute-start.11 = (bf16[512,512]{1,0:T(8,128)(2,1)S(1)}, bf16[512,512]{1,0:T(8,128)(2,1)S(1)}, u32[]{:S(2)}, u32[]{:S(2)}) collective-permute-start(bf16[512,512]{1,0:T(8,128)(2,1)S(1)} %get-tuple-element.46), channel_id=1, source_target_pairs={{0,1},{1,0},{2,3},{3,2},{4,5},{5,4},{6,7},{7,6},{8,9},{9,8},{10,11... | collective-permute-start | bytes 1572872 | tf_op jit(solution)/shard_map/ppermute | solution.py:15
  12.1 95.6 %all-gather.6.cloned.1.call-start = ((), (), s32[]{:S(2)}) async-start(), calls=%async_computation.2 | async-start | bytes 4718592 | tf_op jit(solution)/shard_map/all_gather | solution.py:133
  12.3 13.6 %collective-permute-start = (bf16[512,512]{1,0:T(8,128)(2,1)S(1)}, bf16[512,512]{1,0:T(8,128)(2,1)S(1)}, u32[]{:S(2)}, u32[]{:S(2)}) collective-permute-start(bf16[512,512]{1,0:T(8,128)(2,1)S(1)} %subtract_convert_fusion), channel_id=1, source_target_pairs={{0,8},{2,24},{4,12},{6,28},{8,0},{10,16},{12,4},{14,20},{16,10},{1... | collective-permute-start | bytes 1572872 | tf_op jit(solution)/shard_map/ppermute | solution.py:25
  13.7 12.2 %collective-permute-start.1 = (bf16[512,256]{1,0:T(8,128)(2,1)S(1)}, bf16[512,256]{1,0:T(8,128)(2,1)S(1)}, u32[]{:S(2)}, u32[]{:S(2)}) collective-permute-start(bf16[512,256]{1,0:T(8,128)(2,1)S(1)} %copy-done.6), channel_id=1, source_target_pairs={{2,4},{6,0},{10,12},{14,8},{16,22},{20,18},{24,30},{28,26},{3,5},{... | collective-permute-start | bytes 786440 | tf_op jit(solution)/shard_map/ppermute | solution.py:31
  25.9 38.0 %copy-start.9 = (bf16[512,512]{1,0:T(8,128)(2,1)}, bf16[512,512]{1,0:T(8,128)(2,1)S(1)}, u32[]{:S(2)}) copy-start(bf16[512,512]{1,0:T(8,128)(2,1)S(1)} %collective-permute-done.refs_6_) | copy-start | bytes 1572868
  25.9 16.8 %collective-permute-start.2 = (bf16[512,512]{1,0:T(8,128)(2,1)S(1)}, bf16[512,512]{1,0:T(8,128)(2,1)S(1)}, u32[]{:S(2)}, u32[]{:S(2)}) collective-permute-start(bf16[512,512]{1,0:T(8,128)(2,1)S(1)} %collective-permute-done.refs_6_), channel_id=1, source_target_pairs={{0,2},{2,4},{4,6},{6,0},{1,3},{3,5},{5,7},{7,1},{8,10},{10,12},{12... | collective-permute-start | bytes 1572872 | tf_op jit(solution)/shard_map/ppermute | solution.py:15
  29.4 13.3 %collective-permute-start.3 = (bf16[512,512]{1,0:T(8,128)(2,1)S(1)}, bf16[512,512]{1,0:T(8,128)(2,1)S(1)}, u32[]{:S(2)}, u32[]{:S(2)}) collective-permute-start(bf16[512,512]{1,0:T(8,128)(2,1)S(1)} %collective-permute-done.refs_6_), channel_id=1, source_target_pairs={{0,6},{2,0},{4,2},{6,4},{1,7},{3,1},{5,3},{7,5},{8,14},{10,8},{12,... | collective-permute-start | bytes 1572872 | tf_op jit(solution)/shard_map/ppermute | solution.py:15
  31.5 12.0 %collective-permute-start.4 = (bf16[512,512]{1,0:T(8,128)(2,1)S(1)}, bf16[512,512]{1,0:T(8,128)(2,1)S(1)}, u32[]{:S(2)}, u32[]{:S(2)}) collective-permute-start(bf16[512,512]{1,0:T(8,128)(2,1)S(1)} %collective-permute-done.refs_6_), channel_id=1, source_target_pairs={{0,8},{8,0},{1,9},{9,1},{2,10},{10,2},{3,11},{11,3},{4,12},{12,4},... | collective-permute-start | bytes 1572872 | tf_op jit(solution)/shard_map/ppermute | solution.py:15
  31.5 7.1 %collective-permute-start.5 = (bf16[512,256]{1,0:T(8,128)(2,1)S(1)}, bf16[512,256]{1,0:T(8,128)(2,1)S(1)}, u32[]{:S(2)}, u32[]{:S(2)}) collective-permute-start(bf16[512,256]{1,0:T(8,128)(2,1)S(1)} %collective-permute-done.1), channel_id=1, source_target_pairs={{0,24},{4,28},{8,16},{12,20},{18,10},{22,14},{26,2},{30,6},{1,25},... | collective-permute-start | bytes 786440 | tf_op jit(solution)/shard_map/ppermute | solution.py:31
  42.6 15.6 %copy-start.10 = (bf16[512,512]{1,0:T(8,128)(2,1)}, bf16[512,512]{1,0:T(8,128)(2,1)S(1)}, u32[]{:S(2)}) copy-start(bf16[512,512]{1,0:T(8,128)(2,1)S(1)} %collective-permute-done.2.refs_3_) | copy-start | bytes 1572868
  42.6 0.8 copy-start.11
  43.5 11.4 %copy-start.12 = (bf16[512,512]{1,0:T(8,128)(2,1)}, bf16[512,512]{1,0:T(8,128)(2,1)S(1)}, u32[]{:S(2)}) copy-start(bf16[512,512]{1,0:T(8,128)(2,1)S(1)} %collective-permute-done.4.refs_5_) | copy-start | bytes 1572868
  43.5 11.2 %collective-permute-start.6 = (bf16[512,512]{1,0:T(8,128)(2,1)S(1)}, bf16[512,512]{1,0:T(8,128)(2,1)S(1)}, u32[]{:S(2)}, u32[]{:S(2)}) collective-permute-start(bf16[512,512]{1,0:T(8,128)(2,1)S(1)} %collective-permute-done.2.refs_3_), channel_id=1, source_target_pairs={{0,8},{8,0},{1,9},{9,1},{2,10},{10,2},{3,11},{11,3},{4,12},{12,4},... | collective-permute-start | bytes 1572872 | tf_op jit(solution)/shard_map/ppermute | solution.py:15
  43.5 11.4 %collective-permute-start.7 = (bf16[512,512]{1,0:T(8,128)(2,1)S(1)}, bf16[512,512]{1,0:T(8,128)(2,1)S(1)}, u32[]{:S(2)}, u32[]{:S(2)}) collective-permute-start(bf16[512,512]{1,0:T(8,128)(2,1)S(1)} %collective-permute-done.4.refs_5_), channel_id=1, source_target_pairs={{0,6},{2,0},{4,2},{6,4},{1,7},{3,1},{5,3},{7,5},{8,14},{10,8},{12,... | collective-permute-start | bytes 1572872 | tf_op jit(solution)/shard_map/ppermute | solution.py:15
  45.9 12.2 %collective-permute-start.8 = (bf16[512,512]{1,0:T(8,128)(2,1)S(1)}, bf16[512,512]{1,0:T(8,128)(2,1)}, u32[]{:S(2)}, u32[]{:S(2)}) collective-permute-start(bf16[512,512]{1,0:T(8,128)(2,1)S(1)} %collective-permute-done.2.refs_3_), channel_id=1, source_target_pairs={{0,2},{2,4},{4,6},{6,0},{1,3},{3,5},{5,7},{7,1},{8,10},{10,12},{12... | collective-permute-start | bytes 1572872 | tf_op jit(solution)/shard_map/ppermute | solution.py:15
  54.8 9.1 %copy-start.7 = (bf16[512,512]{1,0:T(8,128)(2,1)}, bf16[512,512]{1,0:T(8,128)(2,1)S(1)}, u32[]{:S(2)}) copy-start(bf16[512,512]{1,0:T(8,128)(2,1)S(1)} %collective-permute-done.6.refs_1_) | copy-start | bytes 1572868
  54.9 9.0 %copy-start.8 = (bf16[512,512]{1,0:T(8,128)(2,1)}, bf16[512,512]{1,0:T(8,128)(2,1)S(1)}, u32[]{:S(2)}) copy-start(bf16[512,512]{1,0:T(8,128)(2,1)S(1)} %collective-permute-done.7.refs_2_) | copy-start | bytes 1572868
  58.2 13.9 %collective-permute-start.9 = (bf16[256,512]{1,0:T(8,128)(2,1)S(1)}, bf16[256,512]{1,0:T(8,128)(2,1)S(1)}, u32[]{:S(2)}, u32[]{:S(2)}) collective-permute-start(bf16[256,512]{1,0:T(8,128)(2,1)S(1)} %slice.25), channel_id=1, source_target_pairs={{0,2},{2,4},{4,6},{6,0},{1,3},{3,5},{5,7},{7,1},{8,10},{10,12},{12... | collective-permute-start | bytes 786440 | tf_op jit(solution)/shard_map/ppermute | solution.py:15
  58.3 13.8 %collective-permute-start.10 = (bf16[256,512]{1,0:T(8,128)(2,1)S(1)}, bf16[256,512]{1,0:T(8,128)(2,1)S(1)}, u32[]{:S(2)}, u32[]{:S(2)}) collective-permute-start(bf16[256,512]{1,0:T(8,128)(2,1)S(1)} %slice.26), channel_id=1, source_target_pairs={{0,6},{2,0},{4,2},{6,4},{1,7},{3,1},{5,3},{7,5},{8,14},{10,8},{12,... | collective-permute-start | bytes 786440 | tf_op jit(solution)/shard_map/ppermute | solution.py:15
  62.7 9.4 %collective-permute-start.12 = (bf16[512,256]{1,0:T(8,128)(2,1)S(1)}, bf16[512,256]{1,0:T(8,128)(2,1)S(1)}, u32[]{:S(2)}, u32[]{:S(2)}) collective-permute-start(bf16[512,256]{1,0:T(8,128)(2,1)S(1)} %broadcast_select_fusion), channel_id=1, source_target_pairs={{0,8},{8,0},{1,9},{9,1},{2,10},{10,2},{3,11},{11,3},{4,12},{12,4},... | collective-permute-start | bytes 786440 | tf_op jit(solution)/shard_map/ppermute | solution.py:15
  72.1 3.7 %copy-start.1 = (f32[512,1024]{1,0:T(8,128)S(1)}, f32[512,1024]{1,0:T(8,128)}, u32[]{:S(2)}) copy-start(f32[512,1024]{1,0:T(8,128)} %get-tuple-element.36) | copy-start | bytes 6291460
  72.1 4.0 %copy-start.13 = (bf16[512,512]{1,0:T(8,128)(2,1)S(1)}, bf16[512,512]{1,0:T(8,128)(2,1)}, u32[]{:S(2)}) copy-start(bf16[512,512]{1,0:T(8,128)(2,1)} %get-tuple-element.40) | copy-start | bytes 1572868
  73.0 8.7 %copy-start.2 = (f32[512,512]{1,0:T(8,128)S(1)}, f32[512,512]{1,0:T(8,128)}, u32[]{:S(2)}) copy-start(f32[512,512]{1,0:T(8,128)} %get-tuple-element.34) | copy-start | bytes 3145732
  76.1 5.6 %collective-permute-start.14 = (bf16[512,512]{1,0:T(8,128)(2,1)S(1)}, bf16[512,512]{1,0:T(8,128)(2,1)S(1)}, u32[]{:S(2)}, u32[]{:S(2)}) collective-permute-start(bf16[512,512]{1,0:T(8,128)(2,1)S(1)} %copy-done.13), channel_id=1, source_target_pairs={{0,1},{1,0},{2,3},{3,2},{4,5},{5,4},{6,7},{7,6},{8,9},{9,8},{10,11... | collective-permute-start | bytes 1572872 | tf_op jit(solution)/shard_map/ppermute | solution.py:15
  79.0 2.8 %collective-permute-start.13 = (bf16[512,512]{1,0:T(8,128)(2,1)S(1)}, bf16[512,512]{1,0:T(8,128)(2,1)S(1)}, u32[]{:S(2)}, u32[]{:S(2)}) collective-permute-start(bf16[512,512]{1,0:T(8,128)(2,1)S(1)} %maximum_add_fusion.1), channel_id=1, source_target_pairs={{0,1},{1,0},{2,3},{3,2},{4,5},{5,4},{6,7},{7,6},{8,9},{9,8},{10,11... | collective-permute-start | bytes 1572872 | tf_op jit(solution)/shard_map/ppermute | solution.py:15
  82.2 14.7 %collective-permute-start.15 = (bf16[512,512]{1,0:T(8,128)(2,1)S(1)}, bf16[512,512]{1,0:T(8,128)(2,1)S(1)}, u32[]{:S(2)}, u32[]{:S(2)}) collective-permute-start(bf16[512,512]{1,0:T(8,128)(2,1)S(1)} %get-tuple-element.41), channel_id=1, source_target_pairs={{0,16},{16,0},{1,17},{17,1},{2,18},{18,2},{3,19},{19,3},{4,20},{20... | collective-permute-start | bytes 1572872 | tf_op jit(solution)/shard_map/ppermute | solution.py:15
  97.1 7.2 %collective-permute-start.19 = (bf16[256,512]{1,0:T(8,128)(2,1)S(1)}, bf16[256,512]{1,0:T(8,128)(2,1)S(1)}, u32[]{:S(2)}, u32[]{:S(2)}) collective-permute-start(bf16[256,512]{1,0:T(8,128)(2,1)S(1)} %get-tuple-element.44), channel_id=1, source_target_pairs={{0,96},{32,0},{64,32},{96,64},{1,97},{33,1},{65,33},{97,65},{2,98}... | collective-permute-start | bytes 786440 | tf_op jit(solution)/shard_map/ppermute | solution.py:15
  99.9 7.8 %collective-permute-start.16 = (bf16[256,512]{1,0:T(8,128)(2,1)S(1)}, bf16[256,512]{1,0:T(8,128)(2,1)S(1)}, u32[]{:S(2)}, u32[]{:S(2)}) collective-permute-start(bf16[256,512]{1,0:T(8,128)(2,1)S(1)} %get-tuple-element.43), channel_id=1, source_target_pairs={{0,32},{32,64},{64,96},{96,0},{1,33},{33,65},{65,97},{97,1},{2,34}... | collective-permute-start | bytes 786440 | tf_op jit(solution)/shard_map/ppermute | solution.py:15
  99.9 13.1 %collective-permute-start.17 = (bf16[256,512]{1,0:T(8,128)(2,1)S(1)}, bf16[256,512]{1,0:T(8,128)(2,1)S(1)}, u32[]{:S(2)}, u32[]{:S(2)}) collective-permute-start(bf16[256,512]{1,0:T(8,128)(2,1)S(1)} %get-tuple-element.44), channel_id=1, source_target_pairs={{0,32},{32,64},{64,96},{96,0},{1,33},{33,65},{65,97},{97,1},{2,34}... | collective-permute-start | bytes 786440 | tf_op jit(solution)/shard_map/ppermute | solution.py:15
  99.9 14.9 %collective-permute-start.18 = (bf16[256,512]{1,0:T(8,128)(2,1)S(1)}, bf16[256,512]{1,0:T(8,128)(2,1)S(1)}, u32[]{:S(2)}, u32[]{:S(2)}) collective-permute-start(bf16[256,512]{1,0:T(8,128)(2,1)S(1)} %get-tuple-element.43), channel_id=1, source_target_pairs={{0,96},{32,0},{64,32},{96,64},{1,97},{33,1},{65,33},{97,65},{2,98}... | collective-permute-start | bytes 786440 | tf_op jit(solution)/shard_map/ppermute | solution.py:15
  104.2 11.2 %collective-permute-start.21 = (bf16[256,512]{1,0:T(8,128)(2,1)S(1)}, bf16[256,512]{1,0:T(8,128)(2,1)S(1)}, u32[]{:S(2)}, u32[]{:S(2)}) collective-permute-start(bf16[256,512]{1,0:T(8,128)(2,1)S(1)} %collective-permute-done.19), channel_id=1, source_target_pairs={{0,96},{32,0},{64,32},{96,64},{1,97},{33,1},{65,33},{97,65},{2,98}... | collective-permute-start | bytes 786440 | tf_op jit(solution)/shard_map/ppermute | solution.py:15
  107.6 11.0 %collective-permute-start.20 = (bf16[256,512]{1,0:T(8,128)(2,1)S(1)}, bf16[256,512]{1,0:T(8,128)(2,1)S(1)}, u32[]{:S(2)}, u32[]{:S(2)}) collective-permute-start(bf16[256,512]{1,0:T(8,128)(2,1)S(1)} %collective-permute-done.16), channel_id=1, source_target_pairs={{0,32},{32,64},{64,96},{96,0},{1,33},{33,65},{65,97},{97,1},{2,34}... | collective-permute-start | bytes 786440 | tf_op jit(solution)/shard_map/ppermute | solution.py:15
  107.7 2.7 %copy-start = (bf16[8192,256]{1,0:T(8,128)(2,1)S(1)}, bf16[8192,256]{1,0:T(8,128)(2,1)}, u32[]{:S(2)}) copy-start(bf16[8192,256]{1,0:T(8,128)(2,1)} %all-gather.6.cloned.1.call-done) | copy-start | bytes 12582916
  119.2 22.7 %copy-start.5 = (bf16[32,8192]{1,0:T(8,128)(2,1)S(1)}, bf16[32,8192]{1,0:T(8,128)(2,1)}, u32[]{:S(2)}) copy-start(bf16[32,8192]{1,0:T(8,128)(2,1)} %param.9) | copy-start | bytes 1572868
Sparse Core Ops, SparseCore 0:
  12.2 50.4 all-gather.3
  73.1 33.0 all-gather.5

commit v8 on v5

--- a/solution.py
+++ b/solution.py
@@ -23,6 +23,12 @@
                 to = ((z & 1) * 2 + 1 - xl) * 4 + (z & ~1) + xh
                 pairs.append(((xh * 2 + xl) * 4 + z, to))
     return lax.ppermute(v, ("xh", "xl", "z"), pairs)
+
+
+def part_ways(v, where, to):
+    every = [(xh, xl, z) for xh in range(2) for xl in range(2) for z in range(4)]
+    pairs = [(p, to(*p)) for p in every if where(*p)]
+    return lax.ppermute(v, ("xh", "xl", "z"), [tuple((q[0] * 2 + q[1]) * 4 + q[2] for q in pair) for pair in pairs])
 
 
 def after(v, *done):
@@ -108,10 +114,13 @@
     pair = jnp.concatenate([mine, shift(other, "core", 1)], axis=1)
     factor = lax.all_gather(pair, "y", axis=0, tiled=True)
 
-    b = turn(change)
-    bm, bp, a = together(shift(b, "z", 1), shift(b, "z", -1), shift(b, "xl", 1))
+    moves = part_ways(output_factor, lambda xh, xl, z: z & 1 != xh, lambda xh, xl, z: (xh, 1 - xl, z ^ 1))
+    b, moves = together(turn(change), moves)
+    moves = part_ways(moves, lambda xh, xl, z: z & 1 == xh, lambda xh, xl, z: (1 - xh, 1 - xl, z))
+    bm, bp, a, moves = together(shift(b, "z", 1), shift(b, "z", -1), shift(b, "xl", 1), moves)
     am, ap, b2 = together(shift(bm, "xl", 1), shift(a, "z", -1), shift(bm, "z", 1))
-    turned = turn(after(output_factor, bm, bp, a))
+    same = (z & 1) == xh
+    turned = jnp.where(same, output_factor, moves)
     far = [shift(am[:half], "z", 1), shift(ap[half:], "z", -1)]
     *far, part = together(*far, shift(after(turned, factor), "xl", 1))
 
@@ -130,19 +139,24 @@
 
     theirs = [after(theirs, more(1)), more(1).astype(BF16)]
     odd, even = [v + shift(w, "core", 1).astype(F32) for v, w in zip((own, more(0)), theirs)]
-    same = (z & 1) == xh
-    send, keep = jnp.where(same, odd, even).astype(BF16), jnp.where(same, even, odd)
-    send = shift(send, "xh", 1)
+    top, rest = slice(half), slice(half, rows)
+    first, second = [jnp.where(same, odd[r], even[r]).astype(BF16) for r in (top, rest)]
+    first = shift(first, "xh", 1)
+    second = shift(after(second, first), "xh", 1)
+    keep = jnp.where(same, even, odd)
 
-    p = [(keep[r] + send[r].astype(F32)).astype(BF16) for r in (slice(half), slice(half, rows))]
-    below = [shift(p[0], "y", 1), shift(p[1], "y", 1)]
-    above = [shift(p[0], "y", -1), shift(p[1], "y", -1)]
+    p = [(keep[top] + first.astype(F32)).astype(BF16)]
+    below, above = [shift(p[0], "y", 1)], [shift(p[0], "y", -1)]
+    second, above[0] = together(second, above[0])
+    p.append((keep[rest] + second.astype(F32)).astype(BF16))
+    below.append(shift(p[1], "y", 1))
+    above.append(shift(p[1], "y", -1))
     beyond = [shift(below[0], "y", 1), shift(above[1], "y", -1)]
 
     def share(blocks, dy):
         at = (y + dy) & 3
         size = (2, rows, half)
-        corners = [(4 * h + (at & 1) * 2, ((at >> 1) ^ xl) * rows, 0) for h in range(2)]
+        corners = [(4 * h + (at & 1) * 2, (1 ^ (at >> 1) ^ xl) * rows, 0) for h in range(2)]
         terms = [dot(lax.dynamic_slice(left, c, size), v) for c, v in zip(corners, blocks)]
         return terms[0] + terms[1]
 

time: 153 us -> 149 us (0.974)
  waiting for transfers between devices: 59.4 us -> 51.9 us
  blocking collectives: 23.1 us -> 26.4 us
  starting transfers between devices: 27.7 us -> 29.6 us
  other arithmetic: 5.86 us -> 4.19 us
    ppermute x19 -> x20, waiting for transfers between devices: 47.3 us -> 33.5 us  [shift(): return lax.ppermute(v, axis, [(i, (i + by) % n) for i in range(n)])]
    ppermute x0 -> x2, waiting for transfers between devices: none -> 12.5 us  [part_ways(): lax.ppermute(v, ('xh', 'xl', 'z'), [tuple(((q[0] * 2 + q[1]) * 4 + q[2] f...]
    ppermute x2 -> x1, waiting for transfers between devices: 11.8 us -> 1.86 us  [turn(): return lax.ppermute(v, ('xh', 'xl', 'z'), pairs)]
    ppermute x0 -> x2, starting transfers between devices: none -> 4.1 us  [part_ways(): lax.ppermute(v, ('xh', 'xl', 'z'), [tuple(((q[0] * 2 + q[1]) * 4 + q[2] f...]
    all_gather x1, waiting for transfers between devices: 0.27 us -> 3.99 us  [body(): factor = lax.all_gather(pair, 'y', axis=0, tiled=True)]
    all_to_all x1, blocking collectives: 23.1 us -> 26.4 us  [body(): lax.all_to_all(penalty, ('xh',) + COL, split_axis=0, concat_axis=0, tiled...]
    ppermute x19 -> x20, starting transfers between devices: 26.3 us -> 24.1 us  [shift(): return lax.ppermute(v, axis, [(i, (i + by) % n) for i in range(n)])]
  transfers between devices with their start and end apart: 23 -> 25, of which waited for: 12 -> 13; matrix products, arithmetic and copies ran while one was open for 9% -> 8% of each run, Pallas kernels for 5% -> 6%
where the time goes in v8:
time: 149 us; the launch traced here: 148 us
  waiting for transfers between devices  51.9 us (35%)
  starting transfers between devices  29.6 us (20%)
  blocking collectives  26.4 us (18%)
  between operations  13.7 us (9%)
  matrix products  11.5 us (8%)
  Pallas kernels  8.19 us (5%)
  other arithmetic  4.19 us (3%)
  local copies, waits for them, and re-layouts  2.79 us (2%)
    ppermute x20, waiting for transfers between devices, shift(): return lax.ppermute(v, axis, [(i, (i + by) % n) for i in range(n)])  33.5 us
    all_to_all x1, blocking collectives, body(): lax.all_to_all(penalty, ('xh',) + COL, split_axis=0, concat_axis=0, tiled...  26.4 us
    ppermute x20, starting transfers between devices, shift(): return lax.ppermute(v, axis, [(i, (i + by) % n) for i in range(n)])  24.1 us
    ppermute x2, waiting for transfers between devices, part_ways(): lax.ppermute(v, ('xh', 'xl', 'z'), [tuple(((q[0] * 2 + q[1]) * 4 + q[2] f...  12.5 us
    dot_general x12, matrix products, dot(): lax.dot_general(a, b, (((a.ndim - 1,), (0,)), ((), ())), preferred_elemen...  11.5 us
    pallas_call x1, Pallas kernels, early(): pl.pallas_call(lambda *refs: early_kernel(n, m, *refs), out_shape=(jax.Sh...  8.19 us
    ppermute x2, starting transfers between devices, part_ways(): lax.ppermute(v, ('xh', 'xl', 'z'), [tuple(((q[0] * 2 + q[1]) * 4 + q[2] f...  4.1 us
    all_gather x1, waiting for transfers between devices, body(): factor = lax.all_gather(pair, 'y', axis=0, tiled=True)  3.99 us
  transfers between devices with their start and end apart: 25, of which 13 were waited for; matrix products, arithmetic and copies ran while one was open for 8% of the time, Pallas kernels for 6%

profile of v8, /device:TPU:1, one launch (start us, length us, event | category | flops | bytes accessed | tf_op | source)
XLA Modules:
  0.0 148.3 jit_solution(2628929080365785744)
XLA Ops:
  6.5 1.3 constant_dynamic-slice_fusion.1
  7.8 1.5 %collective-permute-start.11 = (bf16[512,512]{1,0:T(8,128)(2,1)S(1)}, bf16[512,512]{1,0:T(8,128)(2,1)S(1)}, u32[]{:S(2)}, u32[]{:S(2)}) collective-permute-start(bf16[512,512]{1,0:T(8,128)(2,1)S(1)} %get-tuple-element.53), channel_id=1, source_target_pairs={{0,1},{1,0},{2,3},{3,2},{4,5},{5,4},{6,7},{7,6},{8,9},{9,8},{10,11... | collective-permute-start | bytes 1572872 | tf_op jit(solution)/shard_map/ppermute | solution.py:15
  9.3 1.5 %collective-permute-done.11 = bf16[512,512]{1,0:T(8,128)(2,1)S(1)} collective-permute-done((bf16[512,512]{1,0:T(8,128)(2,1)S(1)}, bf16[512,512]{1,0:T(8,128)(2,1)S(1)}, u32[]{:S(2)}, u32[]{:S(2)}) %collective-permute-start.11) | collective-permute-done | bytes 524320 | tf_op jit(solution)/shard_map/ppermute | solution.py:15
  10.9 1.1 pad_maximum_fusion
  12.0 0.0 all-gather.6.cloned.1.call-start
  12.1 0.1 subtract_convert_fusion
  12.2 1.4 collective-permute-start
  13.6 1.3 collective-permute-start.1
  14.9 8.7 %collective-permute-done.1 = bf16[512,256]{1,0:T(8,128)(2,1)S(1)} collective-permute-done((bf16[512,256]{1,0:T(8,128)(2,1)S(1)}, bf16[512,256]{1,0:T(8,128)(2,1)S(1)}, u32[]{:S(2)}, u32[]{:S(2)}) %collective-permute-start.1) | collective-permute-done | bytes 262176 | tf_op jit(solution)/shard_map/ppermute | solution.py:31
  23.6 1.9 %collective-permute-done.refs_6_ = bf16[512,512]{1,0:T(8,128)(2,1)S(1)} collective-permute-done((bf16[512,512]{1,0:T(8,128)(2,1)S(1)}, bf16[512,512]{1,0:T(8,128)(2,1)S(1)}, u32[]{:S(2)}, u32[]{:S(2)}) %collective-permute-start) | collective-permute-done | bytes 524320 | tf_op jit(solution)/shard_map/ppermute | solution.py:25
  25.5 1.3 collective-permute-start.4
  26.7 4.7 %collective-permute-start.3 = (bf16[512,512]{1,0:T(8,128)(2,1)S(1)}, bf16[512,512]{1,0:T(8,128)(2,1)S(1)}, u32[]{:S(2)}, u32[]{:S(2)}) collective-permute-start(bf16[512,512]{1,0:T(8,128)(2,1)S(1)} %collective-permute-done.refs_6_), channel_id=1, source_target_pairs={{0,6},{2,0},{4,2},{6,4},{1,7},{3,1},{5,3},{7,5},{8,14},{10,8},{12,... | collective-permute-start | bytes 1572872 | tf_op jit(solution)/shard_map/ppermute | solution.py:15
  31.4 2.8 %collective-permute-start.5 = (bf16[512,256]{1,0:T(8,128)(2,1)S(1)}, bf16[512,256]{1,0:T(8,128)(2,1)S(1)}, u32[]{:S(2)}, u32[]{:S(2)}) collective-permute-start(bf16[512,256]{1,0:T(8,128)(2,1)S(1)} %collective-permute-done.1), channel_id=1, source_target_pairs={{0,24},{4,28},{8,16},{12,20},{18,10},{22,14},{26,2},{30,6},{1,25},... | collective-permute-start | bytes 786440 | tf_op jit(solution)/shard_map/ppermute | solution.py:31
  34.2 3.8 %collective-permute-done.5 = bf16[512,256]{1,0:T(8,128)(2,1)S(1)} collective-permute-done((bf16[512,256]{1,0:T(8,128)(2,1)S(1)}, bf16[512,256]{1,0:T(8,128)(2,1)S(1)}, u32[]{:S(2)}, u32[]{:S(2)}) %collective-permute-start.5) | collective-permute-done | bytes 262176 | tf_op jit(solution)/shard_map/ppermute | solution.py:31
  38.0 3.1 %collective-permute-done.3.refs_4_ = bf16[512,512]{1,0:T(8,128)(2,1)S(1)} collective-permute-done((bf16[512,512]{1,0:T(8,128)(2,1)S(1)}, bf16[512,512]{1,0:T(8,128)(2,1)S(1)}, u32[]{:S(2)}, u32[]{:S(2)}) %collective-permute-start.3) | collective-permute-done | bytes 524320 | tf_op jit(solution)/shard_map/ppermute | solution.py:15
  41.1 3.2 %collective-permute-done.2.refs_3_ = bf16[512,512]{1,0:T(8,128)(2,1)} collective-permute-done((bf16[512,512]{1,0:T(8,128)(2,1)S(1)}, bf16[512,512]{1,0:T(8,128)(2,1)}, u32[]{:S(2)}, u32[]{:S(2)}) %collective-permute-start.2) | collective-permute-done | bytes 524320 | tf_op jit(solution)/shard_map/ppermute | solution.py:15
  44.4 0.3 collective-permute-start.7
  44.7 1.2 collective-permute-start.8
  45.8 1.5 collective-permute-start.6
  47.3 0.6 stack.31.refs_0_
  47.9 7.3 %collective-permute-done.7.refs_2_ = bf16[512,512]{1,0:T(8,128)(2,1)S(1)} collective-permute-done((bf16[512,512]{1,0:T(8,128)(2,1)S(1)}, bf16[512,512]{1,0:T(8,128)(2,1)S(1)}, u32[]{:S(2)}, u32[]{:S(2)}) %collective-permute-start.7) | collective-permute-done | bytes 524320 | tf_op jit(solution)/shard_map/ppermute | solution.py:15
  55.2 1.8 %collective-permute-done.8.refs_7_ = bf16[512,512]{1,0:T(8,128)(2,1)} collective-permute-done((bf16[512,512]{1,0:T(8,128)(2,1)}, bf16[512,512]{1,0:T(8,128)(2,1)}, u32[]{:S(2)}, u32[]{:S(2)}) %collective-permute-start.8) | collective-permute-done | bytes 524320 | tf_op jit(solution)/shard_map/ppermute | solution.py:15
  57.1 1.3 collective-permute-start.10
  58.4 0.2 collective-permute-start.9
  58.6 4.0 %all-gather.4.cloned.1.call-done.refs_8_ = bf16[2048,1024]{1,0:T(8,128)(2,1)} async-done(((bf16[512,1024]{1,0:T(8,128)(2,1)}), bf16[2048,1024]{1,0:T(8,128)(2,1)}) %all-gather.4.cloned.1.call-update) | async-done | bytes 4194320 | tf_op jit(solution)/shard_map/all_gather | solution.py:115
  62.6 1.2 collective-permute-start.12
  63.8 8.2 %shard_map.55 = (bf16[512,512]{1,0:T(8,128)(2,1)}, f32[512,512]{1,0:T(8,128)}, f32[512,1024]{1,0:T(8,128)}) custom-call(s32[7]{0:T(128)} %stack.31.refs_0_, bf16[512,512]{1,0:T(8,128)(2,1)} %copy-done.8, bf16[512,512]{1,0:T(8,128)(2,1)} %copy-done.7, bf16[512,512]{1,0:T(8,128)(2,1)} %collective-permute-done.2.refs_3_, bf16[512,512]{1,0:T(8,128)(2,1)} %copy-done.11, ...), custom_call_target="tpu_custom_call" | custom-call | flops 3758096384 | bytes 12582912 | tf_op jit(solution)/shard_map/pallas_call | solution.py:83
  72.1 0.8 pad_maximum_fusion.1
  72.9 1.3 fusion.22
  74.3 1.4 fusion.20
  75.7 0.3 maximum_add_fusion.1
  76.0 1.0 collective-permute-start.14
  77.0 0.1 collective-permute-start.13
  77.1 1.3 fusion.26
  78.4 1.3 fusion.24
  79.8 0.5 broadcast_select_fusion
  80.4 0.1 fusion.3
  80.4 2.5 %collective-permute-start.15 = (bf16[256,512]{1,0:T(8,128)(2,1)S(1)}, bf16[256,512]{1,0:T(8,128)(2,1)S(1)}, u32[]{:S(2)}, u32[]{:S(2)}) collective-permute-start(bf16[256,512]{1,0:T(8,128)(2,1)S(1)} %get-tuple-element.50), channel_id=1, source_target_pairs={{0,16},{16,0},{1,17},{17,1},{2,18},{18,2},{3,19},{19,3},{4,20},{20... | collective-permute-start | bytes 786440 | tf_op jit(solution)/shard_map/ppermute | solution.py:15
  82.9 6.6 %collective-permute-done.15 = bf16[256,512]{1,0:T(8,128)(2,1)S(1)} collective-permute-done((bf16[256,512]{1,0:T(8,128)(2,1)S(1)}, bf16[256,512]{1,0:T(8,128)(2,1)S(1)}, u32[]{:S(2)}, u32[]{:S(2)}) %collective-permute-start.15) | collective-permute-done | bytes 262176 | tf_op jit(solution)/shard_map/ppermute | solution.py:15
  89.5 0.1 fusion.4
  89.6 2.5 %collective-permute-start.17 = (bf16[256,512]{1,0:T(8,128)(2,1)S(1)}, bf16[256,512]{1,0:T(8,128)(2,1)S(1)}, u32[]{:S(2)}, u32[]{:S(2)}) collective-permute-start(bf16[256,512]{1,0:T(8,128)(2,1)S(1)} %fusion.4), channel_id=1, source_target_pairs={{0,96},{32,0},{64,32},{96,64},{1,97},{33,1},{65,33},{97,65},{2,98}... | collective-permute-start | bytes 786440 | tf_op jit(solution)/shard_map/ppermute | solution.py:15
  92.0 1.1 collective-permute-start.16
  93.1 0.4 collective-permute-start.18
  93.6 2.8 %collective-permute-done.17 = bf16[256,512]{1,0:T(8,128)(2,1)S(1)} collective-permute-done((bf16[256,512]{1,0:T(8,128)(2,1)S(1)}, bf16[256,512]{1,0:T(8,128)(2,1)S(1)}, u32[]{:S(2)}, u32[]{:S(2)}) %collective-permute-start.17) | collective-permute-done | bytes 262176 | tf_op jit(solution)/shard_map/ppermute | solution.py:15
  96.4 3.4 %collective-permute-done.16 = bf16[256,512]{1,0:T(8,128)(2,1)S(1)} collective-permute-done((bf16[256,512]{1,0:T(8,128)(2,1)S(1)}, bf16[256,512]{1,0:T(8,128)(2,1)S(1)}, u32[]{:S(2)}, u32[]{:S(2)}) %collective-permute-start.16) | collective-permute-done | bytes 262176 | tf_op jit(solution)/shard_map/ppermute | solution.py:15
  99.8 0.1 fusion.2
  99.9 0.4 collective-permute-start.20
  100.3 1.1 collective-permute-start.19
  101.4 0.0 collective-permute-start.21
  101.4 3.7 %collective-permute-done.20 = bf16[256,512]{1,0:T(8,128)(2,1)S(1)} collective-permute-done((bf16[256,512]{1,0:T(8,128)(2,1)S(1)}, bf16[256,512]{1,0:T(8,128)(2,1)S(1)}, u32[]{:S(2)}, u32[]{:S(2)}) %collective-permute-start.20) | collective-permute-done | bytes 262176 | tf_op jit(solution)/shard_map/ppermute | solution.py:15
  105.2 1.8 %collective-permute-start.22 = (bf16[256,512]{1,0:T(8,128)(2,1)S(1)}, bf16[256,512]{1,0:T(8,128)(2,1)S(1)}, u32[]{:S(2)}, u32[]{:S(2)}) collective-permute-start(bf16[256,512]{1,0:T(8,128)(2,1)S(1)} %collective-permute-done.20), channel_id=1, source_target_pairs={{0,96},{32,0},{64,32},{96,64},{1,97},{33,1},{65,33},{97,65},{2,98}... | collective-permute-start | bytes 786440 | tf_op jit(solution)/shard_map/ppermute | solution.py:15
  107.0 1.6 %fusion.16 = f32[2,512,512]{2,1,0:T(8,128)S(1)} fusion(bf16[8,1024,256]{2,1,0:T(8,128)(2,1)} %bitcast.46, s32[]{:T(128)S(6)} %select_n.90, s32[]{:T(128)S(6)} %select_n.84, bf16[256,512]{1,0:T(8,128)(2,1)S(1)} %fusion.2), kind=kOutput, calls=%fused_computation.29 | convolution fusion | flops 268435456 | bytes 2883592 | tf_op jit(solution)/shard_map/dot_general | solution.py:43
  108.6 1.5 fusion.18
  110.1 0.4 fusion.10
  110.5 0.4 fusion.8
  111.0 0.4 fusion.14
  111.4 0.4 fusion.12
  111.8 0.4 fusion.5
  112.3 0.8 add_convert_fusion
  113.1 26.4 %all_to_all.9 = bf16[32,32,512]{2,1,0:T(8,128)(2,1)S(1)} all-to-all(bf16[32,32,512]{2,1,0:T(8,128)(2,1)S(1)} %bitcast.42), channel_id=1, replica_groups=mesh['y'=4,'xh'=2,'xl'=2,'z'=4,'core'=2] {'xh','xl','z','core'}, dimensions={0} | all-to-all | bytes 2097152 | tf_op jit(solution)/shard_map/all_to_all | solution.py:165
  139.5 0.2 convert_reduce_fusion
  139.7 0.1 copy.7
  139.8 0.7 copy-done.5
  140.6 0.9 add_convert_fusion.1
  (44 shorter events, 0.2 us)
Async XLA Ops:
  6.5 56.1 %all-gather.4.cloned.1.call-start = ((), (), s32[]{:S(2)}) async-start(), calls=%async_computation.1 | async-start | bytes 5242880 | tf_op jit(solution)/shard_map/all_gather | solution.py:115
  7.8 4.3 %copy-start.3 = (bf16[512,512]{1,0:T(8,128)(2,1)S(1)}, bf16[512,512]{1,0:T(8,128)(2,1)}, u32[]{:S(2)}) copy-start(bf16[512,512]{1,0:T(8,128)(2,1)} %param.6) | copy-start | bytes 1572868
  7.8 4.3 %copy-start.4 = (bf16[512,512]{1,0:T(8,128)(2,1)S(1)}, bf16[512,512]{1,0:T(8,128)(2,1)}, u32[]{:S(2)}) copy-start(bf16[512,512]{1,0:T(8,128)(2,1)} %param.5) | copy-start | bytes 1572868
  7.8 3.0 %collective-permute-start.11 = (bf16[512,512]{1,0:T(8,128)(2,1)S(1)}, bf16[512,512]{1,0:T(8,128)(2,1)S(1)}, u32[]{:S(2)}, u32[]{:S(2)}) collective-permute-start(bf16[512,512]{1,0:T(8,128)(2,1)S(1)} %get-tuple-element.53), channel_id=1, source_target_pairs={{0,1},{1,0},{2,3},{3,2},{4,5},{5,4},{6,7},{7,6},{8,9},{9,8},{10,11... | collective-permute-start | bytes 1572872 | tf_op jit(solution)/shard_map/ppermute | solution.py:15
  10.9 2.7 %copy-start.6 = (bf16[512,256]{1,0:T(8,128)(2,1)S(1)}, bf16[512,256]{1,0:T(8,128)(2,1)}, u32[]{:S(2)}) copy-start(bf16[512,256]{1,0:T(8,128)(2,1)} %param.8) | copy-start | bytes 786436
  12.0 95.0 %all-gather.6.cloned.1.call-start = ((), (), s32[]{:S(2)}) async-start(), calls=%async_computation.2 | async-start | bytes 4718592 | tf_op jit(solution)/shard_map/all_gather | solution.py:133
  12.2 13.2 %collective-permute-start = (bf16[512,512]{1,0:T(8,128)(2,1)S(1)}, bf16[512,512]{1,0:T(8,128)(2,1)S(1)}, u32[]{:S(2)}, u32[]{:S(2)}) collective-permute-start(bf16[512,512]{1,0:T(8,128)(2,1)S(1)} %subtract_convert_fusion), channel_id=1, source_target_pairs={{0,8},{2,24},{4,12},{6,28},{8,0},{10,16},{12,4},{14,20},{16,10},{1... | collective-permute-start | bytes 1572872 | tf_op jit(solution)/shard_map/ppermute | solution.py:25
  13.6 10.0 %collective-permute-start.1 = (bf16[512,256]{1,0:T(8,128)(2,1)S(1)}, bf16[512,256]{1,0:T(8,128)(2,1)S(1)}, u32[]{:S(2)}, u32[]{:S(2)}) collective-permute-start(bf16[512,256]{1,0:T(8,128)(2,1)S(1)} %copy-done.6), channel_id=1, source_target_pairs={{2,8},{6,12},{10,0},{14,4},{16,26},{20,30},{24,18},{28,22},{3,9},{... | collective-permute-start | bytes 786440 | tf_op jit(solution)/shard_map/ppermute | solution.py:31
  25.4 38.4 %copy-start.9 = (bf16[512,512]{1,0:T(8,128)(2,1)}, bf16[512,512]{1,0:T(8,128)(2,1)S(1)}, u32[]{:S(2)}) copy-start(bf16[512,512]{1,0:T(8,128)(2,1)S(1)} %collective-permute-done.refs_6_) | copy-start | bytes 1572868
  25.5 12.6 %collective-permute-start.4 = (bf16[512,512]{1,0:T(8,128)(2,1)S(1)}, bf16[512,512]{1,0:T(8,128)(2,1)S(1)}, u32[]{:S(2)}, u32[]{:S(2)}) collective-permute-start(bf16[512,512]{1,0:T(8,128)(2,1)S(1)} %collective-permute-done.refs_6_), channel_id=1, source_target_pairs={{0,8},{8,0},{1,9},{9,1},{2,10},{10,2},{3,11},{11,3},{4,12},{12,4},... | collective-permute-start | bytes 1572872 | tf_op jit(solution)/shard_map/ppermute | solution.py:15
  26.7 14.4 %collective-permute-start.3 = (bf16[512,512]{1,0:T(8,128)(2,1)S(1)}, bf16[512,512]{1,0:T(8,128)(2,1)S(1)}, u32[]{:S(2)}, u32[]{:S(2)}) collective-permute-start(bf16[512,512]{1,0:T(8,128)(2,1)S(1)} %collective-permute-done.refs_6_), channel_id=1, source_target_pairs={{0,6},{2,0},{4,2},{6,4},{1,7},{3,1},{5,3},{7,5},{8,14},{10,8},{12,... | collective-permute-start | bytes 1572872 | tf_op jit(solution)/shard_map/ppermute | solution.py:15
  31.4 13.0 %collective-permute-start.2 = (bf16[512,512]{1,0:T(8,128)(2,1)S(1)}, bf16[512,512]{1,0:T(8,128)(2,1)}, u32[]{:S(2)}, u32[]{:S(2)}) collective-permute-start(bf16[512,512]{1,0:T(8,128)(2,1)S(1)} %collective-permute-done.refs_6_), channel_id=1, source_target_pairs={{0,2},{2,4},{4,6},{6,0},{1,3},{3,5},{5,7},{7,1},{8,10},{10,12},{12... | collective-permute-start | bytes 1572872 | tf_op jit(solution)/shard_map/ppermute | solution.py:15
  31.4 6.6 %collective-permute-start.5 = (bf16[512,256]{1,0:T(8,128)(2,1)S(1)}, bf16[512,256]{1,0:T(8,128)(2,1)S(1)}, u32[]{:S(2)}, u32[]{:S(2)}) collective-permute-start(bf16[512,256]{1,0:T(8,128)(2,1)S(1)} %collective-permute-done.1), channel_id=1, source_target_pairs={{0,24},{4,28},{8,16},{12,20},{18,10},{22,14},{26,2},{30,6},{1,25},... | collective-permute-start | bytes 786440 | tf_op jit(solution)/shard_map/ppermute | solution.py:31
  38.0 19.0 %copy-start.10 = (bf16[512,512]{1,0:T(8,128)(2,1)}, bf16[512,512]{1,0:T(8,128)(2,1)S(1)}, u32[]{:S(2)}) copy-start(bf16[512,512]{1,0:T(8,128)(2,1)S(1)} %collective-permute-done.4.refs_5_) | copy-start | bytes 1572868
  41.1 3.5 %copy-start.11 = (bf16[512,512]{1,0:T(8,128)(2,1)}, bf16[512,512]{1,0:T(8,128)(2,1)S(1)}, u32[]{:S(2)}) copy-start(bf16[512,512]{1,0:T(8,128)(2,1)S(1)} %collective-permute-done.3.refs_4_) | copy-start | bytes 1572868
  44.4 10.8 %collective-permute-start.7 = (bf16[512,512]{1,0:T(8,128)(2,1)S(1)}, bf16[512,512]{1,0:T(8,128)(2,1)S(1)}, u32[]{:S(2)}, u32[]{:S(2)}) collective-permute-start(bf16[512,512]{1,0:T(8,128)(2,1)S(1)} %collective-permute-done.4.refs_5_), channel_id=1, source_target_pairs={{0,6},{2,0},{4,2},{6,4},{1,7},{3,1},{5,3},{7,5},{8,14},{10,8},{12,... | collective-permute-start | bytes 1572872 | tf_op jit(solution)/shard_map/ppermute | solution.py:15
  44.7 12.4 %collective-permute-start.8 = (bf16[512,512]{1,0:T(8,128)(2,1)}, bf16[512,512]{1,0:T(8,128)(2,1)}, u32[]{:S(2)}, u32[]{:S(2)}) collective-permute-start(bf16[512,512]{1,0:T(8,128)(2,1)} %collective-permute-done.2.refs_3_), channel_id=1, source_target_pairs={{0,2},{2,4},{4,6},{6,0},{1,3},{3,5},{5,7},{7,1},{8,10},{10,12},{12... | collective-permute-start | bytes 1572872 | tf_op jit(solution)/shard_map/ppermute | solution.py:15
  45.8 11.2 %collective-permute-start.6 = (bf16[512,512]{1,0:T(8,128)(2,1)}, bf16[512,512]{1,0:T(8,128)(2,1)S(1)}, u32[]{:S(2)}, u32[]{:S(2)}) collective-permute-start(bf16[512,512]{1,0:T(8,128)(2,1)} %collective-permute-done.2.refs_3_), channel_id=1, source_target_pairs={{0,8},{8,0},{1,9},{9,1},{2,10},{10,2},{3,11},{11,3},{4,12},{12,4},... | collective-permute-start | bytes 1572872 | tf_op jit(solution)/shard_map/ppermute | solution.py:15
  55.2 8.6 %copy-start.7 = (bf16[512,512]{1,0:T(8,128)(2,1)}, bf16[512,512]{1,0:T(8,128)(2,1)S(1)}, u32[]{:S(2)}) copy-start(bf16[512,512]{1,0:T(8,128)(2,1)S(1)} %collective-permute-done.7.refs_2_) | copy-start | bytes 1572868
  57.0 6.8 %copy-start.8 = (bf16[512,512]{1,0:T(8,128)(2,1)}, bf16[512,512]{1,0:T(8,128)(2,1)S(1)}, u32[]{:S(2)}) copy-start(bf16[512,512]{1,0:T(8,128)(2,1)S(1)} %collective-permute-done.6.refs_1_) | copy-start | bytes 1572868
  57.1 14.9 %collective-permute-start.10 = (bf16[256,512]{1,0:T(8,128)(2,1)S(1)}, bf16[256,512]{1,0:T(8,128)(2,1)S(1)}, u32[]{:S(2)}, u32[]{:S(2)}) collective-permute-start(bf16[256,512]{1,0:T(8,128)(2,1)S(1)} %slice.32), channel_id=1, source_target_pairs={{0,6},{2,0},{4,2},{6,4},{1,7},{3,1},{5,3},{7,5},{8,14},{10,8},{12,... | collective-permute-start | bytes 786440 | tf_op jit(solution)/shard_map/ppermute | solution.py:15
  58.4 13.6 %collective-permute-start.9 = (bf16[256,512]{1,0:T(8,128)(2,1)S(1)}, bf16[256,512]{1,0:T(8,128)(2,1)S(1)}, u32[]{:S(2)}, u32[]{:S(2)}) collective-permute-start(bf16[256,512]{1,0:T(8,128)(2,1)S(1)} %slice.31), channel_id=1, source_target_pairs={{0,2},{2,4},{4,6},{6,0},{1,3},{3,5},{5,7},{7,1},{8,10},{10,12},{12... | collective-permute-start | bytes 786440 | tf_op jit(solution)/shard_map/ppermute | solution.py:15
  62.6 9.4 %collective-permute-start.12 = (bf16[512,256]{1,0:T(8,128)(2,1)S(1)}, bf16[512,256]{1,0:T(8,128)(2,1)S(1)}, u32[]{:S(2)}, u32[]{:S(2)}) collective-permute-start(bf16[512,256]{1,0:T(8,128)(2,1)S(1)} %broadcast_select_fusion.1), channel_id=1, source_target_pairs={{0,8},{8,0},{1,9},{9,1},{2,10},{10,2},{3,11},{11,3},{4,12},{12,4},... | collective-permute-start | bytes 786440 | tf_op jit(solution)/shard_map/ppermute | solution.py:15
  72.0 3.6 %copy-start.1 = (f32[512,1024]{1,0:T(8,128)S(1)}, f32[512,1024]{1,0:T(8,128)}, u32[]{:S(2)}) copy-start(f32[512,1024]{1,0:T(8,128)} %get-tuple-element.39) | copy-start | bytes 6291460
  74.3 1.7 %copy-start.12 = (bf16[512,512]{1,0:T(8,128)(2,1)S(1)}, bf16[512,512]{1,0:T(8,128)(2,1)}, u32[]{:S(2)}) copy-start(bf16[512,512]{1,0:T(8,128)(2,1)} %get-tuple-element.43) | copy-start | bytes 1572868
  75.7 4.1 %copy-start.2 = (f32[512,512]{1,0:T(8,128)S(1)}, f32[512,512]{1,0:T(8,128)}, u32[]{:S(2)}) copy-start(f32[512,512]{1,0:T(8,128)} %get-tuple-element.37) | copy-start | bytes 3145732
  76.0 3.8 %collective-permute-start.14 = (bf16[512,512]{1,0:T(8,128)(2,1)S(1)}, bf16[512,512]{1,0:T(8,128)(2,1)S(1)}, u32[]{:S(2)}, u32[]{:S(2)}) collective-permute-start(bf16[512,512]{1,0:T(8,128)(2,1)S(1)} %copy-done.12), channel_id=1, source_target_pairs={{0,1},{1,0},{2,3},{3,2},{4,5},{5,4},{6,7},{7,6},{8,9},{9,8},{10,11... | collective-permute-start | bytes 1572872 | tf_op jit(solution)/shard_map/ppermute | solution.py:15
  77.0 2.8 %collective-permute-start.13 = (bf16[512,512]{1,0:T(8,128)(2,1)S(1)}, bf16[512,512]{1,0:T(8,128)(2,1)S(1)}, u32[]{:S(2)}, u32[]{:S(2)}) collective-permute-start(bf16[512,512]{1,0:T(8,128)(2,1)S(1)} %maximum_add_fusion.1), channel_id=1, source_target_pairs={{0,1},{1,0},{2,3},{3,2},{4,5},{5,4},{6,7},{7,6},{8,9},{9,8},{10,11... | collective-permute-start | bytes 1572872 | tf_op jit(solution)/shard_map/ppermute | solution.py:15
  80.4 9.1 %collective-permute-start.15 = (bf16[256,512]{1,0:T(8,128)(2,1)S(1)}, bf16[256,512]{1,0:T(8,128)(2,1)S(1)}, u32[]{:S(2)}, u32[]{:S(2)}) collective-permute-start(bf16[256,512]{1,0:T(8,128)(2,1)S(1)} %get-tuple-element.50), channel_id=1, source_target_pairs={{0,16},{16,0},{1,17},{17,1},{2,18},{18,2},{3,19},{19,3},{4,20},{20... | collective-permute-start | bytes 786440 | tf_op jit(solution)/shard_map/ppermute | solution.py:15
  89.6 6.8 %collective-permute-start.17 = (bf16[256,512]{1,0:T(8,128)(2,1)S(1)}, bf16[256,512]{1,0:T(8,128)(2,1)S(1)}, u32[]{:S(2)}, u32[]{:S(2)}) collective-permute-start(bf16[256,512]{1,0:T(8,128)(2,1)S(1)} %fusion.4), channel_id=1, source_target_pairs={{0,96},{32,0},{64,32},{96,64},{1,97},{33,1},{65,33},{97,65},{2,98}... | collective-permute-start | bytes 786440 | tf_op jit(solution)/shard_map/ppermute | solution.py:15
  92.0 7.8 %collective-permute-start.16 = (bf16[256,512]{1,0:T(8,128)(2,1)S(1)}, bf16[256,512]{1,0:T(8,128)(2,1)S(1)}, u32[]{:S(2)}, u32[]{:S(2)}) collective-permute-start(bf16[256,512]{1,0:T(8,128)(2,1)S(1)} %get-tuple-element.44), channel_id=1, source_target_pairs={{0,16},{16,0},{1,17},{17,1},{2,18},{18,2},{3,19},{19,3},{4,20},{20... | collective-permute-start | bytes 786440 | tf_op jit(solution)/shard_map/ppermute | solution.py:15
  93.1 8.3 %collective-permute-start.18 = (bf16[256,512]{1,0:T(8,128)(2,1)S(1)}, bf16[256,512]{1,0:T(8,128)(2,1)S(1)}, u32[]{:S(2)}, u32[]{:S(2)}) collective-permute-start(bf16[256,512]{1,0:T(8,128)(2,1)S(1)} %fusion.4), channel_id=1, source_target_pairs={{0,32},{32,64},{64,96},{96,0},{1,33},{33,65},{65,97},{97,1},{2,34}... | collective-permute-start | bytes 786440 | tf_op jit(solution)/shard_map/ppermute | solution.py:15
  99.9 5.3 %collective-permute-start.20 = (bf16[256,512]{1,0:T(8,128)(2,1)S(1)}, bf16[256,512]{1,0:T(8,128)(2,1)S(1)}, u32[]{:S(2)}, u32[]{:S(2)}) collective-permute-start(bf16[256,512]{1,0:T(8,128)(2,1)S(1)} %fusion.2), channel_id=1, source_target_pairs={{0,96},{32,0},{64,32},{96,64},{1,97},{33,1},{65,33},{97,65},{2,98}... | collective-permute-start | bytes 786440 | tf_op jit(solution)/shard_map/ppermute | solution.py:15
  100.3 11.1 %collective-permute-start.19 = (bf16[256,512]{1,0:T(8,128)(2,1)S(1)}, bf16[256,512]{1,0:T(8,128)(2,1)S(1)}, u32[]{:S(2)}, u32[]{:S(2)}) collective-permute-start(bf16[256,512]{1,0:T(8,128)(2,1)S(1)} %fusion.2), channel_id=1, source_target_pairs={{0,32},{32,64},{64,96},{96,0},{1,33},{33,65},{65,97},{97,1},{2,34}... | collective-permute-start | bytes 786440 | tf_op jit(solution)/shard_map/ppermute | solution.py:15
  101.4 10.9 %collective-permute-start.21 = (bf16[256,512]{1,0:T(8,128)(2,1)S(1)}, bf16[256,512]{1,0:T(8,128)(2,1)S(1)}, u32[]{:S(2)}, u32[]{:S(2)}) collective-permute-start(bf16[256,512]{1,0:T(8,128)(2,1)S(1)} %collective-permute-done.18), channel_id=1, source_target_pairs={{0,32},{32,64},{64,96},{96,0},{1,33},{33,65},{65,97},{97,1},{2,34}... | collective-permute-start | bytes 786440 | tf_op jit(solution)/shard_map/ppermute | solution.py:15
  105.2 6.7 %collective-permute-start.22 = (bf16[256,512]{1,0:T(8,128)(2,1)S(1)}, bf16[256,512]{1,0:T(8,128)(2,1)S(1)}, u32[]{:S(2)}, u32[]{:S(2)}) collective-permute-start(bf16[256,512]{1,0:T(8,128)(2,1)S(1)} %collective-permute-done.20), channel_id=1, source_target_pairs={{0,96},{32,0},{64,32},{96,64},{1,97},{33,1},{65,33},{97,65},{2,98}... | collective-permute-start | bytes 786440 | tf_op jit(solution)/shard_map/ppermute | solution.py:15
  107.0 3.1 %copy-start = (bf16[8192,256]{1,0:T(8,128)(2,1)S(1)}, bf16[8192,256]{1,0:T(8,128)(2,1)}, u32[]{:S(2)}) copy-start(bf16[8192,256]{1,0:T(8,128)(2,1)} %all-gather.6.cloned.1.call-done) | copy-start | bytes 12582916
  139.5 1.0 copy-start.5
Sparse Core Ops, SparseCore 0:
  12.1 50.4 all-gather.3
  73.0 33.0 all-gather.5

commit v9 on v8

--- a/solution.py
+++ b/solution.py
@@ -145,6 +145,7 @@
     second = shift(after(second, first), "xh", 1)
     keep = jnp.where(same, even, odd)
 
+    grad, first = together(task_grad.astype(F32), first)
     p = [(keep[top] + first.astype(F32)).astype(BF16)]
     below, above = [shift(p[0], "y", 1)], [shift(p[0], "y", -1)]
     second, above[0] = together(second, above[0])
@@ -165,7 +166,7 @@
     owned = lax.all_to_all(penalty, ("xh",) + COL, split_axis=0, concat_axis=0, tiled=True)
     owned = owned.reshape(2, 16, task_grad.shape[0], cols).astype(F32).sum(axis=0)
     owned = owned.transpose(1, 0, 2).reshape(task_grad.shape)
-    return (task_grad.astype(F32) + owned).astype(BF16)
+    return (grad + owned).astype(BF16)
 
 
 def solution(mesh):

time: 149 us -> 148 us (level)
  starting transfers between devices: 29.6 us -> 31.4 us
    ppermute x20, starting transfers between devices: 24.1 us -> 25.9 us  [shift(): return lax.ppermute(v, axis, [(i, (i + by) % n) for i in range(n)])]
  transfers between devices with their start and end apart: 25 -> 25, of which waited for: 13 -> 14; matrix products, arithmetic and copies ran while one was open for 8% -> 8% of each run, Pallas kernels for 6% -> 6%
where the time goes in v9:
time: 148 us
  waiting for transfers between devices  50.6 us (34%)
  starting transfers between devices  31.4 us (21%)
  blocking collectives  26.1 us (18%)
  between operations  13.7 us (9%)
  matrix products  11.5 us (8%)
  Pallas kernels  8.19 us (6%)
  other arithmetic  4.29 us (3%)
  local copies, waits for them, and re-layouts  2.05 us (1%)
    ppermute x20, waiting for transfers between devices, shift(): return lax.ppermute(v, axis, [(i, (i + by) % n) for i in range(n)])  32.2 us
    all_to_all x1, blocking collectives, body(): lax.all_to_all(penalty, ('xh',) + COL, split_axis=0, concat_axis=0, tiled...  26.1 us
    ppermute x20, starting transfers between devices, shift(): return lax.ppermute(v, axis, [(i, (i + by) % n) for i in range(n)])  25.9 us
    ppermute x2, waiting for transfers between devices, part_ways(): lax.ppermute(v, ('xh', 'xl', 'z'), [tuple(((q[0] * 2 + q[1]) * 4 + q[2] f...  12.5 us
    dot_general x12, matrix products, dot(): lax.dot_general(a, b, (((a.ndim - 1,), (0,)), ((), ())), preferred_elemen...  11.5 us
    pallas_call x1, Pallas kernels, early(): pl.pallas_call(lambda *refs: early_kernel(n, m, *refs), out_shape=(jax.Sh...  8.19 us
    ppermute x2, starting transfers between devices, part_ways(): lax.ppermute(v, ('xh', 'xl', 'z'), [tuple(((q[0] * 2 + q[1]) * 4 + q[2] f...  4.1 us
    all_gather x1, waiting for transfers between devices, body(): factor = lax.all_gather(pair, 'y', axis=0, tiled=True)  3.99 us
  transfers between devices with their start and end apart: 25, of which 14 were waited for; matrix products, arithmetic and copies ran while one was open for 8% of the time, Pallas kernels for 6%

profile of v9, /device:TPU:1, one launch (start us, length us, event | category | flops | bytes accessed | tf_op | source)
XLA Modules:
  0.0 147.9 jit_solution(4332490969026808642)
XLA Ops:
  6.5 1.3 constant_dynamic-slice_fusion.1
  7.8 1.5 %collective-permute-start.9 = (bf16[512,512]{1,0:T(8,128)(2,1)S(1)}, bf16[512,512]{1,0:T(8,128)(2,1)S(1)}, u32[]{:S(2)}, u32[]{:S(2)}) collective-permute-start(bf16[512,512]{1,0:T(8,128)(2,1)S(1)} %get-tuple-element.57), channel_id=1, source_target_pairs={{0,1},{1,0},{2,3},{3,2},{4,5},{5,4},{6,7},{7,6},{8,9},{9,8},{10,11... | collective-permute-start | bytes 1572872 | tf_op jit(solution)/shard_map/ppermute | solution.py:15
  9.3 1.5 %collective-permute-done.9 = bf16[512,512]{1,0:T(8,128)(2,1)S(1)} collective-permute-done((bf16[512,512]{1,0:T(8,128)(2,1)S(1)}, bf16[512,512]{1,0:T(8,128)(2,1)S(1)}, u32[]{:S(2)}, u32[]{:S(2)}) %collective-permute-start.9) | collective-permute-done | bytes 524320 | tf_op jit(solution)/shard_map/ppermute | solution.py:15
  10.9 1.1 pad_maximum_fusion
  12.0 0.0 all-gather.4.cloned.1.call-update
  12.0 0.0 all-gather.6.cloned.1.call-start
  12.1 0.1 subtract_convert_fusion
  12.2 1.4 collective-permute-start
  13.6 1.3 collective-permute-start.1
  14.9 8.7 %collective-permute-done.1 = bf16[512,256]{1,0:T(8,128)(2,1)S(1)} collective-permute-done((bf16[512,256]{1,0:T(8,128)(2,1)S(1)}, bf16[512,256]{1,0:T(8,128)(2,1)S(1)}, u32[]{:S(2)}, u32[]{:S(2)}) %collective-permute-start.1) | collective-permute-done | bytes 262176 | tf_op jit(solution)/shard_map/ppermute | solution.py:31
  23.6 1.9 %collective-permute-done.refs_6_ = bf16[512,512]{1,0:T(8,128)(2,1)S(1)} collective-permute-done((bf16[512,512]{1,0:T(8,128)(2,1)S(1)}, bf16[512,512]{1,0:T(8,128)(2,1)S(1)}, u32[]{:S(2)}, u32[]{:S(2)}) %collective-permute-start) | collective-permute-done | bytes 524320 | tf_op jit(solution)/shard_map/ppermute | solution.py:25
  25.5 1.3 collective-permute-start.4
  26.7 4.7 %collective-permute-start.3 = (bf16[512,512]{1,0:T(8,128)(2,1)S(1)}, bf16[512,512]{1,0:T(8,128)(2,1)S(1)}, u32[]{:S(2)}, u32[]{:S(2)}) collective-permute-start(bf16[512,512]{1,0:T(8,128)(2,1)S(1)} %collective-permute-done.refs_6_), channel_id=1, source_target_pairs={{0,6},{2,0},{4,2},{6,4},{1,7},{3,1},{5,3},{7,5},{8,14},{10,8},{12,... | collective-permute-start | bytes 1572872 | tf_op jit(solution)/shard_map/ppermute | solution.py:15
  31.4 2.8 %collective-permute-start.5 = (bf16[512,256]{1,0:T(8,128)(2,1)S(1)}, bf16[512,256]{1,0:T(8,128)(2,1)S(1)}, u32[]{:S(2)}, u32[]{:S(2)}) collective-permute-start(bf16[512,256]{1,0:T(8,128)(2,1)S(1)} %collective-permute-done.1), channel_id=1, source_target_pairs={{0,24},{4,28},{8,16},{12,20},{18,10},{22,14},{26,2},{30,6},{1,25},... | collective-permute-start | bytes 786440 | tf_op jit(solution)/shard_map/ppermute | solution.py:31
  34.2 3.8 %collective-permute-done.5 = bf16[512,256]{1,0:T(8,128)(2,1)S(1)} collective-permute-done((bf16[512,256]{1,0:T(8,128)(2,1)S(1)}, bf16[512,256]{1,0:T(8,128)(2,1)S(1)}, u32[]{:S(2)}, u32[]{:S(2)}) %collective-permute-start.5) | collective-permute-done | bytes 262176 | tf_op jit(solution)/shard_map/ppermute | solution.py:31
  38.0 3.1 %collective-permute-done.3.refs_4_ = bf16[512,512]{1,0:T(8,128)(2,1)S(1)} collective-permute-done((bf16[512,512]{1,0:T(8,128)(2,1)S(1)}, bf16[512,512]{1,0:T(8,128)(2,1)S(1)}, u32[]{:S(2)}, u32[]{:S(2)}) %collective-permute-start.3) | collective-permute-done | bytes 524320 | tf_op jit(solution)/shard_map/ppermute | solution.py:15
  41.1 3.2 %collective-permute-done.2.refs_3_ = bf16[512,512]{1,0:T(8,128)(2,1)} collective-permute-done((bf16[512,512]{1,0:T(8,128)(2,1)S(1)}, bf16[512,512]{1,0:T(8,128)(2,1)}, u32[]{:S(2)}, u32[]{:S(2)}) %collective-permute-start.2) | collective-permute-done | bytes 524320 | tf_op jit(solution)/shard_map/ppermute | solution.py:15
  44.4 0.3 collective-permute-start.7
  44.7 1.2 collective-permute-start.8
  45.8 1.5 collective-permute-start.6
  47.3 0.6 stack.31.refs_0_
  47.9 7.3 %collective-permute-done.7.refs_2_ = bf16[512,512]{1,0:T(8,128)(2,1)S(1)} collective-permute-done((bf16[512,512]{1,0:T(8,128)(2,1)S(1)}, bf16[512,512]{1,0:T(8,128)(2,1)S(1)}, u32[]{:S(2)}, u32[]{:S(2)}) %collective-permute-start.7) | collective-permute-done | bytes 524320 | tf_op jit(solution)/shard_map/ppermute | solution.py:15
  55.2 1.8 %collective-permute-done.8.refs_7_ = bf16[512,512]{1,0:T(8,128)(2,1)} collective-permute-done((bf16[512,512]{1,0:T(8,128)(2,1)}, bf16[512,512]{1,0:T(8,128)(2,1)}, u32[]{:S(2)}, u32[]{:S(2)}) %collective-permute-start.8) | collective-permute-done | bytes 524320 | tf_op jit(solution)/shard_map/ppermute | solution.py:15
  57.1 1.3 collective-permute-start.11
  58.4 0.2 collective-permute-start.10
  58.6 4.0 %all-gather.4.cloned.1.call-done.refs_8_ = bf16[2048,1024]{1,0:T(8,128)(2,1)} async-done(((bf16[512,1024]{1,0:T(8,128)(2,1)}), bf16[2048,1024]{1,0:T(8,128)(2,1)}) %all-gather.4.cloned.1.call-update) | async-done | bytes 4194320 | tf_op jit(solution)/shard_map/all_gather | solution.py:115
  62.6 1.2 collective-permute-start.12
  63.8 8.2 %shard_map.55 = (bf16[512,512]{1,0:T(8,128)(2,1)}, f32[512,512]{1,0:T(8,128)}, f32[512,1024]{1,0:T(8,128)}) custom-call(s32[7]{0:T(128)} %stack.31.refs_0_, bf16[512,512]{1,0:T(8,128)(2,1)} %copy-done.8, bf16[512,512]{1,0:T(8,128)(2,1)} %copy-done.7, bf16[512,512]{1,0:T(8,128)(2,1)} %collective-permute-done.2.refs_3_, bf16[512,512]{1,0:T(8,128)(2,1)} %copy-done.11, ...), custom_call_target="tpu_custom_call" | custom-call | flops 3758096384 | bytes 12582912 | tf_op jit(solution)/shard_map/pallas_call | solution.py:83
  72.1 0.8 pad_maximum_fusion.1
  72.9 1.3 fusion.26
  74.3 1.4 fusion.24
  75.7 0.3 maximum_add_fusion
  76.0 1.0 collective-permute-start.13
  77.0 0.1 collective-permute-start.14
  77.1 1.3 fusion.22
  78.4 1.3 fusion.20
  79.8 0.5 broadcast_select_fusion
  80.4 0.1 fusion.1
  80.4 2.5 %collective-permute-start.15 = (bf16[256,512]{1,0:T(8,128)(2,1)S(1)}, bf16[256,512]{1,0:T(8,128)(2,1)S(1)}, u32[]{:S(2)}, u32[]{:S(2)}) collective-permute-start(bf16[256,512]{1,0:T(8,128)(2,1)S(1)} %get-tuple-element.55), channel_id=1, source_target_pairs={{0,16},{16,0},{1,17},{17,1},{2,18},{18,2},{3,19},{19,3},{4,20},{20... | collective-permute-start | bytes 786440 | tf_op jit(solution)/shard_map/ppermute | solution.py:15
  82.9 0.1 convert_element_type.51
  83.0 6.5 %collective-permute-done.15 = bf16[256,512]{1,0:T(8,128)(2,1)S(1)} collective-permute-done((bf16[256,512]{1,0:T(8,128)(2,1)S(1)}, bf16[256,512]{1,0:T(8,128)(2,1)S(1)}, u32[]{:S(2)}, u32[]{:S(2)}) %collective-permute-start.15) | collective-permute-done | bytes 262176 | tf_op jit(solution)/shard_map/ppermute | solution.py:15
  89.5 2.5 %collective-permute-start.16 = (bf16[256,512]{1,0:T(8,128)(2,1)S(1)}, bf16[256,512]{1,0:T(8,128)(2,1)S(1)}, u32[]{:S(2)}, u32[]{:S(2)}) collective-permute-start(bf16[256,512]{1,0:T(8,128)(2,1)S(1)} %get-tuple-element.48), channel_id=1, source_target_pairs={{0,16},{16,0},{1,17},{17,1},{2,18},{18,2},{3,19},{19,3},{4,20},{20... | collective-permute-start | bytes 786440 | tf_op jit(solution)/shard_map/ppermute | solution.py:15
  92.0 0.1 fusion.3
  92.1 1.1 collective-permute-start.17
  93.1 0.5 collective-permute-start.18
  93.6 3.9 %collective-permute-done.16 = bf16[256,512]{1,0:T(8,128)(2,1)S(1)} collective-permute-done((bf16[256,512]{1,0:T(8,128)(2,1)S(1)}, bf16[256,512]{1,0:T(8,128)(2,1)S(1)}, u32[]{:S(2)}, u32[]{:S(2)}) %collective-permute-start.16) | collective-permute-done | bytes 262176 | tf_op jit(solution)/shard_map/ppermute | solution.py:15
  97.5 1.1 collective-permute-done.17
  98.6 0.1 fusion.2
  98.7 2.2 %collective-permute-start.20 = (bf16[256,512]{1,0:T(8,128)(2,1)S(1)}, bf16[256,512]{1,0:T(8,128)(2,1)S(1)}, u32[]{:S(2)}, u32[]{:S(2)}) collective-permute-start(bf16[256,512]{1,0:T(8,128)(2,1)S(1)} %fusion.2), channel_id=1, source_target_pairs={{0,96},{32,0},{64,32},{96,64},{1,97},{33,1},{65,33},{97,65},{2,98}... | collective-permute-start | bytes 786440 | tf_op jit(solution)/shard_map/ppermute | solution.py:15
  100.9 3.5 %collective-permute-done.20 = bf16[256,512]{1,0:T(8,128)(2,1)S(1)} collective-permute-done((bf16[256,512]{1,0:T(8,128)(2,1)S(1)}, bf16[256,512]{1,0:T(8,128)(2,1)S(1)}, u32[]{:S(2)}, u32[]{:S(2)}) %collective-permute-start.20) | collective-permute-done | bytes 262176 | tf_op jit(solution)/shard_map/ppermute | solution.py:15
  104.4 2.9 %collective-permute-start.22 = (bf16[256,512]{1,0:T(8,128)(2,1)S(1)}, bf16[256,512]{1,0:T(8,128)(2,1)S(1)}, u32[]{:S(2)}, u32[]{:S(2)}) collective-permute-start(bf16[256,512]{1,0:T(8,128)(2,1)S(1)} %collective-permute-done.20), channel_id=1, source_target_pairs={{0,96},{32,0},{64,32},{96,64},{1,97},{33,1},{65,33},{97,65},{2,98}... | collective-permute-start | bytes 786440 | tf_op jit(solution)/shard_map/ppermute | solution.py:15
  107.3 1.6 %fusion.16 = f32[2,512,512]{2,1,0:T(8,128)S(1)} fusion(bf16[8,1024,256]{2,1,0:T(8,128)(2,1)} %bitcast.46, s32[]{:T(128)S(6)} %select_n.90, s32[]{:T(128)S(6)} %select_n.87, bf16[256,512]{1,0:T(8,128)(2,1)S(1)} %fusion.2), kind=kOutput, calls=%fused_computation.29 | convolution fusion | flops 268435456 | bytes 2883592 | tf_op jit(solution)/shard_map/dot_general | solution.py:43
  108.9 1.5 %fusion.18 = f32[2,512,512]{2,1,0:T(8,128)S(1)} fusion(bf16[8,1024,256]{2,1,0:T(8,128)(2,1)} %bitcast.47, s32[]{:T(128)S(6)} %select_n.86, s32[]{:T(128)S(6)} %select_n.87, bf16[256,512]{1,0:T(8,128)(2,1)S(1)} %fusion.3), kind=kOutput, calls=%fused_computation.31 | convolution fusion | flops 268435456 | bytes 2883592 | tf_op jit(solution)/shard_map/dot_general | solution.py:43
  110.4 0.4 fusion.10
  110.9 0.4 fusion.8
  111.3 0.4 fusion.14
  111.8 0.4 fusion.12
  112.2 0.4 fusion.5
  112.6 0.2 collective-permute-done.21
  112.9 0.9 add_convert_fusion
  113.7 26.1 %all_to_all.9 = bf16[32,32,512]{2,1,0:T(8,128)(2,1)S(1)} all-to-all(bf16[32,32,512]{2,1,0:T(8,128)(2,1)S(1)} %bitcast.42), channel_id=1, replica_groups=mesh['y'=4,'xh'=2,'xl'=2,'z'=4,'core'=2] {'xh','xl','z','core'}, dimensions={0} | all-to-all | bytes 2097152 | tf_op jit(solution)/shard_map/all_to_all | solution.py:166
  139.8 0.2 convert_reduce_fusion
  140.1 0.1 copy.7
  140.2 0.9 add_convert_fusion.1
  (45 shorter events, 0.2 us)
Async XLA Ops:
  6.5 56.1 %all-gather.4.cloned.1.call-start = ((), (), s32[]{:S(2)}) async-start(), calls=%async_computation.1 | async-start | bytes 5242880 | tf_op jit(solution)/shard_map/all_gather | solution.py:115
  7.8 4.3 %copy-start.3 = (bf16[512,512]{1,0:T(8,128)(2,1)S(1)}, bf16[512,512]{1,0:T(8,128)(2,1)}, u32[]{:S(2)}) copy-start(bf16[512,512]{1,0:T(8,128)(2,1)} %param.6) | copy-start | bytes 1572868
  7.8 4.3 %copy-start.4 = (bf16[512,512]{1,0:T(8,128)(2,1)S(1)}, bf16[512,512]{1,0:T(8,128)(2,1)}, u32[]{:S(2)}) copy-start(bf16[512,512]{1,0:T(8,128)(2,1)} %param.5) | copy-start | bytes 1572868
  7.8 3.0 %collective-permute-start.9 = (bf16[512,512]{1,0:T(8,128)(2,1)S(1)}, bf16[512,512]{1,0:T(8,128)(2,1)S(1)}, u32[]{:S(2)}, u32[]{:S(2)}) collective-permute-start(bf16[512,512]{1,0:T(8,128)(2,1)S(1)} %get-tuple-element.57), channel_id=1, source_target_pairs={{0,1},{1,0},{2,3},{3,2},{4,5},{5,4},{6,7},{7,6},{8,9},{9,8},{10,11... | collective-permute-start | bytes 1572872 | tf_op jit(solution)/shard_map/ppermute | solution.py:15
  10.9 2.7 %copy-start.6 = (bf16[512,256]{1,0:T(8,128)(2,1)S(1)}, bf16[512,256]{1,0:T(8,128)(2,1)}, u32[]{:S(2)}) copy-start(bf16[512,256]{1,0:T(8,128)(2,1)} %param.8) | copy-start | bytes 786436
  12.0 95.3 %all-gather.6.cloned.1.call-start = ((), (), s32[]{:S(2)}) async-start(), calls=%async_computation.2 | async-start | bytes 4718592 | tf_op jit(solution)/shard_map/all_gather | solution.py:133
  12.2 13.2 %collective-permute-start = (bf16[512,512]{1,0:T(8,128)(2,1)S(1)}, bf16[512,512]{1,0:T(8,128)(2,1)S(1)}, u32[]{:S(2)}, u32[]{:S(2)}) collective-permute-start(bf16[512,512]{1,0:T(8,128)(2,1)S(1)} %subtract_convert_fusion), channel_id=1, source_target_pairs={{0,8},{2,24},{4,12},{6,28},{8,0},{10,16},{12,4},{14,20},{16,10},{1... | collective-permute-start | bytes 1572872 | tf_op jit(solution)/shard_map/ppermute | solution.py:25
  13.6 10.0 %collective-permute-start.1 = (bf16[512,256]{1,0:T(8,128)(2,1)S(1)}, bf16[512,256]{1,0:T(8,128)(2,1)S(1)}, u32[]{:S(2)}, u32[]{:S(2)}) collective-permute-start(bf16[512,256]{1,0:T(8,128)(2,1)S(1)} %copy-done.6), channel_id=1, source_target_pairs={{2,8},{6,12},{10,0},{14,4},{16,26},{20,30},{24,18},{28,22},{3,9},{... | collective-permute-start | bytes 786440 | tf_op jit(solution)/shard_map/ppermute | solution.py:31
  25.4 38.4 %copy-start.9 = (bf16[512,512]{1,0:T(8,128)(2,1)}, bf16[512,512]{1,0:T(8,128)(2,1)S(1)}, u32[]{:S(2)}) copy-start(bf16[512,512]{1,0:T(8,128)(2,1)S(1)} %collective-permute-done.refs_6_) | copy-start | bytes 1572868
  25.5 12.6 %collective-permute-start.4 = (bf16[512,512]{1,0:T(8,128)(2,1)S(1)}, bf16[512,512]{1,0:T(8,128)(2,1)S(1)}, u32[]{:S(2)}, u32[]{:S(2)}) collective-permute-start(bf16[512,512]{1,0:T(8,128)(2,1)S(1)} %collective-permute-done.refs_6_), channel_id=1, source_target_pairs={{0,8},{8,0},{1,9},{9,1},{2,10},{10,2},{3,11},{11,3},{4,12},{12,4},... | collective-permute-start | bytes 1572872 | tf_op jit(solution)/shard_map/ppermute | solution.py:15
  26.7 14.4 %collective-permute-start.3 = (bf16[512,512]{1,0:T(8,128)(2,1)S(1)}, bf16[512,512]{1,0:T(8,128)(2,1)S(1)}, u32[]{:S(2)}, u32[]{:S(2)}) collective-permute-start(bf16[512,512]{1,0:T(8,128)(2,1)S(1)} %collective-permute-done.refs_6_), channel_id=1, source_target_pairs={{0,6},{2,0},{4,2},{6,4},{1,7},{3,1},{5,3},{7,5},{8,14},{10,8},{12,... | collective-permute-start | bytes 1572872 | tf_op jit(solution)/shard_map/ppermute | solution.py:15
  31.4 13.0 %collective-permute-start.2 = (bf16[512,512]{1,0:T(8,128)(2,1)S(1)}, bf16[512,512]{1,0:T(8,128)(2,1)}, u32[]{:S(2)}, u32[]{:S(2)}) collective-permute-start(bf16[512,512]{1,0:T(8,128)(2,1)S(1)} %collective-permute-done.refs_6_), channel_id=1, source_target_pairs={{0,2},{2,4},{4,6},{6,0},{1,3},{3,5},{5,7},{7,1},{8,10},{10,12},{12... | collective-permute-start | bytes 1572872 | tf_op jit(solution)/shard_map/ppermute | solution.py:15
  31.4 6.6 %collective-permute-start.5 = (bf16[512,256]{1,0:T(8,128)(2,1)S(1)}, bf16[512,256]{1,0:T(8,128)(2,1)S(1)}, u32[]{:S(2)}, u32[]{:S(2)}) collective-permute-start(bf16[512,256]{1,0:T(8,128)(2,1)S(1)} %collective-permute-done.1), channel_id=1, source_target_pairs={{0,24},{4,28},{8,16},{12,20},{18,10},{22,14},{26,2},{30,6},{1,25},... | collective-permute-start | bytes 786440 | tf_op jit(solution)/shard_map/ppermute | solution.py:31
  38.0 19.0 %copy-start.10 = (bf16[512,512]{1,0:T(8,128)(2,1)}, bf16[512,512]{1,0:T(8,128)(2,1)S(1)}, u32[]{:S(2)}) copy-start(bf16[512,512]{1,0:T(8,128)(2,1)S(1)} %collective-permute-done.4.refs_5_) | copy-start | bytes 1572868
  41.1 3.5 %copy-start.11 = (bf16[512,512]{1,0:T(8,128)(2,1)}, bf16[512,512]{1,0:T(8,128)(2,1)S(1)}, u32[]{:S(2)}) copy-start(bf16[512,512]{1,0:T(8,128)(2,1)S(1)} %collective-permute-done.3.refs_4_) | copy-start | bytes 1572868
  44.4 10.8 %collective-permute-start.7 = (bf16[512,512]{1,0:T(8,128)(2,1)S(1)}, bf16[512,512]{1,0:T(8,128)(2,1)S(1)}, u32[]{:S(2)}, u32[]{:S(2)}) collective-permute-start(bf16[512,512]{1,0:T(8,128)(2,1)S(1)} %collective-permute-done.4.refs_5_), channel_id=1, source_target_pairs={{0,6},{2,0},{4,2},{6,4},{1,7},{3,1},{5,3},{7,5},{8,14},{10,8},{12,... | collective-permute-start | bytes 1572872 | tf_op jit(solution)/shard_map/ppermute | solution.py:15
  44.7 12.4 %collective-permute-start.8 = (bf16[512,512]{1,0:T(8,128)(2,1)}, bf16[512,512]{1,0:T(8,128)(2,1)}, u32[]{:S(2)}, u32[]{:S(2)}) collective-permute-start(bf16[512,512]{1,0:T(8,128)(2,1)} %collective-permute-done.2.refs_3_), channel_id=1, source_target_pairs={{0,2},{2,4},{4,6},{6,0},{1,3},{3,5},{5,7},{7,1},{8,10},{10,12},{12... | collective-permute-start | bytes 1572872 | tf_op jit(solution)/shard_map/ppermute | solution.py:15
  45.8 11.2 %collective-permute-start.6 = (bf16[512,512]{1,0:T(8,128)(2,1)}, bf16[512,512]{1,0:T(8,128)(2,1)S(1)}, u32[]{:S(2)}, u32[]{:S(2)}) collective-permute-start(bf16[512,512]{1,0:T(8,128)(2,1)} %collective-permute-done.2.refs_3_), channel_id=1, source_target_pairs={{0,8},{8,0},{1,9},{9,1},{2,10},{10,2},{3,11},{11,3},{4,12},{12,4},... | collective-permute-start | bytes 1572872 | tf_op jit(solution)/shard_map/ppermute | solution.py:15
  55.2 8.6 %copy-start.7 = (bf16[512,512]{1,0:T(8,128)(2,1)}, bf16[512,512]{1,0:T(8,128)(2,1)S(1)}, u32[]{:S(2)}) copy-start(bf16[512,512]{1,0:T(8,128)(2,1)S(1)} %collective-permute-done.7.refs_2_) | copy-start | bytes 1572868
  57.0 6.8 %copy-start.8 = (bf16[512,512]{1,0:T(8,128)(2,1)}, bf16[512,512]{1,0:T(8,128)(2,1)S(1)}, u32[]{:S(2)}) copy-start(bf16[512,512]{1,0:T(8,128)(2,1)S(1)} %collective-permute-done.6.refs_1_) | copy-start | bytes 1572868
  57.1 14.9 %collective-permute-start.11 = (bf16[256,512]{1,0:T(8,128)(2,1)S(1)}, bf16[256,512]{1,0:T(8,128)(2,1)S(1)}, u32[]{:S(2)}, u32[]{:S(2)}) collective-permute-start(bf16[256,512]{1,0:T(8,128)(2,1)S(1)} %slice.33), channel_id=1, source_target_pairs={{0,6},{2,0},{4,2},{6,4},{1,7},{3,1},{5,3},{7,5},{8,14},{10,8},{12,... | collective-permute-start | bytes 786440 | tf_op jit(solution)/shard_map/ppermute | solution.py:15
  58.4 13.6 %collective-permute-start.10 = (bf16[256,512]{1,0:T(8,128)(2,1)S(1)}, bf16[256,512]{1,0:T(8,128)(2,1)S(1)}, u32[]{:S(2)}, u32[]{:S(2)}) collective-permute-start(bf16[256,512]{1,0:T(8,128)(2,1)S(1)} %slice.32), channel_id=1, source_target_pairs={{0,2},{2,4},{4,6},{6,0},{1,3},{3,5},{5,7},{7,1},{8,10},{10,12},{12... | collective-permute-start | bytes 786440 | tf_op jit(solution)/shard_map/ppermute | solution.py:15
  62.6 9.4 %collective-permute-start.12 = (bf16[512,256]{1,0:T(8,128)(2,1)S(1)}, bf16[512,256]{1,0:T(8,128)(2,1)S(1)}, u32[]{:S(2)}, u32[]{:S(2)}) collective-permute-start(bf16[512,256]{1,0:T(8,128)(2,1)S(1)} %broadcast_select_fusion.1), channel_id=1, source_target_pairs={{0,8},{8,0},{1,9},{9,1},{2,10},{10,2},{3,11},{11,3},{4,12},{12,4},... | collective-permute-start | bytes 786440 | tf_op jit(solution)/shard_map/ppermute | solution.py:15
  72.0 3.6 %copy-start.1 = (f32[512,1024]{1,0:T(8,128)S(1)}, f32[512,1024]{1,0:T(8,128)}, u32[]{:S(2)}) copy-start(f32[512,1024]{1,0:T(8,128)} %get-tuple-element.38) | copy-start | bytes 6291460
  74.3 1.7 %copy-start.12 = (bf16[512,512]{1,0:T(8,128)(2,1)S(1)}, bf16[512,512]{1,0:T(8,128)(2,1)}, u32[]{:S(2)}) copy-start(bf16[512,512]{1,0:T(8,128)(2,1)} %get-tuple-element.43) | copy-start | bytes 1572868
  75.7 4.1 %copy-start.2 = (f32[512,512]{1,0:T(8,128)S(1)}, f32[512,512]{1,0:T(8,128)}, u32[]{:S(2)}) copy-start(f32[512,512]{1,0:T(8,128)} %get-tuple-element.36) | copy-start | bytes 3145732
  76.0 3.8 %collective-permute-start.13 = (bf16[512,512]{1,0:T(8,128)(2,1)S(1)}, bf16[512,512]{1,0:T(8,128)(2,1)S(1)}, u32[]{:S(2)}, u32[]{:S(2)}) collective-permute-start(bf16[512,512]{1,0:T(8,128)(2,1)S(1)} %copy-done.12), channel_id=1, source_target_pairs={{0,1},{1,0},{2,3},{3,2},{4,5},{5,4},{6,7},{7,6},{8,9},{9,8},{10,11... | collective-permute-start | bytes 1572872 | tf_op jit(solution)/shard_map/ppermute | solution.py:15
  77.0 2.8 %collective-permute-start.14 = (bf16[512,512]{1,0:T(8,128)(2,1)S(1)}, bf16[512,512]{1,0:T(8,128)(2,1)S(1)}, u32[]{:S(2)}, u32[]{:S(2)}) collective-permute-start(bf16[512,512]{1,0:T(8,128)(2,1)S(1)} %maximum_add_fusion), channel_id=1, source_target_pairs={{0,1},{1,0},{2,3},{3,2},{4,5},{5,4},{6,7},{7,6},{8,9},{9,8},{10,11... | collective-permute-start | bytes 1572872 | tf_op jit(solution)/shard_map/ppermute | solution.py:15
  79.8 3.1 %copy-start.5 = (bf16[32,8192]{1,0:T(8,128)(2,1)S(1)}, bf16[32,8192]{1,0:T(8,128)(2,1)}, u32[]{:S(2)}) copy-start(bf16[32,8192]{1,0:T(8,128)(2,1)} %param.9) | copy-start | bytes 1572868
  80.4 9.1 %collective-permute-start.15 = (bf16[256,512]{1,0:T(8,128)(2,1)S(1)}, bf16[256,512]{1,0:T(8,128)(2,1)S(1)}, u32[]{:S(2)}, u32[]{:S(2)}) collective-permute-start(bf16[256,512]{1,0:T(8,128)(2,1)S(1)} %get-tuple-element.55), channel_id=1, source_target_pairs={{0,16},{16,0},{1,17},{17,1},{2,18},{18,2},{3,19},{19,3},{4,20},{20... | collective-permute-start | bytes 786440 | tf_op jit(solution)/shard_map/ppermute | solution.py:15
  89.5 8.1 %collective-permute-start.16 = (bf16[256,512]{1,0:T(8,128)(2,1)S(1)}, bf16[256,512]{1,0:T(8,128)(2,1)S(1)}, u32[]{:S(2)}, u32[]{:S(2)}) collective-permute-start(bf16[256,512]{1,0:T(8,128)(2,1)S(1)} %get-tuple-element.48), channel_id=1, source_target_pairs={{0,16},{16,0},{1,17},{17,1},{2,18},{18,2},{3,19},{19,3},{4,20},{20... | collective-permute-start | bytes 786440 | tf_op jit(solution)/shard_map/ppermute | solution.py:15
  92.1 6.5 %collective-permute-start.17 = (bf16[256,512]{1,0:T(8,128)(2,1)S(1)}, bf16[256,512]{1,0:T(8,128)(2,1)S(1)}, u32[]{:S(2)}, u32[]{:S(2)}) collective-permute-start(bf16[256,512]{1,0:T(8,128)(2,1)S(1)} %fusion.3), channel_id=1, source_target_pairs={{0,96},{32,0},{64,32},{96,64},{1,97},{33,1},{65,33},{97,65},{2,98}... | collective-permute-start | bytes 786440 | tf_op jit(solution)/shard_map/ppermute | solution.py:15
  93.1 7.7 %collective-permute-start.18 = (bf16[256,512]{1,0:T(8,128)(2,1)S(1)}, bf16[256,512]{1,0:T(8,128)(2,1)S(1)}, u32[]{:S(2)}, u32[]{:S(2)}) collective-permute-start(bf16[256,512]{1,0:T(8,128)(2,1)S(1)} %fusion.3), channel_id=1, source_target_pairs={{0,32},{32,64},{64,96},{96,0},{1,33},{33,65},{65,97},{97,1},{2,34}... | collective-permute-start | bytes 786440 | tf_op jit(solution)/shard_map/ppermute | solution.py:15
  98.7 5.7 %collective-permute-start.20 = (bf16[256,512]{1,0:T(8,128)(2,1)S(1)}, bf16[256,512]{1,0:T(8,128)(2,1)S(1)}, u32[]{:S(2)}, u32[]{:S(2)}) collective-permute-start(bf16[256,512]{1,0:T(8,128)(2,1)S(1)} %fusion.2), channel_id=1, source_target_pairs={{0,96},{32,0},{64,32},{96,64},{1,97},{33,1},{65,33},{97,65},{2,98}... | collective-permute-start | bytes 786440 | tf_op jit(solution)/shard_map/ppermute | solution.py:15
  100.9 10.9 %collective-permute-start.19 = (bf16[256,512]{1,0:T(8,128)(2,1)S(1)}, bf16[256,512]{1,0:T(8,128)(2,1)S(1)}, u32[]{:S(2)}, u32[]{:S(2)}) collective-permute-start(bf16[256,512]{1,0:T(8,128)(2,1)S(1)} %fusion.2), channel_id=1, source_target_pairs={{0,32},{32,64},{64,96},{96,0},{1,33},{33,65},{65,97},{97,1},{2,34}... | collective-permute-start | bytes 786440 | tf_op jit(solution)/shard_map/ppermute | solution.py:15
  100.9 12.0 %collective-permute-start.21 = (bf16[256,512]{1,0:T(8,128)(2,1)S(1)}, bf16[256,512]{1,0:T(8,128)(2,1)S(1)}, u32[]{:S(2)}, u32[]{:S(2)}) collective-permute-start(bf16[256,512]{1,0:T(8,128)(2,1)S(1)} %collective-permute-done.18), channel_id=1, source_target_pairs={{0,32},{32,64},{64,96},{96,0},{1,33},{33,65},{65,97},{97,1},{2,34}... | collective-permute-start | bytes 786440 | tf_op jit(solution)/shard_map/ppermute | solution.py:15
  104.4 7.8 %collective-permute-start.22 = (bf16[256,512]{1,0:T(8,128)(2,1)S(1)}, bf16[256,512]{1,0:T(8,128)(2,1)S(1)}, u32[]{:S(2)}, u32[]{:S(2)}) collective-permute-start(bf16[256,512]{1,0:T(8,128)(2,1)S(1)} %collective-permute-done.20), channel_id=1, source_target_pairs={{0,96},{32,0},{64,32},{96,64},{1,97},{33,1},{65,33},{97,65},{2,98}... | collective-permute-start | bytes 786440 | tf_op jit(solution)/shard_map/ppermute | solution.py:15
  107.3 3.1 %copy-start = (bf16[8192,256]{1,0:T(8,128)(2,1)S(1)}, bf16[8192,256]{1,0:T(8,128)(2,1)}, u32[]{:S(2)}) copy-start(bf16[8192,256]{1,0:T(8,128)(2,1)} %all-gather.6.cloned.1.call-done) | copy-start | bytes 12582916
Sparse Core Ops, SparseCore 0:
  12.1 50.4 all-gather.3
  73.0 33.0 all-gather.5

commit v10 on v9

--- a/solution.py
+++ b/solution.py
@@ -121,8 +121,7 @@
     am, ap, b2 = together(shift(bm, "xl", 1), shift(a, "z", -1), shift(bm, "z", 1))
     same = (z & 1) == xh
     turned = jnp.where(same, output_factor, moves)
-    far = [shift(am[:half], "z", 1), shift(ap[half:], "z", -1)]
-    *far, part = together(*far, shift(after(turned, factor), "xl", 1))
+    a2, part = together(shift(am, "z", 1), shift(after(turned, factor), "xl", 1))
 
     def place(dxl, dz):
         return (xl ^ dxl) * 2 + (((z + dz) & 3) >> 1)
@@ -132,13 +131,14 @@
     part = jnp.concatenate([after(part, own), turned], axis=0)
     left = lax.all_gather(part, ("core", "z"), axis=0)
 
-    def more(side):
+    def more(v, side):
         right = lax.dynamic_slice(factor, (place(0, 2) * depth, side * cols), (depth, cols))
-        last = jnp.concatenate([dot(v, right) for v in far], axis=0)
-        return even[:, side * cols : (side + 1) * cols] + last
+        return even[:, side * cols : (side + 1) * cols] + dot(v, right)
 
-    theirs = [after(theirs, more(1)), more(1).astype(BF16)]
-    odd, even = [v + shift(w, "core", 1).astype(F32) for v, w in zip((own, more(0)), theirs)]
+    even_theirs = more(a2, 1).astype(BF16)
+    theirs = [after(theirs, even_theirs), even_theirs]
+    own = [own, *together(more(after(a2, even_theirs), 0))]
+    odd, even = [v + shift(w, "core", 1).astype(F32) for v, w in zip(own, theirs)]
     top, rest = slice(half), slice(half, rows)
     first, second = [jnp.where(same, odd[r], even[r]).astype(BF16) for r in (top, rest)]
     first = shift(first, "xh", 1)

time: 148 us -> 145 us (0.980)
  blocking collectives: 26.1 us -> 23.9 us
  matrix products: 11.5 us -> 9.49 us
    all_to_all x1, blocking collectives: 26.1 us -> 23.9 us  [body(): lax.all_to_all(penalty, ('xh',) + COL, split_axis=0, concat_axis=0, tiled...]
    dot_general x12 -> x10, matrix products: 11.5 us -> 9.49 us  [dot(): lax.dot_general(a, b, (((a.ndim - 1,), (0,)), ((), ())), preferred_elemen...]
    all_gather x1, waiting for transfers between devices: 3.99 us -> 5.61 us  [body(): factor = lax.all_gather(pair, 'y', axis=0, tiled=True)]
    ppermute x20 -> x19, starting transfers between devices: 25.9 us -> 26.5 us  [shift(): return lax.ppermute(v, axis, [(i, (i + by) % n) for i in range(n)])]
    ppermute x20 -> x19, waiting for transfers between devices: 32.2 us -> 31.8 us  [shift(): return lax.ppermute(v, axis, [(i, (i + by) % n) for i in range(n)])]
  transfers between devices with their start and end apart: 25 -> 24, of which waited for: 14 -> 14; matrix products, arithmetic and copies ran while one was open for 8% -> 7% of each run, Pallas kernels for 6% -> 6%
where the time goes in v10:
time: 145 us
  waiting for transfers between devices  51.8 us (36%)
  starting transfers between devices  32.1 us (22%)
  blocking collectives  23.9 us (16%)
  between operations  13.7 us (9%)
  matrix products  9.49 us (7%)
  Pallas kernels  8.19 us (6%)
  other arithmetic  3.89 us (3%)
  local copies, waits for them, and re-layouts  1.98 us (1%)
    ppermute x19, waiting for transfers between devices, shift(): return lax.ppermute(v, axis, [(i, (i + by) % n) for i in range(n)])  31.8 us
    ppermute x19, starting transfers between devices, shift(): return lax.ppermute(v, axis, [(i, (i + by) % n) for i in range(n)])  26.5 us
    all_to_all x1, blocking collectives, body(): lax.all_to_all(penalty, ('xh',) + COL, split_axis=0, concat_axis=0, tiled...  23.9 us
    ppermute x2, waiting for transfers between devices, part_ways(): lax.ppermute(v, ('xh', 'xl', 'z'), [tuple(((q[0] * 2 + q[1]) * 4 + q[2] f...  12.5 us
    dot_general x10, matrix products, dot(): lax.dot_general(a, b, (((a.ndim - 1,), (0,)), ((), ())), preferred_elemen...  9.49 us
    pallas_call x1, Pallas kernels, early(): pl.pallas_call(lambda *refs: early_kernel(n, m, *refs), out_shape=(jax.Sh...  8.19 us
    all_gather x1, waiting for transfers between devices, body(): factor = lax.all_gather(pair, 'y', axis=0, tiled=True)  5.61 us
    ppermute x2, starting transfers between devices, part_ways(): lax.ppermute(v, ('xh', 'xl', 'z'), [tuple(((q[0] * 2 + q[1]) * 4 + q[2] f...  4.1 us
  transfers between devices with their start and end apart: 24, of which 14 were waited for; matrix products, arithmetic and copies ran while one was open for 7% of the time, Pallas kernels for 6%

profile of v10, /device:TPU:1, one launch (start us, length us, event | category | flops | bytes accessed | tf_op | source)
XLA Modules:
  0.0 145.1 jit_solution(9038030554169168679)
XLA Ops:
  6.5 1.3 constant_dynamic-slice_fusion.1
  7.8 0.0 copy-start.3
  7.8 0.0 copy-start.4
  7.8 1.5 %collective-permute-start.9 = (bf16[512,512]{1,0:T(8,128)(2,1)S(1)}, bf16[512,512]{1,0:T(8,128)(2,1)S(1)}, u32[]{:S(2)}, u32[]{:S(2)}) collective-permute-start(bf16[512,512]{1,0:T(8,128)(2,1)S(1)} %get-tuple-element.57), channel_id=1, source_target_pairs={{0,1},{1,0},{2,3},{3,2},{4,5},{5,4},{6,7},{7,6},{8,9},{9,8},{10,11... | collective-permute-start | bytes 1572872 | tf_op jit(solution)/shard_map/ppermute | solution.py:15
  9.3 1.5 %collective-permute-done.9 = bf16[512,512]{1,0:T(8,128)(2,1)S(1)} collective-permute-done((bf16[512,512]{1,0:T(8,128)(2,1)S(1)}, bf16[512,512]{1,0:T(8,128)(2,1)S(1)}, u32[]{:S(2)}, u32[]{:S(2)}) %collective-permute-start.9) | collective-permute-done | bytes 524320 | tf_op jit(solution)/shard_map/ppermute | solution.py:15
  10.9 1.1 pad_maximum_fusion
  12.0 0.0 all-gather.4.cloned.1.call-update
  12.0 0.0 all-gather.6.cloned.1.call-start
  12.1 0.1 subtract_convert_fusion
  12.2 1.4 collective-permute-start
  13.6 1.3 collective-permute-start.1
  14.9 8.7 %collective-permute-done.1 = bf16[512,256]{1,0:T(8,128)(2,1)S(1)} collective-permute-done((bf16[512,256]{1,0:T(8,128)(2,1)S(1)}, bf16[512,256]{1,0:T(8,128)(2,1)S(1)}, u32[]{:S(2)}, u32[]{:S(2)}) %collective-permute-start.1) | collective-permute-done | bytes 262176 | tf_op jit(solution)/shard_map/ppermute | solution.py:31
  23.6 1.9 %collective-permute-done.refs_6_ = bf16[512,512]{1,0:T(8,128)(2,1)S(1)} collective-permute-done((bf16[512,512]{1,0:T(8,128)(2,1)S(1)}, bf16[512,512]{1,0:T(8,128)(2,1)S(1)}, u32[]{:S(2)}, u32[]{:S(2)}) %collective-permute-start) | collective-permute-done | bytes 524320 | tf_op jit(solution)/shard_map/ppermute | solution.py:25
  25.5 1.3 collective-permute-start.4
  26.8 4.7 %collective-permute-start.3 = (bf16[512,512]{1,0:T(8,128)(2,1)S(1)}, bf16[512,512]{1,0:T(8,128)(2,1)S(1)}, u32[]{:S(2)}, u32[]{:S(2)}) collective-permute-start(bf16[512,512]{1,0:T(8,128)(2,1)S(1)} %collective-permute-done.refs_6_), channel_id=1, source_target_pairs={{0,6},{2,0},{4,2},{6,4},{1,7},{3,1},{5,3},{7,5},{8,14},{10,8},{12,... | collective-permute-start | bytes 1572872 | tf_op jit(solution)/shard_map/ppermute | solution.py:15
  31.4 2.8 %collective-permute-start.5 = (bf16[512,256]{1,0:T(8,128)(2,1)S(1)}, bf16[512,256]{1,0:T(8,128)(2,1)S(1)}, u32[]{:S(2)}, u32[]{:S(2)}) collective-permute-start(bf16[512,256]{1,0:T(8,128)(2,1)S(1)} %collective-permute-done.1), channel_id=1, source_target_pairs={{0,24},{4,28},{8,16},{12,20},{18,10},{22,14},{26,2},{30,6},{1,25},... | collective-permute-start | bytes 786440 | tf_op jit(solution)/shard_map/ppermute | solution.py:31
  34.3 3.8 %collective-permute-done.5 = bf16[512,256]{1,0:T(8,128)(2,1)S(1)} collective-permute-done((bf16[512,256]{1,0:T(8,128)(2,1)S(1)}, bf16[512,256]{1,0:T(8,128)(2,1)S(1)}, u32[]{:S(2)}, u32[]{:S(2)}) %collective-permute-start.5) | collective-permute-done | bytes 262176 | tf_op jit(solution)/shard_map/ppermute | solution.py:31
  38.1 0.0 collective-permute-done.4.refs_5_
  38.1 3.1 %collective-permute-done.3.refs_4_ = bf16[512,512]{1,0:T(8,128)(2,1)S(1)} collective-permute-done((bf16[512,512]{1,0:T(8,128)(2,1)S(1)}, bf16[512,512]{1,0:T(8,128)(2,1)S(1)}, u32[]{:S(2)}, u32[]{:S(2)}) %collective-permute-start.3) | collective-permute-done | bytes 524320 | tf_op jit(solution)/shard_map/ppermute | solution.py:15
  41.2 3.2 %collective-permute-done.2.refs_3_ = bf16[512,512]{1,0:T(8,128)(2,1)S(1)} collective-permute-done((bf16[512,512]{1,0:T(8,128)(2,1)S(1)}, bf16[512,512]{1,0:T(8,128)(2,1)S(1)}, u32[]{:S(2)}, u32[]{:S(2)}) %collective-permute-start.2) | collective-permute-done | bytes 524320 | tf_op jit(solution)/shard_map/ppermute | solution.py:15
  44.4 0.3 collective-permute-start.7
  44.7 1.1 collective-permute-start.8
  45.9 1.5 %collective-permute-start.6 = (bf16[512,512]{1,0:T(8,128)(2,1)S(1)}, bf16[512,512]{1,0:T(8,128)(2,1)}, u32[]{:S(2)}, u32[]{:S(2)}) collective-permute-start(bf16[512,512]{1,0:T(8,128)(2,1)S(1)} %collective-permute-done.2.refs_3_), channel_id=1, source_target_pairs={{0,8},{8,0},{1,9},{9,1},{2,10},{10,2},{3,11},{11,3},{4,12},{12,4},... | collective-permute-start | bytes 1572872 | tf_op jit(solution)/shard_map/ppermute | solution.py:15
  47.3 0.6 stack.31.refs_0_
  47.9 7.4 %collective-permute-done.7.refs_2_ = bf16[512,512]{1,0:T(8,128)(2,1)S(1)} collective-permute-done((bf16[512,512]{1,0:T(8,128)(2,1)S(1)}, bf16[512,512]{1,0:T(8,128)(2,1)S(1)}, u32[]{:S(2)}, u32[]{:S(2)}) %collective-permute-start.7) | collective-permute-done | bytes 524320 | tf_op jit(solution)/shard_map/ppermute | solution.py:15
  55.3 1.6 %collective-permute-done.8.refs_7_ = bf16[512,512]{1,0:T(8,128)(2,1)} collective-permute-done((bf16[512,512]{1,0:T(8,128)(2,1)S(1)}, bf16[512,512]{1,0:T(8,128)(2,1)}, u32[]{:S(2)}, u32[]{:S(2)}) %collective-permute-start.8) | collective-permute-done | bytes 524320 | tf_op jit(solution)/shard_map/ppermute | solution.py:15
  56.9 0.1 collective-permute-start.10
  57.0 5.6 %all-gather.4.cloned.1.call-done.refs_8_ = bf16[2048,1024]{1,0:T(8,128)(2,1)} async-done(((bf16[512,1024]{1,0:T(8,128)(2,1)}), bf16[2048,1024]{1,0:T(8,128)(2,1)}) %all-gather.4.cloned.1.call-update) | async-done | bytes 4194320 | tf_op jit(solution)/shard_map/all_gather | solution.py:115
  62.6 1.2 collective-permute-start.11
  63.8 8.2 %shard_map.55 = (bf16[512,512]{1,0:T(8,128)(2,1)}, f32[512,512]{1,0:T(8,128)}, f32[512,1024]{1,0:T(8,128)}) custom-call(s32[7]{0:T(128)} %stack.31.refs_0_, bf16[512,512]{1,0:T(8,128)(2,1)} %collective-permute-done.6.refs_1_, bf16[512,512]{1,0:T(8,128)(2,1)} %copy-done.11, bf16[512,512]{1,0:T(8,128)(2,1)} %copy-done.10, bf16[512,512]{1,0:T(8,128)(2,1)} %copy-done.9, ...), custom_call_target="tpu_custom_call" | custom-call | flops 3758096384 | bytes 12582912 | tf_op jit(solution)/shard_map/pallas_call | solution.py:83
  72.1 0.8 pad_maximum_fusion.1
  72.9 0.0 all-gather.6.cloned.1.call-update
  72.9 1.9 %fusion = bf16[512,512]{1,0:T(8,128)(2,1)S(1)} fusion(bf16[512,512]{1,0:T(8,128)(2,1)S(1)} %collective-permute-done.10, f32[512,1024]{1,0:T(8,128)} %get-tuple-element.38, bf16[2048,1024]{1,0:T(8,128)(2,1)} %all-gather.4.cloned.1.call-done.refs_8_, s32[]{:T(128)S(6)} %select_n.83), kind=kOutput, calls=%fused_computation.4 | convolution fusion | flops 268959744 | bytes 2621444 | tf_op jit(solution)/shard_map/dot_general | solution.py:43
  74.9 1.0 collective-permute-start.12
  75.9 0.1 collective-permute-start.13
  76.0 1.5 %convolution_add_fusion = f32[512,512]{1,0:T(8,128)S(1)} fusion(bf16[512,512]{1,0:T(8,128)(2,1)S(1)} %collective-permute-done.10, f32[512,1024]{1,0:T(8,128)S(1)} %copy-done.1, bf16[2048,1024]{1,0:T(8,128)(2,1)} %all-gather.4.cloned.1.call-done.refs_8_, s32[]{:T(128)S(6)} %select_n.83), kind=kOutput, calls=%fused_computation.2 | convolution fusion | flops 268697600 | bytes 3145732 | tf_op jit(solution)/shard_map/dot_general | solution.py:43
  77.5 0.0 copy-start.5
  77.5 0.7 collective-permute-done.13
  78.2 0.4 broadcast_select_fusion
  78.6 0.1 fusion.1
  78.6 2.5 %collective-permute-start.14 = (bf16[256,512]{1,0:T(8,128)(2,1)S(1)}, bf16[256,512]{1,0:T(8,128)(2,1)S(1)}, u32[]{:S(2)}, u32[]{:S(2)}) collective-permute-start(bf16[256,512]{1,0:T(8,128)(2,1)S(1)} %get-tuple-element.55), channel_id=1, source_target_pairs={{0,16},{16,0},{1,17},{17,1},{2,18},{18,2},{3,19},{19,3},{4,20},{20... | collective-permute-start | bytes 786440 | tf_op jit(solution)/shard_map/ppermute | solution.py:15
  81.1 0.1 convert_element_type.51
  81.2 6.5 %collective-permute-done.14 = bf16[256,512]{1,0:T(8,128)(2,1)S(1)} collective-permute-done((bf16[256,512]{1,0:T(8,128)(2,1)S(1)}, bf16[256,512]{1,0:T(8,128)(2,1)S(1)}, u32[]{:S(2)}, u32[]{:S(2)}) %collective-permute-start.14) | collective-permute-done | bytes 262176 | tf_op jit(solution)/shard_map/ppermute | solution.py:15
  87.8 2.4 %collective-permute-start.15 = (bf16[256,512]{1,0:T(8,128)(2,1)S(1)}, bf16[256,512]{1,0:T(8,128)(2,1)S(1)}, u32[]{:S(2)}, u32[]{:S(2)}) collective-permute-start(bf16[256,512]{1,0:T(8,128)(2,1)S(1)} %get-tuple-element.48), channel_id=1, source_target_pairs={{0,16},{16,0},{1,17},{17,1},{2,18},{18,2},{3,19},{19,3},{4,20},{20... | collective-permute-start | bytes 786440 | tf_op jit(solution)/shard_map/ppermute | solution.py:15
  90.2 0.1 fusion.3
  90.2 2.1 %collective-permute-start.16 = (bf16[256,512]{1,0:T(8,128)(2,1)S(1)}, bf16[256,512]{1,0:T(8,128)(2,1)S(1)}, u32[]{:S(2)}, u32[]{:S(2)}) collective-permute-start(bf16[256,512]{1,0:T(8,128)(2,1)S(1)} %fusion.3), channel_id=1, source_target_pairs={{0,96},{32,0},{64,32},{96,64},{1,97},{33,1},{65,33},{97,65},{2,98}... | collective-permute-start | bytes 786440 | tf_op jit(solution)/shard_map/ppermute | solution.py:15
  92.3 3.5 %collective-permute-done.15 = bf16[256,512]{1,0:T(8,128)(2,1)S(1)} collective-permute-done((bf16[256,512]{1,0:T(8,128)(2,1)S(1)}, bf16[256,512]{1,0:T(8,128)(2,1)S(1)}, u32[]{:S(2)}, u32[]{:S(2)}) %collective-permute-start.15) | collective-permute-done | bytes 262176 | tf_op jit(solution)/shard_map/ppermute | solution.py:15
  95.9 0.9 collective-permute-done.16
  96.7 0.1 fusion.2
  96.8 3.3 %collective-permute-start.19 = (bf16[256,512]{1,0:T(8,128)(2,1)S(1)}, bf16[256,512]{1,0:T(8,128)(2,1)S(1)}, u32[]{:S(2)}, u32[]{:S(2)}) collective-permute-start(bf16[256,512]{1,0:T(8,128)(2,1)S(1)} %fusion.2), channel_id=1, source_target_pairs={{0,96},{32,0},{64,32},{96,64},{1,97},{33,1},{65,33},{97,65},{2,98}... | collective-permute-start | bytes 786440 | tf_op jit(solution)/shard_map/ppermute | solution.py:15
  100.1 3.3 %collective-permute-done.19 = bf16[256,512]{1,0:T(8,128)(2,1)S(1)} collective-permute-done((bf16[256,512]{1,0:T(8,128)(2,1)S(1)}, bf16[256,512]{1,0:T(8,128)(2,1)S(1)}, u32[]{:S(2)}, u32[]{:S(2)}) %collective-permute-start.19) | collective-permute-done | bytes 262176 | tf_op jit(solution)/shard_map/ppermute | solution.py:15
  103.4 3.5 %collective-permute-start.21 = (bf16[256,512]{1,0:T(8,128)(2,1)S(1)}, bf16[256,512]{1,0:T(8,128)(2,1)S(1)}, u32[]{:S(2)}, u32[]{:S(2)}) collective-permute-start(bf16[256,512]{1,0:T(8,128)(2,1)S(1)} %collective-permute-done.19), channel_id=1, source_target_pairs={{0,96},{32,0},{64,32},{96,64},{1,97},{33,1},{65,33},{97,65},{2,98}... | collective-permute-start | bytes 786440 | tf_op jit(solution)/shard_map/ppermute | solution.py:15
  106.9 1.6 %fusion.16 = f32[2,512,512]{2,1,0:T(8,128)S(1)} fusion(bf16[8,1024,256]{2,1,0:T(8,128)(2,1)} %bitcast.44, s32[]{:T(128)S(6)} %select_n.89, s32[]{:T(128)S(6)} %select_n.86, bf16[256,512]{1,0:T(8,128)(2,1)S(1)} %fusion.2), kind=kOutput, calls=%fused_computation.30 | convolution fusion | flops 268435456 | bytes 2883592 | tf_op jit(solution)/shard_map/dot_general | solution.py:43
  108.6 1.5 %fusion.18 = f32[2,512,512]{2,1,0:T(8,128)S(1)} fusion(bf16[8,1024,256]{2,1,0:T(8,128)(2,1)} %bitcast.45, s32[]{:T(128)S(6)} %select_n.85, s32[]{:T(128)S(6)} %select_n.86, bf16[256,512]{1,0:T(8,128)(2,1)S(1)} %fusion.3), kind=kOutput, calls=%fused_computation.32 | convolution fusion | flops 268435456 | bytes 2883592 | tf_op jit(solution)/shard_map/dot_general | solution.py:43
  110.1 0.4 fusion.10
  110.5 0.4 fusion.8
  110.9 0.4 fusion.14
  111.4 0.4 fusion.12
  111.8 0.4 fusion.5
  112.2 0.8 add_convert_fusion
  113.1 23.9 %all_to_all.9 = bf16[32,32,512]{2,1,0:T(8,128)(2,1)S(1)} all-to-all(bf16[32,32,512]{2,1,0:T(8,128)(2,1)S(1)} %bitcast.40), channel_id=1, replica_groups=mesh['y'=4,'xh'=2,'xl'=2,'z'=4,'core'=2] {'xh','xl','z','core'}, dimensions={0} | all-to-all | bytes 2097152 | tf_op jit(solution)/shard_map/all_to_all | solution.py:166
  137.0 0.2 convert_reduce_fusion
  137.3 0.1 copy.7
  137.4 0.9 add_convert_fusion.1
  (38 shorter events, 0.1 us)
Async XLA Ops:
  6.5 56.1 %all-gather.4.cloned.1.call-start = ((), (), s32[]{:S(2)}) async-start(), calls=%async_computation.1 | async-start | bytes 5242880 | tf_op jit(solution)/shard_map/all_gather | solution.py:115
  7.8 4.3 %copy-start.3 = (bf16[512,512]{1,0:T(8,128)(2,1)S(1)}, bf16[512,512]{1,0:T(8,128)(2,1)}, u32[]{:S(2)}) copy-start(bf16[512,512]{1,0:T(8,128)(2,1)} %param.6) | copy-start | bytes 1572868
  7.8 4.3 %copy-start.4 = (bf16[512,512]{1,0:T(8,128)(2,1)S(1)}, bf16[512,512]{1,0:T(8,128)(2,1)}, u32[]{:S(2)}) copy-start(bf16[512,512]{1,0:T(8,128)(2,1)} %param.5) | copy-start | bytes 1572868
  7.8 3.0 %collective-permute-start.9 = (bf16[512,512]{1,0:T(8,128)(2,1)S(1)}, bf16[512,512]{1,0:T(8,128)(2,1)S(1)}, u32[]{:S(2)}, u32[]{:S(2)}) collective-permute-start(bf16[512,512]{1,0:T(8,128)(2,1)S(1)} %get-tuple-element.57), channel_id=1, source_target_pairs={{0,1},{1,0},{2,3},{3,2},{4,5},{5,4},{6,7},{7,6},{8,9},{9,8},{10,11... | collective-permute-start | bytes 1572872 | tf_op jit(solution)/shard_map/ppermute | solution.py:15
  10.9 2.8 %copy-start.6 = (bf16[512,256]{1,0:T(8,128)(2,1)S(1)}, bf16[512,256]{1,0:T(8,128)(2,1)}, u32[]{:S(2)}) copy-start(bf16[512,256]{1,0:T(8,128)(2,1)} %param.8) | copy-start | bytes 786436
  12.0 94.9 %all-gather.6.cloned.1.call-start = ((), (), s32[]{:S(2)}) async-start(), calls=%async_computation.2 | async-start | bytes 4718592 | tf_op jit(solution)/shard_map/all_gather | solution.py:132
  12.2 13.2 %collective-permute-start = (bf16[512,512]{1,0:T(8,128)(2,1)S(1)}, bf16[512,512]{1,0:T(8,128)(2,1)S(1)}, u32[]{:S(2)}, u32[]{:S(2)}) collective-permute-start(bf16[512,512]{1,0:T(8,128)(2,1)S(1)} %subtract_convert_fusion), channel_id=1, source_target_pairs={{0,8},{2,24},{4,12},{6,28},{8,0},{10,16},{12,4},{14,20},{16,10},{1... | collective-permute-start | bytes 1572872 | tf_op jit(solution)/shard_map/ppermute | solution.py:25
  13.6 10.0 %collective-permute-start.1 = (bf16[512,256]{1,0:T(8,128)(2,1)S(1)}, bf16[512,256]{1,0:T(8,128)(2,1)S(1)}, u32[]{:S(2)}, u32[]{:S(2)}) collective-permute-start(bf16[512,256]{1,0:T(8,128)(2,1)S(1)} %copy-done.6), channel_id=1, source_target_pairs={{2,8},{6,12},{10,0},{14,4},{16,26},{20,30},{24,18},{28,22},{3,9},{... | collective-permute-start | bytes 786440 | tf_op jit(solution)/shard_map/ppermute | solution.py:31
  25.5 38.4 %copy-start.7 = (bf16[512,512]{1,0:T(8,128)(2,1)}, bf16[512,512]{1,0:T(8,128)(2,1)S(1)}, u32[]{:S(2)}) copy-start(bf16[512,512]{1,0:T(8,128)(2,1)S(1)} %collective-permute-done.refs_6_) | copy-start | bytes 1572868
  25.5 12.6 %collective-permute-start.4 = (bf16[512,512]{1,0:T(8,128)(2,1)S(1)}, bf16[512,512]{1,0:T(8,128)(2,1)S(1)}, u32[]{:S(2)}, u32[]{:S(2)}) collective-permute-start(bf16[512,512]{1,0:T(8,128)(2,1)S(1)} %collective-permute-done.refs_6_), channel_id=1, source_target_pairs={{0,8},{8,0},{1,9},{9,1},{2,10},{10,2},{3,11},{11,3},{4,12},{12,4},... | collective-permute-start | bytes 1572872 | tf_op jit(solution)/shard_map/ppermute | solution.py:15
  26.8 14.4 %collective-permute-start.3 = (bf16[512,512]{1,0:T(8,128)(2,1)S(1)}, bf16[512,512]{1,0:T(8,128)(2,1)S(1)}, u32[]{:S(2)}, u32[]{:S(2)}) collective-permute-start(bf16[512,512]{1,0:T(8,128)(2,1)S(1)} %collective-permute-done.refs_6_), channel_id=1, source_target_pairs={{0,6},{2,0},{4,2},{6,4},{1,7},{3,1},{5,3},{7,5},{8,14},{10,8},{12,... | collective-permute-start | bytes 1572872 | tf_op jit(solution)/shard_map/ppermute | solution.py:15
  31.4 13.0 %collective-permute-start.2 = (bf16[512,512]{1,0:T(8,128)(2,1)S(1)}, bf16[512,512]{1,0:T(8,128)(2,1)S(1)}, u32[]{:S(2)}, u32[]{:S(2)}) collective-permute-start(bf16[512,512]{1,0:T(8,128)(2,1)S(1)} %collective-permute-done.refs_6_), channel_id=1, source_target_pairs={{0,2},{2,4},{4,6},{6,0},{1,3},{3,5},{5,7},{7,1},{8,10},{10,12},{12... | collective-permute-start | bytes 1572872 | tf_op jit(solution)/shard_map/ppermute | solution.py:15
  31.4 6.6 %collective-permute-start.5 = (bf16[512,256]{1,0:T(8,128)(2,1)S(1)}, bf16[512,256]{1,0:T(8,128)(2,1)S(1)}, u32[]{:S(2)}, u32[]{:S(2)}) collective-permute-start(bf16[512,256]{1,0:T(8,128)(2,1)S(1)} %collective-permute-done.1), channel_id=1, source_target_pairs={{0,24},{4,28},{8,16},{12,20},{18,10},{22,14},{26,2},{30,6},{1,25},... | collective-permute-start | bytes 786440 | tf_op jit(solution)/shard_map/ppermute | solution.py:31
  38.1 25.8 %copy-start.8 = (bf16[512,512]{1,0:T(8,128)(2,1)}, bf16[512,512]{1,0:T(8,128)(2,1)S(1)}, u32[]{:S(2)}) copy-start(bf16[512,512]{1,0:T(8,128)(2,1)S(1)} %collective-permute-done.4.refs_5_) | copy-start | bytes 1572868
  41.2 22.7 %copy-start.9 = (bf16[512,512]{1,0:T(8,128)(2,1)}, bf16[512,512]{1,0:T(8,128)(2,1)S(1)}, u32[]{:S(2)}) copy-start(bf16[512,512]{1,0:T(8,128)(2,1)S(1)} %collective-permute-done.3.refs_4_) | copy-start | bytes 1572868
  44.4 12.5 %copy-start.10 = (bf16[512,512]{1,0:T(8,128)(2,1)}, bf16[512,512]{1,0:T(8,128)(2,1)S(1)}, u32[]{:S(2)}) copy-start(bf16[512,512]{1,0:T(8,128)(2,1)S(1)} %collective-permute-done.2.refs_3_) | copy-start | bytes 1572868
  44.4 10.9 %collective-permute-start.7 = (bf16[512,512]{1,0:T(8,128)(2,1)S(1)}, bf16[512,512]{1,0:T(8,128)(2,1)S(1)}, u32[]{:S(2)}, u32[]{:S(2)}) collective-permute-start(bf16[512,512]{1,0:T(8,128)(2,1)S(1)} %collective-permute-done.4.refs_5_), channel_id=1, source_target_pairs={{0,6},{2,0},{4,2},{6,4},{1,7},{3,1},{5,3},{7,5},{8,14},{10,8},{12,... | collective-permute-start | bytes 1572872 | tf_op jit(solution)/shard_map/ppermute | solution.py:15
  44.7 12.2 %collective-permute-start.8 = (bf16[512,512]{1,0:T(8,128)(2,1)S(1)}, bf16[512,512]{1,0:T(8,128)(2,1)}, u32[]{:S(2)}, u32[]{:S(2)}) collective-permute-start(bf16[512,512]{1,0:T(8,128)(2,1)S(1)} %collective-permute-done.2.refs_3_), channel_id=1, source_target_pairs={{0,2},{2,4},{4,6},{6,0},{1,3},{3,5},{5,7},{7,1},{8,10},{10,12},{12... | collective-permute-start | bytes 1572872 | tf_op jit(solution)/shard_map/ppermute | solution.py:15
  45.9 11.0 %collective-permute-start.6 = (bf16[512,512]{1,0:T(8,128)(2,1)S(1)}, bf16[512,512]{1,0:T(8,128)(2,1)}, u32[]{:S(2)}, u32[]{:S(2)}) collective-permute-start(bf16[512,512]{1,0:T(8,128)(2,1)S(1)} %collective-permute-done.2.refs_3_), channel_id=1, source_target_pairs={{0,8},{8,0},{1,9},{9,1},{2,10},{10,2},{3,11},{11,3},{4,12},{12,4},... | collective-permute-start | bytes 1572872 | tf_op jit(solution)/shard_map/ppermute | solution.py:15
  55.3 1.6 %copy-start.11 = (bf16[512,512]{1,0:T(8,128)(2,1)}, bf16[512,512]{1,0:T(8,128)(2,1)S(1)}, u32[]{:S(2)}) copy-start(bf16[512,512]{1,0:T(8,128)(2,1)S(1)} %collective-permute-done.7.refs_2_) | copy-start | bytes 1572868
  56.9 15.1 %collective-permute-start.10 = (bf16[512,512]{1,0:T(8,128)(2,1)}, bf16[512,512]{1,0:T(8,128)(2,1)S(1)}, u32[]{:S(2)}, u32[]{:S(2)}) collective-permute-start(bf16[512,512]{1,0:T(8,128)(2,1)} %collective-permute-done.6.refs_1_), channel_id=1, source_target_pairs={{0,2},{2,4},{4,6},{6,0},{1,3},{3,5},{5,7},{7,1},{8,10},{10,12},{12... | collective-permute-start | bytes 1572872 | tf_op jit(solution)/shard_map/ppermute | solution.py:15
  62.6 9.4 %collective-permute-start.11 = (bf16[512,256]{1,0:T(8,128)(2,1)S(1)}, bf16[512,256]{1,0:T(8,128)(2,1)S(1)}, u32[]{:S(2)}, u32[]{:S(2)}) collective-permute-start(bf16[512,256]{1,0:T(8,128)(2,1)S(1)} %broadcast_select_fusion.1), channel_id=1, source_target_pairs={{0,8},{8,0},{1,9},{9,1},{2,10},{10,2},{3,11},{11,3},{4,12},{12,4},... | collective-permute-start | bytes 786440 | tf_op jit(solution)/shard_map/ppermute | solution.py:15
  72.1 2.8 %copy-start.12 = (bf16[512,512]{1,0:T(8,128)(2,1)S(1)}, bf16[512,512]{1,0:T(8,128)(2,1)}, u32[]{:S(2)}) copy-start(bf16[512,512]{1,0:T(8,128)(2,1)} %get-tuple-element.42) | copy-start | bytes 1572868
  72.1 3.9 %copy-start.1 = (f32[512,1024]{1,0:T(8,128)S(1)}, f32[512,1024]{1,0:T(8,128)}, u32[]{:S(2)}) copy-start(f32[512,1024]{1,0:T(8,128)} %get-tuple-element.38) | copy-start | bytes 6291460
  74.9 3.3 %copy-start.2 = (f32[512,512]{1,0:T(8,128)S(1)}, f32[512,512]{1,0:T(8,128)}, u32[]{:S(2)}) copy-start(f32[512,512]{1,0:T(8,128)} %get-tuple-element.36) | copy-start | bytes 3145732
  74.9 2.6 %collective-permute-start.12 = (bf16[512,512]{1,0:T(8,128)(2,1)S(1)}, bf16[512,512]{1,0:T(8,128)(2,1)S(1)}, u32[]{:S(2)}, u32[]{:S(2)}) collective-permute-start(bf16[512,512]{1,0:T(8,128)(2,1)S(1)} %copy-done.12), channel_id=1, source_target_pairs={{0,1},{1,0},{2,3},{3,2},{4,5},{5,4},{6,7},{7,6},{8,9},{9,8},{10,11... | collective-permute-start | bytes 1572872 | tf_op jit(solution)/shard_map/ppermute | solution.py:15
  75.9 2.3 %collective-permute-start.13 = (bf16[512,512]{1,0:T(8,128)(2,1)S(1)}, bf16[512,512]{1,0:T(8,128)(2,1)S(1)}, u32[]{:S(2)}, u32[]{:S(2)}) collective-permute-start(bf16[512,512]{1,0:T(8,128)(2,1)S(1)} %fusion), channel_id=1, source_target_pairs={{0,1},{1,0},{2,3},{3,2},{4,5},{5,4},{6,7},{7,6},{8,9},{9,8},{10,11... | collective-permute-start | bytes 1572872 | tf_op jit(solution)/shard_map/ppermute | solution.py:15
  77.5 3.6 %copy-start.5 = (bf16[32,8192]{1,0:T(8,128)(2,1)S(1)}, bf16[32,8192]{1,0:T(8,128)(2,1)}, u32[]{:S(2)}) copy-start(bf16[32,8192]{1,0:T(8,128)(2,1)} %param.9) | copy-start | bytes 1572868
  78.6 9.1 %collective-permute-start.14 = (bf16[256,512]{1,0:T(8,128)(2,1)S(1)}, bf16[256,512]{1,0:T(8,128)(2,1)S(1)}, u32[]{:S(2)}, u32[]{:S(2)}) collective-permute-start(bf16[256,512]{1,0:T(8,128)(2,1)S(1)} %get-tuple-element.55), channel_id=1, source_target_pairs={{0,16},{16,0},{1,17},{17,1},{2,18},{18,2},{3,19},{19,3},{4,20},{20... | collective-permute-start | bytes 786440 | tf_op jit(solution)/shard_map/ppermute | solution.py:15
  87.8 8.1 %collective-permute-start.15 = (bf16[256,512]{1,0:T(8,128)(2,1)S(1)}, bf16[256,512]{1,0:T(8,128)(2,1)S(1)}, u32[]{:S(2)}, u32[]{:S(2)}) collective-permute-start(bf16[256,512]{1,0:T(8,128)(2,1)S(1)} %get-tuple-element.48), channel_id=1, source_target_pairs={{0,16},{16,0},{1,17},{17,1},{2,18},{18,2},{3,19},{19,3},{4,20},{20... | collective-permute-start | bytes 786440 | tf_op jit(solution)/shard_map/ppermute | solution.py:15
  90.2 6.5 %collective-permute-start.16 = (bf16[256,512]{1,0:T(8,128)(2,1)S(1)}, bf16[256,512]{1,0:T(8,128)(2,1)S(1)}, u32[]{:S(2)}, u32[]{:S(2)}) collective-permute-start(bf16[256,512]{1,0:T(8,128)(2,1)S(1)} %fusion.3), channel_id=1, source_target_pairs={{0,96},{32,0},{64,32},{96,64},{1,97},{33,1},{65,33},{97,65},{2,98}... | collective-permute-start | bytes 786440 | tf_op jit(solution)/shard_map/ppermute | solution.py:15
  92.3 7.8 %collective-permute-start.17 = (bf16[256,512]{1,0:T(8,128)(2,1)S(1)}, bf16[256,512]{1,0:T(8,128)(2,1)S(1)}, u32[]{:S(2)}, u32[]{:S(2)}) collective-permute-start(bf16[256,512]{1,0:T(8,128)(2,1)S(1)} %fusion.3), channel_id=1, source_target_pairs={{0,32},{32,64},{64,96},{96,0},{1,33},{33,65},{65,97},{97,1},{2,34}... | collective-permute-start | bytes 786440 | tf_op jit(solution)/shard_map/ppermute | solution.py:15
  96.8 6.6 %collective-permute-start.19 = (bf16[256,512]{1,0:T(8,128)(2,1)S(1)}, bf16[256,512]{1,0:T(8,128)(2,1)S(1)}, u32[]{:S(2)}, u32[]{:S(2)}) collective-permute-start(bf16[256,512]{1,0:T(8,128)(2,1)S(1)} %fusion.2), channel_id=1, source_target_pairs={{0,96},{32,0},{64,32},{96,64},{1,97},{33,1},{65,33},{97,65},{2,98}... | collective-permute-start | bytes 786440 | tf_op jit(solution)/shard_map/ppermute | solution.py:15
  100.1 11.3 %collective-permute-start.18 = (bf16[256,512]{1,0:T(8,128)(2,1)S(1)}, bf16[256,512]{1,0:T(8,128)(2,1)S(1)}, u32[]{:S(2)}, u32[]{:S(2)}) collective-permute-start(bf16[256,512]{1,0:T(8,128)(2,1)S(1)} %fusion.2), channel_id=1, source_target_pairs={{0,32},{32,64},{64,96},{96,0},{1,33},{33,65},{65,97},{97,1},{2,34}... | collective-permute-start | bytes 786440 | tf_op jit(solution)/shard_map/ppermute | solution.py:15
  100.1 12.1 %collective-permute-start.20 = (bf16[256,512]{1,0:T(8,128)(2,1)S(1)}, bf16[256,512]{1,0:T(8,128)(2,1)S(1)}, u32[]{:S(2)}, u32[]{:S(2)}) collective-permute-start(bf16[256,512]{1,0:T(8,128)(2,1)S(1)} %collective-permute-done.17), channel_id=1, source_target_pairs={{0,32},{32,64},{64,96},{96,0},{1,33},{33,65},{65,97},{97,1},{2,34}... | collective-permute-start | bytes 786440 | tf_op jit(solution)/shard_map/ppermute | solution.py:15
  103.4 8.4 %collective-permute-start.21 = (bf16[256,512]{1,0:T(8,128)(2,1)S(1)}, bf16[256,512]{1,0:T(8,128)(2,1)S(1)}, u32[]{:S(2)}, u32[]{:S(2)}) collective-permute-start(bf16[256,512]{1,0:T(8,128)(2,1)S(1)} %collective-permute-done.19), channel_id=1, source_target_pairs={{0,96},{32,0},{64,32},{96,64},{1,97},{33,1},{65,33},{97,65},{2,98}... | collective-permute-start | bytes 786440 | tf_op jit(solution)/shard_map/ppermute | solution.py:15
  106.9 3.1 %copy-start = (bf16[8192,256]{1,0:T(8,128)(2,1)S(1)}, bf16[8192,256]{1,0:T(8,128)(2,1)}, u32[]{:S(2)}) copy-start(bf16[8192,256]{1,0:T(8,128)(2,1)} %all-gather.6.cloned.1.call-done) | copy-start | bytes 12582916
Sparse Core Ops, SparseCore 0:
  12.2 50.4 all-gather.3
  73.1 33.0 all-gather.5

commit v11 on v10

--- a/solution.py
+++ b/solution.py
@@ -95,7 +95,7 @@
             pltpu.VMEM((size, wide), F32),
             pltpu.SemaphoreType.DMA((2 * (n + m),)),
         ],
-        compiler_params=pltpu.CompilerParams(vmem_limit_bytes=56 * 2**20),
+        compiler_params=pltpu.CompilerParams(vmem_limit_bytes=52 * 2**20),
         cost_estimate=pl.CostEstimate(
             flops=2 * (n + m) * size * depth * wide, bytes_accessed=12 * 2**20, transcendentals=0
         ),

time: 145 us -> 145 us (level)
  transfers between devices with their start and end apart: 24 -> 24, of which waited for: 14 -> 14; matrix products, arithmetic and copies ran while one was open for 7% -> 7% of each run, Pallas kernels for 6% -> 5%
where the time goes in v11:
time: 145 us
  waiting for transfers between devices  51.9 us (36%)
  starting transfers between devices  32.2 us (22%)
  blocking collectives  23.9 us (16%)
  between operations  13.7 us (9%)
  matrix products  9.75 us (7%)
  Pallas kernels  7.82 us (5%)
  other arithmetic  3.9 us (3%)
  local copies, waits for them, and re-layouts  1.48 us (1%)
    ppermute x19, waiting for transfers between devices, shift(): return lax.ppermute(v, axis, [(i, (i + by) % n) for i in range(n)])  31.9 us
    ppermute x19, starting transfers between devices, shift(): return lax.ppermute(v, axis, [(i, (i + by) % n) for i in range(n)])  26.7 us
    all_to_all x1, blocking collectives, body(): lax.all_to_all(penalty, ('xh',) + COL, split_axis=0, concat_axis=0, tiled...  23.9 us
    ppermute x2, waiting for transfers between devices, part_ways(): lax.ppermute(v, ('xh', 'xl', 'z'), [tuple(((q[0] * 2 + q[1]) * 4 + q[2] f...  12.5 us
    dot_general x10, matrix products, dot(): lax.dot_general(a, b, (((a.ndim - 1,), (0,)), ((), ())), preferred_elemen...  9.75 us
    pallas_call x1, Pallas kernels, early(): pl.pallas_call(lambda *refs: early_kernel(n, m, *refs), out_shape=(jax.Sh...  7.82 us
    all_gather x1, waiting for transfers between devices, body(): factor = lax.all_gather(pair, 'y', axis=0, tiled=True)  5.68 us
    ppermute x2, starting transfers between devices, part_ways(): lax.ppermute(v, ('xh', 'xl', 'z'), [tuple(((q[0] * 2 + q[1]) * 4 + q[2] f...  4.1 us
  transfers between devices with their start and end apart: 24, of which 14 were waited for; matrix products, arithmetic and copies ran while one was open for 7% of the time, Pallas kernels for 5%

profile of v11, /device:TPU:1, one launch (start us, length us, event | category | flops | bytes accessed | tf_op | source)
XLA Modules:
  0.0 144.7 jit_solution(16990685909675731618)
XLA Ops:
  6.5 1.3 constant_dynamic-slice_fusion.1
  7.8 0.0 copy-start.2
  7.8 0.0 copy-start.3
  7.8 1.5 %collective-permute-start.9 = (bf16[512,512]{1,0:T(8,128)(2,1)S(1)}, bf16[512,512]{1,0:T(8,128)(2,1)S(1)}, u32[]{:S(2)}, u32[]{:S(2)}) collective-permute-start(bf16[512,512]{1,0:T(8,128)(2,1)S(1)} %get-tuple-element.57), channel_id=1, source_target_pairs={{0,1},{1,0},{2,3},{3,2},{4,5},{5,4},{6,7},{7,6},{8,9},{9,8},{10,11... | collective-permute-start | bytes 1572872 | tf_op jit(solution)/shard_map/ppermute | solution.py:15
  9.3 1.5 %collective-permute-done.9 = bf16[512,512]{1,0:T(8,128)(2,1)S(1)} collective-permute-done((bf16[512,512]{1,0:T(8,128)(2,1)S(1)}, bf16[512,512]{1,0:T(8,128)(2,1)S(1)}, u32[]{:S(2)}, u32[]{:S(2)}) %collective-permute-start.9) | collective-permute-done | bytes 524320 | tf_op jit(solution)/shard_map/ppermute | solution.py:15
  10.9 1.1 pad_maximum_fusion
  12.0 0.0 all-gather.4.cloned.1.call-update
  12.0 0.0 all-gather.6.cloned.1.call-start
  12.1 0.1 subtract_convert_fusion
  12.3 1.4 collective-permute-start
  13.6 1.3 collective-permute-start.1
  14.9 8.7 %collective-permute-done.1 = bf16[512,256]{1,0:T(8,128)(2,1)S(1)} collective-permute-done((bf16[512,256]{1,0:T(8,128)(2,1)S(1)}, bf16[512,256]{1,0:T(8,128)(2,1)S(1)}, u32[]{:S(2)}, u32[]{:S(2)}) %collective-permute-start.1) | collective-permute-done | bytes 262176 | tf_op jit(solution)/shard_map/ppermute | solution.py:31
  23.6 1.9 %collective-permute-done.refs_6_ = bf16[512,512]{1,0:T(8,128)(2,1)S(1)} collective-permute-done((bf16[512,512]{1,0:T(8,128)(2,1)S(1)}, bf16[512,512]{1,0:T(8,128)(2,1)S(1)}, u32[]{:S(2)}, u32[]{:S(2)}) %collective-permute-start) | collective-permute-done | bytes 524320 | tf_op jit(solution)/shard_map/ppermute | solution.py:25
  25.5 1.3 collective-permute-start.4
  26.8 4.7 %collective-permute-start.3 = (bf16[512,512]{1,0:T(8,128)(2,1)S(1)}, bf16[512,512]{1,0:T(8,128)(2,1)S(1)}, u32[]{:S(2)}, u32[]{:S(2)}) collective-permute-start(bf16[512,512]{1,0:T(8,128)(2,1)S(1)} %collective-permute-done.refs_6_), channel_id=1, source_target_pairs={{0,6},{2,0},{4,2},{6,4},{1,7},{3,1},{5,3},{7,5},{8,14},{10,8},{12,... | collective-permute-start | bytes 1572872 | tf_op jit(solution)/shard_map/ppermute | solution.py:15
  31.4 0.0 collective-permute-start.2
  31.4 2.8 %collective-permute-start.5 = (bf16[512,256]{1,0:T(8,128)(2,1)S(1)}, bf16[512,256]{1,0:T(8,128)(2,1)S(1)}, u32[]{:S(2)}, u32[]{:S(2)}) collective-permute-start(bf16[512,256]{1,0:T(8,128)(2,1)S(1)} %collective-permute-done.1), channel_id=1, source_target_pairs={{0,24},{4,28},{8,16},{12,20},{18,10},{22,14},{26,2},{30,6},{1,25},... | collective-permute-start | bytes 786440 | tf_op jit(solution)/shard_map/ppermute | solution.py:31
  34.3 3.8 %collective-permute-done.5 = bf16[512,256]{1,0:T(8,128)(2,1)S(1)} collective-permute-done((bf16[512,256]{1,0:T(8,128)(2,1)S(1)}, bf16[512,256]{1,0:T(8,128)(2,1)S(1)}, u32[]{:S(2)}, u32[]{:S(2)}) %collective-permute-start.5) | collective-permute-done | bytes 262176 | tf_op jit(solution)/shard_map/ppermute | solution.py:31
  38.1 3.1 %collective-permute-done.3.refs_4_ = bf16[512,512]{1,0:T(8,128)(2,1)S(1)} collective-permute-done((bf16[512,512]{1,0:T(8,128)(2,1)S(1)}, bf16[512,512]{1,0:T(8,128)(2,1)S(1)}, u32[]{:S(2)}, u32[]{:S(2)}) %collective-permute-start.3) | collective-permute-done | bytes 524320 | tf_op jit(solution)/shard_map/ppermute | solution.py:15
  41.2 3.2 %collective-permute-done.2.refs_3_ = bf16[512,512]{1,0:T(8,128)(2,1)S(1)} collective-permute-done((bf16[512,512]{1,0:T(8,128)(2,1)S(1)}, bf16[512,512]{1,0:T(8,128)(2,1)S(1)}, u32[]{:S(2)}, u32[]{:S(2)}) %collective-permute-start.2) | collective-permute-done | bytes 524320 | tf_op jit(solution)/shard_map/ppermute | solution.py:15
  44.4 0.3 collective-permute-start.7
  44.8 1.1 collective-permute-start.8
  45.9 1.5 %collective-permute-start.6 = (bf16[512,512]{1,0:T(8,128)(2,1)S(1)}, bf16[512,512]{1,0:T(8,128)(2,1)S(1)}, u32[]{:S(2)}, u32[]{:S(2)}) collective-permute-start(bf16[512,512]{1,0:T(8,128)(2,1)S(1)} %collective-permute-done.2.refs_3_), channel_id=1, source_target_pairs={{0,8},{8,0},{1,9},{9,1},{2,10},{10,2},{3,11},{11,3},{4,12},{12,4},... | collective-permute-start | bytes 1572872 | tf_op jit(solution)/shard_map/ppermute | solution.py:15
  47.3 0.1 stack.31.refs_0_
  47.4 7.9 %collective-permute-done.7.refs_2_ = bf16[512,512]{1,0:T(8,128)(2,1)S(1)} collective-permute-done((bf16[512,512]{1,0:T(8,128)(2,1)S(1)}, bf16[512,512]{1,0:T(8,128)(2,1)S(1)}, u32[]{:S(2)}, u32[]{:S(2)}) %collective-permute-start.7) | collective-permute-done | bytes 524320 | tf_op jit(solution)/shard_map/ppermute | solution.py:15
  55.3 1.6 %collective-permute-done.8.refs_7_ = bf16[512,512]{1,0:T(8,128)(2,1)} collective-permute-done((bf16[512,512]{1,0:T(8,128)(2,1)S(1)}, bf16[512,512]{1,0:T(8,128)(2,1)}, u32[]{:S(2)}, u32[]{:S(2)}) %collective-permute-start.8) | collective-permute-done | bytes 524320 | tf_op jit(solution)/shard_map/ppermute | solution.py:15
  57.0 5.7 %all-gather.4.cloned.1.call-done.refs_8_ = bf16[2048,1024]{1,0:T(8,128)(2,1)} async-done(((bf16[512,1024]{1,0:T(8,128)(2,1)}), bf16[2048,1024]{1,0:T(8,128)(2,1)}) %all-gather.4.cloned.1.call-update) | async-done | bytes 4194320 | tf_op jit(solution)/shard_map/all_gather | solution.py:115
  62.6 1.2 collective-permute-start.11
  63.8 7.8 %shard_map.55 = (bf16[512,512]{1,0:T(8,128)(2,1)S(1)}, f32[512,512]{1,0:T(8,128)}, f32[512,1024]{1,0:T(8,128)}) custom-call(s32[7]{0:T(128)S(1)} %stack.31.refs_0_, bf16[512,512]{1,0:T(8,128)(2,1)S(1)} %collective-permute-done.6.refs_1_, bf16[512,512]{1,0:T(8,128)(2,1)S(1)} %collective-permute-done.7.refs_2_, bf16[512,512]{1,0:T(8,128)(2,1)} %copy-done.9, ...), custom_call_target="tpu_custom_call" | custom-call | flops 3758096384 | bytes 12582912 | tf_op jit(solution)/shard_map/pallas_call | solution.py:83
  71.7 0.0 collective-permute-done.10
  71.7 0.8 pad_maximum_fusion.1
  72.5 0.0 all-gather.6.cloned.1.call-update
  72.5 1.8 %fusion = bf16[512,512]{1,0:T(8,128)(2,1)S(1)} fusion(bf16[512,512]{1,0:T(8,128)(2,1)S(1)} %collective-permute-done.10, f32[512,1024]{1,0:T(8,128)} %get-tuple-element.38, bf16[2048,1024]{1,0:T(8,128)(2,1)} %all-gather.4.cloned.1.call-done.refs_8_, s32[]{:T(128)S(6)} %select_n.83), kind=kOutput, calls=%fused_computation.4 | convolution fusion | flops 268959744 | bytes 2621444 | tf_op jit(solution)/shard_map/dot_general | solution.py:43
  74.4 1.0 collective-permute-start.12
  75.4 0.1 collective-permute-start.13
  75.5 1.8 %convolution_add_fusion = f32[512,512]{1,0:T(8,128)S(1)} fusion(bf16[512,512]{1,0:T(8,128)(2,1)S(1)} %collective-permute-done.10, f32[512,1024]{1,0:T(8,128)} %get-tuple-element.38, bf16[2048,1024]{1,0:T(8,128)(2,1)} %all-gather.4.cloned.1.call-done.refs_8_, s32[]{:T(128)S(6)} %select_n.83), kind=kOutput, calls=%fused_computation.2 | convolution fusion | flops 268697600 | bytes 3145732 | tf_op jit(solution)/shard_map/dot_general | solution.py:43
  77.3 0.0 copy-start.4
  77.4 0.3 collective-permute-done.13
  77.7 0.4 broadcast_select_fusion
  78.1 0.1 fusion.1
  78.2 2.5 %collective-permute-start.14 = (bf16[256,512]{1,0:T(8,128)(2,1)S(1)}, bf16[256,512]{1,0:T(8,128)(2,1)S(1)}, u32[]{:S(2)}, u32[]{:S(2)}) collective-permute-start(bf16[256,512]{1,0:T(8,128)(2,1)S(1)} %get-tuple-element.55), channel_id=1, source_target_pairs={{0,16},{16,0},{1,17},{17,1},{2,18},{18,2},{3,19},{19,3},{4,20},{20... | collective-permute-start | bytes 786440 | tf_op jit(solution)/shard_map/ppermute | solution.py:15
  80.6 0.1 convert_element_type.51
  80.7 6.5 %collective-permute-done.14 = bf16[256,512]{1,0:T(8,128)(2,1)S(1)} collective-permute-done((bf16[256,512]{1,0:T(8,128)(2,1)S(1)}, bf16[256,512]{1,0:T(8,128)(2,1)S(1)}, u32[]{:S(2)}, u32[]{:S(2)}) %collective-permute-start.14) | collective-permute-done | bytes 262176 | tf_op jit(solution)/shard_map/ppermute | solution.py:15
  87.3 2.4 %collective-permute-start.15 = (bf16[256,512]{1,0:T(8,128)(2,1)S(1)}, bf16[256,512]{1,0:T(8,128)(2,1)S(1)}, u32[]{:S(2)}, u32[]{:S(2)}) collective-permute-start(bf16[256,512]{1,0:T(8,128)(2,1)S(1)} %get-tuple-element.48), channel_id=1, source_target_pairs={{0,16},{16,0},{1,17},{17,1},{2,18},{18,2},{3,19},{19,3},{4,20},{20... | collective-permute-start | bytes 786440 | tf_op jit(solution)/shard_map/ppermute | solution.py:15
  89.7 0.1 fusion.3
  89.7 2.2 %collective-permute-start.16 = (bf16[256,512]{1,0:T(8,128)(2,1)S(1)}, bf16[256,512]{1,0:T(8,128)(2,1)S(1)}, u32[]{:S(2)}, u32[]{:S(2)}) collective-permute-start(bf16[256,512]{1,0:T(8,128)(2,1)S(1)} %fusion.3), channel_id=1, source_target_pairs={{0,96},{32,0},{64,32},{96,64},{1,97},{33,1},{65,33},{97,65},{2,98}... | collective-permute-start | bytes 786440 | tf_op jit(solution)/shard_map/ppermute | solution.py:15
  91.9 3.4 %collective-permute-done.15 = bf16[256,512]{1,0:T(8,128)(2,1)S(1)} collective-permute-done((bf16[256,512]{1,0:T(8,128)(2,1)S(1)}, bf16[256,512]{1,0:T(8,128)(2,1)S(1)}, u32[]{:S(2)}, u32[]{:S(2)}) %collective-permute-start.15) | collective-permute-done | bytes 262176 | tf_op jit(solution)/shard_map/ppermute | solution.py:15
  95.4 0.9 collective-permute-done.16
  96.2 0.1 fusion.2
  96.3 3.4 %collective-permute-start.19 = (bf16[256,512]{1,0:T(8,128)(2,1)S(1)}, bf16[256,512]{1,0:T(8,128)(2,1)S(1)}, u32[]{:S(2)}, u32[]{:S(2)}) collective-permute-start(bf16[256,512]{1,0:T(8,128)(2,1)S(1)} %fusion.2), channel_id=1, source_target_pairs={{0,96},{32,0},{64,32},{96,64},{1,97},{33,1},{65,33},{97,65},{2,98}... | collective-permute-start | bytes 786440 | tf_op jit(solution)/shard_map/ppermute | solution.py:15
  99.7 3.3 %collective-permute-done.19 = bf16[256,512]{1,0:T(8,128)(2,1)S(1)} collective-permute-done((bf16[256,512]{1,0:T(8,128)(2,1)S(1)}, bf16[256,512]{1,0:T(8,128)(2,1)S(1)}, u32[]{:S(2)}, u32[]{:S(2)}) %collective-permute-start.19) | collective-permute-done | bytes 262176 | tf_op jit(solution)/shard_map/ppermute | solution.py:15
  103.0 3.5 %collective-permute-start.21 = (bf16[256,512]{1,0:T(8,128)(2,1)S(1)}, bf16[256,512]{1,0:T(8,128)(2,1)S(1)}, u32[]{:S(2)}, u32[]{:S(2)}) collective-permute-start(bf16[256,512]{1,0:T(8,128)(2,1)S(1)} %collective-permute-done.19), channel_id=1, source_target_pairs={{0,96},{32,0},{64,32},{96,64},{1,97},{33,1},{65,33},{97,65},{2,98}... | collective-permute-start | bytes 786440 | tf_op jit(solution)/shard_map/ppermute | solution.py:15
  106.5 1.6 %fusion.16 = f32[2,512,512]{2,1,0:T(8,128)S(1)} fusion(bf16[8,1024,256]{2,1,0:T(8,128)(2,1)} %bitcast.44, s32[]{:T(128)S(6)} %select_n.89, s32[]{:T(128)S(6)} %select_n.86, bf16[256,512]{1,0:T(8,128)(2,1)S(1)} %fusion.2), kind=kOutput, calls=%fused_computation.30 | convolution fusion | flops 268435456 | bytes 2883592 | tf_op jit(solution)/shard_map/dot_general | solution.py:43
  108.2 1.5 %fusion.18 = f32[2,512,512]{2,1,0:T(8,128)S(1)} fusion(bf16[8,1024,256]{2,1,0:T(8,128)(2,1)} %bitcast.45, s32[]{:T(128)S(6)} %select_n.85, s32[]{:T(128)S(6)} %select_n.86, bf16[256,512]{1,0:T(8,128)(2,1)S(1)} %fusion.3), kind=kOutput, calls=%fused_computation.32 | convolution fusion | flops 268435456 | bytes 2883592 | tf_op jit(solution)/shard_map/dot_general | solution.py:43
  109.7 0.4 fusion.10
  110.1 0.4 fusion.8
  110.5 0.4 fusion.14
  111.0 0.4 fusion.12
  111.4 0.4 fusion.5
  111.8 0.8 add_convert_fusion
  112.7 23.9 %all_to_all.9 = bf16[32,32,512]{2,1,0:T(8,128)(2,1)S(1)} all-to-all(bf16[32,32,512]{2,1,0:T(8,128)(2,1)S(1)} %bitcast.40), channel_id=1, replica_groups=mesh['y'=4,'xh'=2,'xl'=2,'z'=4,'core'=2] {'xh','xl','z','core'}, dimensions={0} | all-to-all | bytes 2097152 | tf_op jit(solution)/shard_map/all_to_all | solution.py:166
  136.6 0.2 convert_reduce_fusion
  136.9 0.1 copy.7
  137.0 0.9 add_convert_fusion.1
  (32 shorter events, 0.1 us)
Async XLA Ops:
  6.5 56.1 %all-gather.4.cloned.1.call-start = ((), (), s32[]{:S(2)}) async-start(), calls=%async_computation.1 | async-start | bytes 5242880 | tf_op jit(solution)/shard_map/all_gather | solution.py:115
  7.8 4.3 %copy-start.2 = (bf16[512,512]{1,0:T(8,128)(2,1)S(1)}, bf16[512,512]{1,0:T(8,128)(2,1)}, u32[]{:S(2)}) copy-start(bf16[512,512]{1,0:T(8,128)(2,1)} %param.6) | copy-start | bytes 1572868
  7.8 4.3 %copy-start.3 = (bf16[512,512]{1,0:T(8,128)(2,1)S(1)}, bf16[512,512]{1,0:T(8,128)(2,1)}, u32[]{:S(2)}) copy-start(bf16[512,512]{1,0:T(8,128)(2,1)} %param.5) | copy-start | bytes 1572868
  7.8 3.0 %collective-permute-start.9 = (bf16[512,512]{1,0:T(8,128)(2,1)S(1)}, bf16[512,512]{1,0:T(8,128)(2,1)S(1)}, u32[]{:S(2)}, u32[]{:S(2)}) collective-permute-start(bf16[512,512]{1,0:T(8,128)(2,1)S(1)} %get-tuple-element.57), channel_id=1, source_target_pairs={{0,1},{1,0},{2,3},{3,2},{4,5},{5,4},{6,7},{7,6},{8,9},{9,8},{10,11... | collective-permute-start | bytes 1572872 | tf_op jit(solution)/shard_map/ppermute | solution.py:15
  10.9 2.8 %copy-start.5 = (bf16[512,256]{1,0:T(8,128)(2,1)S(1)}, bf16[512,256]{1,0:T(8,128)(2,1)}, u32[]{:S(2)}) copy-start(bf16[512,256]{1,0:T(8,128)(2,1)} %param.8) | copy-start | bytes 786436
  12.0 94.5 %all-gather.6.cloned.1.call-start = ((), (), s32[]{:S(2)}) async-start(), calls=%async_computation.2 | async-start | bytes 4718592 | tf_op jit(solution)/shard_map/all_gather | solution.py:132
  12.3 13.2 %collective-permute-start = (bf16[512,512]{1,0:T(8,128)(2,1)S(1)}, bf16[512,512]{1,0:T(8,128)(2,1)S(1)}, u32[]{:S(2)}, u32[]{:S(2)}) collective-permute-start(bf16[512,512]{1,0:T(8,128)(2,1)S(1)} %subtract_convert_fusion), channel_id=1, source_target_pairs={{0,8},{2,24},{4,12},{6,28},{8,0},{10,16},{12,4},{14,20},{16,10},{1... | collective-permute-start | bytes 1572872 | tf_op jit(solution)/shard_map/ppermute | solution.py:25
  13.6 10.0 %collective-permute-start.1 = (bf16[512,256]{1,0:T(8,128)(2,1)S(1)}, bf16[512,256]{1,0:T(8,128)(2,1)S(1)}, u32[]{:S(2)}, u32[]{:S(2)}) collective-permute-start(bf16[512,256]{1,0:T(8,128)(2,1)S(1)} %copy-done.5), channel_id=1, source_target_pairs={{2,8},{6,12},{10,0},{14,4},{16,26},{20,30},{24,18},{28,22},{3,9},{... | collective-permute-start | bytes 786440 | tf_op jit(solution)/shard_map/ppermute | solution.py:31
  25.5 38.4 %copy-start.6 = (bf16[512,512]{1,0:T(8,128)(2,1)}, bf16[512,512]{1,0:T(8,128)(2,1)S(1)}, u32[]{:S(2)}) copy-start(bf16[512,512]{1,0:T(8,128)(2,1)S(1)} %collective-permute-done.refs_6_) | copy-start | bytes 1572868
  25.5 12.6 %collective-permute-start.4 = (bf16[512,512]{1,0:T(8,128)(2,1)S(1)}, bf16[512,512]{1,0:T(8,128)(2,1)S(1)}, u32[]{:S(2)}, u32[]{:S(2)}) collective-permute-start(bf16[512,512]{1,0:T(8,128)(2,1)S(1)} %collective-permute-done.refs_6_), channel_id=1, source_target_pairs={{0,8},{8,0},{1,9},{9,1},{2,10},{10,2},{3,11},{11,3},{4,12},{12,4},... | collective-permute-start | bytes 1572872 | tf_op jit(solution)/shard_map/ppermute | solution.py:15
  26.8 14.4 %collective-permute-start.3 = (bf16[512,512]{1,0:T(8,128)(2,1)S(1)}, bf16[512,512]{1,0:T(8,128)(2,1)S(1)}, u32[]{:S(2)}, u32[]{:S(2)}) collective-permute-start(bf16[512,512]{1,0:T(8,128)(2,1)S(1)} %collective-permute-done.refs_6_), channel_id=1, source_target_pairs={{0,6},{2,0},{4,2},{6,4},{1,7},{3,1},{5,3},{7,5},{8,14},{10,8},{12,... | collective-permute-start | bytes 1572872 | tf_op jit(solution)/shard_map/ppermute | solution.py:15
  31.4 13.0 %collective-permute-start.2 = (bf16[512,512]{1,0:T(8,128)(2,1)S(1)}, bf16[512,512]{1,0:T(8,128)(2,1)S(1)}, u32[]{:S(2)}, u32[]{:S(2)}) collective-permute-start(bf16[512,512]{1,0:T(8,128)(2,1)S(1)} %collective-permute-done.refs_6_), channel_id=1, source_target_pairs={{0,2},{2,4},{4,6},{6,0},{1,3},{3,5},{5,7},{7,1},{8,10},{10,12},{12... | collective-permute-start | bytes 1572872 | tf_op jit(solution)/shard_map/ppermute | solution.py:15
  31.4 6.6 %collective-permute-start.5 = (bf16[512,256]{1,0:T(8,128)(2,1)S(1)}, bf16[512,256]{1,0:T(8,128)(2,1)S(1)}, u32[]{:S(2)}, u32[]{:S(2)}) collective-permute-start(bf16[512,256]{1,0:T(8,128)(2,1)S(1)} %collective-permute-done.1), channel_id=1, source_target_pairs={{0,24},{4,28},{8,16},{12,20},{18,10},{22,14},{26,2},{30,6},{1,25},... | collective-permute-start | bytes 786440 | tf_op jit(solution)/shard_map/ppermute | solution.py:31
  38.1 25.8 %copy-start.7 = (bf16[512,512]{1,0:T(8,128)(2,1)}, bf16[512,512]{1,0:T(8,128)(2,1)S(1)}, u32[]{:S(2)}) copy-start(bf16[512,512]{1,0:T(8,128)(2,1)S(1)} %collective-permute-done.4.refs_5_) | copy-start | bytes 1572868
  41.2 3.6 %copy-start.8 = (bf16[512,512]{1,0:T(8,128)(2,1)}, bf16[512,512]{1,0:T(8,128)(2,1)S(1)}, u32[]{:S(2)}) copy-start(bf16[512,512]{1,0:T(8,128)(2,1)S(1)} %collective-permute-done.3.refs_4_) | copy-start | bytes 1572868
  44.4 12.5 %copy-start.9 = (bf16[512,512]{1,0:T(8,128)(2,1)}, bf16[512,512]{1,0:T(8,128)(2,1)S(1)}, u32[]{:S(2)}) copy-start(bf16[512,512]{1,0:T(8,128)(2,1)S(1)} %collective-permute-done.2.refs_3_) | copy-start | bytes 1572868
  44.4 10.9 %collective-permute-start.7 = (bf16[512,512]{1,0:T(8,128)(2,1)S(1)}, bf16[512,512]{1,0:T(8,128)(2,1)S(1)}, u32[]{:S(2)}, u32[]{:S(2)}) collective-permute-start(bf16[512,512]{1,0:T(8,128)(2,1)S(1)} %collective-permute-done.4.refs_5_), channel_id=1, source_target_pairs={{0,6},{2,0},{4,2},{6,4},{1,7},{3,1},{5,3},{7,5},{8,14},{10,8},{12,... | collective-permute-start | bytes 1572872 | tf_op jit(solution)/shard_map/ppermute | solution.py:15
  44.8 12.2 %collective-permute-start.8 = (bf16[512,512]{1,0:T(8,128)(2,1)S(1)}, bf16[512,512]{1,0:T(8,128)(2,1)}, u32[]{:S(2)}, u32[]{:S(2)}) collective-permute-start(bf16[512,512]{1,0:T(8,128)(2,1)S(1)} %collective-permute-done.2.refs_3_), channel_id=1, source_target_pairs={{0,2},{2,4},{4,6},{6,0},{1,3},{3,5},{5,7},{7,1},{8,10},{10,12},{12... | collective-permute-start | bytes 1572872 | tf_op jit(solution)/shard_map/ppermute | solution.py:15
  45.9 11.0 %collective-permute-start.6 = (bf16[512,512]{1,0:T(8,128)(2,1)S(1)}, bf16[512,512]{1,0:T(8,128)(2,1)S(1)}, u32[]{:S(2)}, u32[]{:S(2)}) collective-permute-start(bf16[512,512]{1,0:T(8,128)(2,1)S(1)} %collective-permute-done.2.refs_3_), channel_id=1, source_target_pairs={{0,8},{8,0},{1,9},{9,1},{2,10},{10,2},{3,11},{11,3},{4,12},{12,4},... | collective-permute-start | bytes 1572872 | tf_op jit(solution)/shard_map/ppermute | solution.py:15
  56.9 14.8 %collective-permute-start.10 = (bf16[512,512]{1,0:T(8,128)(2,1)S(1)}, bf16[512,512]{1,0:T(8,128)(2,1)S(1)}, u32[]{:S(2)}, u32[]{:S(2)}) collective-permute-start(bf16[512,512]{1,0:T(8,128)(2,1)S(1)} %collective-permute-done.6.refs_1_), channel_id=1, source_target_pairs={{0,2},{2,4},{4,6},{6,0},{1,3},{3,5},{5,7},{7,1},{8,10},{10,12},{12... | collective-permute-start | bytes 1572872 | tf_op jit(solution)/shard_map/ppermute | solution.py:15
  62.6 9.0 %collective-permute-start.11 = (bf16[512,256]{1,0:T(8,128)(2,1)S(1)}, bf16[512,256]{1,0:T(8,128)(2,1)S(1)}, u32[]{:S(2)}, u32[]{:S(2)}) collective-permute-start(bf16[512,256]{1,0:T(8,128)(2,1)S(1)} %broadcast_select_fusion.1), channel_id=1, source_target_pairs={{0,8},{8,0},{1,9},{9,1},{2,10},{10,2},{3,11},{11,3},{4,12},{12,4},... | collective-permute-start | bytes 786440 | tf_op jit(solution)/shard_map/ppermute | solution.py:15
  74.4 3.3 %copy-start.1 = (f32[512,512]{1,0:T(8,128)S(1)}, f32[512,512]{1,0:T(8,128)}, u32[]{:S(2)}) copy-start(f32[512,512]{1,0:T(8,128)} %get-tuple-element.36) | copy-start | bytes 3145732
  74.4 3.0 %collective-permute-start.12 = (bf16[512,512]{1,0:T(8,128)(2,1)S(1)}, bf16[512,512]{1,0:T(8,128)(2,1)S(1)}, u32[]{:S(2)}, u32[]{:S(2)}) collective-permute-start(bf16[512,512]{1,0:T(8,128)(2,1)S(1)} %get-tuple-element.42), channel_id=1, source_target_pairs={{0,1},{1,0},{2,3},{3,2},{4,5},{5,4},{6,7},{7,6},{8,9},{9,8},{10,11... | collective-permute-start | bytes 1572872 | tf_op jit(solution)/shard_map/ppermute | solution.py:15
  75.4 2.3 %collective-permute-start.13 = (bf16[512,512]{1,0:T(8,128)(2,1)S(1)}, bf16[512,512]{1,0:T(8,128)(2,1)S(1)}, u32[]{:S(2)}, u32[]{:S(2)}) collective-permute-start(bf16[512,512]{1,0:T(8,128)(2,1)S(1)} %fusion), channel_id=1, source_target_pairs={{0,1},{1,0},{2,3},{3,2},{4,5},{5,4},{6,7},{7,6},{8,9},{9,8},{10,11... | collective-permute-start | bytes 1572872 | tf_op jit(solution)/shard_map/ppermute | solution.py:15
  77.3 3.3 %copy-start.4 = (bf16[32,8192]{1,0:T(8,128)(2,1)S(1)}, bf16[32,8192]{1,0:T(8,128)(2,1)}, u32[]{:S(2)}) copy-start(bf16[32,8192]{1,0:T(8,128)(2,1)} %param.9) | copy-start | bytes 1572868
  78.2 9.1 %collective-permute-start.14 = (bf16[256,512]{1,0:T(8,128)(2,1)S(1)}, bf16[256,512]{1,0:T(8,128)(2,1)S(1)}, u32[]{:S(2)}, u32[]{:S(2)}) collective-permute-start(bf16[256,512]{1,0:T(8,128)(2,1)S(1)} %get-tuple-element.55), channel_id=1, source_target_pairs={{0,16},{16,0},{1,17},{17,1},{2,18},{18,2},{3,19},{19,3},{4,20},{20... | collective-permute-start | bytes 786440 | tf_op jit(solution)/shard_map/ppermute | solution.py:15
  87.3 8.1 %collective-permute-start.15 = (bf16[256,512]{1,0:T(8,128)(2,1)S(1)}, bf16[256,512]{1,0:T(8,128)(2,1)S(1)}, u32[]{:S(2)}, u32[]{:S(2)}) collective-permute-start(bf16[256,512]{1,0:T(8,128)(2,1)S(1)} %get-tuple-element.48), channel_id=1, source_target_pairs={{0,16},{16,0},{1,17},{17,1},{2,18},{18,2},{3,19},{19,3},{4,20},{20... | collective-permute-start | bytes 786440 | tf_op jit(solution)/shard_map/ppermute | solution.py:15
  89.7 6.5 %collective-permute-start.16 = (bf16[256,512]{1,0:T(8,128)(2,1)S(1)}, bf16[256,512]{1,0:T(8,128)(2,1)S(1)}, u32[]{:S(2)}, u32[]{:S(2)}) collective-permute-start(bf16[256,512]{1,0:T(8,128)(2,1)S(1)} %fusion.3), channel_id=1, source_target_pairs={{0,96},{32,0},{64,32},{96,64},{1,97},{33,1},{65,33},{97,65},{2,98}... | collective-permute-start | bytes 786440 | tf_op jit(solution)/shard_map/ppermute | solution.py:15
  91.9 7.8 %collective-permute-start.17 = (bf16[256,512]{1,0:T(8,128)(2,1)S(1)}, bf16[256,512]{1,0:T(8,128)(2,1)S(1)}, u32[]{:S(2)}, u32[]{:S(2)}) collective-permute-start(bf16[256,512]{1,0:T(8,128)(2,1)S(1)} %fusion.3), channel_id=1, source_target_pairs={{0,32},{32,64},{64,96},{96,0},{1,33},{33,65},{65,97},{97,1},{2,34}... | collective-permute-start | bytes 786440 | tf_op jit(solution)/shard_map/ppermute | solution.py:15
  96.3 6.7 %collective-permute-start.19 = (bf16[256,512]{1,0:T(8,128)(2,1)S(1)}, bf16[256,512]{1,0:T(8,128)(2,1)S(1)}, u32[]{:S(2)}, u32[]{:S(2)}) collective-permute-start(bf16[256,512]{1,0:T(8,128)(2,1)S(1)} %fusion.2), channel_id=1, source_target_pairs={{0,96},{32,0},{64,32},{96,64},{1,97},{33,1},{65,33},{97,65},{2,98}... | collective-permute-start | bytes 786440 | tf_op jit(solution)/shard_map/ppermute | solution.py:15
  99.7 11.3 %collective-permute-start.18 = (bf16[256,512]{1,0:T(8,128)(2,1)S(1)}, bf16[256,512]{1,0:T(8,128)(2,1)S(1)}, u32[]{:S(2)}, u32[]{:S(2)}) collective-permute-start(bf16[256,512]{1,0:T(8,128)(2,1)S(1)} %fusion.2), channel_id=1, source_target_pairs={{0,32},{32,64},{64,96},{96,0},{1,33},{33,65},{65,97},{97,1},{2,34}... | collective-permute-start | bytes 786440 | tf_op jit(solution)/shard_map/ppermute | solution.py:15
  99.7 12.1 %collective-permute-start.20 = (bf16[256,512]{1,0:T(8,128)(2,1)S(1)}, bf16[256,512]{1,0:T(8,128)(2,1)S(1)}, u32[]{:S(2)}, u32[]{:S(2)}) collective-permute-start(bf16[256,512]{1,0:T(8,128)(2,1)S(1)} %collective-permute-done.17), channel_id=1, source_target_pairs={{0,32},{32,64},{64,96},{96,0},{1,33},{33,65},{65,97},{97,1},{2,34}... | collective-permute-start | bytes 786440 | tf_op jit(solution)/shard_map/ppermute | solution.py:15
  103.0 8.4 %collective-permute-start.21 = (bf16[256,512]{1,0:T(8,128)(2,1)S(1)}, bf16[256,512]{1,0:T(8,128)(2,1)S(1)}, u32[]{:S(2)}, u32[]{:S(2)}) collective-permute-start(bf16[256,512]{1,0:T(8,128)(2,1)S(1)} %collective-permute-done.19), channel_id=1, source_target_pairs={{0,96},{32,0},{64,32},{96,64},{1,97},{33,1},{65,33},{97,65},{2,98}... | collective-permute-start | bytes 786440 | tf_op jit(solution)/shard_map/ppermute | solution.py:15
  106.5 3.1 %copy-start = (bf16[8192,256]{1,0:T(8,128)(2,1)S(1)}, bf16[8192,256]{1,0:T(8,128)(2,1)}, u32[]{:S(2)}) copy-start(bf16[8192,256]{1,0:T(8,128)(2,1)} %all-gather.6.cloned.1.call-done) | copy-start | bytes 12582916
Sparse Core Ops, SparseCore 0:
  12.2 50.4 all-gather.3
  72.7 33.0 all-gather.5

commit v12 on v11

--- a/solution.py
+++ b/solution.py
@@ -121,14 +121,15 @@
     am, ap, b2 = together(shift(bm, "xl", 1), shift(a, "z", -1), shift(bm, "z", 1))
     same = (z & 1) == xh
     turned = jnp.where(same, output_factor, moves)
-    a2, part = together(shift(am, "z", 1), shift(after(turned, factor), "xl", 1))
+    a2, part = shift(am, "z", 1), shift(turned, "xl", 1)
 
     def place(dxl, dz):
         return (xl ^ dxl) * 2 + (((z + dz) & 3) >> 1)
 
     at = [place(0, -1), place(0, 1), place(1, -1), place(1, 1), place(0, 0), place(1, 0), place(1, 2)]
     theirs, own, even = early([am, ap, bm, bp], [a, b, b2], factor, at)
-    part = jnp.concatenate([after(part, own), turned], axis=0)
+    a2, part, own = together(a2, part, own)
+    part = jnp.concatenate([part, turned], axis=0)
     left = lax.all_gather(part, ("core", "z"), axis=0)
 
     def more(v, side):

time: 145 us -> 145 us (level)
    all_gather x1, waiting for transfers between devices: 5.68 us -> 4 us  [body(): factor = lax.all_gather(pair, 'y', axis=0, tiled=True)]
where the time goes in v12:
time: 145 us
  waiting for transfers between devices  50.8 us (35%)
  starting transfers between devices  33.6 us (23%)
  blocking collectives  23.8 us (16%)
  between operations  13.7 us (9%)
  matrix products  9.75 us (7%)
  Pallas kernels  7.83 us (5%)
  other arithmetic  3.91 us (3%)
  local copies, waits for them, and re-layouts  1.47 us (1%)
    ppermute x19, waiting for transfers between devices, shift(): return lax.ppermute(v, axis, [(i, (i + by) % n) for i in range(n)])  32.5 us
    ppermute x19, starting transfers between devices, shift(): return lax.ppermute(v, axis, [(i, (i + by) % n) for i in range(n)])  28.1 us
    all_to_all x1, blocking collectives, body(): lax.all_to_all(penalty, ('xh',) + COL, split_axis=0, concat_axis=0, tiled...  23.8 us
    ppermute x2, waiting for transfers between devices, part_ways(): lax.ppermute(v, ('xh', 'xl', 'z'), [tuple(((q[0] * 2 + q[1]) * 4 + q[2] f...  12.5 us
    dot_general x10, matrix products, dot(): lax.dot_general(a, b, (((a.ndim - 1,), (0,)), ((), ())), preferred_elemen...  9.75 us
    pallas_call x1, Pallas kernels, early(): pl.pallas_call(lambda *refs: early_kernel(n, m, *refs), out_shape=(jax.Sh...  7.83 us
    ppermute x2, starting transfers between devices, part_ways(): lax.ppermute(v, ('xh', 'xl', 'z'), [tuple(((q[0] * 2 + q[1]) * 4 + q[2] f...  4.1 us
    all_gather x1, waiting for transfers between devices, body(): factor = lax.all_gather(pair, 'y', axis=0, tiled=True)  4 us
  transfers between devices with their start and end apart: 24, of which 14 were waited for; matrix products, arithmetic and copies ran while one was open for 7% of the time, Pallas kernels for 5%

profile of v12, /device:TPU:1, one launch (start us, length us, event | category | flops | bytes accessed | tf_op | source)
XLA Modules:
  0.0 144.8 jit_solution(10320239638170088457)
XLA Ops:
  6.5 1.3 constant_dynamic-slice_fusion.1
  7.8 0.0 copy-start.2
  7.8 0.0 copy-start.3
  7.8 1.5 %collective-permute-start.11 = (bf16[512,512]{1,0:T(8,128)(2,1)S(1)}, bf16[512,512]{1,0:T(8,128)(2,1)S(1)}, u32[]{:S(2)}, u32[]{:S(2)}) collective-permute-start(bf16[512,512]{1,0:T(8,128)(2,1)S(1)} %get-tuple-element.55), channel_id=1, source_target_pairs={{0,1},{1,0},{2,3},{3,2},{4,5},{5,4},{6,7},{7,6},{8,9},{9,8},{10,11... | collective-permute-start | bytes 1572872 | tf_op jit(solution)/shard_map/ppermute | solution.py:15
  9.3 1.5 %collective-permute-done.11 = bf16[512,512]{1,0:T(8,128)(2,1)S(1)} collective-permute-done((bf16[512,512]{1,0:T(8,128)(2,1)S(1)}, bf16[512,512]{1,0:T(8,128)(2,1)S(1)}, u32[]{:S(2)}, u32[]{:S(2)}) %collective-permute-start.11) | collective-permute-done | bytes 524320 | tf_op jit(solution)/shard_map/ppermute | solution.py:15
  10.9 1.1 pad_maximum_fusion
  12.0 0.0 all-gather.4.cloned.1.call-update
  12.0 0.0 all-gather.6.cloned.1.call-start
  12.1 0.1 subtract_convert_fusion
  12.3 1.4 collective-permute-start
  13.6 1.3 collective-permute-start.1
  14.9 8.7 %collective-permute-done.1 = bf16[512,256]{1,0:T(8,128)(2,1)S(1)} collective-permute-done((bf16[512,256]{1,0:T(8,128)(2,1)S(1)}, bf16[512,256]{1,0:T(8,128)(2,1)S(1)}, u32[]{:S(2)}, u32[]{:S(2)}) %collective-permute-start.1) | collective-permute-done | bytes 262176 | tf_op jit(solution)/shard_map/ppermute | solution.py:31
  23.6 1.9 %collective-permute-done.refs_6_ = bf16[512,512]{1,0:T(8,128)(2,1)S(1)} collective-permute-done((bf16[512,512]{1,0:T(8,128)(2,1)S(1)}, bf16[512,512]{1,0:T(8,128)(2,1)S(1)}, u32[]{:S(2)}, u32[]{:S(2)}) %collective-permute-start) | collective-permute-done | bytes 524320 | tf_op jit(solution)/shard_map/ppermute | solution.py:25
  25.5 1.3 collective-permute-start.4
  26.8 4.7 %collective-permute-start.3 = (bf16[512,512]{1,0:T(8,128)(2,1)S(1)}, bf16[512,512]{1,0:T(8,128)(2,1)S(1)}, u32[]{:S(2)}, u32[]{:S(2)}) collective-permute-start(bf16[512,512]{1,0:T(8,128)(2,1)S(1)} %collective-permute-done.refs_6_), channel_id=1, source_target_pairs={{0,6},{2,0},{4,2},{6,4},{1,7},{3,1},{5,3},{7,5},{8,14},{10,8},{12,... | collective-permute-start | bytes 1572872 | tf_op jit(solution)/shard_map/ppermute | solution.py:15
  31.4 2.8 %collective-permute-start.5 = (bf16[512,256]{1,0:T(8,128)(2,1)S(1)}, bf16[512,256]{1,0:T(8,128)(2,1)S(1)}, u32[]{:S(2)}, u32[]{:S(2)}) collective-permute-start(bf16[512,256]{1,0:T(8,128)(2,1)S(1)} %collective-permute-done.1), channel_id=1, source_target_pairs={{0,24},{4,28},{8,16},{12,20},{18,10},{22,14},{26,2},{30,6},{1,25},... | collective-permute-start | bytes 786440 | tf_op jit(solution)/shard_map/ppermute | solution.py:31
  34.3 3.8 %collective-permute-done.5 = bf16[512,256]{1,0:T(8,128)(2,1)S(1)} collective-permute-done((bf16[512,256]{1,0:T(8,128)(2,1)S(1)}, bf16[512,256]{1,0:T(8,128)(2,1)S(1)}, u32[]{:S(2)}, u32[]{:S(2)}) %collective-permute-start.5) | collective-permute-done | bytes 262176 | tf_op jit(solution)/shard_map/ppermute | solution.py:31
  38.1 3.1 %collective-permute-done.3.refs_4_ = bf16[512,512]{1,0:T(8,128)(2,1)S(1)} collective-permute-done((bf16[512,512]{1,0:T(8,128)(2,1)S(1)}, bf16[512,512]{1,0:T(8,128)(2,1)S(1)}, u32[]{:S(2)}, u32[]{:S(2)}) %collective-permute-start.3) | collective-permute-done | bytes 524320 | tf_op jit(solution)/shard_map/ppermute | solution.py:15
  41.2 3.2 %collective-permute-done.2.refs_3_ = bf16[512,512]{1,0:T(8,128)(2,1)} collective-permute-done((bf16[512,512]{1,0:T(8,128)(2,1)S(1)}, bf16[512,512]{1,0:T(8,128)(2,1)}, u32[]{:S(2)}, u32[]{:S(2)}) %collective-permute-start.2) | collective-permute-done | bytes 524320 | tf_op jit(solution)/shard_map/ppermute | solution.py:15
  44.4 0.3 collective-permute-start.7
  44.7 1.2 collective-permute-start.8
  45.9 1.5 %collective-permute-start.6 = (bf16[512,512]{1,0:T(8,128)(2,1)}, bf16[512,512]{1,0:T(8,128)(2,1)S(1)}, u32[]{:S(2)}, u32[]{:S(2)}) collective-permute-start(bf16[512,512]{1,0:T(8,128)(2,1)} %collective-permute-done.2.refs_3_), channel_id=1, source_target_pairs={{0,8},{8,0},{1,9},{9,1},{2,10},{10,2},{3,11},{11,3},{4,12},{12,4},... | collective-permute-start | bytes 1572872 | tf_op jit(solution)/shard_map/ppermute | solution.py:15
  47.3 0.1 stack.31.refs_0_
  47.4 7.8 %collective-permute-done.7.refs_2_ = bf16[512,512]{1,0:T(8,128)(2,1)S(1)} collective-permute-done((bf16[512,512]{1,0:T(8,128)(2,1)S(1)}, bf16[512,512]{1,0:T(8,128)(2,1)S(1)}, u32[]{:S(2)}, u32[]{:S(2)}) %collective-permute-start.7) | collective-permute-done | bytes 524320 | tf_op jit(solution)/shard_map/ppermute | solution.py:15
  55.2 1.8 %collective-permute-done.8.refs_7_ = bf16[512,512]{1,0:T(8,128)(2,1)} collective-permute-done((bf16[512,512]{1,0:T(8,128)(2,1)}, bf16[512,512]{1,0:T(8,128)(2,1)}, u32[]{:S(2)}, u32[]{:S(2)}) %collective-permute-start.8) | collective-permute-done | bytes 524320 | tf_op jit(solution)/shard_map/ppermute | solution.py:15
  57.1 1.5 %collective-permute-start.10 = (bf16[512,256]{1,0:T(8,128)(2,1)S(1)}, bf16[512,256]{1,0:T(8,128)(2,1)S(1)}, u32[]{:S(2)}, u32[]{:S(2)}) collective-permute-start(bf16[512,256]{1,0:T(8,128)(2,1)S(1)} %broadcast_select_fusion.1), channel_id=1, source_target_pairs={{0,8},{8,0},{1,9},{9,1},{2,10},{10,2},{3,11},{11,3},{4,12},{12,4},... | collective-permute-start | bytes 786440 | tf_op jit(solution)/shard_map/ppermute | solution.py:15
  58.6 4.0 %all-gather.4.cloned.1.call-done.refs_8_ = bf16[2048,1024]{1,0:T(8,128)(2,1)} async-done(((bf16[512,1024]{1,0:T(8,128)(2,1)}), bf16[2048,1024]{1,0:T(8,128)(2,1)}) %all-gather.4.cloned.1.call-update) | async-done | bytes 4194320 | tf_op jit(solution)/shard_map/all_gather | solution.py:115
  62.6 7.8 %shard_map.55 = (bf16[512,512]{1,0:T(8,128)(2,1)S(1)}, f32[512,512]{1,0:T(8,128)}, f32[512,1024]{1,0:T(8,128)}) custom-call(s32[7]{0:T(128)S(1)} %stack.31.refs_0_, bf16[512,512]{1,0:T(8,128)(2,1)S(1)} %collective-permute-done.6.refs_1_, bf16[512,512]{1,0:T(8,128)(2,1)S(1)} %collective-permute-done.7.refs_2_, ...), custom_call_target="tpu_custom_call" | custom-call | flops 3758096384 | bytes 12582912 | tf_op jit(solution)/shard_map/pallas_call | solution.py:83
  70.5 0.8 pad_maximum_fusion.1
  71.3 0.0 all-gather.6.cloned.1.call-update
  71.4 1.8 %fusion = bf16[512,512]{1,0:T(8,128)(2,1)S(1)} fusion(bf16[512,512]{1,0:T(8,128)(2,1)S(1)} %collective-permute-done.9, f32[512,1024]{1,0:T(8,128)} %get-tuple-element.39, bf16[2048,1024]{1,0:T(8,128)(2,1)} %all-gather.4.cloned.1.call-done.refs_8_, s32[]{:T(128)S(6)} %select_n.83), kind=kOutput, calls=%fused_computation.4 | convolution fusion | flops 268959744 | bytes 2621444 | tf_op jit(solution)/shard_map/dot_general | solution.py:43
  73.2 2.2 %collective-permute-start.12 = (bf16[512,512]{1,0:T(8,128)(2,1)S(1)}, bf16[512,512]{1,0:T(8,128)(2,1)S(1)}, u32[]{:S(2)}, u32[]{:S(2)}) collective-permute-start(bf16[512,512]{1,0:T(8,128)(2,1)S(1)} %get-tuple-element.41), channel_id=1, source_target_pairs={{0,1},{1,0},{2,3},{3,2},{4,5},{5,4},{6,7},{7,6},{8,9},{9,8},{10,11... | collective-permute-start | bytes 1572872 | tf_op jit(solution)/shard_map/ppermute | solution.py:15
  75.4 0.1 collective-permute-start.13
  75.5 1.8 %convolution_add_fusion = f32[512,512]{1,0:T(8,128)S(1)} fusion(bf16[512,512]{1,0:T(8,128)(2,1)S(1)} %collective-permute-done.9, f32[512,1024]{1,0:T(8,128)} %get-tuple-element.39, bf16[2048,1024]{1,0:T(8,128)(2,1)} %all-gather.4.cloned.1.call-done.refs_8_, s32[]{:T(128)S(6)} %select_n.83), kind=kOutput, calls=%fused_computation.2 | convolution fusion | flops 268697600 | bytes 3145732 | tf_op jit(solution)/shard_map/dot_general | solution.py:43
  77.3 0.0 copy-start.4
  77.3 0.0 collective-permute-done.12
  77.3 0.3 collective-permute-done.13
  77.7 0.4 broadcast_select_fusion
  78.1 0.1 fusion.1
  78.1 2.0 %collective-permute-start.14 = (bf16[256,512]{1,0:T(8,128)(2,1)S(1)}, bf16[256,512]{1,0:T(8,128)(2,1)S(1)}, u32[]{:S(2)}, u32[]{:S(2)}) collective-permute-start(bf16[256,512]{1,0:T(8,128)(2,1)S(1)} %get-tuple-element.53), channel_id=1, source_target_pairs={{0,16},{16,0},{1,17},{17,1},{2,18},{18,2},{3,19},{19,3},{4,20},{20... | collective-permute-start | bytes 786440 | tf_op jit(solution)/shard_map/ppermute | solution.py:15
  80.1 0.1 convert_element_type.51
  80.2 7.0 %collective-permute-done.14 = bf16[256,512]{1,0:T(8,128)(2,1)S(1)} collective-permute-done((bf16[256,512]{1,0:T(8,128)(2,1)S(1)}, bf16[256,512]{1,0:T(8,128)(2,1)S(1)}, u32[]{:S(2)}, u32[]{:S(2)}) %collective-permute-start.14) | collective-permute-done | bytes 262176 | tf_op jit(solution)/shard_map/ppermute | solution.py:15
  87.2 2.0 %collective-permute-start.15 = (bf16[256,512]{1,0:T(8,128)(2,1)S(1)}, bf16[256,512]{1,0:T(8,128)(2,1)S(1)}, u32[]{:S(2)}, u32[]{:S(2)}) collective-permute-start(bf16[256,512]{1,0:T(8,128)(2,1)S(1)} %get-tuple-element.46), channel_id=1, source_target_pairs={{0,16},{16,0},{1,17},{17,1},{2,18},{18,2},{3,19},{19,3},{4,20},{20... | collective-permute-start | bytes 786440 | tf_op jit(solution)/shard_map/ppermute | solution.py:15
  89.2 0.1 fusion.3
  89.3 2.8 %collective-permute-start.16 = (bf16[256,512]{1,0:T(8,128)(2,1)S(1)}, bf16[256,512]{1,0:T(8,128)(2,1)S(1)}, u32[]{:S(2)}, u32[]{:S(2)}) collective-permute-start(bf16[256,512]{1,0:T(8,128)(2,1)S(1)} %fusion.3), channel_id=1, source_target_pairs={{0,96},{32,0},{64,32},{96,64},{1,97},{33,1},{65,33},{97,65},{2,98}... | collective-permute-start | bytes 786440 | tf_op jit(solution)/shard_map/ppermute | solution.py:15
  92.1 3.2 %collective-permute-done.15 = bf16[256,512]{1,0:T(8,128)(2,1)S(1)} collective-permute-done((bf16[256,512]{1,0:T(8,128)(2,1)S(1)}, bf16[256,512]{1,0:T(8,128)(2,1)S(1)}, u32[]{:S(2)}, u32[]{:S(2)}) %collective-permute-start.15) | collective-permute-done | bytes 262176 | tf_op jit(solution)/shard_map/ppermute | solution.py:15
  95.3 1.0 collective-permute-done.16
  96.3 0.1 fusion.2
  96.4 3.6 %collective-permute-start.19 = (bf16[256,512]{1,0:T(8,128)(2,1)S(1)}, bf16[256,512]{1,0:T(8,128)(2,1)S(1)}, u32[]{:S(2)}, u32[]{:S(2)}) collective-permute-start(bf16[256,512]{1,0:T(8,128)(2,1)S(1)} %fusion.2), channel_id=1, source_target_pairs={{0,96},{32,0},{64,32},{96,64},{1,97},{33,1},{65,33},{97,65},{2,98}... | collective-permute-start | bytes 786440 | tf_op jit(solution)/shard_map/ppermute | solution.py:15
  100.0 3.3 %collective-permute-done.19 = bf16[256,512]{1,0:T(8,128)(2,1)S(1)} collective-permute-done((bf16[256,512]{1,0:T(8,128)(2,1)S(1)}, bf16[256,512]{1,0:T(8,128)(2,1)S(1)}, u32[]{:S(2)}, u32[]{:S(2)}) %collective-permute-start.19) | collective-permute-done | bytes 262176 | tf_op jit(solution)/shard_map/ppermute | solution.py:15
  103.3 3.5 %collective-permute-start.21 = (bf16[256,512]{1,0:T(8,128)(2,1)S(1)}, bf16[256,512]{1,0:T(8,128)(2,1)S(1)}, u32[]{:S(2)}, u32[]{:S(2)}) collective-permute-start(bf16[256,512]{1,0:T(8,128)(2,1)S(1)} %collective-permute-done.19), channel_id=1, source_target_pairs={{0,96},{32,0},{64,32},{96,64},{1,97},{33,1},{65,33},{97,65},{2,98}... | collective-permute-start | bytes 786440 | tf_op jit(solution)/shard_map/ppermute | solution.py:15
  106.8 1.6 %fusion.16 = f32[2,512,512]{2,1,0:T(8,128)S(1)} fusion(bf16[8,1024,256]{2,1,0:T(8,128)(2,1)} %bitcast.44, s32[]{:T(128)S(6)} %select_n.89, s32[]{:T(128)S(6)} %select_n.86, bf16[256,512]{1,0:T(8,128)(2,1)S(1)} %fusion.2), kind=kOutput, calls=%fused_computation.30 | convolution fusion | flops 268435456 | bytes 2883592 | tf_op jit(solution)/shard_map/dot_general | solution.py:43
  108.4 1.5 %fusion.18 = f32[2,512,512]{2,1,0:T(8,128)S(1)} fusion(bf16[8,1024,256]{2,1,0:T(8,128)(2,1)} %bitcast.45, s32[]{:T(128)S(6)} %select_n.85, s32[]{:T(128)S(6)} %select_n.86, bf16[256,512]{1,0:T(8,128)(2,1)S(1)} %fusion.3), kind=kOutput, calls=%fused_computation.32 | convolution fusion | flops 268435456 | bytes 2883592 | tf_op jit(solution)/shard_map/dot_general | solution.py:43
  109.9 0.4 fusion.10
  110.4 0.4 fusion.8
  110.8 0.4 fusion.14
  111.2 0.4 fusion.12
  111.7 0.4 fusion.5
  112.1 0.0 collective-permute-done.20
  112.2 0.9 add_convert_fusion
  113.0 23.8 %all_to_all.9 = bf16[32,32,512]{2,1,0:T(8,128)(2,1)S(1)} all-to-all(bf16[32,32,512]{2,1,0:T(8,128)(2,1)S(1)} %bitcast.40), channel_id=1, replica_groups=mesh['y'=4,'xh'=2,'xl'=2,'z'=4,'core'=2] {'xh','xl','z','core'}, dimensions={0} | all-to-all | bytes 2097152 | tf_op jit(solution)/shard_map/all_to_all | solution.py:167
  136.8 0.2 convert_reduce_fusion
  137.0 0.1 copy.7
  137.1 0.9 add_convert_fusion.1
  (30 shorter events, 0.1 us)
Async XLA Ops:
  6.5 56.1 %all-gather.4.cloned.1.call-start = ((), (), s32[]{:S(2)}) async-start(), calls=%async_computation.1 | async-start | bytes 5242880 | tf_op jit(solution)/shard_map/all_gather | solution.py:115
  7.8 4.3 %copy-start.2 = (bf16[512,512]{1,0:T(8,128)(2,1)S(1)}, bf16[512,512]{1,0:T(8,128)(2,1)}, u32[]{:S(2)}) copy-start(bf16[512,512]{1,0:T(8,128)(2,1)} %param.6) | copy-start | bytes 1572868
  7.8 4.3 %copy-start.3 = (bf16[512,512]{1,0:T(8,128)(2,1)S(1)}, bf16[512,512]{1,0:T(8,128)(2,1)}, u32[]{:S(2)}) copy-start(bf16[512,512]{1,0:T(8,128)(2,1)} %param.5) | copy-start | bytes 1572868
  7.8 3.0 %collective-permute-start.11 = (bf16[512,512]{1,0:T(8,128)(2,1)S(1)}, bf16[512,512]{1,0:T(8,128)(2,1)S(1)}, u32[]{:S(2)}, u32[]{:S(2)}) collective-permute-start(bf16[512,512]{1,0:T(8,128)(2,1)S(1)} %get-tuple-element.55), channel_id=1, source_target_pairs={{0,1},{1,0},{2,3},{3,2},{4,5},{5,4},{6,7},{7,6},{8,9},{9,8},{10,11... | collective-permute-start | bytes 1572872 | tf_op jit(solution)/shard_map/ppermute | solution.py:15
  10.9 2.8 %copy-start.5 = (bf16[512,256]{1,0:T(8,128)(2,1)S(1)}, bf16[512,256]{1,0:T(8,128)(2,1)}, u32[]{:S(2)}) copy-start(bf16[512,256]{1,0:T(8,128)(2,1)} %param.8) | copy-start | bytes 786436
  12.0 94.8 %all-gather.6.cloned.1.call-start = ((), (), s32[]{:S(2)}) async-start(), calls=%async_computation.2 | async-start | bytes 4718592 | tf_op jit(solution)/shard_map/all_gather | solution.py:133
  12.3 13.2 %collective-permute-start = (bf16[512,512]{1,0:T(8,128)(2,1)S(1)}, bf16[512,512]{1,0:T(8,128)(2,1)S(1)}, u32[]{:S(2)}, u32[]{:S(2)}) collective-permute-start(bf16[512,512]{1,0:T(8,128)(2,1)S(1)} %subtract_convert_fusion), channel_id=1, source_target_pairs={{0,8},{2,24},{4,12},{6,28},{8,0},{10,16},{12,4},{14,20},{16,10},{1... | collective-permute-start | bytes 1572872 | tf_op jit(solution)/shard_map/ppermute | solution.py:25
  13.6 10.0 %collective-permute-start.1 = (bf16[512,256]{1,0:T(8,128)(2,1)S(1)}, bf16[512,256]{1,0:T(8,128)(2,1)S(1)}, u32[]{:S(2)}, u32[]{:S(2)}) collective-permute-start(bf16[512,256]{1,0:T(8,128)(2,1)S(1)} %copy-done.5), channel_id=1, source_target_pairs={{2,8},{6,12},{10,0},{14,4},{16,26},{20,30},{24,18},{28,22},{3,9},{... | collective-permute-start | bytes 786440 | tf_op jit(solution)/shard_map/ppermute | solution.py:31
  25.5 37.2 %copy-start.6 = (bf16[512,512]{1,0:T(8,128)(2,1)}, bf16[512,512]{1,0:T(8,128)(2,1)S(1)}, u32[]{:S(2)}) copy-start(bf16[512,512]{1,0:T(8,128)(2,1)S(1)} %collective-permute-done.refs_6_) | copy-start | bytes 1572868
  25.5 12.6 %collective-permute-start.4 = (bf16[512,512]{1,0:T(8,128)(2,1)S(1)}, bf16[512,512]{1,0:T(8,128)(2,1)S(1)}, u32[]{:S(2)}, u32[]{:S(2)}) collective-permute-start(bf16[512,512]{1,0:T(8,128)(2,1)S(1)} %collective-permute-done.refs_6_), channel_id=1, source_target_pairs={{0,8},{8,0},{1,9},{9,1},{2,10},{10,2},{3,11},{11,3},{4,12},{12,4},... | collective-permute-start | bytes 1572872 | tf_op jit(solution)/shard_map/ppermute | solution.py:15
  26.8 14.4 %collective-permute-start.3 = (bf16[512,512]{1,0:T(8,128)(2,1)S(1)}, bf16[512,512]{1,0:T(8,128)(2,1)S(1)}, u32[]{:S(2)}, u32[]{:S(2)}) collective-permute-start(bf16[512,512]{1,0:T(8,128)(2,1)S(1)} %collective-permute-done.refs_6_), channel_id=1, source_target_pairs={{0,6},{2,0},{4,2},{6,4},{1,7},{3,1},{5,3},{7,5},{8,14},{10,8},{12,... | collective-permute-start | bytes 1572872 | tf_op jit(solution)/shard_map/ppermute | solution.py:15
  31.4 13.0 %collective-permute-start.2 = (bf16[512,512]{1,0:T(8,128)(2,1)S(1)}, bf16[512,512]{1,0:T(8,128)(2,1)}, u32[]{:S(2)}, u32[]{:S(2)}) collective-permute-start(bf16[512,512]{1,0:T(8,128)(2,1)S(1)} %collective-permute-done.refs_6_), channel_id=1, source_target_pairs={{0,2},{2,4},{4,6},{6,0},{1,3},{3,5},{5,7},{7,1},{8,10},{10,12},{12... | collective-permute-start | bytes 1572872 | tf_op jit(solution)/shard_map/ppermute | solution.py:15
  31.4 6.6 %collective-permute-start.5 = (bf16[512,256]{1,0:T(8,128)(2,1)S(1)}, bf16[512,256]{1,0:T(8,128)(2,1)S(1)}, u32[]{:S(2)}, u32[]{:S(2)}) collective-permute-start(bf16[512,256]{1,0:T(8,128)(2,1)S(1)} %collective-permute-done.1), channel_id=1, source_target_pairs={{0,24},{4,28},{8,16},{12,20},{18,10},{22,14},{26,2},{30,6},{1,25},... | collective-permute-start | bytes 786440 | tf_op jit(solution)/shard_map/ppermute | solution.py:31
  38.1 19.0 %copy-start.7 = (bf16[512,512]{1,0:T(8,128)(2,1)}, bf16[512,512]{1,0:T(8,128)(2,1)S(1)}, u32[]{:S(2)}) copy-start(bf16[512,512]{1,0:T(8,128)(2,1)S(1)} %collective-permute-done.4.refs_5_) | copy-start | bytes 1572868
  41.2 6.2 %copy-start.8 = (bf16[512,512]{1,0:T(8,128)(2,1)}, bf16[512,512]{1,0:T(8,128)(2,1)S(1)}, u32[]{:S(2)}) copy-start(bf16[512,512]{1,0:T(8,128)(2,1)S(1)} %collective-permute-done.3.refs_4_) | copy-start | bytes 1572868
  44.4 10.8 %collective-permute-start.7 = (bf16[512,512]{1,0:T(8,128)(2,1)S(1)}, bf16[512,512]{1,0:T(8,128)(2,1)S(1)}, u32[]{:S(2)}, u32[]{:S(2)}) collective-permute-start(bf16[512,512]{1,0:T(8,128)(2,1)S(1)} %collective-permute-done.4.refs_5_), channel_id=1, source_target_pairs={{0,6},{2,0},{4,2},{6,4},{1,7},{3,1},{5,3},{7,5},{8,14},{10,8},{12,... | collective-permute-start | bytes 1572872 | tf_op jit(solution)/shard_map/ppermute | solution.py:15
  44.7 12.4 %collective-permute-start.8 = (bf16[512,512]{1,0:T(8,128)(2,1)}, bf16[512,512]{1,0:T(8,128)(2,1)}, u32[]{:S(2)}, u32[]{:S(2)}) collective-permute-start(bf16[512,512]{1,0:T(8,128)(2,1)} %collective-permute-done.2.refs_3_), channel_id=1, source_target_pairs={{0,2},{2,4},{4,6},{6,0},{1,3},{3,5},{5,7},{7,1},{8,10},{10,12},{12... | collective-permute-start | bytes 1572872 | tf_op jit(solution)/shard_map/ppermute | solution.py:15
  45.9 11.2 %collective-permute-start.6 = (bf16[512,512]{1,0:T(8,128)(2,1)}, bf16[512,512]{1,0:T(8,128)(2,1)S(1)}, u32[]{:S(2)}, u32[]{:S(2)}) collective-permute-start(bf16[512,512]{1,0:T(8,128)(2,1)} %collective-permute-done.2.refs_3_), channel_id=1, source_target_pairs={{0,8},{8,0},{1,9},{9,1},{2,10},{10,2},{3,11},{11,3},{4,12},{12,4},... | collective-permute-start | bytes 1572872 | tf_op jit(solution)/shard_map/ppermute | solution.py:15
  57.1 13.4 %collective-permute-start.9 = (bf16[512,512]{1,0:T(8,128)(2,1)S(1)}, bf16[512,512]{1,0:T(8,128)(2,1)S(1)}, u32[]{:S(2)}, u32[]{:S(2)}) collective-permute-start(bf16[512,512]{1,0:T(8,128)(2,1)S(1)} %collective-permute-done.6.refs_1_), channel_id=1, source_target_pairs={{0,2},{2,4},{4,6},{6,0},{1,3},{3,5},{5,7},{7,1},{8,10},{10,12},{12... | collective-permute-start | bytes 1572872 | tf_op jit(solution)/shard_map/ppermute | solution.py:15
  57.1 13.4 %collective-permute-start.10 = (bf16[512,256]{1,0:T(8,128)(2,1)S(1)}, bf16[512,256]{1,0:T(8,128)(2,1)S(1)}, u32[]{:S(2)}, u32[]{:S(2)}) collective-permute-start(bf16[512,256]{1,0:T(8,128)(2,1)S(1)} %broadcast_select_fusion.1), channel_id=1, source_target_pairs={{0,8},{8,0},{1,9},{9,1},{2,10},{10,2},{3,11},{11,3},{4,12},{12,4},... | collective-permute-start | bytes 786440 | tf_op jit(solution)/shard_map/ppermute | solution.py:15
  73.2 4.5 %copy-start.1 = (f32[512,512]{1,0:T(8,128)S(1)}, f32[512,512]{1,0:T(8,128)}, u32[]{:S(2)}) copy-start(f32[512,512]{1,0:T(8,128)} %get-tuple-element.37) | copy-start | bytes 3145732
  73.2 4.1 %collective-permute-start.12 = (bf16[512,512]{1,0:T(8,128)(2,1)S(1)}, bf16[512,512]{1,0:T(8,128)(2,1)S(1)}, u32[]{:S(2)}, u32[]{:S(2)}) collective-permute-start(bf16[512,512]{1,0:T(8,128)(2,1)S(1)} %get-tuple-element.41), channel_id=1, source_target_pairs={{0,1},{1,0},{2,3},{3,2},{4,5},{5,4},{6,7},{7,6},{8,9},{9,8},{10,11... | collective-permute-start | bytes 1572872 | tf_op jit(solution)/shard_map/ppermute | solution.py:15
  75.4 2.3 %collective-permute-start.13 = (bf16[512,512]{1,0:T(8,128)(2,1)S(1)}, bf16[512,512]{1,0:T(8,128)(2,1)S(1)}, u32[]{:S(2)}, u32[]{:S(2)}) collective-permute-start(bf16[512,512]{1,0:T(8,128)(2,1)S(1)} %fusion), channel_id=1, source_target_pairs={{0,1},{1,0},{2,3},{3,2},{4,5},{5,4},{6,7},{7,6},{8,9},{9,8},{10,11... | collective-permute-start | bytes 1572872 | tf_op jit(solution)/shard_map/ppermute | solution.py:15
  77.3 2.8 %copy-start.4 = (bf16[32,8192]{1,0:T(8,128)(2,1)S(1)}, bf16[32,8192]{1,0:T(8,128)(2,1)}, u32[]{:S(2)}) copy-start(bf16[32,8192]{1,0:T(8,128)(2,1)} %param.9) | copy-start | bytes 1572868
  78.1 9.1 %collective-permute-start.14 = (bf16[256,512]{1,0:T(8,128)(2,1)S(1)}, bf16[256,512]{1,0:T(8,128)(2,1)S(1)}, u32[]{:S(2)}, u32[]{:S(2)}) collective-permute-start(bf16[256,512]{1,0:T(8,128)(2,1)S(1)} %get-tuple-element.53), channel_id=1, source_target_pairs={{0,16},{16,0},{1,17},{17,1},{2,18},{18,2},{3,19},{19,3},{4,20},{20... | collective-permute-start | bytes 786440 | tf_op jit(solution)/shard_map/ppermute | solution.py:15
  87.2 8.1 %collective-permute-start.15 = (bf16[256,512]{1,0:T(8,128)(2,1)S(1)}, bf16[256,512]{1,0:T(8,128)(2,1)S(1)}, u32[]{:S(2)}, u32[]{:S(2)}) collective-permute-start(bf16[256,512]{1,0:T(8,128)(2,1)S(1)} %get-tuple-element.46), channel_id=1, source_target_pairs={{0,16},{16,0},{1,17},{17,1},{2,18},{18,2},{3,19},{19,3},{4,20},{20... | collective-permute-start | bytes 786440 | tf_op jit(solution)/shard_map/ppermute | solution.py:15
  89.3 7.0 %collective-permute-start.16 = (bf16[256,512]{1,0:T(8,128)(2,1)S(1)}, bf16[256,512]{1,0:T(8,128)(2,1)S(1)}, u32[]{:S(2)}, u32[]{:S(2)}) collective-permute-start(bf16[256,512]{1,0:T(8,128)(2,1)S(1)} %fusion.3), channel_id=1, source_target_pairs={{0,96},{32,0},{64,32},{96,64},{1,97},{33,1},{65,33},{97,65},{2,98}... | collective-permute-start | bytes 786440 | tf_op jit(solution)/shard_map/ppermute | solution.py:15
  92.1 7.9 %collective-permute-start.17 = (bf16[256,512]{1,0:T(8,128)(2,1)S(1)}, bf16[256,512]{1,0:T(8,128)(2,1)S(1)}, u32[]{:S(2)}, u32[]{:S(2)}) collective-permute-start(bf16[256,512]{1,0:T(8,128)(2,1)S(1)} %fusion.3), channel_id=1, source_target_pairs={{0,32},{32,64},{64,96},{96,0},{1,33},{33,65},{65,97},{97,1},{2,34}... | collective-permute-start | bytes 786440 | tf_op jit(solution)/shard_map/ppermute | solution.py:15
  96.4 6.9 %collective-permute-start.19 = (bf16[256,512]{1,0:T(8,128)(2,1)S(1)}, bf16[256,512]{1,0:T(8,128)(2,1)S(1)}, u32[]{:S(2)}, u32[]{:S(2)}) collective-permute-start(bf16[256,512]{1,0:T(8,128)(2,1)S(1)} %fusion.2), channel_id=1, source_target_pairs={{0,96},{32,0},{64,32},{96,64},{1,97},{33,1},{65,33},{97,65},{2,98}... | collective-permute-start | bytes 786440 | tf_op jit(solution)/shard_map/ppermute | solution.py:15
  100.0 11.2 %collective-permute-start.18 = (bf16[256,512]{1,0:T(8,128)(2,1)S(1)}, bf16[256,512]{1,0:T(8,128)(2,1)S(1)}, u32[]{:S(2)}, u32[]{:S(2)}) collective-permute-start(bf16[256,512]{1,0:T(8,128)(2,1)S(1)} %fusion.2), channel_id=1, source_target_pairs={{0,32},{32,64},{64,96},{96,0},{1,33},{33,65},{65,97},{97,1},{2,34}... | collective-permute-start | bytes 786440 | tf_op jit(solution)/shard_map/ppermute | solution.py:15
  100.0 12.1 %collective-permute-start.20 = (bf16[256,512]{1,0:T(8,128)(2,1)S(1)}, bf16[256,512]{1,0:T(8,128)(2,1)S(1)}, u32[]{:S(2)}, u32[]{:S(2)}) collective-permute-start(bf16[256,512]{1,0:T(8,128)(2,1)S(1)} %collective-permute-done.17), channel_id=1, source_target_pairs={{0,32},{32,64},{64,96},{96,0},{1,33},{33,65},{65,97},{97,1},{2,34}... | collective-permute-start | bytes 786440 | tf_op jit(solution)/shard_map/ppermute | solution.py:15
  103.3 8.3 %collective-permute-start.21 = (bf16[256,512]{1,0:T(8,128)(2,1)S(1)}, bf16[256,512]{1,0:T(8,128)(2,1)S(1)}, u32[]{:S(2)}, u32[]{:S(2)}) collective-permute-start(bf16[256,512]{1,0:T(8,128)(2,1)S(1)} %collective-permute-done.19), channel_id=1, source_target_pairs={{0,96},{32,0},{64,32},{96,64},{1,97},{33,1},{65,33},{97,65},{2,98}... | collective-permute-start | bytes 786440 | tf_op jit(solution)/shard_map/ppermute | solution.py:15
  106.8 3.1 %copy-start = (bf16[8192,256]{1,0:T(8,128)(2,1)S(1)}, bf16[8192,256]{1,0:T(8,128)(2,1)}, u32[]{:S(2)}) copy-start(bf16[8192,256]{1,0:T(8,128)(2,1)} %all-gather.6.cloned.1.call-done) | copy-start | bytes 12582916
Sparse Core Ops, SparseCore 0:
  12.2 50.4 all-gather.3
  71.5 33.0 all-gather.5
